TPU v7x, 32 devices: a whole 2x2x4 slice. The times are simulated.
32 devices in a mesh: face: 4 (over z), blk: 8 (over y, x, core).
Axes of the slice: x: 2, y: 2, z: 4, core: 2. Of those that a mesh axis runs over, the one named last changes fastest.
Arguments:
- air_state: float32 [3, 16, 64, 1024], P(None, None, 'face', 'blk'), may hold values from -6 to 6
- air_wind: float32 [2, 16, 64, 1024], P(None, None, 'face', 'blk'), may hold values from -4 to 4
- jacobian: float32 [64, 1024], P('face', 'blk'), may hold values from 0.5 to 2
- land_area: float32 [64, 1024], P('face', 'blk'), may hold values from 0.1 to 1
- xgrid_rows: int32 [32, 8, 128], P(('face', 'blk')), may hold values from 0 to 2047
- tracers: float32 [2, 16, 65536], P(None, None, ('face', 'blk')), may hold values from -6 to 6
- edge_coef: float32 [6, 65536], P(None, ('face', 'blk')), may hold values from 0.02 to 0.14
- neighbours: int32 [6, 65536], P(None, ('face', 'blk')), may hold values from 0 to 2303
- vert_rate: float32 [65536], P(('face', 'blk')), may hold values from 0.05 to 0.2
- ocean_area: float32 [65536], P(('face', 'blk')), may hold values from 0.5 to 2
- send_list: int32 [32, 256], P(('face', 'blk')), may hold values from 0 to 2047
- xgrid_cols: int32 [32, 8, 128], P(('face', 'blk')), may hold values from 0 to 2047
- xgrid_weights: float32 [32, 8, 128], P(('face', 'blk')), may hold values from 0 to 1, as said below
Outputs:
- air_final: float32 [3, 16, 64, 1024], P(None, None, 'face', 'blk')
- ocean_final: float32 [2, 16, 65536], P(None, None, ('face', 'blk'))
Inputs may be any that keep to these rules, and one draw needn't show every extreme that they name: `xgrid_weights`: in every block of 128 slots the nonzero weights, each at least 0.1, come first and zeros fill the rest; in every draw some blocks of every device are completely full.
All inputs are finite; a program needn't handle non-finite values.
Results may differ from a plain program's by a relative error of at most 0.00016.
Values sent between devices are 32-bit elements; how exact they have to be, the bound alone decides.
No kernel may reach another device: no remote copies, remote signals or barrier semaphores. Data moves between devices by JAX's collectives and lax.ppermute only.
A program may use at most 64 MiB of HBM per device.

v0:
```python
import jax
import jax.numpy as jnp
import numpy as np
from jax import lax
from jax.sharding import PartitionSpec as P

GLL = 4
SUBSTEPS = 2


deriv_table = [
    [-3.0, 4.045084971874737, -1.545084971874737, 0.5],
    [-0.8090169943749475, 0.0, 1.118033988749895, -0.30901699437494745],
    [0.30901699437494745, -1.118033988749895, 0.0, 0.8090169943749475],
    [-0.5, 1.545084971874737, -4.045084971874737, 3.0],
]
time_step = 0.05
relax_rate = 0.3
flux_gain = 0.2


def with_halo(block, sides, width):
    for axis, dim in sides:
        count = lax.axis_size(axis)
        forward = [(i, i + 1) for i in range(count - 1)]
        forward.append((count - 1, 0))
        backward = [(target, source) for source, target in forward]
        low = lax.ppermute(
            lax.slice_in_dim(block, block.shape[dim] - width, None, axis=dim), axis, forward
        )
        high = lax.ppermute(lax.slice_in_dim(block, 0, width, axis=dim), axis, backward)
        block = jnp.concatenate([low, block, high], axis=dim)
    return block


def along_first(field):
    planes, xsize, ysize = field.shape
    blocks = np.kron(np.eye(xsize // GLL), np.array(deriv_table))
    table = jnp.asarray(blocks, jnp.float32)
    return jnp.einsum("ik,aky->aiy", table, field, precision=lax.Precision.HIGHEST)


def along_second(field):
    planes, xsize, ysize = field.shape
    width = min(ysize, 128)
    blocks = np.kron(np.eye(width // GLL), np.array(deriv_table).T)
    table = jnp.asarray(blocks, jnp.float32)
    shaped = field.reshape(planes, xsize, ysize // width, width)
    result = jnp.einsum("axek,ki->axei", shaped, table, precision=lax.Precision.HIGHEST)
    return result.reshape(planes, xsize, ysize)


def sum_rows(widened):
    xsize = widened.shape[1] - 2
    x_pos = jnp.arange(xsize, dtype=jnp.int32) % GLL
    first_row = (x_pos == 0)[:, None]
    last_row = (x_pos == GLL - 1)[:, None]
    return (
        widened[:, 1:-1]
        + jnp.where(first_row, widened[:, :-2], 0.0)
        + jnp.where(last_row, widened[:, 2:], 0.0)
    )


def sum_cols(widened):
    ysize = widened.shape[2] - 2
    y_pos = jnp.arange(ysize, dtype=jnp.int32) % GLL
    first_col = y_pos == 0
    last_col = y_pos == GLL - 1
    return (
        widened[:, :, 1:-1]
        + jnp.where(first_col, widened[:, :, :-2], 0.0)
        + jnp.where(last_col, widened[:, :, 2:], 0.0)
    )


def edge_average(moved, mass_map):
    weighted = jnp.concatenate([mass_map[None] * moved, mass_map[None]], axis=0)
    widened = with_halo(weighted, (("face", 1), ("blk", 2)), 1)
    summed = sum_rows(sum_cols(widened))
    return summed[:-1] / summed[-1:]


def body(
    air_state,
    air_wind,
    jacobian,
    land_area,
    xgrid_rows,
    tracers,
    edge_coef,
    neighbours,
    vert_rate,
    ocean_area,
    send_list,
    xgrid_cols,
    xgrid_weights,
):
    field_count, levels, x_points, y_points = air_state.shape
    planes = field_count * levels
    cell_count = tracers.shape[2]
    send_ids = send_list[0]
    rim_width = send_ids.shape[0] // 2
    outgoing = tracers[:, :, send_ids]
    received = with_halo(outgoing, (("blk", 2),), rim_width)
    extended = jnp.concatenate(
        [tracers, received[:, :, :rim_width], received[:, :, 3 * rim_width :]], axis=2
    )
    adjacent = extended[:, :, neighbours]
    lateral = jnp.sum(edge_coef[None, None] * (adjacent - tracers[:, :, None]), axis=2)
    upper_level = jnp.concatenate([tracers[:, :1], tracers[:, :-1]], axis=1)
    lower_level = jnp.concatenate([tracers[:, 1:], tracers[:, -1:]], axis=1)
    vertical = vert_rate * (upper_level - tracers + (lower_level - tracers))
    ocean_partial = tracers + lateral + vertical
    cell_ids = xgrid_cols[0]
    weights = xgrid_weights[0]
    point_ids = xgrid_rows[0].reshape(-1)
    surface_at = tracers[0, 0][cell_ids]
    payload = jnp.stack([weights * surface_at, weights])
    arrived = lax.all_to_all(payload, "blk", split_axis=1, concat_axis=1, tiled=True)
    sums = (
        jnp.zeros((2, x_points * y_points), jnp.float32)
        .at[:, point_ids]
        .add(arrived.reshape(2, -1))
    )
    heat_map = sums[0].reshape(x_points, y_points)
    frac_map = sums[1].reshape(x_points, y_points)
    t_surf = (heat_map + land_area * air_state[0, 0]) / (frac_map + land_area)
    x_pos = jnp.arange(x_points, dtype=jnp.int32) % GLL
    y_pos = jnp.arange(y_points, dtype=jnp.int32) % GLL
    x_weight = jnp.where((x_pos == 0) | (x_pos == GLL - 1), 1.0 / 6.0, 5.0 / 6.0).astype(
        jnp.float32
    )
    y_weight = jnp.where((y_pos == 0) | (y_pos == GLL - 1), 1.0 / 6.0, 5.0 / 6.0).astype(
        jnp.float32
    )
    mass_map = x_weight[:, None] * y_weight[None, :] * jacobian
    fields = air_state
    for substep in range(SUBSTEPS):
        flat_fields = fields.reshape(planes, x_points, y_points)
        slope_first = along_first(flat_fields).reshape(field_count, levels, x_points, y_points)
        slope_second = along_second(flat_fields).reshape(field_count, levels, x_points, y_points)
        tendency = -(air_wind[0] * slope_first + air_wind[1] * slope_second)
        moved = fields + time_step * tendency
        moved = moved.at[0, 0].add(relax_rate * (t_surf - fields[0, 0]))
        fields = edge_average(moved.reshape(planes, x_points, y_points), mass_map).reshape(
            field_count, levels, x_points, y_points
        )
    sea_flux = (fields[0, 0] - t_surf).reshape(-1)
    flux_slots = sea_flux[xgrid_rows[0]]
    incoming = lax.all_to_all(flux_slots, "blk", split_axis=0, concat_axis=0, tiled=True)
    inflow = (
        jnp.zeros((cell_count,), jnp.float32)
        .at[cell_ids.reshape(-1)]
        .add((weights * incoming).reshape(-1))
    )
    ocean_final = ocean_partial.at[0, 0].add(flux_gain * inflow / ocean_area)
    return (fields, ocean_final)


def solution(mesh):
    return jax.shard_map(
        body,
        mesh=mesh,
        in_specs=(
            P(None, None, "face", "blk"),
            P(None, None, "face", "blk"),
            P("face", "blk"),
            P("face", "blk"),
            P(("face", "blk"), None, None),
            P(None, None, ("face", "blk")),
            P(None, ("face", "blk")),
            P(None, ("face", "blk")),
            P(("face", "blk")),
            P(("face", "blk")),
            P(("face", "blk"), None),
            P(("face", "blk"), None, None),
            P(("face", "blk"), None, None),
        ),
        out_specs=(P(None, None, "face", "blk"), P(None, None, ("face", "blk"))),
        check_vma=False,
    )
```

profile of v0, /device:TPU:0, one launch (start us, length us, event | category | flops | bytes accessed | tf_op | source)
XLA Modules:
  0.0 201.9 jit_solution(11945700929462604183)
XLA Ops:
  0.7 0.9 slice.198
  1.5 0.7 fusion.57
  2.2 6.1 %gather_fusion = f32[1024]{0:T(1024)S(1)} fusion(f32[2048]{0:T(1024)S(1)} %bitcast.133, s32[1024]{0:T(1024)S(1)} %fusion.57), kind=kCustom, calls=%fused_computation | custom fusion | bytes 12288 | tf_op jit(solution)/shard_map/gather | solution.py:118
  8.5 0.6 copy.67
  9.1 5.2 %all-to-all-start = ((f32[2,8,128]{2,0,1:T(2,128)}), f32[2,8,128]{2,0,1:T(2,128)}, u32[]{:S(2)}, u32[]{:S(2)}) async-start(f32[2,8,128]{2,0,1:T(2,128)} %copy.67), calls=%async_computation | async-start | bytes 16384 | tf_op jit(solution)/shard_map/all_to_all | solution.py:120
  14.3 1.0 copy.78
  15.3 1.0 gather_fusion.1
  16.3 0.7 fusion.65
  17.0 0.5 collective-permute-start.8
  17.5 2.2 %collective-permute-start.9 = (f32[2,16,128]{1,0,2:T(2,128)}, f32[2,16,128]{1,0,2:T(2,128)}, u32[]{:S(2)}, u32[]{:S(2)}) collective-permute-start(f32[2,16,128]{1,0,2:T(2,128)} %get-tuple-element.51), channel_id=1, source_target_pairs={{1,0},{2,1},{3,2},{4,3},{5,4},{6,5},{7,6},{0,7},{9,8},{10,9},{11,1... | collective-permute-start | bytes 49160 | tf_op jit(solution)/shard_map/ppermute | solution.py:31
  19.9 0.8 fusion.66
  20.7 0.6 fusion.67
  21.4 1.3 fusion.59
  22.7 1.3 compare_select_fusion.2
  24.0 0.6 broadcast_clamp_fusion
  24.6 1.1 fusion.68
  25.8 1.2 fusion.6
  27.0 0.6 compare_select_fusion.1
  27.6 1.7 copy.68
  29.3 6.7 %scatter_custom_fusion = f32[2,2048]{0,1:T(8,128)S(1)} fusion(s32[1024]{0:T(1024)} %bitcast.149, f32[1024,2]{1,0:T(8,128)} %copy.68, f32[]{:T(128)} %constant.146.clone.1), kind=kCustom, calls=%fused_computation.53 | custom fusion | flops 2048 | bytes 16896 | tf_op jit(solution)/shard_map/scatter-add | solution.py:124
  36.0 0.9 slice_reduce_fusion.1
  36.9 1.3 fusion.53
  38.3 1.0 bitcast_multiply_fusion.1
  39.3 1.9 collective-permute-start
  41.2 2.1 %collective-permute-start.1 = (f32[49,1,128]{2,1,0:T(1,128)S(1)}, f32[49,1,128]{2,1,0:T(1,128)S(1)}, u32[]{:S(2)}, u32[]{:S(2)}) collective-permute-start(f32[49,1,128]{2,1,0:T(1,128)S(1)} %get-tuple-element.49), channel_id=1, source_target_pairs={{8,0},{16,8},{24,16},{0,24},{9,1},{17,9},{25,17},{1,25},{10,2},{18... | collective-permute-start | bytes 75272 | tf_op jit(solution)/shard_map/ppermute | solution.py:31
  43.3 0.6 broadcast_compare_fusion
  43.9 1.3 collective-permute-done
  45.2 0.1 collective-permute-done.1
  45.3 0.6 copy-done.12
  45.9 0.1 fusion.12
  46.0 1.1 fusion.64
  47.1 1.3 copy.69
  48.4 0.8 copy.71
  49.2 2.6 %collective-permute-start.3 = (f32[49,18,1]{0,2,1:T(1,128)}, f32[49,18,1]{0,2,1:T(1,128)}, u32[]{:S(2)}, u32[]{:S(2)}) collective-permute-start(f32[49,18,1]{0,2,1:T(1,128)} %copy.71), channel_id=1, source_target_pairs={{1,0},{2,1},{3,2},{4,3},{5,4},{6,5},{7,6},{0,7},{9,8},{10,9},{11,1... | collective-permute-start | bytes 10592 | tf_op jit(solution)/shard_map/ppermute | solution.py:31
  51.9 0.6 broadcast_compare_fusion.2
  52.5 1.0 copy.70
  53.5 1.9 copy.72
  55.4 1.9 fusion.20
  57.3 0.9 fusion.39
  58.2 0.5 fusion.69
  58.7 0.5 fusion.10
  59.3 1.4 collective-permute-start.4
  60.7 2.6 %collective-permute-start.5 = (f32[49,1,128]{2,1,0:T(1,128)S(1)}, f32[49,1,128]{2,1,0:T(1,128)S(1)}, u32[]{:S(2)}, u32[]{:S(2)}) collective-permute-start(f32[49,1,128]{2,1,0:T(1,128)S(1)} %get-tuple-element.47), channel_id=1, source_target_pairs={{8,0},{16,8},{24,16},{0,24},{9,1},{17,9},{25,17},{1,25},{10,2},{18... | collective-permute-start | bytes 75272 | tf_op jit(solution)/shard_map/ppermute | solution.py:31
  63.3 5.8 %pad_maximum_fusion = f32[2,16,2304]{1,0,2:T(2,128)} fusion(f32[2,16,128]{1,0,2:T(2,128)} %collective-permute-done.9, f32[2,16,128]{1,0,2:T(2,128)} %collective-permute-done.8, f32[2,16,2048]{1,0,2:T(2,128)S(1)} %copy.78), kind=kLoop, calls=%fused_computation.6 | loop fusion | flops 147456 | bytes 589824 | tf_op jit(solution)/shard_map/concatenate | solution.py:106
  69.1 85.5 %gather_fusion.2 = f32[12288,2,16]{2,1,0:T(2,128)} fusion(f32[2,16,2304]{1,0,2:T(2,128)} %pad_maximum_fusion, s32[12288]{0:T(1024)S(1)} %copy-done.8), kind=kCustom, calls=%fused_computation.2 | custom fusion | bytes 3194880 | tf_op jit(solution)/shard_map/gather | solution.py:109
  154.6 12.3 %copy.81 = f32[6,2048,2,16]{1,0,3,2:T(8,128)S(1)} copy(f32[6,2048,2,16]{3,2,1,0:T(2,128)} %bitcast.134) | data formatting | bytes 3145728 | tf_op jit(solution)/shard_map/gather | solution.py:109
  166.9 0.1 fusion.14
  167.0 1.1 fusion.63
  168.1 1.3 copy.73
  169.5 0.3 copy.75
  169.7 2.7 %collective-permute-start.7 = (f32[49,18,1]{0,2,1:T(1,128)S(1)}, f32[49,18,1]{0,2,1:T(1,128)S(1)}, u32[]{:S(2)}, u32[]{:S(2)}) collective-permute-start(f32[49,18,1]{0,2,1:T(1,128)S(1)} %copy.75), channel_id=1, source_target_pairs={{1,0},{2,1},{3,2},{4,3},{5,4},{6,5},{7,6},{0,7},{9,8},{10,9},{11,1... | collective-permute-start | bytes 10592 | tf_op jit(solution)/shard_map/ppermute | solution.py:31
  172.4 0.9 fusion.1
  173.3 0.2 collective-permute-done.6
  173.4 0.3 copy.74
  173.8 0.3 copy.76
  174.2 0.8 fusion.26
  175.0 0.2 fusion.37
  175.3 10.5 %gather_fusion.3 = f32[1024]{0:T(1024)} fusion(f32[2048]{0:T(1024)S(1)} %fusion.47, s32[1024]{0:T(1024)S(1)} %copy-done.24), kind=kCustom, calls=%fused_computation.3 | custom fusion | bytes 12288 | tf_op jit(solution)/shard_map/gather | solution.py:150
  185.8 4.3 %all-to-all-start.1 = ((f32[8,1,128]{2,1,0:T(1,128)}), f32[8,1,128]{2,1,0:T(1,128)S(1)}, u32[]{:S(2)}, u32[]{:S(2)}) async-start(f32[8,1,128]{2,1,0:T(1,128)} %bitcast.43), calls=%async_computation.1 | async-start | bytes 8192 | tf_op jit(solution)/shard_map/all_to_all | solution.py:151
  190.2 0.1 fusion.43
  190.3 4.5 %all-to-all-done.1 = f32[8,1,128]{2,1,0:T(1,128)S(1)} async-done(((f32[8,1,128]{2,1,0:T(1,128)}), f32[8,1,128]{2,1,0:T(1,128)S(1)}, u32[]{:S(2)}, u32[]{:S(2)}) %all-to-all-start.1) | async-done | bytes 4128 | tf_op jit(solution)/shard_map/all_to_all | solution.py:151
  194.8 6.1 %scatter_custom_fusion.1 = f32[2048]{0:T(1024)S(1)} fusion(s32[1024]{0:T(1024)} %bitcast.148, f32[1024]{0:T(1024)S(1)} %bitcast_multiply_fusion.3, f32[]{:T(128)} %constant.146.clone.1), kind=kCustom, calls=%fused_computation.118 | custom fusion | flops 1024 | bytes 8704 | tf_op jit(solution)/shard_map/scatter-add | solution.py:155
  201.0 0.2 scatter-add.33
  201.2 0.7 copy-done.7
  (99 shorter events, 0.7 us)
Async XLA Ops:
  0.6 13.6 %copy-start = (f32[2,16,2048]{2,1,0:T(8,128)S(1)}, f32[2,16,2048]{2,1,0:T(8,128)}, u32[]{:S(2)}) copy-start(f32[2,16,2048]{2,1,0:T(8,128)} %param.28) | copy-start | bytes 786436
  0.6 7.8 %copy-start.19 = (f32[1,8,128]{2,1,0:T(8,128)S(1)}, f32[1,8,128]{2,1,0:T(8,128)}, u32[]{:S(2)}) copy-start(f32[1,8,128]{2,1,0:T(8,128)} %param.35) | copy-start | bytes 12292
  2.2 13.1 %copy-start.33 = (s32[1,256]{1,0:T(1,128)S(1)}, s32[1,256]{1,0:T(1,128)}, u32[]{:S(2)}) copy-start(s32[1,256]{1,0:T(1,128)} %param.33) | copy-start | bytes 3076
  8.4 11.3 %copy-start.22 = (f32[16,128]{1,0:T(8,128)S(1)}, f32[16,128]{1,0:T(8,128)}, u32[]{:S(2)}) copy-start(f32[16,128]{1,0:T(8,128)} %param.25) | copy-start | bytes 24580
  8.4 12.9 %copy-start.11 = (f32[2,16,16,128]{3,2,1,0:T(8,128)S(1)}, f32[2,16,16,128]{3,2,1,0:T(8,128)}, u32[]{:S(2)}) copy-start(f32[2,16,16,128]{3,2,1,0:T(8,128)} %param.24) | copy-start | bytes 786436
  8.4 15.5 %copy-start.17 = (s32[6,2048]{1,0:T(8,128)S(1)}, s32[6,2048]{1,0:T(8,128)}, u32[]{:S(2)}) copy-start(s32[6,2048]{1,0:T(8,128)} %param.30) | copy-start | bytes 147460
  9.1 18.6 %all-to-all-start = ((f32[2,8,128]{2,0,1:T(2,128)}), f32[2,8,128]{2,0,1:T(2,128)}, u32[]{:S(2)}, u32[]{:S(2)}) async-start(f32[2,8,128]{2,0,1:T(2,128)} %copy.67), calls=%async_computation | async-start | bytes 16384 | tf_op jit(solution)/shard_map/all_to_all | solution.py:120
  14.2 10.4 %copy-start.1 = (f32[3,16,16,128]{3,2,1,0:T(8,128)S(1)}, f32[3,16,16,128]{3,2,1,0:T(8,128)}, u32[]{:S(2)}) copy-start(f32[3,16,16,128]{3,2,1,0:T(8,128)} %param.23) | copy-start | bytes 1179652
  14.3 11.5 %copy-start.9 = (f32[128,128,1,1]{1,0,3,2:T(8,128)S(1)}, f32[128,128,1,1]{1,0,3,2:T(8,128)}, u32[]{:S(2)}) copy-start(f32[128,128,1,1]{1,0,3,2:T(8,128)} %constant.158) | copy-start | bytes 196612
  17.0 10.0 %copy-start.23 = (s32[1,8,128]{2,1,0:T(8,128)S(1)}, s32[1,8,128]{2,1,0:T(8,128)}, u32[]{:S(2)}) copy-start(s32[1,8,128]{2,1,0:T(8,128)} %param.34) | copy-start | bytes 12292
  17.0 46.2 %collective-permute-start.8 = (f32[2,16,128]{1,0,2:T(2,128)}, f32[2,16,128]{1,0,2:T(2,128)}, u32[]{:S(2)}, u32[]{:S(2)}) collective-permute-start(f32[2,16,128]{1,0,2:T(2,128)} %get-tuple-element.50), channel_id=1, source_target_pairs={{0,1},{1,2},{2,3},{3,4},{4,5},{5,6},{6,7},{7,0},{8,9},{9,10},{10,1... | collective-permute-start | bytes 49160 | tf_op jit(solution)/shard_map/ppermute | solution.py:28
  17.5 45.8 %collective-permute-start.9 = (f32[2,16,128]{1,0,2:T(2,128)}, f32[2,16,128]{1,0,2:T(2,128)}, u32[]{:S(2)}, u32[]{:S(2)}) collective-permute-start(f32[2,16,128]{1,0,2:T(2,128)} %get-tuple-element.51), channel_id=1, source_target_pairs={{1,0},{2,1},{3,2},{4,3},{5,4},{6,5},{7,6},{0,7},{9,8},{10,9},{11,1... | collective-permute-start | bytes 49160 | tf_op jit(solution)/shard_map/ppermute | solution.py:31
  21.3 8.0 %copy-start.2 = (f32[16,16,128]{2,1,0:T(8,128)}, f32[16,16,128]{2,1,0:T(8,128)S(1)}, u32[]{:S(2)}) copy-start(f32[16,16,128]{2,1,0:T(8,128)S(1)} %get-tuple-element.57) | copy-start | bytes 393220
  38.3 21.0 %copy-start.13 = (f32[16,128]{1,0:T(8,128)}, f32[16,128]{1,0:T(8,128)S(1)}, u32[]{:S(2)}) copy-start(f32[16,128]{1,0:T(8,128)S(1)} %get-tuple-element.41) | copy-start | bytes 24580
  39.3 5.8 %collective-permute-start = (f32[49,1,128]{2,1,0:T(1,128)S(1)}, f32[49,1,128]{2,1,0:T(1,128)S(1)}, u32[]{:S(2)}, u32[]{:S(2)}) collective-permute-start(f32[49,1,128]{2,1,0:T(1,128)S(1)} %get-tuple-element.48), channel_id=1, source_target_pairs={{0,8},{8,16},{16,24},{24,0},{1,9},{9,17},{17,25},{25,1},{2,10},{10... | collective-permute-start | bytes 75272 | tf_op jit(solution)/shard_map/ppermute | solution.py:28
  41.2 4.1 %collective-permute-start.1 = (f32[49,1,128]{2,1,0:T(1,128)S(1)}, f32[49,1,128]{2,1,0:T(1,128)S(1)}, u32[]{:S(2)}, u32[]{:S(2)}) collective-permute-start(f32[49,1,128]{2,1,0:T(1,128)S(1)} %get-tuple-element.49), channel_id=1, source_target_pairs={{8,0},{16,8},{24,16},{0,24},{9,1},{17,9},{25,17},{1,25},{10,2},{18... | collective-permute-start | bytes 75272 | tf_op jit(solution)/shard_map/ppermute | solution.py:31
  43.9 13.4 %copy-start.27 = (pred[128]{0:T(512)(128)(4,1)}, pred[128]{0:T(512)(128)(4,1)S(1)}, u32[]{:S(2)}) copy-start(pred[128]{0:T(512)(128)(4,1)S(1)} %get-tuple-element.58) | copy-start | bytes 388
  45.3 0.6 copy-start.12
  48.4 4.1 %collective-permute-start.2 = (f32[49,18,1]{0,2,1:T(1,128)S(1)}, f32[49,18,1]{0,2,1:T(1,128)}, u32[]{:S(2)}, u32[]{:S(2)}) collective-permute-start(f32[49,18,1]{0,2,1:T(1,128)S(1)} %copy.69), channel_id=1, source_target_pairs={{0,1},{1,2},{2,3},{3,4},{4,5},{5,6},{6,7},{7,0},{8,9},{9,10},{10,1... | collective-permute-start | bytes 10592 | tf_op jit(solution)/shard_map/ppermute | solution.py:28
  49.2 4.3 %collective-permute-start.3 = (f32[49,18,1]{0,2,1:T(1,128)}, f32[49,18,1]{0,2,1:T(1,128)}, u32[]{:S(2)}, u32[]{:S(2)}) collective-permute-start(f32[49,18,1]{0,2,1:T(1,128)} %copy.71), channel_id=1, source_target_pairs={{1,0},{2,1},{3,2},{4,3},{5,4},{6,5},{7,6},{0,7},{9,8},{10,9},{11,1... | collective-permute-start | bytes 10592 | tf_op jit(solution)/shard_map/ppermute | solution.py:31
  52.5 4.8 %copy-start.30 = (pred[16]{0:T(512)(128)(4,1)S(1)}, pred[16]{0:T(512)(128)(4,1)}, u32[]{:S(2)}) copy-start(pred[16]{0:T(512)(128)(4,1)} %get-tuple-element.60) | copy-start | bytes 52
  55.4 2.9 %copy-start.21 = (f32[16,16,1]{1,0,2:T(8,128)S(1)}, f32[16,16,1]{1,0,2:T(8,128)}, u32[]{:S(2)}) copy-start(f32[16,16,1]{1,0,2:T(8,128)} %constant.157) | copy-start | bytes 3076
  55.4 3.3 %copy-start.3 = (f32[16,16,128]{2,1,0:T(8,128)S(1)}, f32[16,16,128]{2,1,0:T(8,128)}, u32[]{:S(2)}) copy-start(f32[16,16,128]{2,1,0:T(8,128)} %copy-done.2) | copy-start | bytes 393220
  55.4 3.3 %copy-start.10 = (f32[128,128,1,1]{1,0,3,2:T(8,128)S(1)}, f32[128,128,1,1]{1,0,3,2:T(8,128)}, u32[]{:S(2)}) copy-start(f32[128,128,1,1]{1,0,3,2:T(8,128)} %constant.158) | copy-start | bytes 196612
  59.3 107.6 %collective-permute-start.4 = (f32[49,1,128]{2,1,0:T(1,128)S(1)}, f32[49,1,128]{2,1,0:T(1,128)S(1)}, u32[]{:S(2)}, u32[]{:S(2)}) collective-permute-start(f32[49,1,128]{2,1,0:T(1,128)S(1)} %get-tuple-element.46), channel_id=1, source_target_pairs={{0,8},{8,16},{16,24},{24,0},{1,9},{9,17},{17,25},{25,1},{2,10},{10... | collective-permute-start | bytes 75272 | tf_op jit(solution)/shard_map/ppermute | solution.py:28
  60.7 8.4 %copy-start.8 = (s32[12288]{0:T(1024)S(1)}, s32[12288]{0:T(1024)}, u32[]{:S(2)}) copy-start(s32[12288]{0:T(1024)} %broadcast_clamp_fusion) | copy-start | bytes 147460
  60.7 106.2 %collective-permute-start.5 = (f32[49,1,128]{2,1,0:T(1,128)S(1)}, f32[49,1,128]{2,1,0:T(1,128)S(1)}, u32[]{:S(2)}, u32[]{:S(2)}) collective-permute-start(f32[49,1,128]{2,1,0:T(1,128)S(1)} %get-tuple-element.47), channel_id=1, source_target_pairs={{8,0},{16,8},{24,16},{0,24},{9,1},{17,9},{25,17},{1,25},{10,2},{18... | collective-permute-start | bytes 75272 | tf_op jit(solution)/shard_map/ppermute | solution.py:31
  166.9 5.5 %copy-start.18 = (f32[6,2048]{1,0:T(8,128)S(1)}, f32[6,2048]{1,0:T(8,128)}, u32[]{:S(2)}) copy-start(f32[6,2048]{1,0:T(8,128)} %param.29) | copy-start | bytes 147460
  169.4 4.7 %copy-start.28 = (pred[128]{0:T(512)(128)(4,1)S(1)}, pred[128]{0:T(512)(128)(4,1)}, u32[]{:S(2)}) copy-start(pred[128]{0:T(512)(128)(4,1)} %copy-done.27) | copy-start | bytes 388
  169.4 4.8 %copy-start.29 = (pred[128]{0:T(512)(128)(4,1)S(1)}, pred[128]{0:T(512)(128)(4,1)}, u32[]{:S(2)}) copy-start(pred[128]{0:T(512)(128)(4,1)} %get-tuple-element.59) | copy-start | bytes 388
  169.4 4.0 %collective-permute-start.6 = (f32[49,18,1]{0,2,1:T(1,128)S(1)}, f32[49,18,1]{0,2,1:T(1,128)S(1)}, u32[]{:S(2)}, u32[]{:S(2)}) collective-permute-start(f32[49,18,1]{0,2,1:T(1,128)S(1)} %copy.73), channel_id=1, source_target_pairs={{0,1},{1,2},{2,3},{3,4},{4,5},{5,6},{6,7},{7,0},{8,9},{9,10},{10,1... | collective-permute-start | bytes 10592 | tf_op jit(solution)/shard_map/ppermute | solution.py:28
  169.7 4.1 %collective-permute-start.7 = (f32[49,18,1]{0,2,1:T(1,128)S(1)}, f32[49,18,1]{0,2,1:T(1,128)S(1)}, u32[]{:S(2)}, u32[]{:S(2)}) collective-permute-start(f32[49,18,1]{0,2,1:T(1,128)S(1)} %copy.75), channel_id=1, source_target_pairs={{1,0},{2,1},{3,2},{4,3},{5,4},{6,5},{7,6},{0,7},{9,8},{10,9},{11,1... | collective-permute-start | bytes 10592 | tf_op jit(solution)/shard_map/ppermute | solution.py:31
  173.2 1.7 copy-start.31
  173.3 1.7 copy-start.32
  174.2 1.1 copy-start.14
  174.2 1.1 copy-start.24
  175.2 15.0 %copy-start.4 = (f32[2,15,2048]{2,1,0:T(8,128)S(1)}, f32[2,15,2048]{2,1,0:T(8,128)}, u32[]{:S(2)}) copy-start(f32[2,15,2048]{2,1,0:T(8,128)} %get-tuple-element.52) | copy-start | bytes 737284
  175.2 15.0 %copy-start.5 = (f32[2,15,2048]{2,1,0:T(8,128)S(1)}, f32[2,15,2048]{2,1,0:T(8,128)}, u32[]{:S(2)}) copy-start(f32[2,15,2048]{2,1,0:T(8,128)} %get-tuple-element.53) | copy-start | bytes 737284
  175.2 15.0 %copy-start.15 = (f32[2,1,2048]{2,1,0:T(1,128)S(1)}, f32[2,1,2048]{2,1,0:T(1,128)}, u32[]{:S(2)}) copy-start(f32[2,1,2048]{2,1,0:T(1,128)} %get-tuple-element.54) | copy-start | bytes 49156
  175.2 15.0 %copy-start.16 = (f32[2,1,2048]{2,1,0:T(1,128)S(1)}, f32[2,1,2048]{2,1,0:T(1,128)}, u32[]{:S(2)}) copy-start(f32[2,1,2048]{2,1,0:T(1,128)} %get-tuple-element.55) | copy-start | bytes 49156
  175.2 15.0 %copy-start.25 = (f32[2048]{0:T(1024)S(1)}, f32[2048]{0:T(1024)}, u32[]{:S(2)}) copy-start(f32[2048]{0:T(1024)} %param.31) | copy-start | bytes 24580
  175.3 15.0 %copy-start.6 = (f32[48,16,128]{2,1,0:T(8,128)}, f32[48,16,128]{2,1,0:T(8,128)S(1)}, u32[]{:S(2)}) copy-start(f32[48,16,128]{2,1,0:T(8,128)S(1)} %slice_divide_fusion) | copy-start | bytes 1179652
  175.3 19.5 %copy-start.20 = (f32[1,8,128]{2,1,0:T(8,128)S(1)}, f32[1,8,128]{2,1,0:T(8,128)}, u32[]{:S(2)}) copy-start(f32[1,8,128]{2,1,0:T(8,128)} %param.35) | copy-start | bytes 12292
  175.3 25.6 %copy-start.26 = (f32[2048]{0:T(1024)S(1)}, f32[2048]{0:T(1024)}, u32[]{:S(2)}) copy-start(f32[2048]{0:T(1024)} %param.32) | copy-start | bytes 24580
  185.8 8.9 %all-to-all-start.1 = ((f32[8,1,128]{2,1,0:T(1,128)}), f32[8,1,128]{2,1,0:T(1,128)S(1)}, u32[]{:S(2)}, u32[]{:S(2)}) async-start(f32[8,1,128]{2,1,0:T(1,128)} %bitcast.43), calls=%async_computation.1 | async-start | bytes 8192 | tf_op jit(solution)/shard_map/all_to_all | solution.py:151
  201.2 0.7 copy-start.7
where the time goes:
time: 203 us; the launch traced here: 202 us
  local copies, waits for them, and re-layouts  134 us (66%)
  other arithmetic  31.9 us (16%)
  starting transfers between devices  25.4 us (13%)
  waiting for transfers between devices  6.1 us (3%)
  matrix products  3.34 us (2%)
    gather x2, local copies, waits for them, and re-layouts, body(): adjacent = extended[:, :, neighbours]  97.8 us
    ppermute x5, starting transfers between devices, with_halo(): lax.ppermute(lax.slice_in_dim(block, 0, width, axis=dim), axis, backward)  12.1 us
    gather x1, local copies, waits for them, and re-layouts, body(): flux_slots = sea_flux[xgrid_rows[0]]  10.5 us
    scatter-add x1, other arithmetic, body(): sums = jnp.zeros((2, x_points * y_points), jnp.float32).at[:, point_ids]....  6.67 us
    gather x1, local copies, waits for them, and re-layouts, body(): surface_at = tracers[0, 0][cell_ids]  6.14 us
    scatter-add x1, other arithmetic, body(): inflow = jnp.zeros((cell_count,), jnp.float32).at[cell_ids.reshape(-1)].a...  6.13 us
    concatenate x1, other arithmetic, body(): jnp.concatenate([tracers, received[:, :, :rim_width], received[:, :, 3 *...  5.81 us
    slice x5, local copies, waits for them, and re-layouts, with_halo(): lax.slice_in_dim(block, block.shape[dim] - width, None, axis=dim)  5.44 us
  transfers between devices with their start and end apart: 12, of which 4 were waited for; matrix products, arithmetic and copies ran while one was open for 69% of the time, Pallas kernels for 0%

commit v1 on v0

v1 whole, which is shorter than its diff:
```python
import functools

import jax
import jax.numpy as jnp
from jax import lax
from jax.experimental import pallas as pl
from jax.experimental.pallas import tpu as pltpu
from jax.sharding import PartitionSpec as P

GLL = 4
ROWS = 8
LANES = 128

deriv_table = [
    [-3.0, 4.045084971874737, -1.545084971874737, 0.5],
    [-0.8090169943749475, 0.0, 1.118033988749895, -0.30901699437494745],
    [0.30901699437494745, -1.118033988749895, 0.0, 0.8090169943749475],
    [-0.5, 1.545084971874737, -4.045084971874737, 3.0],
]
time_step = 0.05
relax_rate = 0.3
flux_gain = 0.2

PAIRS = LANES // 2
HEAD = 8
AVG, MASS_SUM, MASS, COEF_X, COEF_Y, SURF = range(6)
SURF_ARRAYS = 6


def iota(shape, dim):
    return lax.broadcasted_iota(jnp.int32, shape, dim)


def take(values, index, axis):
    return jnp.take_along_axis(values, index, axis=axis, mode="promise_in_bounds")


def by_position(pos, values):
    result = jnp.full(pos.shape, values[-1], jnp.float32)
    for i, value in enumerate(values[:-1]):
        result = jnp.where(pos == i, value, result)
    return result


def spread(row):
    return jnp.broadcast_to(row, (ROWS, LANES))


class Geometry:
    def __init__(self):
        shape = (ROWS, LANES)
        self.row, self.lane = iota(shape, 0), iota(shape, 1)
        x_pos, y_pos = self.row & (GLL - 1), self.lane & (GLL - 1)
        self.x_from = [self.row - x_pos + j for j in range(GLL)]
        self.y_from = [self.lane - y_pos + j for j in range(GLL)]
        columns = [[line[j] for line in deriv_table] for j in range(GLL)]
        self.x_coef = [by_position(x_pos, column) for column in columns]
        self.y_coef = [by_position(y_pos, column) for column in columns]
        self.x_swap = (
            self.row + jnp.where(x_pos == GLL - 1, 1, 0) - jnp.where(x_pos == 0, 1, 0)
        ) & (ROWS - 1)
        self.y_swap = (
            self.lane + jnp.where(y_pos == GLL - 1, 1, 0) - jnp.where(y_pos == 0, 1, 0)
        ) & (LANES - 1)
        self.x_edge = (x_pos == 0) | (x_pos == GLL - 1)
        self.y_edge = (y_pos == 0) | (y_pos == GLL - 1)
        self.first_row, self.last_row = self.row == 0, self.row == ROWS - 1
        self.outer_lane = (self.lane == 0) | (self.lane == LANES - 1)
        self.weight = jnp.where(self.x_edge, 1.0 / 6.0, 5.0 / 6.0) * jnp.where(
            self.y_edge, 1.0 / 6.0, 5.0 / 6.0
        )

    def d_x(self, tile):
        return sum(self.x_coef[j] * take(tile, self.x_from[j], 0) for j in range(GLL))

    def d_y(self, tile):
        return sum(self.y_coef[j] * take(tile, self.y_from[j], 1) for j in range(GLL))

    def sum_x(self, low, high, before, after):
        low_swap, high_swap = take(low, self.x_swap, 0), take(high, self.x_swap, 0)
        low_other = jnp.where(
            self.first_row, before, jnp.where(self.last_row, high_swap, low_swap)
        )
        high_other = jnp.where(
            self.first_row, low_swap, jnp.where(self.last_row, after, high_swap)
        )
        return (
            low + jnp.where(self.x_edge, low_other, 0.0),
            high + jnp.where(self.x_edge, high_other, 0.0),
        )

    def sum_y(self, tile, outer):
        other = jnp.where(self.outer_lane, outer, take(tile, self.y_swap, 1))
        return tile + jnp.where(self.y_edge, other, 0.0)

    def sum_y_pair(self, own, strip):
        own_swap, strip_swap = take(own, self.y_swap, 1), take(strip, self.y_swap, 1)
        own_other = jnp.where(self.outer_lane, strip_swap, own_swap)
        strip_other = jnp.where(self.outer_lane, own_swap, strip_swap)
        return (
            own + jnp.where(self.y_edge, own_other, 0.0),
            strip + jnp.where(self.y_edge, strip_other, 0.0),
        )


def pack_edges(geo, packs, tile, number):
    at = number % PAIRS
    rolled = pltpu.roll(tile, (2 * at + 1) % LANES, 1)
    packs[number // PAIRS] = jnp.where(
        (geo.lane >> 1) == at, rolled, packs[number // PAIRS]
    )


def join_edges(geo, from_left, from_right):
    odd = (geo.lane & 1) == 1
    return jnp.where(
        odd, pltpu.roll(from_left, 1, 1), pltpu.roll(from_right, LANES - 1, 1)
    )


def outer_edges(joined, number):
    at = number % PAIRS
    return pltpu.roll(joined[number // PAIRS], (-(2 * at + 1)) % LANES, 1)


def neighbours_of(blocks):
    here = lax.axis_index("blk")
    return lax.rem(here + blocks - 1, blocks), lax.rem(here + 1, blocks)


def scatter_sum(lines, index, bins, allowed=None):
    count = index.shape[0]
    split = []
    for values in lines:
        for part in range(3):
            short = values.astype(jnp.bfloat16).astype(jnp.float32)
            split.append(short)
            values = values - short
    high, low = index >> 7, index & (LANES - 1)
    bin_at = iota((bins, LANES), 0)
    lane_at = iota((LANES, LANES), 0)
    if allowed is not None:
        lane_at = jnp.where(allowed(lane_at), lane_at, -1)
    left, right = [], []
    for c in range(count):
        hit = bin_at == high[c : c + 1]
        left.append(
            jnp.concatenate(
                [jnp.where(hit, part[c : c + 1], 0.0) for part in split], axis=0
            ).astype(jnp.bfloat16)
        )
        right.append(
            jnp.where(lane_at == low[c : c + 1], 1.0, 0.0).astype(jnp.bfloat16)
        )
    total = lax.dot_general(
        jnp.concatenate(left, axis=1),
        jnp.concatenate(right, axis=1),
        (((1,), (1,)), ((), ())),
        preferred_element_type=jnp.float32,
    )
    sums = []
    for i in range(len(lines)):
        part = total[3 * i * bins : 3 * (i + 1) * bins]
        sums.append(part[:bins] + part[bins : 2 * bins] + part[2 * bins :])
    return sums


def start_kernel(
    planes,
    air_ref,
    wind_ref,
    jac_ref,
    land_ref,
    rows_ref,
    tracers_ref,
    send_ref,
    cols_ref,
    weights_ref,
    slab_ref,
    moved_ref,
):
    geo = Geometry()
    blocks = cols_ref.shape[0]
    left, right = neighbours_of(blocks)
    levels = wind_ref.shape[0] // 32
    chunks = tracers_ref.shape[1] // LANES

    def source(group, chunk):
        return tracers_ref[
            ROWS * group : ROWS * (group + 1), LANES * chunk : LANES * (chunk + 1)
        ]

    for group in range(blocks // ROWS):
        at = slice(ROWS * group, ROWS * (group + 1))
        cells = cols_ref[at, :]
        high, low = cells >> 7, cells & (LANES - 1)
        surface = jnp.zeros((ROWS, LANES), jnp.float32)
        for k in range(chunks):
            line = spread(tracers_ref[0:1, LANES * k : LANES * (k + 1)])
            surface = jnp.where(high == k, take(line, low, 1), surface)
        area = weights_ref[at, :]
        heat = area * surface
        for c in range(ROWS):
            owner = ROWS * group + c
            for place, step in enumerate((1, 0, -1)):
                to = (owner + step) % blocks
                slab_ref[to, 2 * place : 2 * place + 1, :] = heat[c : c + 1]
                slab_ref[to, 2 * place + 1 : 2 * place + 2, :] = area[c : c + 1]

    mass = [geo.weight * jac_ref[ROWS * h : ROWS * (h + 1), :] for h in range(2)]
    packs = [
        jnp.zeros((ROWS, LANES), jnp.float32) for _ in range(-(-2 * planes // PAIRS))
    ]
    for level in range(levels):
        wind = [
            [
                time_step * wind_ref[pl.ds((i * levels + level) * 16 + ROWS * h, ROWS), :]
                for h in range(2)
            ]
            for i in range(2)
        ]
        for plane in range(level, planes, levels):
            for h in range(2):
                at = pl.ds(plane * 16 + ROWS * h, ROWS)
                field = air_ref[at, :]
                moved = mass[h] * (
                    field - (wind[0][h] * geo.d_x(field) + wind[1][h] * geo.d_y(field))
                )
                moved_ref[at, :] = moved
                pack_edges(geo, packs, moved, 2 * plane + h)

    base = HEAD
    edge_rows = ROWS * len(packs)
    for to in (left, right):
        for q, pack in enumerate(packs):
            slab_ref[to, base + ROWS * q : base + ROWS * (q + 1), :] = pack
    base += edge_rows
    for h in range(2):
        half = slice(ROWS * h, ROWS * (h + 1))
        strips = [
            air_ref[half, :],
            wind_ref[half, :],
            wind_ref[levels * 16 + ROWS * h : levels * 16 + ROWS * (h + 1), :],
            jac_ref[half, :],
            land_ref[half, :],
        ]
        pack = jnp.zeros((ROWS, LANES), jnp.float32)
        for i, strip in enumerate(strips):
            pack = jnp.where(
                (geo.lane >> 4) == i, pltpu.roll(strip, 16 * i + 8, 1), pack
            )
        for to in (left, right):
            slab_ref[to, base + ROWS * h : base + ROWS * (h + 1), :] = pack
    base += 2 * ROWS
    ids = rows_ref[...].astype(jnp.float32)
    for to in (left, right):
        slab_ref[to, base : base + blocks, :] = ids
    base += blocks
    for part, to in enumerate((left, right)):
        cells = spread(send_ref[0:1, LANES * part : LANES * (part + 1)])
        high, low = cells >> 7, cells & (LANES - 1)
        for group in range(tracers_ref.shape[0] // ROWS):
            rim = jnp.zeros((ROWS, LANES), jnp.float32)
            for k in range(chunks):
                rim = jnp.where(high == k, take(source(group, k), low, 1), rim)
            slab_ref[to, base + ROWS * group : base + ROWS * (group + 1), :] = rim


def panel_kernel(
    planes,
    moved_ref,
    recv_ref,
    air_ref,
    wind_ref,
    jac_ref,
    land_ref,
    rows_ref,
    avg_ref,
    down_ref,
    up_ref,
    surf_ref,
):
    geo = Geometry()
    blocks = rows_ref.shape[0]
    left, right = neighbours_of(blocks)
    levels = wind_ref.shape[0] // 32
    pack_count = -(-2 * planes // PAIRS)
    base = HEAD + ROWS * pack_count

    ids_at = base + 2 * ROWS
    own_ids = rows_ref[...]
    left_ids = recv_ref[left, ids_at : ids_at + blocks, :].astype(jnp.int32)
    right_ids = recv_ref[right, ids_at : ids_at + blocks, :].astype(jnp.int32)
    head = [
        jnp.concatenate([recv_ref[c, i : i + 1, :] for c in range(blocks)], axis=0)
        for i in range(6)
    ]
    heat, frac = scatter_sum(head[2:4], own_ids, 2 * ROWS)
    from_left = scatter_sum(
        head[0:2], left_ids, 2 * ROWS, lambda lane: lane >= LANES - ROWS
    )
    from_right = scatter_sum(head[4:6], right_ids, 2 * ROWS, lambda lane: lane < ROWS)
    strip_heat = from_left[0] + from_right[0]
    strip_frac = from_left[1] + from_right[1]

    in_strip = (geo.lane < ROWS) | (geo.lane >= LANES - ROWS)
    own, strip = [], []
    for h in range(2):
        half = slice(ROWS * h, ROWS * (h + 1))
        pack = jnp.where(
            ((geo.lane >> 3) & 1) == 1,
            recv_ref[right, base + ROWS * h : base + ROWS * (h + 1), :],
            recv_ref[left, base + ROWS * h : base + ROWS * (h + 1), :],
        )
        strip.append(
            [
                jnp.where(
                    in_strip, pltpu.roll(pack, (-(16 * i + 8)) % LANES, 1), 1.0
                )
                for i in range(5)
            ]
        )
        own.append(
            [
                air_ref[half, :],
                wind_ref[half, :],
                wind_ref[levels * 16 + ROWS * h : levels * 16 + ROWS * (h + 1), :],
                jac_ref[half, :],
                land_ref[half, :],
            ]
        )
    for h in range(2):
        half = slice(ROWS * h, ROWS * (h + 1))
        pair = []
        for tile, ((field, wind_x, wind_y, jac, land), tile_heat, tile_frac) in enumerate(
            ((own[h], heat[half], frac[half]), (strip[h], strip_heat[half], strip_frac[half]))
        ):
            mass = geo.weight * jac
            if tile == 1:
                tile_heat = jnp.where(in_strip, tile_heat, 0.0)
                tile_frac = jnp.where(in_strip, tile_frac, 0.0)
            surf = (tile_heat + land * field) / (tile_frac + land)
            coef_x, coef_y = time_step * mass * wind_x, time_step * mass * wind_y
            moved = (
                mass * (field + relax_rate * (surf - field))
                - coef_x * geo.d_x(field)
                - coef_y * geo.d_y(field)
            )
            pair.append((moved, mass))
            at = 2 * ROWS * tile + ROWS * h
            for number, value in (
                (MASS, mass),
                (COEF_X, coef_x),
                (COEF_Y, coef_y),
                (SURF, surf),
            ):
                surf_ref[4 * ROWS * number + at : 4 * ROWS * number + at + ROWS, :] = value
        for number, i in ((AVG, 0), (MASS_SUM, 1)):
            for tile, value in enumerate(geo.sum_y_pair(pair[0][i], pair[1][i])):
                at = 4 * ROWS * number + 2 * ROWS * tile + ROWS * h
                surf_ref[at : at + ROWS, :] = value

    joined = [
        join_edges(
            geo,
            recv_ref[left, HEAD + ROWS * q : HEAD + ROWS * (q + 1), :],
            recv_ref[right, HEAD + ROWS * q : HEAD + ROWS * (q + 1), :],
        )
        for q in range(pack_count)
    ]
    for plane in range(planes):
        for h in range(2):
            at = pl.ds(plane * 16 + ROWS * h, ROWS)
            avg_ref[at, :] = geo.sum_y(
                moved_ref[at, :], outer_edges(joined, 2 * plane + h)
            )

    def line(r):
        return avg_ref[pl.ds(r, planes, stride=16), :]

    def surf_line(number, r):
        return surf_ref[pl.ds(4 * ROWS * number + r, 2, stride=16), :]

    def first_step(get, mass_at):
        return (
            [
                get(1) / mass_at(1),
                get(2) / mass_at(2),
                (get(3) + get(4)) / (mass_at(3) + mass_at(4)),
            ],
            [
                (get(11) + get(12)) / (mass_at(11) + mass_at(12)),
                get(13) / mass_at(13),
                get(14) / mass_at(14),
            ],
        )

    def own_mass_sum(r):
        return surf_ref[4 * ROWS * MASS_SUM + r : 4 * ROWS * MASS_SUM + r + 1, :]

    low_lines, high_lines = first_step(line, own_mass_sum)
    surf_low, surf_high = first_step(
        functools.partial(surf_line, AVG), functools.partial(surf_line, MASS_SUM)
    )
    for out_ref, r, lines, surf_lines, coefs in (
        (down_ref, 0, low_lines, surf_low, deriv_table[0][1:]),
        (up_ref, 15, high_lines, surf_high, deriv_table[3][:3]),
    ):
        slope = sum(coef * value for coef, value in zip(coefs, lines))
        surf_slope = sum(coef * value for coef, value in zip(coefs, surf_lines))
        mass = surf_ref[4 * ROWS * MASS + r : 4 * ROWS * MASS + r + 1, :]
        wind = time_step * mass * wind_ref[pl.ds(r, 2 * levels, stride=16), :]
        out_ref[0:planes, :] = line(r)
        for first in range(0, planes, levels):
            out_ref[planes + first : planes + first + levels, :] = (
                wind[:levels] * slope[first : first + levels]
            )
        base = 2 * planes
        out_ref[base : base + 2 * levels, :] = wind
        base += 2 * levels
        for number in range(SURF_ARRAYS):
            out_ref[base + 2 * number : base + 2 * number + 2, :] = surf_line(number, r)
        base += 2 * SURF_ARRAYS
        out_ref[base : base + 2, :] = surf_line(COEF_X, r) * surf_slope


def second_kernel(
    planes,
    avg_ref,
    surf_ref,
    low_ref,
    high_ref,
    wind_ref,
    rows_ref,
    slab_ref,
    sums_ref,
    final_ref,
    inverse_ref,
    low_halo,
    high_halo,
):
    geo = Geometry()
    blocks = rows_ref.shape[0]
    left, right = neighbours_of(blocks)
    levels = wind_ref.shape[0] // 32
    base = 2 * planes + 2 * levels

    def surf_tile(number, tile, h):
        at = 4 * ROWS * number + 2 * ROWS * tile + ROWS * h
        return surf_ref[at : at + ROWS, :]

    def beside(ref, number, tile):
        at = base + 2 * number + tile
        return spread(ref[at : at + 1, :])

    ends = []
    inverse = []
    for tile in range(2):
        total = geo.sum_x(
            surf_tile(MASS_SUM, tile, 0),
            surf_tile(MASS_SUM, tile, 1),
            beside(low_ref, MASS_SUM, tile),
            beside(high_ref, MASS_SUM, tile),
        )
        inverse.append([1.0 / value for value in total])
        summed = geo.sum_x(
            surf_tile(AVG, tile, 0),
            surf_tile(AVG, tile, 1),
            beside(low_ref, AVG, tile),
            beside(high_ref, AVG, tile),
        )
        fields = [value * scale for value, scale in zip(summed, inverse[tile])]
        moved = []
        for h in range(2):
            field = fields[h]
            moved.append(
                surf_tile(MASS, tile, h)
                * (field + relax_rate * (surf_tile(SURF, tile, h) - field))
                - surf_tile(COEF_X, tile, h) * geo.d_x(field)
                - surf_tile(COEF_Y, tile, h) * geo.d_y(field)
            )
        halos = []
        for ref, field, own_coef in (
            (low_ref, spread(fields[0][:1]), deriv_table[3][3]),
            (high_ref, spread(fields[1][ROWS - 1 :]), deriv_table[0][0]),
        ):
            halos.append(
                beside(ref, MASS, tile)
                * (field + relax_rate * (beside(ref, SURF, tile) - field))
                - beside(ref, SURF_ARRAYS, tile)
                - beside(ref, COEF_X, tile) * (own_coef * field)
                - beside(ref, COEF_Y, tile) * geo.d_y(field)
            )
        ends.append(geo.sum_x(moved[0], moved[1], halos[0], halos[1]))
    final = []
    for h in range(2):
        summed, _ = geo.sum_y_pair(ends[0][h], ends[1][h])
        final.append(summed * inverse[0][h])
        final_ref[ROWS * h : ROWS * (h + 1), :] = final[h]
        inverse_ref[ROWS * h : ROWS * (h + 1), :] = inverse[0][h]
    flux = [final[h] - surf_tile(SURF, 0, h) for h in range(2)]
    for group in range(blocks // ROWS):
        ids = rows_ref[ROWS * group : ROWS * (group + 1), :]
        high, low = ids >> 7, ids & (LANES - 1)
        picked = jnp.zeros((ROWS, LANES), jnp.float32)
        for x in range(2 * ROWS):
            line = spread(flux[x // ROWS][x % ROWS : x % ROWS + 1])
            picked = jnp.where(high == x, take(line, low, 1), picked)
        for c in range(ROWS):
            slab_ref[ROWS * group + c, 0:1, :] = picked[c : c + 1]

    for ref, halo, r, own_coef, scale in (
        (low_ref, low_halo, 0, deriv_table[3][3], inverse[0][0][:1]),
        (high_ref, high_halo, 15, deriv_table[0][0], inverse[0][1][ROWS - 1 :]),
    ):
        field = (avg_ref[pl.ds(r, planes, stride=16), :] + ref[0:planes, :]) * scale
        mass = beside(ref, MASS, 0)
        for first in range(0, planes, ROWS):
            part = field[first : first + ROWS]
            wind_at = 2 * planes + first % levels
            halo[first : first + ROWS, :] = (
                mass * part
                - ref[planes + first : planes + first + ROWS, :]
                - ref[wind_at : wind_at + ROWS, :] * (own_coef * part)
                - ref[wind_at + levels : wind_at + levels + ROWS, :] * geo.d_y(part)
            )

    mass = [surf_tile(MASS, 0, h) for h in range(2)]
    packs = [
        jnp.zeros((ROWS, LANES), jnp.float32) for _ in range(-(-2 * planes // PAIRS))
    ]
    for level in range(levels):
        wind = [
            [
                time_step * wind_ref[pl.ds((i * levels + level) * 16 + ROWS * h, ROWS), :]
                for h in range(2)
            ]
            for i in range(2)
        ]
        for plane in range(level, planes, levels):
            summed = geo.sum_x(
                avg_ref[pl.ds(plane * 16, ROWS), :],
                avg_ref[pl.ds(plane * 16 + ROWS, ROWS), :],
                spread(low_ref[plane : plane + 1, :]),
                spread(high_ref[plane : plane + 1, :]),
            )
            moved = []
            for h in range(2):
                field = summed[h] * inverse[0][h]
                moved.append(
                    mass[h]
                    * (
                        field
                        - (wind[0][h] * geo.d_x(field) + wind[1][h] * geo.d_y(field))
                    )
                )
            summed = geo.sum_x(
                moved[0],
                moved[1],
                spread(low_halo[plane : plane + 1, :]),
                spread(high_halo[plane : plane + 1, :]),
            )
            for h in range(2):
                sums_ref[pl.ds(plane * 16 + ROWS * h, ROWS), :] = summed[h]
                pack_edges(geo, packs, summed[h], 2 * plane + h)
    for to in (left, right):
        for q, pack in enumerate(packs):
            slab_ref[to, HEAD + ROWS * q : HEAD + ROWS * (q + 1), :] = pack


def end_kernel(
    planes,
    sums_ref,
    recv_ref,
    final_ref,
    inverse_ref,
    cols_ref,
    weights_ref,
    area_ref,
    ocean_ref,
    air_out,
    ocean_out,
):
    geo = Geometry()
    blocks = cols_ref.shape[0]
    left, right = neighbours_of(blocks)
    chunks = area_ref.shape[0]
    arrived = jnp.concatenate([recv_ref[c, 0:1, :] for c in range(blocks)], axis=0)
    (inflow,) = scatter_sum([weights_ref[...] * arrived], cols_ref[...], chunks)
    gain = flux_gain * inflow / area_ref[...]
    ocean_out[...] = ocean_ref[...]
    for k in range(chunks):
        at = slice(LANES * k, LANES * (k + 1))
        ocean_out[0:1, at] = ocean_ref[0:1, at] + gain[k : k + 1]

    joined = [
        join_edges(
            geo,
            recv_ref[left, HEAD + ROWS * q : HEAD + ROWS * (q + 1), :],
            recv_ref[right, HEAD + ROWS * q : HEAD + ROWS * (q + 1), :],
        )
        for q in range(-(-2 * planes // PAIRS))
    ]
    inverse = [inverse_ref[ROWS * h : ROWS * (h + 1), :] for h in range(2)]
    for plane in range(planes):
        for h in range(2):
            at = pl.ds(plane * 16 + ROWS * h, ROWS)
            if plane == 0:
                air_out[at, :] = final_ref[ROWS * h : ROWS * (h + 1), :]
            else:
                air_out[at, :] = inverse[h] * geo.sum_y(
                    sums_ref[at, :], outer_edges(joined, 2 * plane + h)
                )


def gathered(ids, coefs, source, sources, groups, first=0):
    totals = [jnp.zeros((ROWS, LANES), jnp.float32) for _ in range(groups)]
    for edge in range(ids.shape[0]):
        cell = spread(ids[edge : edge + 1])
        coef = spread(coefs[edge : edge + 1])
        high, low = cell >> 7, cell & (LANES - 1)
        for s in range(sources):
            scaled = jnp.where(high == first + s, coef, 0.0)
            for group in range(groups):
                totals[group] += scaled * take(source(group, s), low, 1)
    return totals


def ocean_kernel(levels, tracers_ref, coef_ref, near_ref, rate_ref, out_ref):
    chunks = tracers_ref.shape[1] // LANES
    groups = tracers_ref.shape[0] // ROWS
    row = iota((ROWS, LANES), 0)

    def source(group, s):
        return tracers_ref[
            ROWS * group : ROWS * (group + 1), LANES * s : LANES * (s + 1)
        ]

    def one_chunk(k, carry):
        at = pl.ds(pl.multiple_of(k * LANES, LANES), LANES)
        ids, coefs = near_ref[:, at], coef_ref[:, at]
        totals = gathered(ids, coefs, source, chunks, groups)
        coef_sum = spread(jnp.sum(coefs, axis=0, keepdims=True))
        rate = spread(rate_ref[pl.ds(k, 1), :])
        tiles = [tracers_ref[ROWS * g : ROWS * (g + 1), at] for g in range(groups)]
        for g in range(groups):
            tile = tiles[g]
            above = pltpu.roll(tile, 1, 0)
            below = pltpu.roll(tile, ROWS - 1, 0)
            top = tile
            if (ROWS * g) % levels:
                top = pltpu.roll(tiles[g - 1], 1, 0)
            bottom = tile
            if (ROWS * (g + 1)) % levels:
                bottom = pltpu.roll(tiles[g + 1], ROWS - 1, 0)
            above = jnp.where(row == 0, top, above)
            below = jnp.where(row == ROWS - 1, bottom, below)
            vertical = rate * ((above - tile) + (below - tile))
            out_ref[ROWS * g : ROWS * (g + 1), at] = (
                tile + (totals[g] - coef_sum * tile) + vertical
            )
        return carry

    lax.fori_loop(0, chunks, one_chunk, 0)


def rim_kernel(rim_at, partial_ref, recv_ref, coef_ref, near_ref, out_ref):
    chunks = partial_ref.shape[1] // LANES
    groups = partial_ref.shape[0] // ROWS
    sides = neighbours_of(recv_ref.shape[0])

    def source(group, s):
        return recv_ref[sides[s], rim_at + ROWS * group : rim_at + ROWS * (group + 1), :]

    for k in range(chunks):
        at = slice(LANES * k, LANES * (k + 1))
        totals = gathered(near_ref[:, at], coef_ref[:, at], source, 2, groups, chunks)
        for g in range(groups):
            half = slice(ROWS * g, ROWS * (g + 1))
            out_ref[half, at] = partial_ref[half, at] + totals[g]


def call(kernel, outs, scratch=(), aliases=None):
    return pl.pallas_call(
        kernel,
        out_shape=[jax.ShapeDtypeStruct(shape, jnp.float32) for shape in outs],
        scratch_shapes=[pltpu.VMEM(shape, jnp.float32) for shape in scratch],
        input_output_aliases=aliases or {},
        compiler_params=pltpu.CompilerParams(vmem_limit_bytes=32 * 2**20),
        name=getattr(kernel, "func", kernel).__name__,
    )


def body(
    air_state,
    air_wind,
    jacobian,
    land_area,
    xgrid_rows,
    tracers,
    edge_coef,
    neighbours,
    vert_rate,
    ocean_area,
    send_list,
    xgrid_cols,
    xgrid_weights,
):
    field_count, levels, x_points, y_points = air_state.shape
    planes = field_count * levels
    ocean_levels, cells = tracers.shape[1:]
    ocean_planes = tracers.shape[0] * ocean_levels
    faces, blocks = lax.axis_size("face"), lax.axis_size("blk")
    air = air_state.reshape(planes * x_points, y_points)
    wind = air_wind.reshape(2 * levels * x_points, y_points)
    ocean = tracers.reshape(ocean_planes, cells)
    point_ids, cell_ids, weights = xgrid_rows[0], xgrid_cols[0], xgrid_weights[0]
    rate = vert_rate.reshape(cells // LANES, LANES)
    area = ocean_area.reshape(cells // LANES, LANES)
    edge_rows = ROWS * (-(-2 * planes // PAIRS))
    rim_at = HEAD + edge_rows + 2 * ROWS + blocks

    slab, moved = call(
        functools.partial(start_kernel, planes),
        [(blocks, rim_at + ocean_planes, LANES), air.shape],
    )(
        air,
        wind,
        jacobian,
        land_area,
        point_ids,
        ocean,
        send_list,
        cell_ids,
        weights,
    )
    recv = lax.all_to_all(slab, "blk", split_axis=0, concat_axis=0, tiled=True)
    (partial,) = call(
        functools.partial(ocean_kernel, ocean_levels), [ocean.shape]
    )(ocean, edge_coef, neighbours, rate)

    side_rows = 2 * planes + 2 * levels + 2 * SURF_ARRAYS + 4
    avg, down, up, surf = call(
        functools.partial(panel_kernel, planes),
        [air.shape, (side_rows, LANES), (side_rows, LANES), (4 * ROWS * SURF_ARRAYS, LANES)],
    )(moved, recv, air, wind, jacobian, land_area, point_ids)
    ring = [(i, (i + 1) % faces) for i in range(faces)]
    low = lax.ppermute(up, "face", ring)
    high = lax.ppermute(down, "face", [(target, source) for source, target in ring])
    (partial,) = call(functools.partial(rim_kernel, rim_at), [ocean.shape])(
        partial, recv, edge_coef, neighbours
    )

    slab, sums, final, inverse = call(
        functools.partial(second_kernel, planes),
        [
            (blocks, HEAD + edge_rows, LANES),
            air.shape,
            (x_points, y_points),
            (x_points, y_points),
        ],
        scratch=[(planes, LANES), (planes, LANES)],
    )(avg, surf, low, high, wind, point_ids)
    recv = lax.all_to_all(slab, "blk", split_axis=0, concat_axis=0, tiled=True)
    air_final, ocean_final = call(
        functools.partial(end_kernel, planes), [air.shape, ocean.shape]
    )(sums, recv, final, inverse, cell_ids, weights, area, partial)
    return air_final.reshape(air_state.shape), ocean_final.reshape(tracers.shape)


def solution(mesh):
    return jax.shard_map(
        body,
        mesh=mesh,
        in_specs=(
            P(None, None, "face", "blk"),
            P(None, None, "face", "blk"),
            P("face", "blk"),
            P("face", "blk"),
            P(("face", "blk"), None, None),
            P(None, None, ("face", "blk")),
            P(None, ("face", "blk")),
            P(None, ("face", "blk")),
            P(("face", "blk")),
            P(("face", "blk")),
            P(("face", "blk"), None),
            P(("face", "blk"), None, None),
            P(("face", "blk"), None, None),
        ),
        out_specs=(P(None, None, "face", "blk"), P(None, None, ("face", "blk"))),
        check_vma=False,
    )
```

time: 203 us -> 54.4 us (0.27)
  local copies, waits for them, and re-layouts: 134 us -> 6.35 us
  other arithmetic: 31.9 us -> 0 us
  Pallas kernels: 0 us -> 23.7 us
  starting transfers between devices: 25.4 us -> 7.37 us
  blocking collectives: 0 us -> 12.6 us
  matrix products: 3.34 us -> 0 us
  waiting for transfers between devices: 6.1 us -> 2.99 us
    gather x5 -> x0, local copies, waits for them, and re-layouts: 115 us -> none  [the longest x2 97.8 us: body(): adjacent = extended[:, :, neighbours]]
    pallas_call x0 -> x6, Pallas kernels: none -> 23.7 us  [the longest x1 7.97 us: body(): call(functools.partial(ocean_kernel, ocean_levels), [ocean.shape])]
    scatter-add x4 -> x0, other arithmetic: 14.1 us -> none  [the longest x1 6.67 us: body(): sums = jnp.zeros((2, x_points * y_points), jnp.float32).at[:, point_ids]....]
    all_to_all x0 -> x1, blocking collectives: none -> 12.6 us  [body(): recv = lax.all_to_all(slab, 'blk', split_axis=0, concat_axis=0, tiled=True)]
    ppermute x10 -> x2, starting transfers between devices: 15.9 us -> 3.88 us  [the longest x1 2.25 us: body(): lax.ppermute(down, 'face', [(target, source) for source, target in ring])]
    slice x11 -> x0, local copies, waits for them, and re-layouts: 9.78 us -> none  [the longest x5 5.44 us: with_halo(): lax.slice_in_dim(block, block.shape[dim] - width, None, axis=dim)]
    concatenate x5 -> x0, other arithmetic: 6.07 us -> none  [the longest x1 5.81 us: body(): jnp.concatenate([tracers, received[:, :, :rim_width], received[:, :, 3 *...]
    all_to_all x2 -> x1, starting transfers between devices: 9.46 us -> 3.49 us  [body(): recv = lax.all_to_all(slab, 'blk', split_axis=0, concat_axis=0, tiled=True)]
  transfers between devices with their start and end apart: 12 -> 3, of which waited for: 4 -> 2; matrix products, arithmetic and copies ran while one was open for 69% -> 0% of each run, Pallas kernels for 0% -> 17%
where the time goes in v1:
time: 54.4 us; the launch traced here: 53.8 us
  Pallas kernels  23.7 us (44%)
  blocking collectives  12.6 us (23%)
  starting transfers between devices  7.37 us (14%)
  local copies, waits for them, and re-layouts  6.35 us (12%)
  waiting for transfers between devices  2.99 us (5%)
  between operations  0.76 us (1%)
    all_to_all x1, blocking collectives, body(): recv = lax.all_to_all(slab, 'blk', split_axis=0, concat_axis=0, tiled=True)  12.6 us
    pallas_call x1, Pallas kernels, body(): call(functools.partial(ocean_kernel, ocean_levels), [ocean.shape])  7.97 us
    pallas_call x1, Pallas kernels, body(): call(functools.partial(start_kernel, planes), [(blocks, rim_at + ocean_pl...  7.57 us
    unnamed x32, local copies, waits for them, and re-layouts  6.35 us
    pallas_call x1, Pallas kernels, body(): call(functools.partial(second_kernel, planes), [(blocks, HEAD + edge_rows...  5.34 us
    all_to_all x1, starting transfers between devices, body(): recv = lax.all_to_all(slab, 'blk', split_axis=0, concat_axis=0, tiled=True)  3.49 us
    ppermute x1, waiting for transfers between devices, body(): low = lax.ppermute(up, 'face', ring)  2.8 us
    ppermute x1, starting transfers between devices, body(): lax.ppermute(down, 'face', [(target, source) for source, target in ring])  2.25 us
  transfers between devices with their start and end apart: 3, of which 2 were waited for; matrix products, arithmetic and copies ran while one was open for 0% of the time, Pallas kernels for 17%

profile of v1, /device:TPU:0, one launch (start us, length us, event | category | flops | bytes accessed | tf_op | source)
XLA Modules:
  0.0 53.8 jit_solution(1774987903146182115)
XLA Ops:
  0.6 0.0 copy-start.10
  0.6 0.0 copy-start.7
  0.7 0.0 copy-start.15
  0.7 0.7 %copy-done.10 = s32[1,8,128]{2,1,0:T(8,128)S(1)} copy-done((s32[1,8,128]{2,1,0:T(8,128)S(1)}, s32[1,8,128]{2,1,0:T(8,128)}, u32[]{:S(2)}) %copy-start.10) | copy-done | bytes 4120
  1.3 0.0 copy-done.7
  1.3 0.0 copy-done.15
  1.3 0.0 copy-start
  1.3 0.9 %copy-done = f32[2,16,16,128]{3,2,1,0:T(8,128)S(1)} copy-done((f32[2,16,16,128]{3,2,1,0:T(8,128)S(1)}, f32[2,16,16,128]{3,2,1,0:T(8,128)}, u32[]{:S(2)}) %copy-start) | copy-done | bytes 262168
  2.3 0.0 copy-start.2
  2.3 1.0 %copy-done.2 = f32[3,16,16,128]{3,2,1,0:T(8,128)S(1)} copy-done((f32[3,16,16,128]{3,2,1,0:T(8,128)S(1)}, f32[3,16,16,128]{3,2,1,0:T(8,128)}, u32[]{:S(2)}) %copy-start.2) | copy-done | bytes 393240
  3.3 0.0 copy-start.3
  3.3 0.9 %copy-done.3 = f32[2,16,2048]{2,1,0:T(8,128)S(1)} copy-done((f32[2,16,2048]{2,1,0:T(8,128)S(1)}, f32[2,16,2048]{2,1,0:T(8,128)}, u32[]{:S(2)}) %copy-start.3) | copy-done | bytes 262168
  4.2 0.0 copy-start.8
  4.2 0.7 %copy-done.8 = f32[16,128]{1,0:T(8,128)S(1)} copy-done((f32[16,128]{1,0:T(8,128)S(1)}, f32[16,128]{1,0:T(8,128)}, u32[]{:S(2)}) %copy-start.8) | copy-done | bytes 8216
  4.9 0.0 copy-start.9
  4.9 0.7 %copy-done.9 = f32[16,128]{1,0:T(8,128)S(1)} copy-done((f32[16,128]{1,0:T(8,128)S(1)}, f32[16,128]{1,0:T(8,128)}, u32[]{:S(2)}) %copy-start.9) | copy-done | bytes 8216
  5.6 0.0 copy-start.11
  5.6 0.7 %copy-done.11 = f32[1,8,128]{2,1,0:T(8,128)S(1)} copy-done((f32[1,8,128]{2,1,0:T(8,128)S(1)}, f32[1,8,128]{2,1,0:T(8,128)}, u32[]{:S(2)}) %copy-start.11) | copy-done | bytes 4120
  6.3 7.6 %start_kernel.1 = (f32[8,80,128]{2,1,0:T(8,128)S(1)}, f32[768,128]{1,0:T(8,128)S(1)}) custom-call(f32[768,128]{1,0:T(8,128)S(1)} %bitcast.13, f32[512,128]{1,0:T(8,128)S(1)} %bitcast.10, f32[16,128]{1,0:T(8,128)S(1)} %copy-done.8, f32[16,128]{1,0:T(8,128)S(1)} %copy-done.9, s32[8,128]{1,0:T(8,128)S(1)} %bitcast.17, f32[32,2048]{1,0:T(8,128)S(1)} %bitcast.15, ...), custom_call_target="tpu_custom_call" | custom-call | tf_op jit(solution)/shard_map/start_kernel/pallas_call | solution.py:723
  13.9 12.6 %all_to_all.10.recv_ref = f32[8,80,128]{2,1,0:T(8,128)S(1)} all-to-all(f32[8,80,128]{2,1,0:T(8,128)S(1)} %get-tuple-element.15), channel_id=1, replica_groups=mesh['face'=4,'blk'=8] {'blk'}, dimensions={0} | all-to-all | bytes 655360 | tf_op jit(solution)/shard_map/all_to_all | solution.py:737
  26.5 0.0 copy-start.1
  26.5 0.5 %panel_kernel.1 = (f32[768,128]{1,0:T(8,128)S(1)}, f32[144,128]{1,0:T(8,128)S(1)}, f32[144,128]{1,0:T(8,128)S(1)}, f32[192,128]{1,0:T(8,128)S(1)}) custom-call(f32[768,128]{1,0:T(8,128)S(1)} %get-tuple-element.14.moved_ref, f32[8,80,128]{2,1,0:T(8,128)S(1)} %all_to_all.10.recv_ref, f32[768,128]{1,0:T(8,128)S(1)} %bitcast.14, f32[512,128]{1,0:T(8,128)S(1)} %bitcast.11, ...), custom_call_target="tpu_custom_call" | custom-call | tf_op jit(solution)/shard_map/panel_kernel/pallas_call | solution.py:743
  27.0 1.6 %collective-permute-start = (f32[144,128]{1,0:T(8,128)S(1)}, f32[144,128]{1,0:T(8,128)S(1)}, u32[]{:S(2)}, u32[]{:S(2)}) collective-permute-start(f32[144,128]{1,0:T(8,128)S(1)} %get-tuple-element.18), channel_id=1, source_target_pairs={{0,8},{8,16},{16,24},{24,0},{1,9},{9,17},{17,25},{25,1},{2,10},{10... | collective-permute-start | bytes 221192 | tf_op jit(solution)/shard_map/ppermute | solution.py:748
  28.7 2.2 %collective-permute-start.1 = (f32[144,128]{1,0:T(8,128)S(1)}, f32[144,128]{1,0:T(8,128)S(1)}, u32[]{:S(2)}, u32[]{:S(2)}) collective-permute-start(f32[144,128]{1,0:T(8,128)S(1)} %get-tuple-element.19), channel_id=1, source_target_pairs={{8,0},{16,8},{24,16},{0,24},{9,1},{17,9},{25,17},{1,25},{10,2},{18... | collective-permute-start | bytes 221192 | tf_op jit(solution)/shard_map/ppermute | solution.py:749
  30.9 2.8 %collective-permute-done.low_ref = f32[144,128]{1,0:T(8,128)S(1)} collective-permute-done((f32[144,128]{1,0:T(8,128)S(1)}, f32[144,128]{1,0:T(8,128)S(1)}, u32[]{:S(2)}, u32[]{:S(2)}) %collective-permute-start) | collective-permute-done | bytes 73760 | tf_op jit(solution)/shard_map/ppermute | solution.py:748
  33.7 0.2 collective-permute-done.1.high_ref
  33.9 0.0 copy-done.1
  33.9 0.0 copy-start.4
  33.9 5.3 %second_kernel.1 = (f32[8,24,128]{2,1,0:T(8,128)}, f32[768,128]{1,0:T(8,128)S(1)}, f32[16,128]{1,0:T(8,128)S(1)}, f32[16,128]{1,0:T(8,128)S(1)}) custom-call(f32[768,128]{1,0:T(8,128)S(1)} %get-tuple-element.16.avg_ref, f32[192,128]{1,0:T(8,128)S(1)} %get-tuple-element.17.surf_ref, f32[144,128]{1,0:T(8,128)S(1)} %collective-permute-done.low_ref, ...), custom_call_target="tpu_custom_call" | custom-call | tf_op jit(solution)/shard_map/second_kernel/pallas_call | solution.py:754
  39.3 0.0 copy-start.5
  39.3 0.0 copy-start.6
  39.3 0.0 copy-start.14
  39.3 3.5 %all-to-all-start.1 = ((f32[8,24,128]{2,1,0:T(8,128)}), f32[8,24,128]{2,1,0:T(8,128)S(1)}, u32[]{:S(2)}, u32[]{:S(2)}) async-start(f32[8,24,128]{2,1,0:T(8,128)} %get-tuple-element.21), calls=%async_computation.1 | async-start | bytes 196608 | tf_op jit(solution)/shard_map/all_to_all | solution.py:764
  42.8 0.0 copy-done.4
  42.8 0.0 copy-done.5
  42.8 0.0 copy-done.6
  42.8 0.0 copy-done.14
  42.8 8.0 %ocean_kernel.1.partial_ref = f32[32,2048]{1,0:T(8,128)S(1)} custom-call(f32[32,2048]{1,0:T(8,128)S(1)} %bitcast.16, f32[6,2048]{1,0:T(8,128)S(1)} %copy-done.5, s32[6,2048]{1,0:T(8,128)S(1)} %copy-done.6, f32[16,128]{1,0:T(8,128)S(1)} %bitcast.25), custom_call_target="tpu_custom_call" | custom-call | tf_op jit(solution)/shard_map/ocean_kernel/pallas_call | solution.py:738
  50.8 0.0 copy-start.13
  50.8 1.2 %rim_kernel.1.ocean_ref = f32[32,2048]{1,0:T(8,128)S(1)} custom-call(f32[32,2048]{1,0:T(8,128)S(1)} %ocean_kernel.1.partial_ref, f32[8,80,128]{2,1,0:T(8,128)S(1)} %all_to_all.10.recv_ref, f32[6,2048]{1,0:T(8,128)S(1)} %copy-done.5, s32[6,2048]{1,0:T(8,128)S(1)} %copy-done.6), custom_call_target="tpu_custom_call" | custom-call | tf_op jit(solution)/shard_map/rim_kernel/pallas_call | solution.py:750
  52.0 0.0 copy-start.12
  52.0 0.0 all-to-all-done.1.recv_ref
  52.0 0.0 copy-done.13
  52.0 0.7 %copy-done.12 = f32[1,8,128]{2,1,0:T(8,128)S(1)} copy-done((f32[1,8,128]{2,1,0:T(8,128)S(1)}, f32[1,8,128]{2,1,0:T(8,128)}, u32[]{:S(2)}) %copy-start.12) | copy-done | bytes 4120
  52.7 1.1 %end_kernel.1 = (f32[768,128]{1,0:T(8,128)}, f32[32,2048]{1,0:T(8,128)}) custom-call(f32[768,128]{1,0:T(8,128)S(1)} %get-tuple-element.20.sums_ref, f32[8,24,128]{2,1,0:T(8,128)S(1)} %all-to-all-done.1.recv_ref, f32[16,128]{1,0:T(8,128)S(1)} %get-tuple-element.22.final_ref, f32[16,128]{1,0:T(8,128)S(1)} %get-tuple-element.23.inverse_ref, ...), custom_call_target="tpu_custom_call" | custom-call | tf_op jit(solution)/shard_map/end_kernel/pallas_call | solution.py:765
Async XLA Ops:
  0.6 0.7 %copy-start.10 = (s32[1,8,128]{2,1,0:T(8,128)S(1)}, s32[1,8,128]{2,1,0:T(8,128)}, u32[]{:S(2)}) copy-start(s32[1,8,128]{2,1,0:T(8,128)} %param.24) | copy-start | bytes 12292
  0.6 0.7 %copy-start.7 = (s32[1,8,128]{2,1,0:T(8,128)S(1)}, s32[1,8,128]{2,1,0:T(8,128)}, u32[]{:S(2)}) copy-start(s32[1,8,128]{2,1,0:T(8,128)} %param.17) | copy-start | bytes 12292
  0.7 0.7 %copy-start.15 = (s32[1,256]{1,0:T(1,128)S(1)}, s32[1,256]{1,0:T(1,128)}, u32[]{:S(2)}) copy-start(s32[1,256]{1,0:T(1,128)} %send_ref.1) | copy-start | bytes 3076
  1.3 0.9 %copy-start = (f32[2,16,16,128]{3,2,1,0:T(8,128)S(1)}, f32[2,16,16,128]{3,2,1,0:T(8,128)}, u32[]{:S(2)}) copy-start(f32[2,16,16,128]{3,2,1,0:T(8,128)} %param.14) | copy-start | bytes 786436
  2.3 1.0 %copy-start.2 = (f32[3,16,16,128]{3,2,1,0:T(8,128)S(1)}, f32[3,16,16,128]{3,2,1,0:T(8,128)}, u32[]{:S(2)}) copy-start(f32[3,16,16,128]{3,2,1,0:T(8,128)} %param.13) | copy-start | bytes 1179652
  3.3 0.9 %copy-start.3 = (f32[2,16,2048]{2,1,0:T(8,128)S(1)}, f32[2,16,2048]{2,1,0:T(8,128)}, u32[]{:S(2)}) copy-start(f32[2,16,2048]{2,1,0:T(8,128)} %param.18) | copy-start | bytes 786436
  4.2 0.7 %copy-start.8 = (f32[16,128]{1,0:T(8,128)S(1)}, f32[16,128]{1,0:T(8,128)}, u32[]{:S(2)}) copy-start(f32[16,128]{1,0:T(8,128)} %jac_ref.3) | copy-start | bytes 24580
  4.9 0.7 %copy-start.9 = (f32[16,128]{1,0:T(8,128)S(1)}, f32[16,128]{1,0:T(8,128)}, u32[]{:S(2)}) copy-start(f32[16,128]{1,0:T(8,128)} %land_ref.3) | copy-start | bytes 24580
  5.6 0.7 %copy-start.11 = (f32[1,8,128]{2,1,0:T(8,128)S(1)}, f32[1,8,128]{2,1,0:T(8,128)}, u32[]{:S(2)}) copy-start(f32[1,8,128]{2,1,0:T(8,128)} %param.25) | copy-start | bytes 12292
  26.5 7.4 %copy-start.1 = (f32[2,16,16,128]{3,2,1,0:T(8,128)S(1)}, f32[2,16,16,128]{3,2,1,0:T(8,128)}, u32[]{:S(2)}) copy-start(f32[2,16,16,128]{3,2,1,0:T(8,128)} %param.14) | copy-start | bytes 786436
  27.0 6.7 %collective-permute-start = (f32[144,128]{1,0:T(8,128)S(1)}, f32[144,128]{1,0:T(8,128)S(1)}, u32[]{:S(2)}, u32[]{:S(2)}) collective-permute-start(f32[144,128]{1,0:T(8,128)S(1)} %get-tuple-element.18), channel_id=1, source_target_pairs={{0,8},{8,16},{16,24},{24,0},{1,9},{9,17},{17,25},{25,1},{2,10},{10... | collective-permute-start | bytes 221192 | tf_op jit(solution)/shard_map/ppermute | solution.py:748
  28.7 5.2 %collective-permute-start.1 = (f32[144,128]{1,0:T(8,128)S(1)}, f32[144,128]{1,0:T(8,128)S(1)}, u32[]{:S(2)}, u32[]{:S(2)}) collective-permute-start(f32[144,128]{1,0:T(8,128)S(1)} %get-tuple-element.19), channel_id=1, source_target_pairs={{8,0},{16,8},{24,16},{0,24},{9,1},{17,9},{25,17},{1,25},{10,2},{18... | collective-permute-start | bytes 221192 | tf_op jit(solution)/shard_map/ppermute | solution.py:749
  33.9 8.9 %copy-start.4 = (f32[2,16,2048]{2,1,0:T(8,128)S(1)}, f32[2,16,2048]{2,1,0:T(8,128)}, u32[]{:S(2)}) copy-start(f32[2,16,2048]{2,1,0:T(8,128)} %param.18) | copy-start | bytes 786436
  39.3 3.5 %copy-start.5 = (f32[6,2048]{1,0:T(8,128)S(1)}, f32[6,2048]{1,0:T(8,128)}, u32[]{:S(2)}) copy-start(f32[6,2048]{1,0:T(8,128)} %coef_ref.3) | copy-start | bytes 147460
  39.3 3.5 %copy-start.6 = (s32[6,2048]{1,0:T(8,128)S(1)}, s32[6,2048]{1,0:T(8,128)}, u32[]{:S(2)}) copy-start(s32[6,2048]{1,0:T(8,128)} %near_ref.3) | copy-start | bytes 147460
  39.3 3.5 %copy-start.14 = (f32[2048]{0:T(1024)S(1)}, f32[2048]{0:T(1024)}, u32[]{:S(2)}) copy-start(f32[2048]{0:T(1024)} %param.21) | copy-start | bytes 24580
  39.3 12.7 %all-to-all-start.1 = ((f32[8,24,128]{2,1,0:T(8,128)}), f32[8,24,128]{2,1,0:T(8,128)S(1)}, u32[]{:S(2)}, u32[]{:S(2)}) async-start(f32[8,24,128]{2,1,0:T(8,128)} %get-tuple-element.21), calls=%async_computation.1 | async-start | bytes 196608 | tf_op jit(solution)/shard_map/all_to_all | solution.py:764
  50.8 1.2 %copy-start.13 = (f32[2048]{0:T(1024)S(1)}, f32[2048]{0:T(1024)}, u32[]{:S(2)}) copy-start(f32[2048]{0:T(1024)} %param.22) | copy-start | bytes 24580
  52.0 0.7 %copy-start.12 = (f32[1,8,128]{2,1,0:T(8,128)S(1)}, f32[1,8,128]{2,1,0:T(8,128)}, u32[]{:S(2)}) copy-start(f32[1,8,128]{2,1,0:T(8,128)} %param.25) | copy-start | bytes 12292

commit v2 on v1

--- a/solution.py
+++ b/solution.py
@@ -51,38 +51,60 @@
         shape = (ROWS, LANES)
         self.row, self.lane = iota(shape, 0), iota(shape, 1)
         x_pos, y_pos = self.row & (GLL - 1), self.lane & (GLL - 1)
-        self.x_from = [self.row - x_pos + j for j in range(GLL)]
         self.y_from = [self.lane - y_pos + j for j in range(GLL)]
         columns = [[line[j] for line in deriv_table] for j in range(GLL)]
-        self.x_coef = [by_position(x_pos, column) for column in columns]
+        self.x_coef = {
+            step: by_position(
+                x_pos,
+                [
+                    deriv_table[i][i + step] if 0 <= i + step < GLL else 0.0
+                    for i in range(GLL)
+                ],
+            )
+            for step in range(1 - GLL, GLL)
+        }
         self.y_coef = [by_position(y_pos, column) for column in columns]
-        self.x_swap = (
-            self.row + jnp.where(x_pos == GLL - 1, 1, 0) - jnp.where(x_pos == 0, 1, 0)
-        ) & (ROWS - 1)
         self.y_swap = (
             self.lane + jnp.where(y_pos == GLL - 1, 1, 0) - jnp.where(y_pos == 0, 1, 0)
         ) & (LANES - 1)
         self.x_edge = (x_pos == 0) | (x_pos == GLL - 1)
         self.y_edge = (y_pos == 0) | (y_pos == GLL - 1)
         self.first_row, self.last_row = self.row == 0, self.row == ROWS - 1
+        self.middle_row = self.row == GLL
         self.outer_lane = (self.lane == 0) | (self.lane == LANES - 1)
         self.weight = jnp.where(self.x_edge, 1.0 / 6.0, 5.0 / 6.0) * jnp.where(
             self.y_edge, 1.0 / 6.0, 5.0 / 6.0
         )
 
     def d_x(self, tile):
-        return sum(self.x_coef[j] * take(tile, self.x_from[j], 0) for j in range(GLL))
-
-    def d_y(self, tile):
-        return sum(self.y_coef[j] * take(tile, self.y_from[j], 1) for j in range(GLL))
+        return sum(
+            coef * (pltpu.roll(tile, -step % ROWS, 0) if step else tile)
+            for step, coef in self.x_coef.items()
+        )
+
+    def d_y(self, *tiles):
+        totals = [0.0] * len(tiles)
+        for j in range(GLL):
+            for i, tile in enumerate(tiles):
+                totals[i] += self.y_coef[j] * take(tile, self.y_from[j], 1)
+        return totals
 
     def sum_x(self, low, high, before, after):
-        low_swap, high_swap = take(low, self.x_swap, 0), take(high, self.x_swap, 0)
+        low_down, low_up = pltpu.roll(low, 1, 0), pltpu.roll(low, ROWS - 1, 0)
+        high_down, high_up = pltpu.roll(high, 1, 0), pltpu.roll(high, ROWS - 1, 0)
         low_other = jnp.where(
-            self.first_row, before, jnp.where(self.last_row, high_swap, low_swap)
+            self.first_row,
+            before,
+            jnp.where(
+                self.middle_row, low_down, jnp.where(self.last_row, high_up, low_up)
+            ),
         )
         high_other = jnp.where(
-            self.first_row, low_swap, jnp.where(self.last_row, after, high_swap)
+            self.first_row,
+            low_down,
+            jnp.where(
+                self.middle_row, high_down, jnp.where(self.last_row, after, high_up)
+            ),
         )
         return (
             low + jnp.where(self.x_edge, low_other, 0.0),
@@ -165,20 +187,31 @@
     return sums
 
 
-def start_kernel(
-    planes,
-    air_ref,
-    wind_ref,
-    jac_ref,
-    land_ref,
-    rows_ref,
-    tracers_ref,
-    send_ref,
-    cols_ref,
-    weights_ref,
-    slab_ref,
-    moved_ref,
-):
+def start_kernel(planes, inputs, *refs):
+    sources, (slab_ref, moved_ref), held = (
+        refs[:inputs],
+        refs[inputs : inputs + 2],
+        refs[inputs + 2 : -1],
+    )
+    copies = [
+        pltpu.make_async_copy(source, target, refs[-1].at[i])
+        for i, (source, target) in enumerate(zip(sources, held))
+    ]
+    for copy in copies:
+        copy.start()
+    (
+        cols_ref,
+        weights_ref,
+        tracers_ref,
+        send_ref,
+        rows_ref,
+        jac_ref,
+        land_ref,
+        wind_ref,
+        air_ref,
+    ) = held
+    for copy in copies[:4]:
+        copy.wait()
     geo = Geometry()
     blocks = cols_ref.shape[0]
     left, right = neighbours_of(blocks)
@@ -207,6 +240,18 @@
                 slab_ref[to, 2 * place : 2 * place + 1, :] = heat[c : c + 1]
                 slab_ref[to, 2 * place + 1 : 2 * place + 2, :] = area[c : c + 1]
 
+    base = HEAD + ROWS * (-(-2 * planes // PAIRS)) + 2 * ROWS + blocks
+    for part, to in enumerate((left, right)):
+        cells = spread(send_ref[0:1, LANES * part : LANES * (part + 1)])
+        high, low = cells >> 7, cells & (LANES - 1)
+        for group in range(tracers_ref.shape[0] // ROWS):
+            rim = jnp.zeros((ROWS, LANES), jnp.float32)
+            for k in range(chunks):
+                rim = jnp.where(high == k, take(source(group, k), low, 1), rim)
+            slab_ref[to, base + ROWS * group : base + ROWS * (group + 1), :] = rim
+
+    for copy in copies[4:]:
+        copy.wait()
     mass = [geo.weight * jac_ref[ROWS * h : ROWS * (h + 1), :] for h in range(2)]
     packs = [
         jnp.zeros((ROWS, LANES), jnp.float32) for _ in range(-(-2 * planes // PAIRS))
@@ -219,15 +264,16 @@
             ]
             for i in range(2)
         ]
-        for plane in range(level, planes, levels):
-            for h in range(2):
-                at = pl.ds(plane * 16 + ROWS * h, ROWS)
-                field = air_ref[at, :]
-                moved = mass[h] * (
-                    field - (wind[0][h] * geo.d_x(field) + wind[1][h] * geo.d_y(field))
-                )
-                moved_ref[at, :] = moved
-                pack_edges(geo, packs, moved, 2 * plane + h)
+        places = [
+            (plane, h) for plane in range(level, planes, levels) for h in range(2)
+        ]
+        fields = [air_ref[pl.ds(plane * 16 + ROWS * h, ROWS), :] for plane, h in places]
+        for (plane, h), field, slope in zip(places, fields, geo.d_y(*fields)):
+            moved = mass[h] * (
+                field - (wind[0][h] * geo.d_x(field) + wind[1][h] * slope)
+            )
+            moved_ref[pl.ds(plane * 16 + ROWS * h, ROWS), :] = moved
+            pack_edges(geo, packs, moved, 2 * plane + h)
 
     base = HEAD
     edge_rows = ROWS * len(packs)
@@ -255,15 +301,6 @@
     ids = rows_ref[...].astype(jnp.float32)
     for to in (left, right):
         slab_ref[to, base : base + blocks, :] = ids
-    base += blocks
-    for part, to in enumerate((left, right)):
-        cells = spread(send_ref[0:1, LANES * part : LANES * (part + 1)])
-        high, low = cells >> 7, cells & (LANES - 1)
-        for group in range(tracers_ref.shape[0] // ROWS):
-            rim = jnp.zeros((ROWS, LANES), jnp.float32)
-            for k in range(chunks):
-                rim = jnp.where(high == k, take(source(group, k), low, 1), rim)
-            slab_ref[to, base + ROWS * group : base + ROWS * (group + 1), :] = rim
 
 
 def panel_kernel(
@@ -275,6 +312,7 @@
     jac_ref,
     land_ref,
     rows_ref,
+    after_ref,
     avg_ref,
     down_ref,
     up_ref,
@@ -344,7 +382,7 @@
             moved = (
                 mass * (field + relax_rate * (surf - field))
                 - coef_x * geo.d_x(field)
-                - coef_y * geo.d_y(field)
+                - coef_y * geo.d_y(field)[0]
             )
             pair.append((moved, mass))
             at = 2 * ROWS * tile + ROWS * h
@@ -432,6 +470,7 @@
     high_ref,
     wind_ref,
     rows_ref,
+    after_ref,
     slab_ref,
     sums_ref,
     final_ref,
@@ -477,7 +516,7 @@
                 surf_tile(MASS, tile, h)
                 * (field + relax_rate * (surf_tile(SURF, tile, h) - field))
                 - surf_tile(COEF_X, tile, h) * geo.d_x(field)
-                - surf_tile(COEF_Y, tile, h) * geo.d_y(field)
+                - surf_tile(COEF_Y, tile, h) * geo.d_y(field)[0]
             )
         halos = []
         for ref, field, own_coef in (
@@ -489,7 +528,7 @@
                 * (field + relax_rate * (beside(ref, SURF, tile) - field))
                 - beside(ref, SURF_ARRAYS, tile)
                 - beside(ref, COEF_X, tile) * (own_coef * field)
-                - beside(ref, COEF_Y, tile) * geo.d_y(field)
+                - beside(ref, COEF_Y, tile) * geo.d_y(field)[0]
             )
         ends.append(geo.sum_x(moved[0], moved[1], halos[0], halos[1]))
     final = []
@@ -522,7 +561,7 @@
                 mass * part
                 - ref[planes + first : planes + first + ROWS, :]
                 - ref[wind_at : wind_at + ROWS, :] * (own_coef * part)
-                - ref[wind_at + levels : wind_at + levels + ROWS, :] * geo.d_y(part)
+                - ref[wind_at + levels : wind_at + levels + ROWS, :] * geo.d_y(part)[0]
             )
 
     mass = [surf_tile(MASS, 0, h) for h in range(2)]
@@ -537,21 +576,29 @@
             ]
             for i in range(2)
         ]
-        for plane in range(level, planes, levels):
+        group = list(range(level, planes, levels))
+        fields = []
+        for plane in group:
             summed = geo.sum_x(
                 avg_ref[pl.ds(plane * 16, ROWS), :],
                 avg_ref[pl.ds(plane * 16 + ROWS, ROWS), :],
                 spread(low_ref[plane : plane + 1, :]),
                 spread(high_ref[plane : plane + 1, :]),
             )
+            fields += [summed[h] * inverse[0][h] for h in range(2)]
+        slopes = geo.d_y(*fields)
+        for number, plane in enumerate(group):
             moved = []
             for h in range(2):
-                field = summed[h] * inverse[0][h]
+                field = fields[2 * number + h]
                 moved.append(
                     mass[h]
                     * (
                         field
-                        - (wind[0][h] * geo.d_x(field) + wind[1][h] * geo.d_y(field))
+                        - (
+                            wind[0][h] * geo.d_x(field)
+                            + wind[1][h] * slopes[2 * number + h]
+                        )
                     )
                 )
             summed = geo.sum_x(
@@ -576,7 +623,7 @@
     inverse_ref,
     cols_ref,
     weights_ref,
-    area_ref,
+    gain_ref,
     ocean_ref,
     air_out,
     ocean_out,
@@ -584,10 +631,10 @@
     geo = Geometry()
     blocks = cols_ref.shape[0]
     left, right = neighbours_of(blocks)
-    chunks = area_ref.shape[0]
+    chunks = gain_ref.shape[0]
     arrived = jnp.concatenate([recv_ref[c, 0:1, :] for c in range(blocks)], axis=0)
     (inflow,) = scatter_sum([weights_ref[...] * arrived], cols_ref[...], chunks)
-    gain = flux_gain * inflow / area_ref[...]
+    gain = inflow * gain_ref[...]
     ocean_out[...] = ocean_ref[...]
     for k in range(chunks):
         at = slice(LANES * k, LANES * (k + 1))
@@ -626,14 +673,15 @@
     return totals
 
 
-def ocean_kernel(levels, tracers_ref, coef_ref, near_ref, rate_ref, out_ref):
+def ocean_kernel(levels, number, tracers_ref, coef_ref, near_ref, rate_ref, after_ref, out_ref):
     chunks = tracers_ref.shape[1] // LANES
-    groups = tracers_ref.shape[0] // ROWS
+    groups = levels // ROWS
+    base = levels * number
     row = iota((ROWS, LANES), 0)
 
     def source(group, s):
         return tracers_ref[
-            ROWS * group : ROWS * (group + 1), LANES * s : LANES * (s + 1)
+            base + ROWS * group : base + ROWS * (group + 1), LANES * s : LANES * (s + 1)
         ]
 
     def one_chunk(k, carry):
@@ -642,16 +690,17 @@
         totals = gathered(ids, coefs, source, chunks, groups)
         coef_sum = spread(jnp.sum(coefs, axis=0, keepdims=True))
         rate = spread(rate_ref[pl.ds(k, 1), :])
-        tiles = [tracers_ref[ROWS * g : ROWS * (g + 1), at] for g in range(groups)]
+        tiles = [
+            tracers_ref[base + ROWS * g : base + ROWS * (g + 1), at]
+            for g in range(groups)
+        ]
         for g in range(groups):
             tile = tiles[g]
             above = pltpu.roll(tile, 1, 0)
             below = pltpu.roll(tile, ROWS - 1, 0)
-            top = tile
-            if (ROWS * g) % levels:
-                top = pltpu.roll(tiles[g - 1], 1, 0)
+            top = pltpu.roll(tiles[g - 1], 1, 0) if g else tile
             bottom = tile
-            if (ROWS * (g + 1)) % levels:
+            if g + 1 < groups:
                 bottom = pltpu.roll(tiles[g + 1], ROWS - 1, 0)
             above = jnp.where(row == 0, top, above)
             below = jnp.where(row == ROWS - 1, bottom, below)
@@ -664,10 +713,22 @@
     lax.fori_loop(0, chunks, one_chunk, 0)
 
 
-def rim_kernel(rim_at, partial_ref, recv_ref, coef_ref, near_ref, out_ref):
-    chunks = partial_ref.shape[1] // LANES
-    groups = partial_ref.shape[0] // ROWS
+def rim_kernel(
+    rim_at,
+    parts,
+    recv_ref,
+    coef_ref,
+    near_ref,
+    area_ref,
+    after_ref,
+    *refs,
+):
+    partial_refs, (out_ref, gain_ref) = refs[:parts], refs[parts:]
+    chunks = coef_ref.shape[1] // LANES
+    groups = out_ref.shape[0] // ROWS
+    part_groups = groups // parts
     sides = neighbours_of(recv_ref.shape[0])
+    gain_ref[...] = flux_gain / area_ref[...]
 
     def source(group, s):
         return recv_ref[sides[s], rim_at + ROWS * group : rim_at + ROWS * (group + 1), :]
@@ -676,16 +737,26 @@
         at = slice(LANES * k, LANES * (k + 1))
         totals = gathered(near_ref[:, at], coef_ref[:, at], source, 2, groups, chunks)
         for g in range(groups):
-            half = slice(ROWS * g, ROWS * (g + 1))
-            out_ref[half, at] = partial_ref[half, at] + totals[g]
-
-
-def call(kernel, outs, scratch=(), aliases=None):
+            place = ROWS * (g % part_groups)
+            partial = partial_refs[g // part_groups][place : place + ROWS, at]
+            out_ref[ROWS * g : ROWS * (g + 1), at] = partial + totals[g]
+
+
+VMEM_SPEC = pl.BlockSpec(memory_space=pltpu.VMEM)
+ANY_SPEC = pl.BlockSpec(memory_space=pl.ANY)
+HBM_SPEC = pl.BlockSpec(memory_space=pltpu.HBM)
+
+
+def call(kernel, outs, specs, scratch=(), cost=0):
+    estimate = None
+    if cost:
+        estimate = pl.CostEstimate(flops=0, bytes_accessed=cost, transcendentals=0)
     return pl.pallas_call(
         kernel,
         out_shape=[jax.ShapeDtypeStruct(shape, jnp.float32) for shape in outs],
-        scratch_shapes=[pltpu.VMEM(shape, jnp.float32) for shape in scratch],
-        input_output_aliases=aliases or {},
+        in_specs=specs,
+        scratch_shapes=list(scratch),
+        cost_estimate=estimate,
         compiler_params=pltpu.CompilerParams(vmem_limit_bytes=32 * 2**20),
         name=getattr(kernel, "func", kernel).__name__,
     )
@@ -720,36 +791,49 @@
     edge_rows = ROWS * (-(-2 * planes // PAIRS))
     rim_at = HEAD + edge_rows + 2 * ROWS + blocks
 
-    slab, moved = call(
-        functools.partial(start_kernel, planes),
-        [(blocks, rim_at + ocean_planes, LANES), air.shape],
-    )(
-        air,
-        wind,
+    first_inputs = (
+        cell_ids,
+        weights,
+        ocean,
+        send_list,
+        point_ids,
         jacobian,
         land_area,
-        point_ids,
-        ocean,
-        send_list,
-        cell_ids,
-        weights,
+        wind,
+        air,
     )
+    slab, moved = call(
+        functools.partial(start_kernel, planes, len(first_inputs)),
+        [(blocks, rim_at + ocean_planes, LANES), air.shape],
+        [HBM_SPEC] * len(first_inputs),
+        [pltpu.VMEM(array.shape, array.dtype) for array in first_inputs]
+        + [pltpu.SemaphoreType.DMA((len(first_inputs),))],
+    )(*(pltpu.with_memory_space_constraint(array, pltpu.HBM) for array in first_inputs))
     recv = lax.all_to_all(slab, "blk", split_axis=0, concat_axis=0, tiled=True)
-    (partial,) = call(
-        functools.partial(ocean_kernel, ocean_levels), [ocean.shape]
-    )(ocean, edge_coef, neighbours, rate)
-
+
+    parts = tracers.shape[0]
+    tile_reads = edge_coef.shape[0] * (cells // LANES) ** 2 * ocean_levels // ROWS
+
+    def ocean_part(number, after):
+        (result,) = call(
+            functools.partial(ocean_kernel, ocean_levels, number),
+            [(ocean_levels, cells)],
+            [VMEM_SPEC] * 4 + [ANY_SPEC],
+            cost=tile_reads * ROWS * LANES * 4,
+        )(ocean, edge_coef, neighbours, rate, after)
+        return result
+
+    first_part = ocean_part(0, moved)
     side_rows = 2 * planes + 2 * levels + 2 * SURF_ARRAYS + 4
     avg, down, up, surf = call(
         functools.partial(panel_kernel, planes),
         [air.shape, (side_rows, LANES), (side_rows, LANES), (4 * ROWS * SURF_ARRAYS, LANES)],
-    )(moved, recv, air, wind, jacobian, land_area, point_ids)
+        [VMEM_SPEC] * 7 + [ANY_SPEC],
+    )(moved, recv, air, wind, jacobian, land_area, point_ids, first_part)
     ring = [(i, (i + 1) % faces) for i in range(faces)]
     low = lax.ppermute(up, "face", ring)
     high = lax.ppermute(down, "face", [(target, source) for source, target in ring])
-    (partial,) = call(functools.partial(rim_kernel, rim_at), [ocean.shape])(
-        partial, recv, edge_coef, neighbours
-    )
+    second_part = ocean_part(1, surf)
 
     slab, sums, final, inverse = call(
         functools.partial(second_kernel, planes),
@@ -759,12 +843,21 @@
             (x_points, y_points),
             (x_points, y_points),
         ],
-        scratch=[(planes, LANES), (planes, LANES)],
-    )(avg, surf, low, high, wind, point_ids)
-    recv = lax.all_to_all(slab, "blk", split_axis=0, concat_axis=0, tiled=True)
+        [VMEM_SPEC] * 6 + [ANY_SPEC],
+        [pltpu.VMEM((planes, LANES), jnp.float32) for _ in range(2)],
+    )(avg, surf, low, high, wind, point_ids, second_part)
+    arrived = lax.all_to_all(slab, "blk", split_axis=0, concat_axis=0, tiled=True)
+    partial, gain = call(
+        functools.partial(rim_kernel, rim_at, parts),
+        [ocean.shape, area.shape],
+        [VMEM_SPEC] * 4 + [ANY_SPEC] + [VMEM_SPEC] * parts,
+        cost=tile_reads * ROWS * LANES,
+    )(recv, edge_coef, neighbours, area, final, first_part, second_part)
     air_final, ocean_final = call(
-        functools.partial(end_kernel, planes), [air.shape, ocean.shape]
-    )(sums, recv, final, inverse, cell_ids, weights, area, partial)
+        functools.partial(end_kernel, planes),
+        [air.shape, ocean.shape],
+        [VMEM_SPEC] * 8,
+    )(sums, arrived, final, inverse, cell_ids, weights, gain, partial)
     return air_final.reshape(air_state.shape), ocean_final.reshape(tracers.shape)
 
 

time: 54.4 us -> 39.5 us (0.73)
  blocking collectives: 12.6 us -> 0 us
  local copies, waits for them, and re-layouts: 6.35 us -> 0.07 us
  starting transfers between devices: 7.37 us -> 12.7 us
  Pallas kernels: 23.7 us -> 18.8 us
  waiting for transfers between devices: 2.99 us -> 6.7 us
    all_to_all x1 -> x0, blocking collectives: 12.6 us -> none  [body(): recv = lax.all_to_all(slab, 'blk', split_axis=0, concat_axis=0, tiled=True)]
    unnamed x32 -> x24, local copies, waits for them, and re-layouts: 6.35 us -> 0.07 us
    all_to_all x0 -> x1, waiting for transfers between devices: none -> 3.9 us  [body(): lax.all_to_all(slab, 'blk', split_axis=0, concat_axis=0, tiled=True)]
    all_to_all x0 -> x1, starting transfers between devices: none -> 3.49 us  [body(): lax.all_to_all(slab, 'blk', split_axis=0, concat_axis=0, tiled=True)]
    ppermute x1, waiting for transfers between devices: 2.8 us -> 0.01 us  [body(): low = lax.ppermute(up, 'face', ring)]
    all_to_all x1, waiting for transfers between devices: 0.01 us -> 2.8 us  [body(): recv = lax.all_to_all(slab, 'blk', split_axis=0, concat_axis=0, tiled=True)]
    pallas_call x1, Pallas kernels: 5.34 us -> 2.72 us  [body(): call(functools.partial(second_kernel, planes), [(blocks, HEAD + edge_rows...]
    pallas_call x4 -> x5, Pallas kernels: 17.8 us -> 15.5 us  [the longest x2 9.48 us: ocean_part(): call(functools.partial(ocean_kernel, ocean_levels, number), [(ocean_level...]
  transfers between devices with their start and end apart: 3 -> 4, of which waited for: 2 -> 2; matrix products, arithmetic and copies ran while one was open for 0% -> 0% of each run, Pallas kernels for 17% -> 27%
where the time goes in v2:
time: 39.5 us; the launch traced here: 39.1 us
  Pallas kernels  18.8 us (48%)
  starting transfers between devices  12.7 us (32%)
  waiting for transfers between devices  6.7 us (17%)
  between operations  0.83 us (2%)
    pallas_call x2, Pallas kernels, ocean_part(): call(functools.partial(ocean_kernel, ocean_levels, number), [(ocean_level...  9.48 us
    all_to_all x1, starting transfers between devices, body(): recv = lax.all_to_all(slab, 'blk', split_axis=0, concat_axis=0, tiled=True)  5.31 us
    all_to_all x1, waiting for transfers between devices, body(): lax.all_to_all(slab, 'blk', split_axis=0, concat_axis=0, tiled=True)  3.9 us
    pallas_call x1, Pallas kernels, body(): call(functools.partial(start_kernel, planes, len(first_inputs)), [(blocks...  3.75 us
    all_to_all x1, starting transfers between devices, body(): lax.all_to_all(slab, 'blk', split_axis=0, concat_axis=0, tiled=True)  3.49 us
    all_to_all x1, waiting for transfers between devices, body(): recv = lax.all_to_all(slab, 'blk', split_axis=0, concat_axis=0, tiled=True)  2.8 us
    pallas_call x1, Pallas kernels, body(): call(functools.partial(second_kernel, planes), [(blocks, HEAD + edge_rows...  2.72 us
    ppermute x1, starting transfers between devices, body(): lax.ppermute(down, 'face', [(target, source) for source, target in ring])  2.25 us
  transfers between devices with their start and end apart: 4, of which 2 were waited for; matrix products, arithmetic and copies ran while one was open for 0% of the time, Pallas kernels for 27%

profile of v2, /device:TPU:0, one launch (start us, length us, event | category | flops | bytes accessed | tf_op | source)
XLA Modules:
  0.0 39.1 jit_solution(14754008168048480508)
XLA Ops:
  0.6 3.8 %start_kernel.1 = (f32[8,80,128]{2,1,0:T(8,128)}, f32[768,128]{1,0:T(8,128)S(1)}) custom-call(s32[8,128]{1,0:T(8,128)} %bitcast.23, f32[8,128]{1,0:T(8,128)} %bitcast.25, f32[32,2048]{1,0:T(8,128)} %bitcast.10, s32[1,256]{1,0:T(1,128)} %refs_3_.1, s32[8,128]{1,0:T(8,128)} %bitcast.18, f32[16,128]{1,0:T(8,128)} %jac_ref.1, f32[16,128]{1,0:T(8,128)} %land_ref.1, ...), custom_call_target="tpu_custom_call" | custom-call | tf_op jit(solution)/shard_map/start_kernel/pallas_call | solution.py:805
  4.4 0.0 copy-start
  4.4 0.0 copy-start.3
  4.4 0.0 copy-start.4
  4.4 0.0 copy-start.8
  4.4 5.3 %all-to-all-start = ((f32[8,80,128]{2,1,0:T(8,128)}), f32[8,80,128]{2,1,0:T(8,128)S(1)}, u32[]{:S(2)}, u32[]{:S(2)}) async-start(f32[8,80,128]{2,1,0:T(8,128)} %get-tuple-element.17), calls=%async_computation | async-start | bytes 655360 | tf_op jit(solution)/shard_map/all_to_all | solution.py:812
  9.8 0.0 copy-done
  9.8 0.0 copy-done.3
  9.8 0.0 copy-done.4
  9.8 0.0 copy-done.8
  9.8 0.0 copy-start.1
  9.8 0.0 copy-start.2
  9.8 0.0 copy-start.5
  9.8 0.0 copy-start.6
  9.8 0.0 copy-start.7
  9.8 4.7 %ocean_kernel.2.after_ref.refs_0_ = f32[16,2048]{1,0:T(8,128)S(1)} custom-call(f32[32,2048]{1,0:T(8,128)S(1)} %bitcast.11, f32[6,2048]{1,0:T(8,128)S(1)} %copy-done.3, s32[6,2048]{1,0:T(8,128)S(1)} %copy-done.4, f32[16,128]{1,0:T(8,128)S(1)} %bitcast.21, f32[768,128]{1,0:T(8,128)S(1)} %get-tuple-element.16.after_ref.moved_ref), custom_call_target="tpu_custom_call" | custom-call | bytes 12582912 | tf_op jit(solution)/shard_map/ocean_kernel/pallas_call | solution.py:818
  14.6 2.8 %all-to-all-done.recv_ref = f32[8,80,128]{2,1,0:T(8,128)S(1)} async-done(((f32[8,80,128]{2,1,0:T(8,128)}), f32[8,80,128]{2,1,0:T(8,128)S(1)}, u32[]{:S(2)}, u32[]{:S(2)}) %all-to-all-start) | async-done | bytes 327712 | tf_op jit(solution)/shard_map/all_to_all | solution.py:812
  17.4 0.0 copy-done.1
  17.4 0.0 copy-done.2
  17.4 0.0 copy-done.5
  17.4 0.0 copy-done.6
  17.4 0.0 copy-done.7
  17.4 0.5 %panel_kernel.1 = (f32[768,128]{1,0:T(8,128)S(1)}, f32[144,128]{1,0:T(8,128)S(1)}, f32[144,128]{1,0:T(8,128)S(1)}, f32[192,128]{1,0:T(8,128)S(1)}) custom-call(f32[768,128]{1,0:T(8,128)S(1)} %get-tuple-element.16.after_ref.moved_ref, f32[8,80,128]{2,1,0:T(8,128)S(1)} %all-to-all-done.recv_ref, f32[768,128]{1,0:T(8,128)S(1)} %bitcast.17, ...), custom_call_target="tpu_custom_call" | custom-call | tf_op jit(solution)/shard_map/panel_kernel/pallas_call | solution.py:828
  18.0 1.6 %collective-permute-start = (f32[144,128]{1,0:T(8,128)S(1)}, f32[144,128]{1,0:T(8,128)S(1)}, u32[]{:S(2)}, u32[]{:S(2)}) collective-permute-start(f32[144,128]{1,0:T(8,128)S(1)} %get-tuple-element.20), channel_id=1, source_target_pairs={{0,8},{8,16},{16,24},{24,0},{1,9},{9,17},{17,25},{25,1},{2,10},{10... | collective-permute-start | bytes 221192 | tf_op jit(solution)/shard_map/ppermute | solution.py:834
  19.6 2.2 %collective-permute-start.1 = (f32[144,128]{1,0:T(8,128)S(1)}, f32[144,128]{1,0:T(8,128)S(1)}, u32[]{:S(2)}, u32[]{:S(2)}) collective-permute-start(f32[144,128]{1,0:T(8,128)S(1)} %get-tuple-element.21), channel_id=1, source_target_pairs={{8,0},{16,8},{24,16},{0,24},{9,1},{17,9},{25,17},{1,25},{10,2},{18... | collective-permute-start | bytes 221192 | tf_op jit(solution)/shard_map/ppermute | solution.py:835
  21.9 4.7 %ocean_kernel.3.after_ref.refs_1_ = f32[16,2048]{1,0:T(8,128)S(1)} custom-call(f32[32,2048]{1,0:T(8,128)S(1)} %bitcast.12, f32[6,2048]{1,0:T(8,128)S(1)} %copy-done.3, s32[6,2048]{1,0:T(8,128)S(1)} %copy-done.4, f32[16,128]{1,0:T(8,128)S(1)} %bitcast.22, f32[192,128]{1,0:T(8,128)S(1)} %get-tuple-element.19.after_ref.surf_ref), custom_call_target="tpu_custom_call" | custom-call | bytes 12582912 | tf_op jit(solution)/shard_map/ocean_kernel/pallas_call | solution.py:818
  26.6 0.0 collective-permute-done.low_ref
  26.6 0.0 collective-permute-done.1.high_ref
  26.6 2.7 %second_kernel.1 = (f32[8,24,128]{2,1,0:T(8,128)}, f32[768,128]{1,0:T(8,128)S(1)}, f32[16,128]{1,0:T(8,128)S(1)}, f32[16,128]{1,0:T(8,128)S(1)}) custom-call(f32[768,128]{1,0:T(8,128)S(1)} %get-tuple-element.18.avg_ref, f32[192,128]{1,0:T(8,128)S(1)} %get-tuple-element.19.after_ref.surf_ref, f32[144,128]{1,0:T(8,128)S(1)} %collective-permute-done.low_ref, ...), custom_call_target="tpu_custom_call" | custom-call | tf_op jit(solution)/shard_map/second_kernel/pallas_call | solution.py:838
  29.3 0.0 copy-start.11
  29.3 3.5 %all-to-all-start.1 = ((f32[8,24,128]{2,1,0:T(8,128)}), f32[8,24,128]{2,1,0:T(8,128)S(1)}, u32[]{:S(2)}, u32[]{:S(2)}) async-start(f32[8,24,128]{2,1,0:T(8,128)} %get-tuple-element.23), calls=%async_computation.1 | async-start | bytes 196608 | tf_op jit(solution)/shard_map/all_to_all | solution.py:849
  32.8 0.0 copy-done.11
  32.8 0.0 copy-start.10
  32.9 1.2 %rim_kernel.1 = (f32[32,2048]{1,0:T(8,128)S(1)}, f32[16,128]{1,0:T(8,128)S(1)}) custom-call(f32[8,80,128]{2,1,0:T(8,128)S(1)} %all-to-all-done.recv_ref, f32[6,2048]{1,0:T(8,128)S(1)} %copy-done.3, s32[6,2048]{1,0:T(8,128)S(1)} %copy-done.4, f32[16,128]{1,0:T(8,128)S(1)} %bitcast.27, f32[16,128]{1,0:T(8,128)S(1)} %get-tuple-element.24.after_ref.final_ref, ...), custom_call_target="tpu_custom_call" | custom-call | bytes 3145728 | tf_op jit(solution)/shard_map/rim_kernel/pallas_call | solution.py:850
  34.1 0.0 copy-start.9
  34.1 3.9 %all-to-all-done.1.recv_ref = f32[8,24,128]{2,1,0:T(8,128)S(1)} async-done(((f32[8,24,128]{2,1,0:T(8,128)}), f32[8,24,128]{2,1,0:T(8,128)S(1)}, u32[]{:S(2)}, u32[]{:S(2)}) %all-to-all-start.1) | async-done | bytes 98336 | tf_op jit(solution)/shard_map/all_to_all | solution.py:849
  38.0 0.0 copy-done.10
  38.0 0.0 copy-done.9
  38.0 1.1 %end_kernel.1 = (f32[768,128]{1,0:T(8,128)}, f32[32,2048]{1,0:T(8,128)}) custom-call(f32[768,128]{1,0:T(8,128)S(1)} %get-tuple-element.22.sums_ref, f32[8,24,128]{2,1,0:T(8,128)S(1)} %all-to-all-done.1.recv_ref, f32[16,128]{1,0:T(8,128)S(1)} %get-tuple-element.24.after_ref.final_ref, f32[16,128]{1,0:T(8,128)S(1)} %get-tuple-element.25.inverse_ref, ...), custom_call_target="tpu_custom_call" | custom-call | tf_op jit(solution)/shard_map/end_kernel/pallas_call | solution.py:856
Async XLA Ops:
  4.4 5.4 %copy-start = (f32[2,16,2048]{2,1,0:T(8,128)S(1)}, f32[2,16,2048]{2,1,0:T(8,128)}, u32[]{:S(2)}) copy-start(f32[2,16,2048]{2,1,0:T(8,128)} %param.18) | copy-start | bytes 786436
  4.4 5.4 %copy-start.3 = (f32[6,2048]{1,0:T(8,128)S(1)}, f32[6,2048]{1,0:T(8,128)}, u32[]{:S(2)}) copy-start(f32[6,2048]{1,0:T(8,128)} %coef_ref.5) | copy-start | bytes 147460
  4.4 5.4 %copy-start.4 = (s32[6,2048]{1,0:T(8,128)S(1)}, s32[6,2048]{1,0:T(8,128)}, u32[]{:S(2)}) copy-start(s32[6,2048]{1,0:T(8,128)} %near_ref.5) | copy-start | bytes 147460
  4.4 5.4 %copy-start.8 = (f32[2048]{0:T(1024)S(1)}, f32[2048]{0:T(1024)}, u32[]{:S(2)}) copy-start(f32[2048]{0:T(1024)} %param.21) | copy-start | bytes 24580
  4.4 13.0 %all-to-all-start = ((f32[8,80,128]{2,1,0:T(8,128)}), f32[8,80,128]{2,1,0:T(8,128)S(1)}, u32[]{:S(2)}, u32[]{:S(2)}) async-start(f32[8,80,128]{2,1,0:T(8,128)} %get-tuple-element.17), calls=%async_computation | async-start | bytes 655360 | tf_op jit(solution)/shard_map/all_to_all | solution.py:812
  9.8 7.6 %copy-start.1 = (f32[2,16,16,128]{3,2,1,0:T(8,128)S(1)}, f32[2,16,16,128]{3,2,1,0:T(8,128)}, u32[]{:S(2)}) copy-start(f32[2,16,16,128]{3,2,1,0:T(8,128)} %param.14) | copy-start | bytes 786436
  9.8 7.6 %copy-start.2 = (f32[3,16,16,128]{3,2,1,0:T(8,128)S(1)}, f32[3,16,16,128]{3,2,1,0:T(8,128)}, u32[]{:S(2)}) copy-start(f32[3,16,16,128]{3,2,1,0:T(8,128)} %param.13) | copy-start | bytes 1179652
  9.8 7.6 %copy-start.5 = (s32[1,8,128]{2,1,0:T(8,128)S(1)}, s32[1,8,128]{2,1,0:T(8,128)}, u32[]{:S(2)}) copy-start(s32[1,8,128]{2,1,0:T(8,128)} %param.17) | copy-start | bytes 12292
  9.8 7.6 %copy-start.6 = (f32[16,128]{1,0:T(8,128)S(1)}, f32[16,128]{1,0:T(8,128)}, u32[]{:S(2)}) copy-start(f32[16,128]{1,0:T(8,128)} %jac_ref.1) | copy-start | bytes 24580
  9.8 7.6 %copy-start.7 = (f32[16,128]{1,0:T(8,128)S(1)}, f32[16,128]{1,0:T(8,128)}, u32[]{:S(2)}) copy-start(f32[16,128]{1,0:T(8,128)} %land_ref.1) | copy-start | bytes 24580
  18.0 8.6 %collective-permute-start = (f32[144,128]{1,0:T(8,128)S(1)}, f32[144,128]{1,0:T(8,128)S(1)}, u32[]{:S(2)}, u32[]{:S(2)}) collective-permute-start(f32[144,128]{1,0:T(8,128)S(1)} %get-tuple-element.20), channel_id=1, source_target_pairs={{0,8},{8,16},{16,24},{24,0},{1,9},{9,17},{17,25},{25,1},{2,10},{10... | collective-permute-start | bytes 221192 | tf_op jit(solution)/shard_map/ppermute | solution.py:834
  19.6 7.0 %collective-permute-start.1 = (f32[144,128]{1,0:T(8,128)S(1)}, f32[144,128]{1,0:T(8,128)S(1)}, u32[]{:S(2)}, u32[]{:S(2)}) collective-permute-start(f32[144,128]{1,0:T(8,128)S(1)} %get-tuple-element.21), channel_id=1, source_target_pairs={{8,0},{16,8},{24,16},{0,24},{9,1},{17,9},{25,17},{1,25},{10,2},{18... | collective-permute-start | bytes 221192 | tf_op jit(solution)/shard_map/ppermute | solution.py:835
  29.3 3.5 %copy-start.11 = (f32[2048]{0:T(1024)S(1)}, f32[2048]{0:T(1024)}, u32[]{:S(2)}) copy-start(f32[2048]{0:T(1024)} %param.22) | copy-start | bytes 24580
  29.3 8.6 %all-to-all-start.1 = ((f32[8,24,128]{2,1,0:T(8,128)}), f32[8,24,128]{2,1,0:T(8,128)S(1)}, u32[]{:S(2)}, u32[]{:S(2)}) async-start(f32[8,24,128]{2,1,0:T(8,128)} %get-tuple-element.23), calls=%async_computation.1 | async-start | bytes 196608 | tf_op jit(solution)/shard_map/all_to_all | solution.py:849
  32.8 5.1 %copy-start.10 = (f32[1,8,128]{2,1,0:T(8,128)S(1)}, f32[1,8,128]{2,1,0:T(8,128)}, u32[]{:S(2)}) copy-start(f32[1,8,128]{2,1,0:T(8,128)} %param.25) | copy-start | bytes 12292
  34.1 3.9 %copy-start.9 = (s32[1,8,128]{2,1,0:T(8,128)S(1)}, s32[1,8,128]{2,1,0:T(8,128)}, u32[]{:S(2)}) copy-start(s32[1,8,128]{2,1,0:T(8,128)} %param.24) | copy-start | bytes 12292

commit v3 on v2

--- a/solution.py
+++ b/solution.py
@@ -22,7 +22,6 @@
 flux_gain = 0.2
 
 PAIRS = LANES // 2
-HEAD = 8
 AVG, MASS_SUM, MASS, COEF_X, COEF_Y, SURF = range(6)
 SURF_ARRAYS = 6
 
@@ -214,7 +213,6 @@
         copy.wait()
     geo = Geometry()
     blocks = cols_ref.shape[0]
-    left, right = neighbours_of(blocks)
     levels = wind_ref.shape[0] // 32
     chunks = tracers_ref.shape[1] // LANES
 
@@ -233,22 +231,19 @@
             surface = jnp.where(high == k, take(line, low, 1), surface)
         area = weights_ref[at, :]
         heat = area * surface
-        for c in range(ROWS):
-            owner = ROWS * group + c
-            for place, step in enumerate((1, 0, -1)):
-                to = (owner + step) % blocks
-                slab_ref[to, 2 * place : 2 * place + 1, :] = heat[c : c + 1]
-                slab_ref[to, 2 * place + 1 : 2 * place + 2, :] = area[c : c + 1]
-
-    base = HEAD + ROWS * (-(-2 * planes // PAIRS)) + 2 * ROWS + blocks
-    for part, to in enumerate((left, right)):
+        slab_ref[at, :] = heat
+        slab_ref[blocks + ROWS * group : blocks + ROWS * (group + 1), :] = area
+
+    base = 2 * blocks + ROWS * (-(-2 * planes // PAIRS)) + 2 * ROWS + blocks
+    for part in range(2):
         cells = spread(send_ref[0:1, LANES * part : LANES * (part + 1)])
         high, low = cells >> 7, cells & (LANES - 1)
         for group in range(tracers_ref.shape[0] // ROWS):
             rim = jnp.zeros((ROWS, LANES), jnp.float32)
             for k in range(chunks):
                 rim = jnp.where(high == k, take(source(group, k), low, 1), rim)
-            slab_ref[to, base + ROWS * group : base + ROWS * (group + 1), :] = rim
+            at = base + tracers_ref.shape[0] * part + ROWS * group
+            slab_ref[at : at + ROWS, :] = rim
 
     for copy in copies[4:]:
         copy.wait()
@@ -275,11 +270,10 @@
             moved_ref[pl.ds(plane * 16 + ROWS * h, ROWS), :] = moved
             pack_edges(geo, packs, moved, 2 * plane + h)
 
-    base = HEAD
+    base = 2 * blocks
     edge_rows = ROWS * len(packs)
-    for to in (left, right):
-        for q, pack in enumerate(packs):
-            slab_ref[to, base + ROWS * q : base + ROWS * (q + 1), :] = pack
+    for q, pack in enumerate(packs):
+        slab_ref[base + ROWS * q : base + ROWS * (q + 1), :] = pack
     base += edge_rows
     for h in range(2):
         half = slice(ROWS * h, ROWS * (h + 1))
@@ -295,12 +289,10 @@
             pack = jnp.where(
                 (geo.lane >> 4) == i, pltpu.roll(strip, 16 * i + 8, 1), pack
             )
-        for to in (left, right):
-            slab_ref[to, base + ROWS * h : base + ROWS * (h + 1), :] = pack
+        slab_ref[base + ROWS * h : base + ROWS * (h + 1), :] = pack
     base += 2 * ROWS
     ids = rows_ref[...].astype(jnp.float32)
-    for to in (left, right):
-        slab_ref[to, base : base + blocks, :] = ids
+    slab_ref[base : base + blocks, :] = ids
 
 
 def panel_kernel(
@@ -323,15 +315,19 @@
     left, right = neighbours_of(blocks)
     levels = wind_ref.shape[0] // 32
     pack_count = -(-2 * planes // PAIRS)
-    base = HEAD + ROWS * pack_count
+    base = 2 * blocks + ROWS * pack_count
+    here = lax.axis_index("blk")
 
     ids_at = base + 2 * ROWS
     own_ids = rows_ref[...]
     left_ids = recv_ref[left, ids_at : ids_at + blocks, :].astype(jnp.int32)
     right_ids = recv_ref[right, ids_at : ids_at + blocks, :].astype(jnp.int32)
     head = [
-        jnp.concatenate([recv_ref[c, i : i + 1, :] for c in range(blocks)], axis=0)
-        for i in range(6)
+        jnp.concatenate(
+            [recv_ref[c, pl.ds(first + owner, 1), :] for c in range(blocks)], axis=0
+        )
+        for owner in (left, here, right)
+        for first in (0, blocks)
     ]
     heat, frac = scatter_sum(head[2:4], own_ids, 2 * ROWS)
     from_left = scatter_sum(
@@ -401,8 +397,8 @@
     joined = [
         join_edges(
             geo,
-            recv_ref[left, HEAD + ROWS * q : HEAD + ROWS * (q + 1), :],
-            recv_ref[right, HEAD + ROWS * q : HEAD + ROWS * (q + 1), :],
+            recv_ref[left, 2 * blocks + ROWS * q : 2 * blocks + ROWS * (q + 1), :],
+            recv_ref[right, 2 * blocks + ROWS * q : 2 * blocks + ROWS * (q + 1), :],
         )
         for q in range(pack_count)
     ]
@@ -480,7 +476,6 @@
 ):
     geo = Geometry()
     blocks = rows_ref.shape[0]
-    left, right = neighbours_of(blocks)
     levels = wind_ref.shape[0] // 32
     base = 2 * planes + 2 * levels
 
@@ -545,8 +540,7 @@
         for x in range(2 * ROWS):
             line = spread(flux[x // ROWS][x % ROWS : x % ROWS + 1])
             picked = jnp.where(high == x, take(line, low, 1), picked)
-        for c in range(ROWS):
-            slab_ref[ROWS * group + c, 0:1, :] = picked[c : c + 1]
+        slab_ref[ROWS * group : ROWS * (group + 1), :] = picked
 
     for ref, halo, r, own_coef, scale in (
         (low_ref, low_halo, 0, deriv_table[3][3], inverse[0][0][:1]),
@@ -610,9 +604,8 @@
             for h in range(2):
                 sums_ref[pl.ds(plane * 16 + ROWS * h, ROWS), :] = summed[h]
                 pack_edges(geo, packs, summed[h], 2 * plane + h)
-    for to in (left, right):
-        for q, pack in enumerate(packs):
-            slab_ref[to, HEAD + ROWS * q : HEAD + ROWS * (q + 1), :] = pack
+    for q, pack in enumerate(packs):
+        slab_ref[blocks + ROWS * q : blocks + ROWS * (q + 1), :] = pack
 
 
 def end_kernel(
@@ -632,7 +625,10 @@
     blocks = cols_ref.shape[0]
     left, right = neighbours_of(blocks)
     chunks = gain_ref.shape[0]
-    arrived = jnp.concatenate([recv_ref[c, 0:1, :] for c in range(blocks)], axis=0)
+    here = lax.axis_index("blk")
+    arrived = jnp.concatenate(
+        [recv_ref[c, pl.ds(here, 1), :] for c in range(blocks)], axis=0
+    )
     (inflow,) = scatter_sum([weights_ref[...] * arrived], cols_ref[...], chunks)
     gain = inflow * gain_ref[...]
     ocean_out[...] = ocean_ref[...]
@@ -643,8 +639,8 @@
     joined = [
         join_edges(
             geo,
-            recv_ref[left, HEAD + ROWS * q : HEAD + ROWS * (q + 1), :],
-            recv_ref[right, HEAD + ROWS * q : HEAD + ROWS * (q + 1), :],
+            recv_ref[left, blocks + ROWS * q : blocks + ROWS * (q + 1), :],
+            recv_ref[right, blocks + ROWS * q : blocks + ROWS * (q + 1), :],
         )
         for q in range(-(-2 * planes // PAIRS))
     ]
@@ -731,7 +727,8 @@
     gain_ref[...] = flux_gain / area_ref[...]
 
     def source(group, s):
-        return recv_ref[sides[s], rim_at + ROWS * group : rim_at + ROWS * (group + 1), :]
+        at = rim_at + ROWS * groups * (1 - s) + ROWS * group
+        return recv_ref[sides[s], at : at + ROWS, :]
 
     for k in range(chunks):
         at = slice(LANES * k, LANES * (k + 1))
@@ -789,7 +786,7 @@
     rate = vert_rate.reshape(cells // LANES, LANES)
     area = ocean_area.reshape(cells // LANES, LANES)
     edge_rows = ROWS * (-(-2 * planes // PAIRS))
-    rim_at = HEAD + edge_rows + 2 * ROWS + blocks
+    rim_at = 2 * blocks + edge_rows + 2 * ROWS + blocks
 
     first_inputs = (
         cell_ids,
@@ -804,12 +801,12 @@
     )
     slab, moved = call(
         functools.partial(start_kernel, planes, len(first_inputs)),
-        [(blocks, rim_at + ocean_planes, LANES), air.shape],
+        [(rim_at + 2 * ocean_planes, LANES), air.shape],
         [HBM_SPEC] * len(first_inputs),
         [pltpu.VMEM(array.shape, array.dtype) for array in first_inputs]
         + [pltpu.SemaphoreType.DMA((len(first_inputs),))],
     )(*(pltpu.with_memory_space_constraint(array, pltpu.HBM) for array in first_inputs))
-    recv = lax.all_to_all(slab, "blk", split_axis=0, concat_axis=0, tiled=True)
+    recv = lax.all_gather(slab, "blk")
 
     parts = tracers.shape[0]
     tile_reads = edge_coef.shape[0] * (cells // LANES) ** 2 * ocean_levels // ROWS
@@ -838,7 +835,7 @@
     slab, sums, final, inverse = call(
         functools.partial(second_kernel, planes),
         [
-            (blocks, HEAD + edge_rows, LANES),
+            (blocks + edge_rows, LANES),
             air.shape,
             (x_points, y_points),
             (x_points, y_points),
@@ -846,7 +843,7 @@
         [VMEM_SPEC] * 6 + [ANY_SPEC],
         [pltpu.VMEM((planes, LANES), jnp.float32) for _ in range(2)],
     )(avg, surf, low, high, wind, point_ids, second_part)
-    arrived = lax.all_to_all(slab, "blk", split_axis=0, concat_axis=0, tiled=True)
+    arrived = lax.all_gather(slab, "blk")
     partial, gain = call(
         functools.partial(rim_kernel, rim_at, parts),
         [ocean.shape, area.shape],

time: 39.5 us -> 43.9 us (1.11)
  blocking collectives: 0 us -> 20.8 us
  starting transfers between devices: 12.7 us -> 3.89 us
  waiting for transfers between devices: 6.7 us -> 0.01 us
  Pallas kernels: 18.8 us -> 17.4 us
  local copies, waits for them, and re-layouts: 0.07 us -> 0.75 us
    all_gather x0 -> x2, blocking collectives: none -> 20.8 us  [the longest x1 11.4 us: body(): recv = lax.all_gather(slab, 'blk')]
    all_to_all x2 -> x0, starting transfers between devices: 8.81 us -> none  [the longest x1 5.31 us: body(): recv = lax.all_to_all(slab, 'blk', split_axis=0, concat_axis=0, tiled=True)]
    all_to_all x2 -> x0, waiting for transfers between devices: 6.69 us -> none  [the longest x1 3.9 us: body(): lax.all_to_all(slab, 'blk', split_axis=0, concat_axis=0, tiled=True)]
    pallas_call x2, Pallas kernels: 6.47 us -> 5.09 us  [the longest x1 3.02 us: body(): call(functools.partial(start_kernel, planes, len(first_inputs)), [(rim_at...]
    unnamed x24, local copies, waits for them, and re-layouts: 0.07 us -> 0.75 us
  transfers between devices with their start and end apart: 4 -> 2, of which waited for: 2 -> 0; matrix products, arithmetic and copies ran while one was open for 0% -> 0% of each run, Pallas kernels for 27% -> 11%
where the time goes in v3:
time: 43.9 us; the launch traced here: 43.7 us
  blocking collectives  20.8 us (47%)
  Pallas kernels  17.4 us (40%)
  starting transfers between devices  3.89 us (9%)
  between operations  0.81 us (2%)
  local copies, waits for them, and re-layouts  0.75 us (2%)
    all_gather x1, blocking collectives, body(): recv = lax.all_gather(slab, 'blk')  11.4 us
    pallas_call x2, Pallas kernels, ocean_part(): call(functools.partial(ocean_kernel, ocean_levels, number), [(ocean_level...  9.48 us
    all_gather x1, blocking collectives, body(): arrived = lax.all_gather(slab, 'blk')  9.33 us
    pallas_call x1, Pallas kernels, body(): call(functools.partial(start_kernel, planes, len(first_inputs)), [(rim_at...  3.02 us
    ppermute x1, starting transfers between devices, body(): lax.ppermute(down, 'face', [(target, source) for source, target in ring])  2.25 us
    pallas_call x1, Pallas kernels, body(): call(functools.partial(second_kernel, planes), [(blocks + edge_rows, LANE...  2.07 us
    ppermute x1, starting transfers between devices, body(): low = lax.ppermute(up, 'face', ring)  1.64 us
    pallas_call x1, Pallas kernels, body(): call(functools.partial(rim_kernel, rim_at, parts), [ocean.shape, area.sha...  1.19 us
  transfers between devices with their start and end apart: 2, of which 0 were waited for; matrix products, arithmetic and copies ran while one was open for 0% of the time, Pallas kernels for 11%

profile of v3, /device:TPU:0, one launch (start us, length us, event | category | flops | bytes accessed | tf_op | source)
XLA Modules:
  0.0 43.7 jit_solution(17005718297594544209)
XLA Ops:
  0.6 3.0 %start_kernel.1 = (f32[120,128]{1,0:T(8,128)S(1)}, f32[768,128]{1,0:T(8,128)S(1)}) custom-call(s32[8,128]{1,0:T(8,128)} %bitcast.28, f32[8,128]{1,0:T(8,128)} %bitcast.30, f32[32,2048]{1,0:T(8,128)} %bitcast.14, s32[1,256]{1,0:T(1,128)} %refs_3_.1, s32[8,128]{1,0:T(8,128)} %bitcast.23, f32[16,128]{1,0:T(8,128)} %jac_ref.1, f32[16,128]{1,0:T(8,128)} %land_ref.1, ...), custom_call_target="tpu_custom_call" | custom-call | tf_op jit(solution)/shard_map/start_kernel/pallas_call | solution.py:802
  3.7 0.0 copy-start
  3.7 0.0 copy-start.3
  3.7 0.0 copy-start.4
  3.7 0.0 copy-start.8
  3.7 11.4 %all-gather = f32[960,128]{1,0:T(8,128)S(1)} all-gather(f32[120,128]{1,0:T(8,128)S(1)} %get-tuple-element.17), channel_id=2, replica_groups=mesh['face'=4,'blk'=8] {'blk'}, dimensions={0}, use_global_device_ids=true | all-gather | bytes 552960 | tf_op jit(solution)/shard_map/all_gather | solution.py:809
  15.2 0.0 copy-done
  15.2 0.0 copy-done.3
  15.2 0.0 copy-done.4
  15.2 0.0 copy-done.8
  15.2 0.0 copy-start.1
  15.2 0.0 copy-start.2
  15.2 0.0 copy-start.5
  15.2 0.0 copy-start.6
  15.2 0.0 copy-start.7
  15.2 4.7 %ocean_kernel.2.after_ref.refs_0_ = f32[16,2048]{1,0:T(8,128)S(1)} custom-call(f32[32,2048]{1,0:T(8,128)S(1)} %bitcast.15, f32[6,2048]{1,0:T(8,128)S(1)} %copy-done.3, s32[6,2048]{1,0:T(8,128)S(1)} %copy-done.4, f32[16,128]{1,0:T(8,128)S(1)} %bitcast.26, f32[768,128]{1,0:T(8,128)S(1)} %get-tuple-element.16.after_ref.moved_ref), custom_call_target="tpu_custom_call" | custom-call | bytes 12582912 | tf_op jit(solution)/shard_map/ocean_kernel/pallas_call | solution.py:815
  20.0 0.0 copy-done.1
  20.0 0.0 copy-done.2
  20.0 0.0 copy-done.5
  20.0 0.0 copy-done.6
  20.0 0.0 copy-done.7
  20.0 0.5 %panel_kernel.1 = (f32[768,128]{1,0:T(8,128)S(1)}, f32[144,128]{1,0:T(8,128)S(1)}, f32[144,128]{1,0:T(8,128)S(1)}, f32[192,128]{1,0:T(8,128)S(1)}) custom-call(f32[768,128]{1,0:T(8,128)S(1)} %get-tuple-element.16.after_ref.moved_ref, f32[8,120,128]{2,1,0:T(8,128)S(1)} %bitcast.12, f32[768,128]{1,0:T(8,128)S(1)} %bitcast.21, f32[512,128]{1,0:T(8,128)S(1)} %bitcast.18, ...), custom_call_target="tpu_custom_call" | custom-call | tf_op jit(solution)/shard_map/panel_kernel/pallas_call | solution.py:825
  20.6 1.6 %collective-permute-start = (f32[144,128]{1,0:T(8,128)S(1)}, f32[144,128]{1,0:T(8,128)S(1)}, u32[]{:S(2)}, u32[]{:S(2)}) collective-permute-start(f32[144,128]{1,0:T(8,128)S(1)} %get-tuple-element.20), channel_id=1, source_target_pairs={{0,8},{8,16},{16,24},{24,0},{1,9},{9,17},{17,25},{25,1},{2,10},{10... | collective-permute-start | bytes 221192 | tf_op jit(solution)/shard_map/ppermute | solution.py:831
  22.2 2.2 %collective-permute-start.1 = (f32[144,128]{1,0:T(8,128)S(1)}, f32[144,128]{1,0:T(8,128)S(1)}, u32[]{:S(2)}, u32[]{:S(2)}) collective-permute-start(f32[144,128]{1,0:T(8,128)S(1)} %get-tuple-element.21), channel_id=1, source_target_pairs={{8,0},{16,8},{24,16},{0,24},{9,1},{17,9},{25,17},{1,25},{10,2},{18... | collective-permute-start | bytes 221192 | tf_op jit(solution)/shard_map/ppermute | solution.py:832
  24.5 4.7 %ocean_kernel.3.after_ref.refs_1_ = f32[16,2048]{1,0:T(8,128)S(1)} custom-call(f32[32,2048]{1,0:T(8,128)S(1)} %bitcast.16, f32[6,2048]{1,0:T(8,128)S(1)} %copy-done.3, s32[6,2048]{1,0:T(8,128)S(1)} %copy-done.4, f32[16,128]{1,0:T(8,128)S(1)} %bitcast.27, f32[192,128]{1,0:T(8,128)S(1)} %get-tuple-element.19.after_ref.surf_ref), custom_call_target="tpu_custom_call" | custom-call | bytes 12582912 | tf_op jit(solution)/shard_map/ocean_kernel/pallas_call | solution.py:815
  29.2 0.0 collective-permute-done.low_ref
  29.2 0.0 collective-permute-done.1.high_ref
  29.2 2.1 %second_kernel.1 = (f32[24,128]{1,0:T(8,128)S(1)}, f32[768,128]{1,0:T(8,128)S(1)}, f32[16,128]{1,0:T(8,128)S(1)}, f32[16,128]{1,0:T(8,128)S(1)}) custom-call(f32[768,128]{1,0:T(8,128)S(1)} %get-tuple-element.18.avg_ref, f32[192,128]{1,0:T(8,128)S(1)} %get-tuple-element.19.after_ref.surf_ref, f32[144,128]{1,0:T(8,128)S(1)} %collective-permute-done.low_ref, ...), custom_call_target="tpu_custom_call" | custom-call | tf_op jit(solution)/shard_map/second_kernel/pallas_call | solution.py:835
  31.3 0.0 copy-start.11
  31.3 9.3 %all-gather.1 = f32[192,128]{1,0:T(8,128)S(1)} all-gather(f32[24,128]{1,0:T(8,128)S(1)} %get-tuple-element.23), channel_id=3, replica_groups=mesh['face'=4,'blk'=8] {'blk'}, dimensions={0}, use_global_device_ids=true | all-gather | bytes 110592 | tf_op jit(solution)/shard_map/all_gather | solution.py:846
  40.6 0.0 copy-done.11
  40.6 1.2 %rim_kernel.1 = (f32[32,2048]{1,0:T(8,128)S(1)}, f32[16,128]{1,0:T(8,128)S(1)}) custom-call(f32[8,120,128]{2,1,0:T(8,128)S(1)} %bitcast.13, f32[6,2048]{1,0:T(8,128)S(1)} %copy-done.3, s32[6,2048]{1,0:T(8,128)S(1)} %copy-done.4, f32[16,128]{1,0:T(8,128)S(1)} %bitcast.32, f32[16,128]{1,0:T(8,128)S(1)} %get-tuple-element.24.after_ref.final_ref, ...), custom_call_target="tpu_custom_call" | custom-call | bytes 3145728 | tf_op jit(solution)/shard_map/rim_kernel/pallas_call | solution.py:847
  41.8 0.0 copy-start.10
  41.8 0.0 copy-start.9
  41.9 0.7 %copy-done.10 = f32[1,8,128]{2,1,0:T(8,128)S(1)} copy-done((f32[1,8,128]{2,1,0:T(8,128)S(1)}, f32[1,8,128]{2,1,0:T(8,128)}, u32[]{:S(2)}) %copy-start.10) | copy-done | bytes 4120
  42.5 0.0 copy-done.9
  42.5 1.1 %end_kernel.1 = (f32[768,128]{1,0:T(8,128)}, f32[32,2048]{1,0:T(8,128)}) custom-call(f32[768,128]{1,0:T(8,128)S(1)} %get-tuple-element.22.sums_ref, f32[8,24,128]{2,1,0:T(8,128)S(1)} %bitcast.22, f32[16,128]{1,0:T(8,128)S(1)} %get-tuple-element.24.after_ref.final_ref, f32[16,128]{1,0:T(8,128)S(1)} %get-tuple-element.25.inverse_ref, s32[8,128]{1,0:T(8,128)S(1)} %bitcast.29, ...), custom_call_target="tpu_custom_call" | custom-call | tf_op jit(solution)/shard_map/end_kernel/pallas_call | solution.py:853
Async XLA Ops:
  3.7 11.5 %copy-start = (f32[2,16,2048]{2,1,0:T(8,128)S(1)}, f32[2,16,2048]{2,1,0:T(8,128)}, u32[]{:S(2)}) copy-start(f32[2,16,2048]{2,1,0:T(8,128)} %param.18) | copy-start | bytes 786436
  3.7 11.5 %copy-start.3 = (f32[6,2048]{1,0:T(8,128)S(1)}, f32[6,2048]{1,0:T(8,128)}, u32[]{:S(2)}) copy-start(f32[6,2048]{1,0:T(8,128)} %coef_ref.5) | copy-start | bytes 147460
  3.7 11.5 %copy-start.4 = (s32[6,2048]{1,0:T(8,128)S(1)}, s32[6,2048]{1,0:T(8,128)}, u32[]{:S(2)}) copy-start(s32[6,2048]{1,0:T(8,128)} %near_ref.5) | copy-start | bytes 147460
  3.7 11.5 %copy-start.8 = (f32[2048]{0:T(1024)S(1)}, f32[2048]{0:T(1024)}, u32[]{:S(2)}) copy-start(f32[2048]{0:T(1024)} %param.21) | copy-start | bytes 24580
  15.2 4.8 %copy-start.1 = (f32[2,16,16,128]{3,2,1,0:T(8,128)S(1)}, f32[2,16,16,128]{3,2,1,0:T(8,128)}, u32[]{:S(2)}) copy-start(f32[2,16,16,128]{3,2,1,0:T(8,128)} %param.14) | copy-start | bytes 786436
  15.2 4.8 %copy-start.2 = (f32[3,16,16,128]{3,2,1,0:T(8,128)S(1)}, f32[3,16,16,128]{3,2,1,0:T(8,128)}, u32[]{:S(2)}) copy-start(f32[3,16,16,128]{3,2,1,0:T(8,128)} %param.13) | copy-start | bytes 1179652
  15.2 4.8 %copy-start.5 = (s32[1,8,128]{2,1,0:T(8,128)S(1)}, s32[1,8,128]{2,1,0:T(8,128)}, u32[]{:S(2)}) copy-start(s32[1,8,128]{2,1,0:T(8,128)} %param.17) | copy-start | bytes 12292
  15.2 4.8 %copy-start.6 = (f32[16,128]{1,0:T(8,128)S(1)}, f32[16,128]{1,0:T(8,128)}, u32[]{:S(2)}) copy-start(f32[16,128]{1,0:T(8,128)} %jac_ref.1) | copy-start | bytes 24580
  15.2 4.8 %copy-start.7 = (f32[16,128]{1,0:T(8,128)S(1)}, f32[16,128]{1,0:T(8,128)}, u32[]{:S(2)}) copy-start(f32[16,128]{1,0:T(8,128)} %land_ref.1) | copy-start | bytes 24580
  20.6 8.6 %collective-permute-start = (f32[144,128]{1,0:T(8,128)S(1)}, f32[144,128]{1,0:T(8,128)S(1)}, u32[]{:S(2)}, u32[]{:S(2)}) collective-permute-start(f32[144,128]{1,0:T(8,128)S(1)} %get-tuple-element.20), channel_id=1, source_target_pairs={{0,8},{8,16},{16,24},{24,0},{1,9},{9,17},{17,25},{25,1},{2,10},{10... | collective-permute-start | bytes 221192 | tf_op jit(solution)/shard_map/ppermute | solution.py:831
  22.2 7.0 %collective-permute-start.1 = (f32[144,128]{1,0:T(8,128)S(1)}, f32[144,128]{1,0:T(8,128)S(1)}, u32[]{:S(2)}, u32[]{:S(2)}) collective-permute-start(f32[144,128]{1,0:T(8,128)S(1)} %get-tuple-element.21), channel_id=1, source_target_pairs={{8,0},{16,8},{24,16},{0,24},{9,1},{17,9},{25,17},{1,25},{10,2},{18... | collective-permute-start | bytes 221192 | tf_op jit(solution)/shard_map/ppermute | solution.py:832
  31.3 9.3 %copy-start.11 = (f32[2048]{0:T(1024)S(1)}, f32[2048]{0:T(1024)}, u32[]{:S(2)}) copy-start(f32[2048]{0:T(1024)} %param.22) | copy-start | bytes 24580
  41.8 0.7 %copy-start.10 = (f32[1,8,128]{2,1,0:T(8,128)S(1)}, f32[1,8,128]{2,1,0:T(8,128)}, u32[]{:S(2)}) copy-start(f32[1,8,128]{2,1,0:T(8,128)} %param.25) | copy-start | bytes 12292
  41.8 0.7 %copy-start.9 = (s32[1,8,128]{2,1,0:T(8,128)S(1)}, s32[1,8,128]{2,1,0:T(8,128)}, u32[]{:S(2)}) copy-start(s32[1,8,128]{2,1,0:T(8,128)} %param.24) | copy-start | bytes 12292

commit v4 on v2

--- a/solution.py
+++ b/solution.py
@@ -21,8 +21,7 @@
 relax_rate = 0.3
 flux_gain = 0.2
 
-PAIRS = LANES // 2
-HEAD = 8
+HEAD, EDGE_AT, STRIP_AT, IDS_AT = 8, 8, 16, 24
 AVG, MASS_SUM, MASS, COEF_X, COEF_Y, SURF = range(6)
 SURF_ARRAYS = 6
 
@@ -125,24 +124,43 @@
         )
 
 
-def pack_edges(geo, packs, tile, number):
-    at = number % PAIRS
-    rolled = pltpu.roll(tile, (2 * at + 1) % LANES, 1)
-    packs[number // PAIRS] = jnp.where(
-        (geo.lane >> 1) == at, rolled, packs[number // PAIRS]
-    )
-
-
-def join_edges(geo, from_left, from_right):
-    odd = (geo.lane & 1) == 1
-    return jnp.where(
-        odd, pltpu.roll(from_left, 1, 1), pltpu.roll(from_right, LANES - 1, 1)
-    )
-
-
-def outer_edges(joined, number):
-    at = number % PAIRS
-    return pltpu.roll(joined[number // PAIRS], (-(2 * at + 1)) % LANES, 1)
+def edge_place(x, group):
+    return x // ROWS, LANES // 2 * (x % 2) + ROWS * group + 2 * (x % ROWS // 2)
+
+
+def pack_edges(geo, packs, tile, x, group):
+    q, at = edge_place(x, group)
+    rolled = pltpu.roll(tile, (at + 1) % LANES, 1)
+    packs[q] = jnp.where((geo.lane >> 1) == at // 2, rolled, packs[q])
+
+
+def outer_edges(joined, x, group):
+    q, at = edge_place(x, group)
+    return pltpu.roll(joined[q], (-(at + 1)) % LANES, 1)
+
+
+def split_sides(geo, first, second, unit):
+    odd = (geo.lane & unit) != 0
+    return (
+        jnp.where(odd, pltpu.roll(second, unit, 1), first),
+        jnp.where(odd, second, pltpu.roll(first, LANES - unit, 1)),
+    )
+
+
+def join_sides(geo, before, after, unit):
+    odd = (geo.lane & unit) != 0
+    return (
+        jnp.where(odd, pltpu.roll(after, unit, 1), before),
+        jnp.where(odd, after, pltpu.roll(before, LANES - unit, 1)),
+    )
+
+
+def join_edges(geo, before, after):
+    odd = (geo.lane & 1) != 0
+    return (
+        jnp.where(odd, pltpu.roll(before, 1, 1), after),
+        jnp.where(odd, before, pltpu.roll(after, LANES - 1, 1)),
+    )
 
 
 def neighbours_of(blocks):
@@ -188,11 +206,7 @@
 
 
 def start_kernel(planes, inputs, *refs):
-    sources, (slab_ref, moved_ref), held = (
-        refs[:inputs],
-        refs[inputs : inputs + 2],
-        refs[inputs + 2 : -1],
-    )
+    sources, slab_ref, held = refs[:inputs], refs[inputs], refs[inputs + 1 : -1]
     copies = [
         pltpu.make_async_copy(source, target, refs[-1].at[i])
         for i, (source, target) in enumerate(zip(sources, held))
@@ -210,13 +224,14 @@
         wind_ref,
         air_ref,
     ) = held
-    for copy in copies[:4]:
-        copy.wait()
     geo = Geometry()
     blocks = cols_ref.shape[0]
+    x_points = jac_ref.shape[0]
     left, right = neighbours_of(blocks)
-    levels = wind_ref.shape[0] // 32
+    levels = wind_ref.shape[0] // (2 * x_points)
     chunks = tracers_ref.shape[1] // LANES
+    for copy in copies[:5]:
+        copy.wait()
 
     def source(group, chunk):
         return tracers_ref[
@@ -240,7 +255,9 @@
                 slab_ref[to, 2 * place : 2 * place + 1, :] = heat[c : c + 1]
                 slab_ref[to, 2 * place + 1 : 2 * place + 2, :] = area[c : c + 1]
 
-    base = HEAD + ROWS * (-(-2 * planes // PAIRS)) + 2 * ROWS + blocks
+    ids = rows_ref[...].astype(jnp.float32)
+    for to in (left, right):
+        slab_ref[to, IDS_AT : IDS_AT + blocks, :] = ids
     for part, to in enumerate((left, right)):
         cells = spread(send_ref[0:1, LANES * part : LANES * (part + 1)])
         high, low = cells >> 7, cells & (LANES - 1)
@@ -248,59 +265,124 @@
             rim = jnp.zeros((ROWS, LANES), jnp.float32)
             for k in range(chunks):
                 rim = jnp.where(high == k, take(source(group, k), low, 1), rim)
-            slab_ref[to, base + ROWS * group : base + ROWS * (group + 1), :] = rim
-
-    for copy in copies[4:]:
+            at = IDS_AT + blocks + ROWS * group
+            slab_ref[to, at : at + ROWS, :] = rim
+
+    for copy in copies[5:]:
         copy.wait()
-    mass = [geo.weight * jac_ref[ROWS * h : ROWS * (h + 1), :] for h in range(2)]
-    packs = [
-        jnp.zeros((ROWS, LANES), jnp.float32) for _ in range(-(-2 * planes // PAIRS))
-    ]
-    for level in range(levels):
-        wind = [
-            [
-                time_step * wind_ref[pl.ds((i * levels + level) * 16 + ROWS * h, ROWS), :]
-                for h in range(2)
-            ]
-            for i in range(2)
-        ]
-        places = [
-            (plane, h) for plane in range(level, planes, levels) for h in range(2)
-        ]
-        fields = [air_ref[pl.ds(plane * 16 + ROWS * h, ROWS), :] for plane, h in places]
-        for (plane, h), field, slope in zip(places, fields, geo.d_y(*fields)):
-            moved = mass[h] * (
-                field - (wind[0][h] * geo.d_x(field) + wind[1][h] * slope)
-            )
-            moved_ref[pl.ds(plane * 16 + ROWS * h, ROWS), :] = moved
-            pack_edges(geo, packs, moved, 2 * plane + h)
-
-    base = HEAD
-    edge_rows = ROWS * len(packs)
-    for to in (left, right):
-        for q, pack in enumerate(packs):
-            slab_ref[to, base + ROWS * q : base + ROWS * (q + 1), :] = pack
-    base += edge_rows
+    strips = []
     for h in range(2):
         half = slice(ROWS * h, ROWS * (h + 1))
-        strips = [
-            air_ref[half, :],
-            wind_ref[half, :],
-            wind_ref[levels * 16 + ROWS * h : levels * 16 + ROWS * (h + 1), :],
-            jac_ref[half, :],
-            land_ref[half, :],
-        ]
+        second = levels * x_points
         pack = jnp.zeros((ROWS, LANES), jnp.float32)
-        for i, strip in enumerate(strips):
+        for i, strip in enumerate(
+            (
+                air_ref[half, :],
+                wind_ref[half, :],
+                wind_ref[second + ROWS * h : second + ROWS * (h + 1), :],
+                jac_ref[half, :],
+                land_ref[half, :],
+            )
+        ):
             pack = jnp.where(
                 (geo.lane >> 4) == i, pltpu.roll(strip, 16 * i + 8, 1), pack
             )
-        for to in (left, right):
-            slab_ref[to, base + ROWS * h : base + ROWS * (h + 1), :] = pack
-    base += 2 * ROWS
-    ids = rows_ref[...].astype(jnp.float32)
-    for to in (left, right):
-        slab_ref[to, base : base + blocks, :] = ids
+        strips.append(pack)
+    to_right, to_left = split_sides(geo, strips[0], strips[1], ROWS)
+    slab_ref[right, STRIP_AT : STRIP_AT + ROWS, :] = to_right
+    slab_ref[left, STRIP_AT : STRIP_AT + ROWS, :] = to_left
+
+    level_groups = levels // ROWS
+    eight = geo.lane >> 3
+
+    def edge_tile(get, groups, repeat):
+        pack = pltpu.roll(get(0), GLL, 1)
+        for group in range(1, groups):
+            pack = jnp.where(
+                eight == group, pltpu.roll(get(group), ROWS * group + GLL, 1), pack
+            )
+        return take(pack, geo.lane & (ROWS * groups - 1), 1) if repeat else pack
+
+    y_weight = jnp.where(geo.y_edge, 1.0 / 6.0, 5.0 / 6.0)
+    packs = [jnp.zeros((ROWS, LANES), jnp.float32) for _ in range(2)]
+    for element in range(x_points // GLL):
+        lines = [GLL * element + i for i in range(GLL)]
+        fields = [
+            edge_tile(
+                lambda g: air_ref[pl.ds(ROWS * g * x_points + x, ROWS, stride=x_points), :],
+                planes // ROWS,
+                False,
+            )
+            for x in lines
+        ]
+        slopes = geo.d_y(*fields)
+        for i, x in enumerate(lines):
+            wind = [
+                edge_tile(
+                    lambda g: wind_ref[
+                        pl.ds(
+                            (levels * part + ROWS * g) * x_points + x,
+                            ROWS,
+                            stride=x_points,
+                        ),
+                        :,
+                    ],
+                    level_groups,
+                    True,
+                )
+                for part in range(2)
+            ]
+            jac = edge_tile(lambda g: spread(jac_ref[x : x + 1, :]), 1, True)
+            x_weight = 1.0 / 6.0 if i in (0, GLL - 1) else 5.0 / 6.0
+            slope = sum(deriv_table[i][j] * fields[j] for j in range(GLL))
+            moved = (x_weight * y_weight * jac) * (
+                fields[i] - time_step * (wind[0] * slope + wind[1] * slopes[i])
+            )
+            q, at = edge_place(x, 0)
+            mine = ((geo.lane & (ROWS - 1)) >> 1 == at % ROWS // 2) & (
+                (geo.lane >> 6) == at // (LANES // 2)
+            )
+            packs[q] = jnp.where(mine, pltpu.roll(moved, (at - GLL + 1) % LANES, 1), packs[q])
+    to_right, to_left = split_sides(geo, packs[0], packs[1], 1)
+    slab_ref[right, EDGE_AT : EDGE_AT + ROWS, :] = to_right
+    slab_ref[left, EDGE_AT : EDGE_AT + ROWS, :] = to_left
+
+
+def moved_kernel(planes, air_ref, wind_ref, jac_ref, after_ref, moved_ref):
+    geo = Geometry()
+    x_points = jac_ref.shape[0]
+    levels = wind_ref.shape[0] // (2 * x_points)
+    y_weight = jnp.where(geo.y_edge, 1.0 / 6.0, 5.0 / 6.0)
+    for element in range(x_points // GLL):
+        lines = [GLL * element + i for i in range(GLL)]
+        mass = [
+            (1.0 / 6.0 if i in (0, GLL - 1) else 5.0 / 6.0)
+            * y_weight
+            * spread(jac_ref[x : x + 1, :])
+            for i, x in enumerate(lines)
+        ]
+        for level in range(0, levels, ROWS):
+            wind = [
+                [
+                    time_step
+                    * wind_ref[
+                        pl.ds((levels * part + level) * x_points + x, ROWS, stride=x_points), :
+                    ]
+                    for x in lines
+                ]
+                for part in range(2)
+            ]
+            for plane in range(level, planes, levels):
+                fields = [
+                    air_ref[pl.ds(plane * x_points + x, ROWS, stride=x_points), :]
+                    for x in lines
+                ]
+                slopes = geo.d_y(*fields)
+                for i, x in enumerate(lines):
+                    slope = sum(deriv_table[i][j] * fields[j] for j in range(GLL))
+                    moved_ref[planes * x + plane : planes * x + plane + ROWS, :] = mass[
+                        i
+                    ] * (fields[i] - (wind[0][i] * slope + wind[1][i] * slopes[i]))
 
 
 def panel_kernel(
@@ -321,14 +403,12 @@
     geo = Geometry()
     blocks = rows_ref.shape[0]
     left, right = neighbours_of(blocks)
-    levels = wind_ref.shape[0] // 32
-    pack_count = -(-2 * planes // PAIRS)
-    base = HEAD + ROWS * pack_count
-
-    ids_at = base + 2 * ROWS
+    x_points = jac_ref.shape[0]
+    levels = wind_ref.shape[0] // (2 * x_points)
+
     own_ids = rows_ref[...]
-    left_ids = recv_ref[left, ids_at : ids_at + blocks, :].astype(jnp.int32)
-    right_ids = recv_ref[right, ids_at : ids_at + blocks, :].astype(jnp.int32)
+    left_ids = recv_ref[left, IDS_AT : IDS_AT + blocks, :].astype(jnp.int32)
+    right_ids = recv_ref[right, IDS_AT : IDS_AT + blocks, :].astype(jnp.int32)
     head = [
         jnp.concatenate([recv_ref[c, i : i + 1, :] for c in range(blocks)], axis=0)
         for i in range(6)
@@ -342,14 +422,15 @@
     strip_frac = from_left[1] + from_right[1]
 
     in_strip = (geo.lane < ROWS) | (geo.lane >= LANES - ROWS)
+    packs = join_sides(
+        geo,
+        recv_ref[left, STRIP_AT : STRIP_AT + ROWS, :],
+        recv_ref[right, STRIP_AT : STRIP_AT + ROWS, :],
+        ROWS,
+    )
     own, strip = [], []
-    for h in range(2):
+    for h, pack in enumerate(packs):
         half = slice(ROWS * h, ROWS * (h + 1))
-        pack = jnp.where(
-            ((geo.lane >> 3) & 1) == 1,
-            recv_ref[right, base + ROWS * h : base + ROWS * (h + 1), :],
-            recv_ref[left, base + ROWS * h : base + ROWS * (h + 1), :],
-        )
         strip.append(
             [
                 jnp.where(
@@ -362,7 +443,9 @@
             [
                 air_ref[half, :],
                 wind_ref[half, :],
-                wind_ref[levels * 16 + ROWS * h : levels * 16 + ROWS * (h + 1), :],
+                wind_ref[
+                    levels * x_points + ROWS * h : levels * x_points + ROWS * (h + 1), :
+                ],
                 jac_ref[half, :],
                 land_ref[half, :],
             ]
@@ -398,26 +481,21 @@
                 at = 4 * ROWS * number + 2 * ROWS * tile + ROWS * h
                 surf_ref[at : at + ROWS, :] = value
 
-    joined = [
-        join_edges(
-            geo,
-            recv_ref[left, HEAD + ROWS * q : HEAD + ROWS * (q + 1), :],
-            recv_ref[right, HEAD + ROWS * q : HEAD + ROWS * (q + 1), :],
-        )
-        for q in range(pack_count)
-    ]
-    for plane in range(planes):
-        for h in range(2):
-            at = pl.ds(plane * 16 + ROWS * h, ROWS)
-            avg_ref[at, :] = geo.sum_y(
-                moved_ref[at, :], outer_edges(joined, 2 * plane + h)
-            )
+    joined = join_edges(
+        geo,
+        recv_ref[left, EDGE_AT : EDGE_AT + ROWS, :],
+        recv_ref[right, EDGE_AT : EDGE_AT + ROWS, :],
+    )
+    for x in range(x_points):
+        for group in range(planes // ROWS):
+            at = slice(planes * x + ROWS * group, planes * x + ROWS * (group + 1))
+            avg_ref[at, :] = geo.sum_y(moved_ref[at, :], outer_edges(joined, x, group))
 
     def line(r):
-        return avg_ref[pl.ds(r, planes, stride=16), :]
+        return avg_ref[planes * r : planes * (r + 1), :]
 
     def surf_line(number, r):
-        return surf_ref[pl.ds(4 * ROWS * number + r, 2, stride=16), :]
+        return surf_ref[pl.ds(4 * ROWS * number + r, 2, stride=x_points), :]
 
     def first_step(get, mass_at):
         return (
@@ -447,7 +525,7 @@
         slope = sum(coef * value for coef, value in zip(coefs, lines))
         surf_slope = sum(coef * value for coef, value in zip(coefs, surf_lines))
         mass = surf_ref[4 * ROWS * MASS + r : 4 * ROWS * MASS + r + 1, :]
-        wind = time_step * mass * wind_ref[pl.ds(r, 2 * levels, stride=16), :]
+        wind = time_step * mass * wind_ref[pl.ds(r, 2 * levels, stride=x_points), :]
         out_ref[0:planes, :] = line(r)
         for first in range(0, planes, levels):
             out_ref[planes + first : planes + first + levels, :] = (
@@ -462,27 +540,12 @@
         out_ref[base : base + 2, :] = surf_line(COEF_X, r) * surf_slope
 
 
-def second_kernel(
-    planes,
-    avg_ref,
-    surf_ref,
-    low_ref,
-    high_ref,
-    wind_ref,
-    rows_ref,
-    after_ref,
-    slab_ref,
-    sums_ref,
-    final_ref,
-    inverse_ref,
-    low_halo,
-    high_halo,
+def surface_kernel(
+    surf_ref, low_ref, high_ref, rows_ref, after_ref, slab_ref, final_ref, inverse_ref
 ):
     geo = Geometry()
     blocks = rows_ref.shape[0]
-    left, right = neighbours_of(blocks)
-    levels = wind_ref.shape[0] // 32
-    base = 2 * planes + 2 * levels
+    base = low_ref.shape[0] - 2 * SURF_ARRAYS - 4
 
     def surf_tile(number, tile, h):
         at = 4 * ROWS * number + 2 * ROWS * tile + ROWS * h
@@ -548,76 +611,99 @@
         for c in range(ROWS):
             slab_ref[ROWS * group + c, 0:1, :] = picked[c : c + 1]
 
-    for ref, halo, r, own_coef, scale in (
-        (low_ref, low_halo, 0, deriv_table[3][3], inverse[0][0][:1]),
-        (high_ref, high_halo, 15, deriv_table[0][0], inverse[0][1][ROWS - 1 :]),
-    ):
-        field = (avg_ref[pl.ds(r, planes, stride=16), :] + ref[0:planes, :]) * scale
-        mass = beside(ref, MASS, 0)
-        for first in range(0, planes, ROWS):
-            part = field[first : first + ROWS]
-            wind_at = 2 * planes + first % levels
-            halo[first : first + ROWS, :] = (
-                mass * part
-                - ref[planes + first : planes + first + ROWS, :]
-                - ref[wind_at : wind_at + ROWS, :] * (own_coef * part)
-                - ref[wind_at + levels : wind_at + levels + ROWS, :] * geo.d_y(part)[0]
-            )
-
-    mass = [surf_tile(MASS, 0, h) for h in range(2)]
-    packs = [
-        jnp.zeros((ROWS, LANES), jnp.float32) for _ in range(-(-2 * planes // PAIRS))
-    ]
-    for level in range(levels):
-        wind = [
-            [
-                time_step * wind_ref[pl.ds((i * levels + level) * 16 + ROWS * h, ROWS), :]
-                for h in range(2)
-            ]
-            for i in range(2)
-        ]
-        group = list(range(level, planes, levels))
-        fields = []
-        for plane in group:
-            summed = geo.sum_x(
-                avg_ref[pl.ds(plane * 16, ROWS), :],
-                avg_ref[pl.ds(plane * 16 + ROWS, ROWS), :],
-                spread(low_ref[plane : plane + 1, :]),
-                spread(high_ref[plane : plane + 1, :]),
-            )
-            fields += [summed[h] * inverse[0][h] for h in range(2)]
-        slopes = geo.d_y(*fields)
-        for number, plane in enumerate(group):
+
+def second_kernel(
+    planes,
+    avg_ref,
+    surf_ref,
+    inverse_ref,
+    low_ref,
+    high_ref,
+    wind_ref,
+    sums_ref,
+    edges_ref,
+):
+    geo = Geometry()
+    x_points = inverse_ref.shape[0]
+    levels = wind_ref.shape[0] // (2 * x_points)
+    surf_base = low_ref.shape[0] - 2 * SURF_ARRAYS - 4
+    packs = [jnp.zeros((ROWS, LANES), jnp.float32) for _ in range(2)]
+
+    def put(x, plane, value):
+        sums_ref[planes * x + plane : planes * x + plane + ROWS, :] = value
+        pack_edges(geo, packs, value, x, plane // ROWS)
+
+    def beyond(ref, plane, field, slope, own_coef):
+        mass_at = surf_base + 2 * MASS
+        wind_at = 2 * planes + plane % levels
+        return (
+            spread(ref[mass_at : mass_at + 1, :]) * field
+            - ref[planes + plane : planes + plane + ROWS, :]
+            - ref[wind_at : wind_at + ROWS, :] * (own_coef * field)
+            - ref[wind_at + levels : wind_at + levels + ROWS, :] * slope
+        )
+
+    for plane in range(0, planes, ROWS):
+        here = slice(plane, plane + ROWS)
+        held = None
+        for element in range(x_points // GLL):
+            lines = [GLL * element + i for i in range(GLL)]
+            fields = []
+            for i, x in enumerate(lines):
+                total = avg_ref[planes * x + plane : planes * x + plane + ROWS, :]
+                other = x - 1 if i == 0 else x + 1
+                if other < 0:
+                    total = total + low_ref[here, :]
+                elif other == x_points:
+                    total = total + high_ref[here, :]
+                elif i in (0, GLL - 1):
+                    at = planes * other + plane
+                    total = total + avg_ref[at : at + ROWS, :]
+                fields.append(total * spread(inverse_ref[x : x + 1, :]))
+            slopes = geo.d_y(*fields)
             moved = []
-            for h in range(2):
-                field = fields[2 * number + h]
+            for i, x in enumerate(lines):
+                wind = [
+                    time_step
+                    * wind_ref[
+                        pl.ds(
+                            (levels * part + plane % levels) * x_points + x,
+                            ROWS,
+                            stride=x_points,
+                        ),
+                        :,
+                    ]
+                    for part in range(2)
+                ]
+                slope = sum(deriv_table[i][j] * fields[j] for j in range(GLL))
+                mass_at = 4 * ROWS * MASS + x
                 moved.append(
-                    mass[h]
-                    * (
-                        field
-                        - (
-                            wind[0][h] * geo.d_x(field)
-                            + wind[1][h] * slopes[2 * number + h]
-                        )
-                    )
+                    spread(surf_ref[mass_at : mass_at + 1, :])
+                    * (fields[i] - (wind[0] * slope + wind[1] * slopes[i]))
                 )
-            summed = geo.sum_x(
-                moved[0],
-                moved[1],
-                spread(low_halo[plane : plane + 1, :]),
-                spread(high_halo[plane : plane + 1, :]),
-            )
-            for h in range(2):
-                sums_ref[pl.ds(plane * 16 + ROWS * h, ROWS), :] = summed[h]
-                pack_edges(geo, packs, summed[h], 2 * plane + h)
-    for to in (left, right):
-        for q, pack in enumerate(packs):
-            slab_ref[to, HEAD + ROWS * q : HEAD + ROWS * (q + 1), :] = pack
+            first, last = lines[0], lines[-1]
+            if first == 0:
+                before = beyond(low_ref, plane, fields[0], slopes[0], deriv_table[3][3])
+                put(first, plane, before + moved[0])
+            else:
+                shared = held + moved[0]
+                put(first - 1, plane, shared)
+                put(first, plane, shared)
+            for i in range(1, GLL - 1):
+                put(lines[i], plane, moved[i])
+            held = moved[-1]
+            if last == x_points - 1:
+                after = beyond(high_ref, plane, fields[-1], slopes[-1], deriv_table[0][0])
+                put(last, plane, held + after)
+    for q, pack in enumerate(packs):
+        edges_ref[ROWS * q : ROWS * (q + 1), :] = pack
 
 
 def end_kernel(
     planes,
     sums_ref,
+    before_ref,
+    after_ref,
     recv_ref,
     final_ref,
     inverse_ref,
@@ -630,7 +716,6 @@
 ):
     geo = Geometry()
     blocks = cols_ref.shape[0]
-    left, right = neighbours_of(blocks)
     chunks = gain_ref.shape[0]
     arrived = jnp.concatenate([recv_ref[c, 0:1, :] for c in range(blocks)], axis=0)
     (inflow,) = scatter_sum([weights_ref[...] * arrived], cols_ref[...], chunks)
@@ -640,24 +725,25 @@
         at = slice(LANES * k, LANES * (k + 1))
         ocean_out[0:1, at] = ocean_ref[0:1, at] + gain[k : k + 1]
 
+    x_points = inverse_ref.shape[0]
+    odd = (geo.lane & 1) != 0
     joined = [
-        join_edges(
-            geo,
-            recv_ref[left, HEAD + ROWS * q : HEAD + ROWS * (q + 1), :],
-            recv_ref[right, HEAD + ROWS * q : HEAD + ROWS * (q + 1), :],
-        )
-        for q in range(-(-2 * planes // PAIRS))
+        jnp.where(
+            odd,
+            pltpu.roll(before_ref[ROWS * q : ROWS * (q + 1), :], 1, 1),
+            pltpu.roll(after_ref[ROWS * q : ROWS * (q + 1), :], LANES - 1, 1),
+        )
+        for q in range(2)
     ]
-    inverse = [inverse_ref[ROWS * h : ROWS * (h + 1), :] for h in range(2)]
-    for plane in range(planes):
-        for h in range(2):
-            at = pl.ds(plane * 16 + ROWS * h, ROWS)
-            if plane == 0:
-                air_out[at, :] = final_ref[ROWS * h : ROWS * (h + 1), :]
-            else:
-                air_out[at, :] = inverse[h] * geo.sum_y(
-                    sums_ref[at, :], outer_edges(joined, 2 * plane + h)
-                )
+    for x in range(x_points):
+        inverse = spread(inverse_ref[x : x + 1, :])
+        for group in range(planes // ROWS):
+            at = planes * x + ROWS * group
+            air_out[pl.ds(ROWS * group * x_points + x, ROWS, stride=x_points), :] = (
+                inverse
+                * geo.sum_y(sums_ref[at : at + ROWS, :], outer_edges(joined, x, group))
+            )
+    air_out[0:x_points, :] = final_ref[...]
 
 
 def gathered(ids, coefs, source, sources, groups, first=0):
@@ -673,49 +759,47 @@
     return totals
 
 
-def ocean_kernel(levels, number, tracers_ref, coef_ref, near_ref, rate_ref, after_ref, out_ref):
+def ocean_kernel(
+    levels, start, tracers_ref, coef_ref, near_ref, rate_ref, after_ref, out_ref
+):
     chunks = tracers_ref.shape[1] // LANES
-    groups = levels // ROWS
-    base = levels * number
+    groups = tracers_ref.shape[0] // ROWS
     row = iota((ROWS, LANES), 0)
 
     def source(group, s):
         return tracers_ref[
-            base + ROWS * group : base + ROWS * (group + 1), LANES * s : LANES * (s + 1)
+            ROWS * group : ROWS * (group + 1), LANES * s : LANES * (s + 1)
         ]
 
-    def one_chunk(k, carry):
+    def one_chunk(number, carry):
+        k = number + start
         at = pl.ds(pl.multiple_of(k * LANES, LANES), LANES)
+        out_at = pl.ds(pl.multiple_of(number * LANES, LANES), LANES)
         ids, coefs = near_ref[:, at], coef_ref[:, at]
         totals = gathered(ids, coefs, source, chunks, groups)
         coef_sum = spread(jnp.sum(coefs, axis=0, keepdims=True))
         rate = spread(rate_ref[pl.ds(k, 1), :])
-        tiles = [
-            tracers_ref[base + ROWS * g : base + ROWS * (g + 1), at]
-            for g in range(groups)
-        ]
+        tiles = [tracers_ref[ROWS * g : ROWS * (g + 1), at] for g in range(groups)]
         for g in range(groups):
             tile = tiles[g]
-            above = pltpu.roll(tile, 1, 0)
-            below = pltpu.roll(tile, ROWS - 1, 0)
-            top = pltpu.roll(tiles[g - 1], 1, 0) if g else tile
-            bottom = tile
-            if g + 1 < groups:
+            top = bottom = tile
+            if (ROWS * g) % levels:
+                top = pltpu.roll(tiles[g - 1], 1, 0)
+            if (ROWS * (g + 1)) % levels:
                 bottom = pltpu.roll(tiles[g + 1], ROWS - 1, 0)
-            above = jnp.where(row == 0, top, above)
-            below = jnp.where(row == ROWS - 1, bottom, below)
+            above = jnp.where(row == 0, top, pltpu.roll(tile, 1, 0))
+            below = jnp.where(row == ROWS - 1, bottom, pltpu.roll(tile, ROWS - 1, 0))
             vertical = rate * ((above - tile) + (below - tile))
-            out_ref[ROWS * g : ROWS * (g + 1), at] = (
+            out_ref[ROWS * g : ROWS * (g + 1), out_at] = (
                 tile + (totals[g] - coef_sum * tile) + vertical
             )
         return carry
 
-    lax.fori_loop(0, chunks, one_chunk, 0)
+    lax.fori_loop(0, out_ref.shape[1] // LANES, one_chunk, 0)
 
 
 def rim_kernel(
-    rim_at,
-    parts,
+    starts,
     recv_ref,
     coef_ref,
     near_ref,
@@ -723,23 +807,25 @@
     after_ref,
     *refs,
 ):
-    partial_refs, (out_ref, gain_ref) = refs[:parts], refs[parts:]
+    partial_refs, (out_ref, gain_ref) = refs[: len(starts)], refs[len(starts) :]
     chunks = coef_ref.shape[1] // LANES
     groups = out_ref.shape[0] // ROWS
-    part_groups = groups // parts
-    sides = neighbours_of(recv_ref.shape[0])
+    blocks = recv_ref.shape[0]
+    sides = neighbours_of(blocks)
     gain_ref[...] = flux_gain / area_ref[...]
 
     def source(group, s):
-        return recv_ref[sides[s], rim_at + ROWS * group : rim_at + ROWS * (group + 1), :]
+        at = IDS_AT + blocks + ROWS * group
+        return recv_ref[sides[s], at : at + ROWS, :]
 
     for k in range(chunks):
         at = slice(LANES * k, LANES * (k + 1))
         totals = gathered(near_ref[:, at], coef_ref[:, at], source, 2, groups, chunks)
+        part = max(i for i, start in enumerate(starts) if start <= k)
+        place = slice(LANES * (k - starts[part]), LANES * (k - starts[part] + 1))
         for g in range(groups):
-            place = ROWS * (g % part_groups)
-            partial = partial_refs[g // part_groups][place : place + ROWS, at]
-            out_ref[ROWS * g : ROWS * (g + 1), at] = partial + totals[g]
+            half = slice(ROWS * g, ROWS * (g + 1))
+            out_ref[half, at] = partial_refs[part][half, place] + totals[g]
 
 
 VMEM_SPEC = pl.BlockSpec(memory_space=pltpu.VMEM)
@@ -788,9 +874,6 @@
     point_ids, cell_ids, weights = xgrid_rows[0], xgrid_cols[0], xgrid_weights[0]
     rate = vert_rate.reshape(cells // LANES, LANES)
     area = ocean_area.reshape(cells // LANES, LANES)
-    edge_rows = ROWS * (-(-2 * planes // PAIRS))
-    rim_at = HEAD + edge_rows + 2 * ROWS + blocks
-
     first_inputs = (
         cell_ids,
         weights,
@@ -802,62 +885,72 @@
         wind,
         air,
     )
-    slab, moved = call(
+    (slab,) = call(
         functools.partial(start_kernel, planes, len(first_inputs)),
-        [(blocks, rim_at + ocean_planes, LANES), air.shape],
+        [(blocks, IDS_AT + blocks + ocean_planes, LANES)],
         [HBM_SPEC] * len(first_inputs),
         [pltpu.VMEM(array.shape, array.dtype) for array in first_inputs]
         + [pltpu.SemaphoreType.DMA((len(first_inputs),))],
     )(*(pltpu.with_memory_space_constraint(array, pltpu.HBM) for array in first_inputs))
     recv = lax.all_to_all(slab, "blk", split_axis=0, concat_axis=0, tiled=True)
 
-    parts = tracers.shape[0]
-    tile_reads = edge_coef.shape[0] * (cells // LANES) ** 2 * ocean_levels // ROWS
-
-    def ocean_part(number, after):
+    chunks = cells // LANES
+    reads_per_chunk = edge_coef.shape[0] * chunks * (ocean_planes // ROWS)
+    starts = (0, chunks * 5 // 8)
+
+    def ocean_part(start, end, after):
         (result,) = call(
-            functools.partial(ocean_kernel, ocean_levels, number),
-            [(ocean_levels, cells)],
+            functools.partial(ocean_kernel, ocean_levels, start),
+            [(ocean_planes, (end - start) * LANES)],
             [VMEM_SPEC] * 4 + [ANY_SPEC],
-            cost=tile_reads * ROWS * LANES * 4,
+            cost=(end - start) * reads_per_chunk * ROWS * LANES * 4,
         )(ocean, edge_coef, neighbours, rate, after)
         return result
 
-    first_part = ocean_part(0, moved)
+    (moved,) = call(
+        functools.partial(moved_kernel, planes),
+        [air.shape],
+        [VMEM_SPEC] * 3 + [ANY_SPEC],
+        cost=4 * air.size * 4,
+    )(air, wind, jacobian, slab)
+    first_part = ocean_part(starts[0], starts[1], slab)
     side_rows = 2 * planes + 2 * levels + 2 * SURF_ARRAYS + 4
     avg, down, up, surf = call(
         functools.partial(panel_kernel, planes),
         [air.shape, (side_rows, LANES), (side_rows, LANES), (4 * ROWS * SURF_ARRAYS, LANES)],
         [VMEM_SPEC] * 7 + [ANY_SPEC],
     )(moved, recv, air, wind, jacobian, land_area, point_ids, first_part)
-    ring = [(i, (i + 1) % faces) for i in range(faces)]
-    low = lax.ppermute(up, "face", ring)
-    high = lax.ppermute(down, "face", [(target, source) for source, target in ring])
-    second_part = ocean_part(1, surf)
-
-    slab, sums, final, inverse = call(
+    after_me = [(i, (i + 1) % faces) for i in range(faces)]
+    low = lax.ppermute(up, "face", after_me)
+    high = lax.ppermute(down, "face", [(to, source) for source, to in after_me])
+    second_part = ocean_part(starts[1], chunks, surf)
+
+    slab, final, inverse = call(
+        surface_kernel,
+        [(blocks, ROWS, LANES), (x_points, y_points), (x_points, y_points)],
+        [VMEM_SPEC] * 4 + [ANY_SPEC],
+    )(surf, low, high, point_ids, second_part)
+    arrived = lax.all_to_all(slab, "blk", split_axis=0, concat_axis=0, tiled=True)
+    sums, edges = call(
         functools.partial(second_kernel, planes),
-        [
-            (blocks, HEAD + edge_rows, LANES),
-            air.shape,
-            (x_points, y_points),
-            (x_points, y_points),
-        ],
-        [VMEM_SPEC] * 6 + [ANY_SPEC],
-        [pltpu.VMEM((planes, LANES), jnp.float32) for _ in range(2)],
-    )(avg, surf, low, high, wind, point_ids, second_part)
-    arrived = lax.all_to_all(slab, "blk", split_axis=0, concat_axis=0, tiled=True)
+        [air.shape, (2 * ROWS, LANES)],
+        [VMEM_SPEC] * 6,
+        cost=4 * air.size * 4,
+    )(avg, surf, inverse, low, high, wind)
+    after_me = [(i, (i + 1) % blocks) for i in range(blocks)]
+    before = lax.ppermute(edges, "blk", after_me)
+    after = lax.ppermute(edges, "blk", [(to, source) for source, to in after_me])
     partial, gain = call(
-        functools.partial(rim_kernel, rim_at, parts),
+        functools.partial(rim_kernel, starts),
         [ocean.shape, area.shape],
-        [VMEM_SPEC] * 4 + [ANY_SPEC] + [VMEM_SPEC] * parts,
-        cost=tile_reads * ROWS * LANES,
-    )(recv, edge_coef, neighbours, area, final, first_part, second_part)
+        [VMEM_SPEC] * 4 + [ANY_SPEC] + [VMEM_SPEC] * len(starts),
+        cost=chunks * reads_per_chunk // 8 * ROWS * LANES * 4,
+    )(recv, edge_coef, neighbours, area, edges, first_part, second_part)
     air_final, ocean_final = call(
         functools.partial(end_kernel, planes),
         [air.shape, ocean.shape],
-        [VMEM_SPEC] * 8,
-    )(sums, arrived, final, inverse, cell_ids, weights, gain, partial)
+        [VMEM_SPEC] * 10,
+    )(sums, before, after, arrived, final, inverse, cell_ids, weights, gain, partial)
     return air_final.reshape(air_state.shape), ocean_final.reshape(tracers.shape)
 
 

time: 39.5 us -> 39.4 us (level)
  waiting for transfers between devices: 6.7 us -> 3.72 us
  starting transfers between devices: 12.7 us -> 15.5 us
    all_to_all x1, waiting for transfers between devices: 3.9 us -> 0.01 us  [body(): lax.all_to_all(slab, 'blk', split_axis=0, concat_axis=0, tiled=True)]
    ppermute x2 -> x4, waiting for transfers between devices: 0.01 us -> 2.77 us  [the longest x1 2.61 us: body(): before = lax.ppermute(edges, 'blk', after_me)]
    ppermute x2 -> x4, starting transfers between devices: 3.88 us -> 6.59 us  [the longest x1 2.71 us: body(): lax.ppermute(edges, 'blk', [(to, source) for source, to in after_me])]
    all_to_all x1, waiting for transfers between devices: 2.8 us -> 0.94 us  [body(): recv = lax.all_to_all(slab, 'blk', split_axis=0, concat_axis=0, tiled=True)]
    pallas_call x4 -> x6, Pallas kernels: 13.4 us -> 13 us  [the longest x2 7.97 us: ocean_part(): call(functools.partial(ocean_kernel, ocean_levels, start), [(ocean_planes...]
  transfers between devices with their start and end apart: 4 -> 6, of which waited for: 2 -> 3; matrix products, arithmetic and copies ran while one was open for 0% -> 0% of each run, Pallas kernels for 27% -> 31%
where the time goes in v4:
time: 39.4 us; the launch traced here: 39 us
  Pallas kernels  18.8 us (48%)
  starting transfers between devices  15.5 us (39%)
  waiting for transfers between devices  3.72 us (9%)
  between operations  0.8 us (2%)
    pallas_call x2, Pallas kernels, ocean_part(): call(functools.partial(ocean_kernel, ocean_levels, start), [(ocean_planes...  7.97 us
    all_to_all x1, starting transfers between devices, body(): recv = lax.all_to_all(slab, 'blk', split_axis=0, concat_axis=0, tiled=True)  5.31 us
    pallas_call x1, Pallas kernels, body(): call(functools.partial(start_kernel, planes, len(first_inputs)), [(blocks...  4.08 us
    all_to_all x1, starting transfers between devices, body(): lax.all_to_all(slab, 'blk', split_axis=0, concat_axis=0, tiled=True)  3.63 us
    ppermute x1, starting transfers between devices, body(): lax.ppermute(edges, 'blk', [(to, source) for source, to in after_me])  2.71 us
    ppermute x1, waiting for transfers between devices, body(): before = lax.ppermute(edges, 'blk', after_me)  2.61 us
    ppermute x1, starting transfers between devices, body(): high = lax.ppermute(down, 'face', [(to, source) for source, to in after_me])  2.25 us
    pallas_call x1, Pallas kernels, body(): call(functools.partial(second_kernel, planes), [air.shape, (2 * ROWS, LAN...  2.19 us
  transfers between devices with their start and end apart: 6, of which 3 were waited for; matrix products, arithmetic and copies ran while one was open for 0% of the time, Pallas kernels for 31%

profile of v4, /device:TPU:0, one launch (start us, length us, event | category | flops | bytes accessed | tf_op | source)
XLA Modules:
  0.0 39.0 jit_solution(13679731543984244698)
XLA Ops:
  0.6 0.0 copy-start.1
  0.6 4.1 %start_kernel.1.after_ref = f32[8,64,128]{2,1,0:T(8,128)} custom-call(s32[8,128]{1,0:T(8,128)} %bitcast.25, f32[8,128]{1,0:T(8,128)} %bitcast.27, f32[32,2048]{1,0:T(8,128)} %bitcast.17, s32[1,256]{1,0:T(1,128)} %refs_3_.1, s32[8,128]{1,0:T(8,128)} %bitcast.20, f32[16,128]{1,0:T(8,128)} %jac_ref.3, f32[16,128]{1,0:T(8,128)} %land_ref.1, ...), custom_call_target="tpu_custom_call" | custom-call | tf_op jit(solution)/shard_map/start_kernel/pallas_call | solution.py:888
  4.7 0.0 copy-start
  4.7 0.0 copy-start.5
  4.8 5.3 %all-to-all-start = ((f32[8,64,128]{2,1,0:T(8,128)}), f32[8,64,128]{2,1,0:T(8,128)S(1)}, u32[]{:S(2)}, u32[]{:S(2)}) async-start(f32[8,64,128]{2,1,0:T(8,128)} %start_kernel.1.after_ref), calls=%async_computation | async-start | bytes 524288 | tf_op jit(solution)/shard_map/all_to_all | solution.py:895
  10.1 0.0 copy-done.1
  10.1 0.0 copy-done
  10.1 0.0 copy-done.5
  10.1 0.0 copy-start.2
  10.1 0.0 copy-start.3
  10.1 0.0 copy-start.4
  10.1 0.0 copy-start.8
  10.1 0.8 %moved_kernel.1.moved_ref = f32[768,128]{1,0:T(8,128)S(1)} custom-call(f32[768,128]{1,0:T(8,128)S(1)} %bitcast.15, f32[512,128]{1,0:T(8,128)S(1)} %bitcast.11, f32[16,128]{1,0:T(8,128)S(1)} %copy-done.5, f32[8,64,128]{2,1,0:T(8,128)} %start_kernel.1.after_ref), custom_call_target="tpu_custom_call" | custom-call | bytes 1572864 | tf_op jit(solution)/shard_map/moved_kernel/pallas_call | solution.py:910
  10.9 0.1 copy-done.2
  11.0 0.0 copy-done.3
  11.0 0.0 copy-done.4
  11.1 0.0 copy-done.8
  11.1 0.0 copy-start.6
  11.1 0.0 copy-start.7
  11.1 5.0 %ocean_kernel.2.after_ref.refs_0_ = f32[32,1280]{1,0:T(8,128)S(1)} custom-call(f32[32,2048]{1,0:T(8,128)S(1)} %bitcast.18, f32[6,2048]{1,0:T(8,128)S(1)} %copy-done.3, s32[6,2048]{1,0:T(8,128)S(1)} %copy-done.4, f32[16,128]{1,0:T(8,128)S(1)} %bitcast.23, f32[8,64,128]{2,1,0:T(8,128)} %start_kernel.1.after_ref), custom_call_target="tpu_custom_call" | custom-call | bytes 15728640 | tf_op jit(solution)/shard_map/ocean_kernel/pallas_call | solution.py:902
  16.1 0.9 %all-to-all-done.recv_ref = f32[8,64,128]{2,1,0:T(8,128)S(1)} async-done(((f32[8,64,128]{2,1,0:T(8,128)}), f32[8,64,128]{2,1,0:T(8,128)S(1)}, u32[]{:S(2)}, u32[]{:S(2)}) %all-to-all-start) | async-done | bytes 262176 | tf_op jit(solution)/shard_map/all_to_all | solution.py:895
  17.0 0.0 copy-done.6
  17.0 0.0 copy-done.7
  17.0 0.5 %panel_kernel.1 = (f32[768,128]{1,0:T(8,128)S(1)}, f32[144,128]{1,0:T(8,128)S(1)}, f32[144,128]{1,0:T(8,128)S(1)}, f32[192,128]{1,0:T(8,128)S(1)}) custom-call(f32[768,128]{1,0:T(8,128)S(1)} %moved_kernel.1.moved_ref, f32[8,64,128]{2,1,0:T(8,128)S(1)} %all-to-all-done.recv_ref, f32[768,128]{1,0:T(8,128)S(1)} %bitcast.16, f32[512,128]{1,0:T(8,128)S(1)} %bitcast.12, ...), custom_call_target="tpu_custom_call" | custom-call | tf_op jit(solution)/shard_map/panel_kernel/pallas_call | solution.py:918
  17.5 1.6 %collective-permute-start = (f32[144,128]{1,0:T(8,128)S(1)}, f32[144,128]{1,0:T(8,128)S(1)}, u32[]{:S(2)}, u32[]{:S(2)}) collective-permute-start(f32[144,128]{1,0:T(8,128)S(1)} %get-tuple-element.17), channel_id=1, source_target_pairs={{0,8},{8,16},{16,24},{24,0},{1,9},{9,17},{17,25},{25,1},{2,10},{10... | collective-permute-start | bytes 221192 | tf_op jit(solution)/shard_map/ppermute | solution.py:924
  19.1 2.2 %collective-permute-start.1 = (f32[144,128]{1,0:T(8,128)S(1)}, f32[144,128]{1,0:T(8,128)S(1)}, u32[]{:S(2)}, u32[]{:S(2)}) collective-permute-start(f32[144,128]{1,0:T(8,128)S(1)} %get-tuple-element.18), channel_id=1, source_target_pairs={{8,0},{16,8},{24,16},{0,24},{9,1},{17,9},{25,17},{1,25},{10,2},{18... | collective-permute-start | bytes 221192 | tf_op jit(solution)/shard_map/ppermute | solution.py:925
  21.4 3.0 %ocean_kernel.3.after_ref.refs_1_ = f32[32,768]{1,0:T(8,128)S(1)} custom-call(f32[32,2048]{1,0:T(8,128)S(1)} %bitcast.19, f32[6,2048]{1,0:T(8,128)S(1)} %copy-done.3, s32[6,2048]{1,0:T(8,128)S(1)} %copy-done.4, f32[16,128]{1,0:T(8,128)S(1)} %bitcast.24, f32[192,128]{1,0:T(8,128)S(1)} %get-tuple-element.16.after_ref.surf_ref), custom_call_target="tpu_custom_call" | custom-call | bytes 9437184 | tf_op jit(solution)/shard_map/ocean_kernel/pallas_call | solution.py:902
  24.4 0.0 collective-permute-done.low_ref
  24.4 0.0 collective-permute-done.1.high_ref
  24.4 0.9 %surface_kernel.1 = (f32[8,8,128]{2,1,0:T(8,128)}, f32[16,128]{1,0:T(8,128)S(1)}, f32[16,128]{1,0:T(8,128)S(1)}) custom-call(f32[192,128]{1,0:T(8,128)S(1)} %get-tuple-element.16.after_ref.surf_ref, f32[144,128]{1,0:T(8,128)S(1)} %collective-permute-done.low_ref, f32[144,128]{1,0:T(8,128)S(1)} %collective-permute-done.1.high_ref, s32[8,128]{1,0:T(8,128)S(1)} %bitcast.22, ...), custom_call_target="tpu_custom_call" | custom-call | tf_op jit(solution)/shard_map/surface_kernel/pallas_call | solution.py:928
  25.3 3.6 %all-to-all-start.1 = ((f32[8,8,128]{2,1,0:T(8,128)}), f32[8,8,128]{2,1,0:T(8,128)S(1)}, u32[]{:S(2)}, u32[]{:S(2)}) async-start(f32[8,8,128]{2,1,0:T(8,128)} %get-tuple-element.22), calls=%async_computation.1 | async-start | bytes 65536 | tf_op jit(solution)/shard_map/all_to_all | solution.py:933
  29.0 0.0 copy-start.11
  29.0 2.2 %second_kernel.1 = (f32[768,128]{1,0:T(8,128)S(1)}, f32[16,128]{1,0:T(8,128)S(1)}) custom-call(f32[768,128]{1,0:T(8,128)S(1)} %get-tuple-element.15.avg_ref, f32[192,128]{1,0:T(8,128)S(1)} %get-tuple-element.16.after_ref.surf_ref, f32[16,128]{1,0:T(8,128)S(1)} %get-tuple-element.19.inverse_ref, f32[144,128]{1,0:T(8,128)S(1)} %collective-permute-done.low_ref, ...), custom_call_target="tpu_custom_call" | custom-call | bytes 1572864 | tf_op jit(solution)/shard_map/second_kernel/pallas_call | solution.py:934
  31.2 2.7 %collective-permute-start.3 = (f32[16,128]{1,0:T(8,128)S(1)}, f32[16,128]{1,0:T(8,128)S(1)}, u32[]{:S(2)}, u32[]{:S(2)}) collective-permute-start(f32[16,128]{1,0:T(8,128)S(1)} %get-tuple-element.21.after_ref), channel_id=1, source_target_pairs={{1,0},{2,1},{3,2},{4,3},{5,4},{6,5},{7,6},{0,7},{9,8},{10,9},{11,1... | collective-permute-start | bytes 24584 | tf_op jit(solution)/shard_map/ppermute | solution.py:942
  33.9 0.0 collective-permute-start.2
  33.9 0.0 copy-done.11
  33.9 0.0 copy-start.10
  33.9 1.2 %rim_kernel.1 = (f32[32,2048]{1,0:T(8,128)S(1)}, f32[16,128]{1,0:T(8,128)S(1)}) custom-call(f32[8,64,128]{2,1,0:T(8,128)S(1)} %all-to-all-done.recv_ref, f32[6,2048]{1,0:T(8,128)S(1)} %copy-done.3, s32[6,2048]{1,0:T(8,128)S(1)} %copy-done.4, f32[16,128]{1,0:T(8,128)S(1)} %bitcast.29, f32[16,128]{1,0:T(8,128)S(1)} %get-tuple-element.21.after_ref, ...), custom_call_target="tpu_custom_call" | custom-call | bytes 3145728 | tf_op jit(solution)/shard_map/rim_kernel/pallas_call | solution.py:943
  35.1 0.0 copy-start.9
  35.1 0.2 collective-permute-done.3.after_ref
  35.2 2.6 %collective-permute-done.2.before_ref = f32[16,128]{1,0:T(8,128)S(1)} collective-permute-done((f32[16,128]{1,0:T(8,128)S(1)}, f32[16,128]{1,0:T(8,128)S(1)}, u32[]{:S(2)}, u32[]{:S(2)}) %collective-permute-start.2) | collective-permute-done | bytes 8224 | tf_op jit(solution)/shard_map/ppermute | solution.py:941
  37.9 0.0 all-to-all-done.1.recv_ref
  37.9 0.0 copy-done.10
  37.9 0.0 copy-done.9
  37.9 1.2 %end_kernel.1 = (f32[768,128]{1,0:T(8,128)}, f32[32,2048]{1,0:T(8,128)}) custom-call(f32[768,128]{1,0:T(8,128)S(1)} %get-tuple-element.20.sums_ref, f32[16,128]{1,0:T(8,128)S(1)} %collective-permute-done.2.before_ref, f32[16,128]{1,0:T(8,128)S(1)} %collective-permute-done.3.after_ref, f32[8,8,128]{2,1,0:T(8,128)S(1)} %all-to-all-done.1.recv_ref, ...), custom_call_target="tpu_custom_call" | custom-call | tf_op jit(solution)/shard_map/end_kernel/pallas_call | solution.py:949
Async XLA Ops:
  0.6 9.4 %copy-start.1 = (f32[3,16,16,128]{3,2,1,0:T(8,128)S(1)}, f32[3,16,16,128]{3,2,1,0:T(8,128)}, u32[]{:S(2)}) copy-start(f32[3,16,16,128]{3,2,1,0:T(8,128)} %param.13) | copy-start | bytes 1179652
  4.7 5.3 %copy-start = (f32[2,16,16,128]{3,2,1,0:T(8,128)S(1)}, f32[2,16,16,128]{3,2,1,0:T(8,128)}, u32[]{:S(2)}) copy-start(f32[2,16,16,128]{3,2,1,0:T(8,128)} %param.14) | copy-start | bytes 786436
  4.7 5.3 %copy-start.5 = (f32[16,128]{1,0:T(8,128)S(1)}, f32[16,128]{1,0:T(8,128)}, u32[]{:S(2)}) copy-start(f32[16,128]{1,0:T(8,128)} %jac_ref.3) | copy-start | bytes 24580
  4.8 12.3 %all-to-all-start = ((f32[8,64,128]{2,1,0:T(8,128)}), f32[8,64,128]{2,1,0:T(8,128)S(1)}, u32[]{:S(2)}, u32[]{:S(2)}) async-start(f32[8,64,128]{2,1,0:T(8,128)} %start_kernel.1.after_ref), calls=%async_computation | async-start | bytes 524288 | tf_op jit(solution)/shard_map/all_to_all | solution.py:895
  10.1 1.0 %copy-start.2 = (f32[2,16,2048]{2,1,0:T(8,128)S(1)}, f32[2,16,2048]{2,1,0:T(8,128)}, u32[]{:S(2)}) copy-start(f32[2,16,2048]{2,1,0:T(8,128)} %param.18) | copy-start | bytes 786436
  10.1 0.9 %copy-start.3 = (f32[6,2048]{1,0:T(8,128)S(1)}, f32[6,2048]{1,0:T(8,128)}, u32[]{:S(2)}) copy-start(f32[6,2048]{1,0:T(8,128)} %coef_ref.5) | copy-start | bytes 147460
  10.1 0.9 %copy-start.4 = (s32[6,2048]{1,0:T(8,128)S(1)}, s32[6,2048]{1,0:T(8,128)}, u32[]{:S(2)}) copy-start(s32[6,2048]{1,0:T(8,128)} %near_ref.5) | copy-start | bytes 147460
  10.1 0.9 %copy-start.8 = (f32[2048]{0:T(1024)S(1)}, f32[2048]{0:T(1024)}, u32[]{:S(2)}) copy-start(f32[2048]{0:T(1024)} %param.21) | copy-start | bytes 24580
  11.1 6.0 %copy-start.6 = (s32[1,8,128]{2,1,0:T(8,128)S(1)}, s32[1,8,128]{2,1,0:T(8,128)}, u32[]{:S(2)}) copy-start(s32[1,8,128]{2,1,0:T(8,128)} %param.17) | copy-start | bytes 12292
  11.1 5.9 %copy-start.7 = (f32[16,128]{1,0:T(8,128)S(1)}, f32[16,128]{1,0:T(8,128)}, u32[]{:S(2)}) copy-start(f32[16,128]{1,0:T(8,128)} %land_ref.1) | copy-start | bytes 24580
  17.5 6.9 %collective-permute-start = (f32[144,128]{1,0:T(8,128)S(1)}, f32[144,128]{1,0:T(8,128)S(1)}, u32[]{:S(2)}, u32[]{:S(2)}) collective-permute-start(f32[144,128]{1,0:T(8,128)S(1)} %get-tuple-element.17), channel_id=1, source_target_pairs={{0,8},{8,16},{16,24},{24,0},{1,9},{9,17},{17,25},{25,1},{2,10},{10... | collective-permute-start | bytes 221192 | tf_op jit(solution)/shard_map/ppermute | solution.py:924
  19.1 5.3 %collective-permute-start.1 = (f32[144,128]{1,0:T(8,128)S(1)}, f32[144,128]{1,0:T(8,128)S(1)}, u32[]{:S(2)}, u32[]{:S(2)}) collective-permute-start(f32[144,128]{1,0:T(8,128)S(1)} %get-tuple-element.18), channel_id=1, source_target_pairs={{8,0},{16,8},{24,16},{0,24},{9,1},{17,9},{25,17},{1,25},{10,2},{18... | collective-permute-start | bytes 221192 | tf_op jit(solution)/shard_map/ppermute | solution.py:925
  25.3 12.5 %all-to-all-start.1 = ((f32[8,8,128]{2,1,0:T(8,128)}), f32[8,8,128]{2,1,0:T(8,128)S(1)}, u32[]{:S(2)}, u32[]{:S(2)}) async-start(f32[8,8,128]{2,1,0:T(8,128)} %get-tuple-element.22), calls=%async_computation.1 | async-start | bytes 65536 | tf_op jit(solution)/shard_map/all_to_all | solution.py:933
  29.0 4.9 %copy-start.11 = (f32[2048]{0:T(1024)S(1)}, f32[2048]{0:T(1024)}, u32[]{:S(2)}) copy-start(f32[2048]{0:T(1024)} %param.22) | copy-start | bytes 24580
  31.2 4.1 %collective-permute-start.3 = (f32[16,128]{1,0:T(8,128)S(1)}, f32[16,128]{1,0:T(8,128)S(1)}, u32[]{:S(2)}, u32[]{:S(2)}) collective-permute-start(f32[16,128]{1,0:T(8,128)S(1)} %get-tuple-element.21.after_ref), channel_id=1, source_target_pairs={{1,0},{2,1},{3,2},{4,3},{5,4},{6,5},{7,6},{0,7},{9,8},{10,9},{11,1... | collective-permute-start | bytes 24584 | tf_op jit(solution)/shard_map/ppermute | solution.py:942
  33.9 4.0 %collective-permute-start.2 = (f32[16,128]{1,0:T(8,128)S(1)}, f32[16,128]{1,0:T(8,128)S(1)}, u32[]{:S(2)}, u32[]{:S(2)}) collective-permute-start(f32[16,128]{1,0:T(8,128)S(1)} %get-tuple-element.21.after_ref), channel_id=1, source_target_pairs={{0,1},{1,2},{2,3},{3,4},{4,5},{5,6},{6,7},{7,0},{8,9},{9,10},{10,1... | collective-permute-start | bytes 24584 | tf_op jit(solution)/shard_map/ppermute | solution.py:941
  33.9 4.0 %copy-start.10 = (f32[1,8,128]{2,1,0:T(8,128)S(1)}, f32[1,8,128]{2,1,0:T(8,128)}, u32[]{:S(2)}) copy-start(f32[1,8,128]{2,1,0:T(8,128)} %param.25) | copy-start | bytes 12292
  35.1 2.8 %copy-start.9 = (s32[1,8,128]{2,1,0:T(8,128)S(1)}, s32[1,8,128]{2,1,0:T(8,128)}, u32[]{:S(2)}) copy-start(s32[1,8,128]{2,1,0:T(8,128)} %param.24) | copy-start | bytes 12292

commit v5 on v4

--- a/solution.py
+++ b/solution.py
@@ -205,8 +205,26 @@
     return sums
 
 
+def wind_tiles(wind_ref, x_points, level, lines):
+    levels = wind_ref.shape[0] // (2 * x_points)
+    return [
+        [
+            time_step
+            * wind_ref[
+                pl.ds((levels * part + level) * x_points + x, ROWS, stride=x_points), :
+            ]
+            for x in lines
+        ]
+        for part in range(2)
+    ]
+
+
 def start_kernel(planes, inputs, *refs):
-    sources, slab_ref, held = refs[:inputs], refs[inputs], refs[inputs + 1 : -1]
+    sources, (slab_ref, moved_ref), held = (
+        refs[:inputs],
+        refs[inputs : inputs + 2],
+        refs[inputs + 2 : -1],
+    )
     copies = [
         pltpu.make_async_copy(source, target, refs[-1].at[i])
         for i, (source, target) in enumerate(zip(sources, held))
@@ -292,67 +310,8 @@
     slab_ref[right, STRIP_AT : STRIP_AT + ROWS, :] = to_right
     slab_ref[left, STRIP_AT : STRIP_AT + ROWS, :] = to_left
 
-    level_groups = levels // ROWS
-    eight = geo.lane >> 3
-
-    def edge_tile(get, groups, repeat):
-        pack = pltpu.roll(get(0), GLL, 1)
-        for group in range(1, groups):
-            pack = jnp.where(
-                eight == group, pltpu.roll(get(group), ROWS * group + GLL, 1), pack
-            )
-        return take(pack, geo.lane & (ROWS * groups - 1), 1) if repeat else pack
-
     y_weight = jnp.where(geo.y_edge, 1.0 / 6.0, 5.0 / 6.0)
     packs = [jnp.zeros((ROWS, LANES), jnp.float32) for _ in range(2)]
-    for element in range(x_points // GLL):
-        lines = [GLL * element + i for i in range(GLL)]
-        fields = [
-            edge_tile(
-                lambda g: air_ref[pl.ds(ROWS * g * x_points + x, ROWS, stride=x_points), :],
-                planes // ROWS,
-                False,
-            )
-            for x in lines
-        ]
-        slopes = geo.d_y(*fields)
-        for i, x in enumerate(lines):
-            wind = [
-                edge_tile(
-                    lambda g: wind_ref[
-                        pl.ds(
-                            (levels * part + ROWS * g) * x_points + x,
-                            ROWS,
-                            stride=x_points,
-                        ),
-                        :,
-                    ],
-                    level_groups,
-                    True,
-                )
-                for part in range(2)
-            ]
-            jac = edge_tile(lambda g: spread(jac_ref[x : x + 1, :]), 1, True)
-            x_weight = 1.0 / 6.0 if i in (0, GLL - 1) else 5.0 / 6.0
-            slope = sum(deriv_table[i][j] * fields[j] for j in range(GLL))
-            moved = (x_weight * y_weight * jac) * (
-                fields[i] - time_step * (wind[0] * slope + wind[1] * slopes[i])
-            )
-            q, at = edge_place(x, 0)
-            mine = ((geo.lane & (ROWS - 1)) >> 1 == at % ROWS // 2) & (
-                (geo.lane >> 6) == at // (LANES // 2)
-            )
-            packs[q] = jnp.where(mine, pltpu.roll(moved, (at - GLL + 1) % LANES, 1), packs[q])
-    to_right, to_left = split_sides(geo, packs[0], packs[1], 1)
-    slab_ref[right, EDGE_AT : EDGE_AT + ROWS, :] = to_right
-    slab_ref[left, EDGE_AT : EDGE_AT + ROWS, :] = to_left
-
-
-def moved_kernel(planes, air_ref, wind_ref, jac_ref, after_ref, moved_ref):
-    geo = Geometry()
-    x_points = jac_ref.shape[0]
-    levels = wind_ref.shape[0] // (2 * x_points)
-    y_weight = jnp.where(geo.y_edge, 1.0 / 6.0, 5.0 / 6.0)
     for element in range(x_points // GLL):
         lines = [GLL * element + i for i in range(GLL)]
         mass = [
@@ -362,16 +321,7 @@
             for i, x in enumerate(lines)
         ]
         for level in range(0, levels, ROWS):
-            wind = [
-                [
-                    time_step
-                    * wind_ref[
-                        pl.ds((levels * part + level) * x_points + x, ROWS, stride=x_points), :
-                    ]
-                    for x in lines
-                ]
-                for part in range(2)
-            ]
+            wind = wind_tiles(wind_ref, x_points, level, lines)
             for plane in range(level, planes, levels):
                 fields = [
                     air_ref[pl.ds(plane * x_points + x, ROWS, stride=x_points), :]
@@ -380,9 +330,14 @@
                 slopes = geo.d_y(*fields)
                 for i, x in enumerate(lines):
                     slope = sum(deriv_table[i][j] * fields[j] for j in range(GLL))
-                    moved_ref[planes * x + plane : planes * x + plane + ROWS, :] = mass[
-                        i
-                    ] * (fields[i] - (wind[0][i] * slope + wind[1][i] * slopes[i]))
+                    moved = mass[i] * (
+                        fields[i] - (wind[0][i] * slope + wind[1][i] * slopes[i])
+                    )
+                    moved_ref[planes * x + plane : planes * x + plane + ROWS, :] = moved
+                    pack_edges(geo, packs, moved, x, plane // ROWS)
+    to_right, to_left = split_sides(geo, packs[0], packs[1], 1)
+    slab_ref[right, EDGE_AT : EDGE_AT + ROWS, :] = to_right
+    slab_ref[left, EDGE_AT : EDGE_AT + ROWS, :] = to_left
 
 
 def panel_kernel(
@@ -540,11 +495,25 @@
         out_ref[base : base + 2, :] = surf_line(COEF_X, r) * surf_slope
 
 
-def surface_kernel(
-    surf_ref, low_ref, high_ref, rows_ref, after_ref, slab_ref, final_ref, inverse_ref
+def second_kernel(
+    planes,
+    avg_ref,
+    surf_ref,
+    low_ref,
+    high_ref,
+    wind_ref,
+    rows_ref,
+    after_ref,
+    slab_ref,
+    sums_ref,
+    final_ref,
+    inverse_ref,
 ):
     geo = Geometry()
     blocks = rows_ref.shape[0]
+    left, right = neighbours_of(blocks)
+    x_points = final_ref.shape[0]
+    levels = wind_ref.shape[0] // (2 * x_points)
     base = low_ref.shape[0] - 2 * SURF_ARRAYS - 4
 
     def surf_tile(number, tile, h):
@@ -611,22 +580,6 @@
         for c in range(ROWS):
             slab_ref[ROWS * group + c, 0:1, :] = picked[c : c + 1]
 
-
-def second_kernel(
-    planes,
-    avg_ref,
-    surf_ref,
-    inverse_ref,
-    low_ref,
-    high_ref,
-    wind_ref,
-    sums_ref,
-    edges_ref,
-):
-    geo = Geometry()
-    x_points = inverse_ref.shape[0]
-    levels = wind_ref.shape[0] // (2 * x_points)
-    surf_base = low_ref.shape[0] - 2 * SURF_ARRAYS - 4
     packs = [jnp.zeros((ROWS, LANES), jnp.float32) for _ in range(2)]
 
     def put(x, plane, value):
@@ -634,76 +587,70 @@
         pack_edges(geo, packs, value, x, plane // ROWS)
 
     def beyond(ref, plane, field, slope, own_coef):
-        mass_at = surf_base + 2 * MASS
         wind_at = 2 * planes + plane % levels
         return (
-            spread(ref[mass_at : mass_at + 1, :]) * field
+            beside(ref, MASS, 0) * field
             - ref[planes + plane : planes + plane + ROWS, :]
             - ref[wind_at : wind_at + ROWS, :] * (own_coef * field)
             - ref[wind_at + levels : wind_at + levels + ROWS, :] * slope
         )
 
-    for plane in range(0, planes, ROWS):
-        here = slice(plane, plane + ROWS)
-        held = None
-        for element in range(x_points // GLL):
-            lines = [GLL * element + i for i in range(GLL)]
-            fields = []
-            for i, x in enumerate(lines):
-                total = avg_ref[planes * x + plane : planes * x + plane + ROWS, :]
-                other = x - 1 if i == 0 else x + 1
-                if other < 0:
-                    total = total + low_ref[here, :]
-                elif other == x_points:
-                    total = total + high_ref[here, :]
-                elif i in (0, GLL - 1):
-                    at = planes * other + plane
-                    total = total + avg_ref[at : at + ROWS, :]
-                fields.append(total * spread(inverse_ref[x : x + 1, :]))
-            slopes = geo.d_y(*fields)
-            moved = []
-            for i, x in enumerate(lines):
-                wind = [
-                    time_step
-                    * wind_ref[
-                        pl.ds(
-                            (levels * part + plane % levels) * x_points + x,
-                            ROWS,
-                            stride=x_points,
-                        ),
-                        :,
-                    ]
-                    for part in range(2)
-                ]
-                slope = sum(deriv_table[i][j] * fields[j] for j in range(GLL))
-                mass_at = 4 * ROWS * MASS + x
-                moved.append(
-                    spread(surf_ref[mass_at : mass_at + 1, :])
-                    * (fields[i] - (wind[0] * slope + wind[1] * slopes[i]))
-                )
-            first, last = lines[0], lines[-1]
-            if first == 0:
-                before = beyond(low_ref, plane, fields[0], slopes[0], deriv_table[3][3])
-                put(first, plane, before + moved[0])
-            else:
-                shared = held + moved[0]
-                put(first - 1, plane, shared)
-                put(first, plane, shared)
-            for i in range(1, GLL - 1):
-                put(lines[i], plane, moved[i])
-            held = moved[-1]
-            if last == x_points - 1:
-                after = beyond(high_ref, plane, fields[-1], slopes[-1], deriv_table[0][0])
-                put(last, plane, held + after)
-    for q, pack in enumerate(packs):
-        edges_ref[ROWS * q : ROWS * (q + 1), :] = pack
+    def row_of(tiles, x):
+        return spread(tiles[x // ROWS][x % ROWS : x % ROWS + 1])
+
+    masses = [surf_tile(MASS, 0, h) for h in range(2)]
+    held = {}
+    for element in range(x_points // GLL):
+        lines = [GLL * element + i for i in range(GLL)]
+        first, last = lines[0], lines[-1]
+        scale = [row_of(inverse[0], x) for x in lines]
+        mass = [row_of(masses, x) for x in lines]
+        for level in range(0, levels, ROWS):
+            wind = wind_tiles(wind_ref, x_points, level, lines)
+            for plane in range(level, planes, levels):
+                here = slice(plane, plane + ROWS)
+                fields = []
+                for i, x in enumerate(lines):
+                    total = avg_ref[planes * x + plane : planes * x + plane + ROWS, :]
+                    other = x - 1 if i == 0 else x + 1
+                    if other < 0:
+                        total = total + low_ref[here, :]
+                    elif other == x_points:
+                        total = total + high_ref[here, :]
+                    elif i in (0, GLL - 1):
+                        at = planes * other + plane
+                        total = total + avg_ref[at : at + ROWS, :]
+                    fields.append(total * scale[i])
+                slopes = geo.d_y(*fields)
+                moved = []
+                for i, x in enumerate(lines):
+                    slope = sum(deriv_table[i][j] * fields[j] for j in range(GLL))
+                    moved.append(
+                        mass[i] * (fields[i] - (wind[0][i] * slope + wind[1][i] * slopes[i]))
+                    )
+                if first == 0:
+                    before = beyond(low_ref, plane, fields[0], slopes[0], deriv_table[3][3])
+                    put(first, plane, before + moved[0])
+                else:
+                    shared = held[plane] + moved[0]
+                    put(first - 1, plane, shared)
+                    put(first, plane, shared)
+                for i in range(1, GLL - 1):
+                    put(lines[i], plane, moved[i])
+                held[plane] = moved[-1]
+                if last == x_points - 1:
+                    after = beyond(
+                        high_ref, plane, fields[-1], slopes[-1], deriv_table[0][0]
+                    )
+                    put(last, plane, held[plane] + after)
+    to_right, to_left = split_sides(geo, packs[0], packs[1], 1)
+    slab_ref[right, EDGE_AT : EDGE_AT + ROWS, :] = to_right
+    slab_ref[left, EDGE_AT : EDGE_AT + ROWS, :] = to_left
 
 
 def end_kernel(
     planes,
     sums_ref,
-    before_ref,
-    after_ref,
     recv_ref,
     final_ref,
     inverse_ref,
@@ -716,6 +663,7 @@
 ):
     geo = Geometry()
     blocks = cols_ref.shape[0]
+    left, right = neighbours_of(blocks)
     chunks = gain_ref.shape[0]
     arrived = jnp.concatenate([recv_ref[c, 0:1, :] for c in range(blocks)], axis=0)
     (inflow,) = scatter_sum([weights_ref[...] * arrived], cols_ref[...], chunks)
@@ -726,15 +674,11 @@
         ocean_out[0:1, at] = ocean_ref[0:1, at] + gain[k : k + 1]
 
     x_points = inverse_ref.shape[0]
-    odd = (geo.lane & 1) != 0
-    joined = [
-        jnp.where(
-            odd,
-            pltpu.roll(before_ref[ROWS * q : ROWS * (q + 1), :], 1, 1),
-            pltpu.roll(after_ref[ROWS * q : ROWS * (q + 1), :], LANES - 1, 1),
-        )
-        for q in range(2)
-    ]
+    joined = join_edges(
+        geo,
+        recv_ref[left, EDGE_AT : EDGE_AT + ROWS, :],
+        recv_ref[right, EDGE_AT : EDGE_AT + ROWS, :],
+    )
     for x in range(x_points):
         inverse = spread(inverse_ref[x : x + 1, :])
         for group in range(planes // ROWS):
@@ -833,13 +777,18 @@
 HBM_SPEC = pl.BlockSpec(memory_space=pltpu.HBM)
 
 
-def call(kernel, outs, specs, scratch=(), cost=0):
+def call(kernel, outs, specs, scratch=(), cost=0, in_vmem=()):
     estimate = None
     if cost:
         estimate = pl.CostEstimate(flops=0, bytes_accessed=cost, transcendentals=0)
     return pl.pallas_call(
         kernel,
-        out_shape=[jax.ShapeDtypeStruct(shape, jnp.float32) for shape in outs],
+        out_shape=[
+            pltpu.VMEM(shape, jnp.float32)
+            if number in in_vmem
+            else jax.ShapeDtypeStruct(shape, jnp.float32)
+            for number, shape in enumerate(outs)
+        ],
         in_specs=specs,
         scratch_shapes=list(scratch),
         cost_estimate=estimate,
@@ -885,18 +834,19 @@
         wind,
         air,
     )
-    (slab,) = call(
+    slab, moved = call(
         functools.partial(start_kernel, planes, len(first_inputs)),
-        [(blocks, IDS_AT + blocks + ocean_planes, LANES)],
+        [(blocks, IDS_AT + blocks + ocean_planes, LANES), air.shape],
         [HBM_SPEC] * len(first_inputs),
         [pltpu.VMEM(array.shape, array.dtype) for array in first_inputs]
         + [pltpu.SemaphoreType.DMA((len(first_inputs),))],
+        in_vmem=(0,),
     )(*(pltpu.with_memory_space_constraint(array, pltpu.HBM) for array in first_inputs))
     recv = lax.all_to_all(slab, "blk", split_axis=0, concat_axis=0, tiled=True)
 
     chunks = cells // LANES
     reads_per_chunk = edge_coef.shape[0] * chunks * (ocean_planes // ROWS)
-    starts = (0, chunks * 5 // 8)
+    starts = (0, chunks * 11 // 16)
 
     def ocean_part(start, end, after):
         (result,) = call(
@@ -907,13 +857,7 @@
         )(ocean, edge_coef, neighbours, rate, after)
         return result
 
-    (moved,) = call(
-        functools.partial(moved_kernel, planes),
-        [air.shape],
-        [VMEM_SPEC] * 3 + [ANY_SPEC],
-        cost=4 * air.size * 4,
-    )(air, wind, jacobian, slab)
-    first_part = ocean_part(starts[0], starts[1], slab)
+    first_part = ocean_part(starts[0], starts[1], moved)
     side_rows = 2 * planes + 2 * levels + 2 * SURF_ARRAYS + 4
     avg, down, up, surf = call(
         functools.partial(panel_kernel, planes),
@@ -925,32 +869,29 @@
     high = lax.ppermute(down, "face", [(to, source) for source, to in after_me])
     second_part = ocean_part(starts[1], chunks, surf)
 
-    slab, final, inverse = call(
-        surface_kernel,
-        [(blocks, ROWS, LANES), (x_points, y_points), (x_points, y_points)],
-        [VMEM_SPEC] * 4 + [ANY_SPEC],
-    )(surf, low, high, point_ids, second_part)
+    slab, sums, final, inverse = call(
+        functools.partial(second_kernel, planes),
+        [
+            (blocks, EDGE_AT + ROWS, LANES),
+            air.shape,
+            (x_points, y_points),
+            (x_points, y_points),
+        ],
+        [VMEM_SPEC] * 6 + [ANY_SPEC],
+        in_vmem=(0,),
+    )(avg, surf, low, high, wind, point_ids, second_part)
     arrived = lax.all_to_all(slab, "blk", split_axis=0, concat_axis=0, tiled=True)
-    sums, edges = call(
-        functools.partial(second_kernel, planes),
-        [air.shape, (2 * ROWS, LANES)],
-        [VMEM_SPEC] * 6,
-        cost=4 * air.size * 4,
-    )(avg, surf, inverse, low, high, wind)
-    after_me = [(i, (i + 1) % blocks) for i in range(blocks)]
-    before = lax.ppermute(edges, "blk", after_me)
-    after = lax.ppermute(edges, "blk", [(to, source) for source, to in after_me])
     partial, gain = call(
         functools.partial(rim_kernel, starts),
         [ocean.shape, area.shape],
         [VMEM_SPEC] * 4 + [ANY_SPEC] + [VMEM_SPEC] * len(starts),
         cost=chunks * reads_per_chunk // 8 * ROWS * LANES * 4,
-    )(recv, edge_coef, neighbours, area, edges, first_part, second_part)
+    )(recv, edge_coef, neighbours, area, final, first_part, second_part)
     air_final, ocean_final = call(
         functools.partial(end_kernel, planes),
         [air.shape, ocean.shape],
-        [VMEM_SPEC] * 10,
-    )(sums, before, after, arrived, final, inverse, cell_ids, weights, gain, partial)
+        [VMEM_SPEC] * 8,
+    )(sums, arrived, final, inverse, cell_ids, weights, gain, partial)
     return air_final.reshape(air_state.shape), ocean_final.reshape(tracers.shape)
 
 

time: 39.4 us -> 37.7 us (0.957)
  starting transfers between devices: 15.5 us -> 12.7 us
  waiting for transfers between devices: 3.72 us -> 5.54 us
  Pallas kernels: 18.8 us -> 18.2 us
    all_to_all x1, waiting for transfers between devices: 0.01 us -> 3.73 us  [body(): lax.all_to_all(slab, 'blk', split_axis=0, concat_axis=0, tiled=True)]
    ppermute x2 -> x0, waiting for transfers between devices: 2.77 us -> none  [the longest x1 2.61 us: body(): before = lax.ppermute(edges, 'blk', after_me)]
    ppermute x2 -> x0, starting transfers between devices: 2.71 us -> none  [the longest x1 2.71 us: body(): lax.ppermute(edges, 'blk', [(to, source) for source, to in after_me])]
    pallas_call x3 -> x1, Pallas kernels: 3.9 us -> 3.08 us  [body(): call(functools.partial(second_kernel, planes), [(blocks, EDGE_AT + ROWS,...]
    ppermute x1, waiting for transfers between devices: 0.01 us -> 0.46 us  [body(): low = lax.ppermute(up, 'face', after_me)]
    all_to_all x1, waiting for transfers between devices: 0.94 us -> 1.35 us  [body(): recv = lax.all_to_all(slab, 'blk', split_axis=0, concat_axis=0, tiled=True)]
  transfers between devices with their start and end apart: 6 -> 4, of which waited for: 3 -> 3; matrix products, arithmetic and copies ran while one was open for 0% -> 0% of each run, Pallas kernels for 31% -> 25%
where the time goes in v5:
time: 37.7 us; the launch traced here: 37.3 us
  Pallas kernels  18.2 us (48%)
  starting transfers between devices  12.7 us (34%)
  waiting for transfers between devices  5.54 us (15%)
  between operations  0.82 us (2%)
    pallas_call x2, Pallas kernels, ocean_part(): call(functools.partial(ocean_kernel, ocean_levels, start), [(ocean_planes...  7.97 us
    all_to_all x1, starting transfers between devices, body(): recv = lax.all_to_all(slab, 'blk', split_axis=0, concat_axis=0, tiled=True)  5.31 us
    pallas_call x1, Pallas kernels, body(): call(functools.partial(start_kernel, planes, len(first_inputs)), [(blocks...  4.29 us
    all_to_all x1, waiting for transfers between devices, body(): lax.all_to_all(slab, 'blk', split_axis=0, concat_axis=0, tiled=True)  3.73 us
    all_to_all x1, starting transfers between devices, body(): lax.all_to_all(slab, 'blk', split_axis=0, concat_axis=0, tiled=True)  3.48 us
    pallas_call x1, Pallas kernels, body(): call(functools.partial(second_kernel, planes), [(blocks, EDGE_AT + ROWS,...  3.08 us
    ppermute x1, starting transfers between devices, body(): high = lax.ppermute(down, 'face', [(to, source) for source, to in after_me])  2.25 us
    ppermute x1, starting transfers between devices, body(): low = lax.ppermute(up, 'face', after_me)  1.63 us
  transfers between devices with their start and end apart: 4, of which 3 were waited for; matrix products, arithmetic and copies ran while one was open for 0% of the time, Pallas kernels for 25%

profile of v5, /device:TPU:0, one launch (start us, length us, event | category | flops | bytes accessed | tf_op | source)
XLA Modules:
  0.0 37.3 jit_solution(13628786942759041797)
XLA Ops:
  0.6 4.3 %start_kernel.1 = (f32[8,64,128]{2,1,0:T(8,128)}, f32[768,128]{1,0:T(8,128)S(1)}) custom-call(s32[8,128]{1,0:T(8,128)} %bitcast.23, f32[8,128]{1,0:T(8,128)} %bitcast.25, f32[32,2048]{1,0:T(8,128)} %bitcast.10, s32[1,256]{1,0:T(1,128)} %refs_3_.1, s32[8,128]{1,0:T(8,128)} %bitcast.18, f32[16,128]{1,0:T(8,128)} %jac_ref.1, f32[16,128]{1,0:T(8,128)} %land_ref.1, ...), custom_call_target="tpu_custom_call" | custom-call | tf_op jit(solution)/shard_map/start_kernel/pallas_call | solution.py:837
  4.9 0.0 copy-start
  4.9 0.0 copy-start.3
  5.0 0.0 copy-start.4
  5.0 0.0 copy-start.8
  5.0 5.3 %all-to-all-start = ((f32[8,64,128]{2,1,0:T(8,128)}), f32[8,64,128]{2,1,0:T(8,128)S(1)}, u32[]{:S(2)}, u32[]{:S(2)}) async-start(f32[8,64,128]{2,1,0:T(8,128)} %get-tuple-element.17), calls=%async_computation | async-start | bytes 524288 | tf_op jit(solution)/shard_map/all_to_all | solution.py:845
  10.3 0.0 copy-done
  10.3 0.0 copy-done.3
  10.3 0.0 copy-done.4
  10.3 0.0 copy-done.8
  10.3 0.0 copy-start.1
  10.3 0.0 copy-start.2
  10.3 0.0 copy-start.5
  10.4 0.0 copy-start.6
  10.4 0.0 copy-start.7
  10.4 5.5 %ocean_kernel.2.after_ref.refs_0_ = f32[32,1408]{1,0:T(8,128)S(1)} custom-call(f32[32,2048]{1,0:T(8,128)S(1)} %bitcast.11, f32[6,2048]{1,0:T(8,128)S(1)} %copy-done.3, s32[6,2048]{1,0:T(8,128)S(1)} %copy-done.4, f32[16,128]{1,0:T(8,128)S(1)} %bitcast.21, f32[768,128]{1,0:T(8,128)S(1)} %get-tuple-element.16.after_ref.moved_ref), custom_call_target="tpu_custom_call" | custom-call | bytes 17301504 | tf_op jit(solution)/shard_map/ocean_kernel/pallas_call | solution.py:852
  15.9 1.4 %all-to-all-done.recv_ref = f32[8,64,128]{2,1,0:T(8,128)S(1)} async-done(((f32[8,64,128]{2,1,0:T(8,128)}), f32[8,64,128]{2,1,0:T(8,128)S(1)}, u32[]{:S(2)}, u32[]{:S(2)}) %all-to-all-start) | async-done | bytes 262176 | tf_op jit(solution)/shard_map/all_to_all | solution.py:845
  17.2 0.0 copy-done.1
  17.2 0.0 copy-done.2
  17.2 0.0 copy-done.5
  17.2 0.0 copy-done.6
  17.2 0.0 copy-done.7
  17.3 0.5 %panel_kernel.1 = (f32[768,128]{1,0:T(8,128)S(1)}, f32[144,128]{1,0:T(8,128)S(1)}, f32[144,128]{1,0:T(8,128)S(1)}, f32[192,128]{1,0:T(8,128)S(1)}) custom-call(f32[768,128]{1,0:T(8,128)S(1)} %get-tuple-element.16.after_ref.moved_ref, f32[8,64,128]{2,1,0:T(8,128)S(1)} %all-to-all-done.recv_ref, f32[768,128]{1,0:T(8,128)S(1)} %bitcast.17, ...), custom_call_target="tpu_custom_call" | custom-call | tf_op jit(solution)/shard_map/panel_kernel/pallas_call | solution.py:862
  17.8 1.6 %collective-permute-start = (f32[144,128]{1,0:T(8,128)S(1)}, f32[144,128]{1,0:T(8,128)S(1)}, u32[]{:S(2)}, u32[]{:S(2)}) collective-permute-start(f32[144,128]{1,0:T(8,128)S(1)} %get-tuple-element.20), channel_id=1, source_target_pairs={{0,8},{8,16},{16,24},{24,0},{1,9},{9,17},{17,25},{25,1},{2,10},{10... | collective-permute-start | bytes 221192 | tf_op jit(solution)/shard_map/ppermute | solution.py:868
  19.4 2.2 %collective-permute-start.1 = (f32[144,128]{1,0:T(8,128)S(1)}, f32[144,128]{1,0:T(8,128)S(1)}, u32[]{:S(2)}, u32[]{:S(2)}) collective-permute-start(f32[144,128]{1,0:T(8,128)S(1)} %get-tuple-element.21), channel_id=1, source_target_pairs={{8,0},{16,8},{24,16},{0,24},{9,1},{17,9},{25,17},{1,25},{10,2},{18... | collective-permute-start | bytes 221192 | tf_op jit(solution)/shard_map/ppermute | solution.py:869
  21.6 2.5 %ocean_kernel.3.after_ref.refs_1_ = f32[32,640]{1,0:T(8,128)S(1)} custom-call(f32[32,2048]{1,0:T(8,128)S(1)} %bitcast.12, f32[6,2048]{1,0:T(8,128)S(1)} %copy-done.3, s32[6,2048]{1,0:T(8,128)S(1)} %copy-done.4, f32[16,128]{1,0:T(8,128)S(1)} %bitcast.22, f32[192,128]{1,0:T(8,128)S(1)} %get-tuple-element.19.after_ref.surf_ref), custom_call_target="tpu_custom_call" | custom-call | bytes 7864320 | tf_op jit(solution)/shard_map/ocean_kernel/pallas_call | solution.py:852
  24.1 0.5 %collective-permute-done.low_ref = f32[144,128]{1,0:T(8,128)S(1)} collective-permute-done((f32[144,128]{1,0:T(8,128)S(1)}, f32[144,128]{1,0:T(8,128)S(1)}, u32[]{:S(2)}, u32[]{:S(2)}) %collective-permute-start) | collective-permute-done | bytes 73760 | tf_op jit(solution)/shard_map/ppermute | solution.py:868
  24.6 0.0 collective-permute-done.1.high_ref
  24.6 3.1 %second_kernel.1 = (f32[8,16,128]{2,1,0:T(8,128)}, f32[768,128]{1,0:T(8,128)S(1)}, f32[16,128]{1,0:T(8,128)S(1)}, f32[16,128]{1,0:T(8,128)S(1)}) custom-call(f32[768,128]{1,0:T(8,128)S(1)} %get-tuple-element.18.avg_ref, f32[192,128]{1,0:T(8,128)S(1)} %get-tuple-element.19.after_ref.surf_ref, f32[144,128]{1,0:T(8,128)S(1)} %collective-permute-done.low_ref, ...), custom_call_target="tpu_custom_call" | custom-call | tf_op jit(solution)/shard_map/second_kernel/pallas_call | solution.py:872
  27.7 0.0 copy-start.11
  27.7 3.5 %all-to-all-start.1 = ((f32[8,16,128]{2,1,0:T(8,128)}), f32[8,16,128]{2,1,0:T(8,128)S(1)}, u32[]{:S(2)}, u32[]{:S(2)}) async-start(f32[8,16,128]{2,1,0:T(8,128)} %get-tuple-element.23), calls=%async_computation.1 | async-start | bytes 131072 | tf_op jit(solution)/shard_map/all_to_all | solution.py:883
  31.2 0.0 copy-done.11
  31.2 0.0 copy-start.10
  31.2 1.2 %rim_kernel.1 = (f32[32,2048]{1,0:T(8,128)S(1)}, f32[16,128]{1,0:T(8,128)S(1)}) custom-call(f32[8,64,128]{2,1,0:T(8,128)S(1)} %all-to-all-done.recv_ref, f32[6,2048]{1,0:T(8,128)S(1)} %copy-done.3, s32[6,2048]{1,0:T(8,128)S(1)} %copy-done.4, f32[16,128]{1,0:T(8,128)S(1)} %bitcast.27, f32[16,128]{1,0:T(8,128)S(1)} %get-tuple-element.24.after_ref.final_ref, ...), custom_call_target="tpu_custom_call" | custom-call | bytes 3145728 | tf_op jit(solution)/shard_map/rim_kernel/pallas_call | solution.py:884
  32.4 0.0 copy-start.9
  32.4 3.7 %all-to-all-done.1.recv_ref = f32[8,16,128]{2,1,0:T(8,128)S(1)} async-done(((f32[8,16,128]{2,1,0:T(8,128)}), f32[8,16,128]{2,1,0:T(8,128)S(1)}, u32[]{:S(2)}, u32[]{:S(2)}) %all-to-all-start.1) | async-done | bytes 65568 | tf_op jit(solution)/shard_map/all_to_all | solution.py:883
  36.1 0.0 copy-done.10
  36.1 0.0 copy-done.9
  36.1 1.2 %end_kernel.1 = (f32[768,128]{1,0:T(8,128)}, f32[32,2048]{1,0:T(8,128)}) custom-call(f32[768,128]{1,0:T(8,128)S(1)} %get-tuple-element.22.sums_ref, f32[8,16,128]{2,1,0:T(8,128)S(1)} %all-to-all-done.1.recv_ref, f32[16,128]{1,0:T(8,128)S(1)} %get-tuple-element.24.after_ref.final_ref, f32[16,128]{1,0:T(8,128)S(1)} %get-tuple-element.25.inverse_ref, ...), custom_call_target="tpu_custom_call" | custom-call | tf_op jit(solution)/shard_map/end_kernel/pallas_call | solution.py:890
Async XLA Ops:
  4.9 5.4 %copy-start = (f32[2,16,2048]{2,1,0:T(8,128)S(1)}, f32[2,16,2048]{2,1,0:T(8,128)}, u32[]{:S(2)}) copy-start(f32[2,16,2048]{2,1,0:T(8,128)} %param.18) | copy-start | bytes 786436
  4.9 5.4 %copy-start.3 = (f32[6,2048]{1,0:T(8,128)S(1)}, f32[6,2048]{1,0:T(8,128)}, u32[]{:S(2)}) copy-start(f32[6,2048]{1,0:T(8,128)} %coef_ref.5) | copy-start | bytes 147460
  5.0 5.4 %copy-start.4 = (s32[6,2048]{1,0:T(8,128)S(1)}, s32[6,2048]{1,0:T(8,128)}, u32[]{:S(2)}) copy-start(s32[6,2048]{1,0:T(8,128)} %near_ref.5) | copy-start | bytes 147460
  5.0 5.4 %copy-start.8 = (f32[2048]{0:T(1024)S(1)}, f32[2048]{0:T(1024)}, u32[]{:S(2)}) copy-start(f32[2048]{0:T(1024)} %param.21) | copy-start | bytes 24580
  5.0 12.3 %all-to-all-start = ((f32[8,64,128]{2,1,0:T(8,128)}), f32[8,64,128]{2,1,0:T(8,128)S(1)}, u32[]{:S(2)}, u32[]{:S(2)}) async-start(f32[8,64,128]{2,1,0:T(8,128)} %get-tuple-element.17), calls=%async_computation | async-start | bytes 524288 | tf_op jit(solution)/shard_map/all_to_all | solution.py:845
  10.3 6.9 %copy-start.1 = (f32[2,16,16,128]{3,2,1,0:T(8,128)S(1)}, f32[2,16,16,128]{3,2,1,0:T(8,128)}, u32[]{:S(2)}) copy-start(f32[2,16,16,128]{3,2,1,0:T(8,128)} %param.14) | copy-start | bytes 786436
  10.3 6.9 %copy-start.2 = (f32[3,16,16,128]{3,2,1,0:T(8,128)S(1)}, f32[3,16,16,128]{3,2,1,0:T(8,128)}, u32[]{:S(2)}) copy-start(f32[3,16,16,128]{3,2,1,0:T(8,128)} %param.13) | copy-start | bytes 1179652
  10.3 6.9 %copy-start.5 = (s32[1,8,128]{2,1,0:T(8,128)S(1)}, s32[1,8,128]{2,1,0:T(8,128)}, u32[]{:S(2)}) copy-start(s32[1,8,128]{2,1,0:T(8,128)} %param.17) | copy-start | bytes 12292
  10.4 6.9 %copy-start.6 = (f32[16,128]{1,0:T(8,128)S(1)}, f32[16,128]{1,0:T(8,128)}, u32[]{:S(2)}) copy-start(f32[16,128]{1,0:T(8,128)} %jac_ref.1) | copy-start | bytes 24580
  10.4 6.9 %copy-start.7 = (f32[16,128]{1,0:T(8,128)S(1)}, f32[16,128]{1,0:T(8,128)}, u32[]{:S(2)}) copy-start(f32[16,128]{1,0:T(8,128)} %land_ref.1) | copy-start | bytes 24580
  17.8 6.8 %collective-permute-start = (f32[144,128]{1,0:T(8,128)S(1)}, f32[144,128]{1,0:T(8,128)S(1)}, u32[]{:S(2)}, u32[]{:S(2)}) collective-permute-start(f32[144,128]{1,0:T(8,128)S(1)} %get-tuple-element.20), channel_id=1, source_target_pairs={{0,8},{8,16},{16,24},{24,0},{1,9},{9,17},{17,25},{25,1},{2,10},{10... | collective-permute-start | bytes 221192 | tf_op jit(solution)/shard_map/ppermute | solution.py:868
  19.4 5.2 %collective-permute-start.1 = (f32[144,128]{1,0:T(8,128)S(1)}, f32[144,128]{1,0:T(8,128)S(1)}, u32[]{:S(2)}, u32[]{:S(2)}) collective-permute-start(f32[144,128]{1,0:T(8,128)S(1)} %get-tuple-element.21), channel_id=1, source_target_pairs={{8,0},{16,8},{24,16},{0,24},{9,1},{17,9},{25,17},{1,25},{10,2},{18... | collective-permute-start | bytes 221192 | tf_op jit(solution)/shard_map/ppermute | solution.py:869
  27.7 3.5 %copy-start.11 = (f32[2048]{0:T(1024)S(1)}, f32[2048]{0:T(1024)}, u32[]{:S(2)}) copy-start(f32[2048]{0:T(1024)} %param.22) | copy-start | bytes 24580
  27.7 8.4 %all-to-all-start.1 = ((f32[8,16,128]{2,1,0:T(8,128)}), f32[8,16,128]{2,1,0:T(8,128)S(1)}, u32[]{:S(2)}, u32[]{:S(2)}) async-start(f32[8,16,128]{2,1,0:T(8,128)} %get-tuple-element.23), calls=%async_computation.1 | async-start | bytes 131072 | tf_op jit(solution)/shard_map/all_to_all | solution.py:883
  31.2 4.9 %copy-start.10 = (f32[1,8,128]{2,1,0:T(8,128)S(1)}, f32[1,8,128]{2,1,0:T(8,128)}, u32[]{:S(2)}) copy-start(f32[1,8,128]{2,1,0:T(8,128)} %param.25) | copy-start | bytes 12292
  32.4 3.7 %copy-start.9 = (s32[1,8,128]{2,1,0:T(8,128)S(1)}, s32[1,8,128]{2,1,0:T(8,128)}, u32[]{:S(2)}) copy-start(s32[1,8,128]{2,1,0:T(8,128)} %param.24) | copy-start | bytes 12292

commit v6 on v5

--- a/solution.py
+++ b/solution.py
@@ -128,10 +128,15 @@
     return x // ROWS, LANES // 2 * (x % 2) + ROWS * group + 2 * (x % ROWS // 2)
 
 
-def pack_edges(geo, packs, tile, x, group):
-    q, at = edge_place(x, group)
-    rolled = pltpu.roll(tile, (at + 1) % LANES, 1)
-    packs[q] = jnp.where((geo.lane >> 1) == at // 2, rolled, packs[q])
+def all_edges(geo, ref, planes, x_points):
+    packs = [jnp.zeros((ROWS, LANES), jnp.float32) for _ in range(2)]
+    for x in range(x_points):
+        for group in range(planes // ROWS):
+            q, at = edge_place(x, group)
+            tile = ref[planes * x + ROWS * group : planes * x + ROWS * (group + 1), :]
+            rolled = pltpu.roll(tile, (at + 1) % LANES, 1)
+            packs[q] = jnp.where((geo.lane >> 1) == at // 2, rolled, packs[q])
+    return packs
 
 
 def outer_edges(joined, x, group):
@@ -226,7 +231,7 @@
         refs[inputs + 2 : -1],
     )
     copies = [
-        pltpu.make_async_copy(source, target, refs[-1].at[i])
+        pltpu.make_async_copy(source.at[: target.shape[0]], target, refs[-1].at[i])
         for i, (source, target) in enumerate(zip(sources, held))
     ]
     for copy in copies:
@@ -235,7 +240,6 @@
         cols_ref,
         weights_ref,
         tracers_ref,
-        send_ref,
         rows_ref,
         jac_ref,
         land_ref,
@@ -248,13 +252,8 @@
     left, right = neighbours_of(blocks)
     levels = wind_ref.shape[0] // (2 * x_points)
     chunks = tracers_ref.shape[1] // LANES
-    for copy in copies[:5]:
+    for copy in copies[:4]:
         copy.wait()
-
-    def source(group, chunk):
-        return tracers_ref[
-            ROWS * group : ROWS * (group + 1), LANES * chunk : LANES * (chunk + 1)
-        ]
 
     for group in range(blocks // ROWS):
         at = slice(ROWS * group, ROWS * (group + 1))
@@ -276,17 +275,7 @@
     ids = rows_ref[...].astype(jnp.float32)
     for to in (left, right):
         slab_ref[to, IDS_AT : IDS_AT + blocks, :] = ids
-    for part, to in enumerate((left, right)):
-        cells = spread(send_ref[0:1, LANES * part : LANES * (part + 1)])
-        high, low = cells >> 7, cells & (LANES - 1)
-        for group in range(tracers_ref.shape[0] // ROWS):
-            rim = jnp.zeros((ROWS, LANES), jnp.float32)
-            for k in range(chunks):
-                rim = jnp.where(high == k, take(source(group, k), low, 1), rim)
-            at = IDS_AT + blocks + ROWS * group
-            slab_ref[to, at : at + ROWS, :] = rim
-
-    for copy in copies[5:]:
+    for copy in copies[4:]:
         copy.wait()
     strips = []
     for h in range(2):
@@ -311,7 +300,6 @@
     slab_ref[left, STRIP_AT : STRIP_AT + ROWS, :] = to_left
 
     y_weight = jnp.where(geo.y_edge, 1.0 / 6.0, 5.0 / 6.0)
-    packs = [jnp.zeros((ROWS, LANES), jnp.float32) for _ in range(2)]
     for element in range(x_points // GLL):
         lines = [GLL * element + i for i in range(GLL)]
         mass = [
@@ -334,7 +322,7 @@
                         fields[i] - (wind[0][i] * slope + wind[1][i] * slopes[i])
                     )
                     moved_ref[planes * x + plane : planes * x + plane + ROWS, :] = moved
-                    pack_edges(geo, packs, moved, x, plane // ROWS)
+    packs = all_edges(geo, moved_ref, planes, x_points)
     to_right, to_left = split_sides(geo, packs[0], packs[1], 1)
     slab_ref[right, EDGE_AT : EDGE_AT + ROWS, :] = to_right
     slab_ref[left, EDGE_AT : EDGE_AT + ROWS, :] = to_left
@@ -350,6 +338,8 @@
     land_ref,
     rows_ref,
     after_ref,
+    rim_before_ref,
+    rim_after_ref,
     avg_ref,
     down_ref,
     up_ref,
@@ -580,11 +570,8 @@
         for c in range(ROWS):
             slab_ref[ROWS * group + c, 0:1, :] = picked[c : c + 1]
 
-    packs = [jnp.zeros((ROWS, LANES), jnp.float32) for _ in range(2)]
-
     def put(x, plane, value):
         sums_ref[planes * x + plane : planes * x + plane + ROWS, :] = value
-        pack_edges(geo, packs, value, x, plane // ROWS)
 
     def beyond(ref, plane, field, slope, own_coef):
         wind_at = 2 * planes + plane % levels
@@ -643,6 +630,7 @@
                         high_ref, plane, fields[-1], slopes[-1], deriv_table[0][0]
                     )
                     put(last, plane, held[plane] + after)
+    packs = all_edges(geo, sums_ref, planes, x_points)
     to_right, to_left = split_sides(geo, packs[0], packs[1], 1)
     slab_ref[right, EDGE_AT : EDGE_AT + ROWS, :] = to_right
     slab_ref[left, EDGE_AT : EDGE_AT + ROWS, :] = to_left
@@ -742,25 +730,37 @@
     lax.fori_loop(0, out_ref.shape[1] // LANES, one_chunk, 0)
 
 
+def send_kernel(tracers_ref, send_ref, after_ref, *rim_refs):
+    chunks = tracers_ref.shape[1] // LANES
+    for part, rim_ref in enumerate(rim_refs):
+        cells = spread(send_ref[0:1, LANES * part : LANES * (part + 1)])
+        high, low = cells >> 7, cells & (LANES - 1)
+        for group in range(tracers_ref.shape[0] // ROWS):
+            half = slice(ROWS * group, ROWS * (group + 1))
+            rim = jnp.zeros((ROWS, LANES), jnp.float32)
+            for k in range(chunks):
+                tile = tracers_ref[half, LANES * k : LANES * (k + 1)]
+                rim = jnp.where(high == k, take(tile, low, 1), rim)
+            rim_ref[half, :] = rim
+
+
 def rim_kernel(
     starts,
-    recv_ref,
+    before_ref,
+    after_ref,
     coef_ref,
     near_ref,
     area_ref,
-    after_ref,
     *refs,
 ):
     partial_refs, (out_ref, gain_ref) = refs[: len(starts)], refs[len(starts) :]
     chunks = coef_ref.shape[1] // LANES
     groups = out_ref.shape[0] // ROWS
-    blocks = recv_ref.shape[0]
-    sides = neighbours_of(blocks)
+    sides = before_ref, after_ref
     gain_ref[...] = flux_gain / area_ref[...]
 
     def source(group, s):
-        at = IDS_AT + blocks + ROWS * group
-        return recv_ref[sides[s], at : at + ROWS, :]
+        return sides[s][ROWS * group : ROWS * (group + 1), :]
 
     for k in range(chunks):
         at = slice(LANES * k, LANES * (k + 1))
@@ -777,18 +777,13 @@
 HBM_SPEC = pl.BlockSpec(memory_space=pltpu.HBM)
 
 
-def call(kernel, outs, specs, scratch=(), cost=0, in_vmem=()):
+def call(kernel, outs, specs, scratch=(), cost=0):
     estimate = None
     if cost:
         estimate = pl.CostEstimate(flops=0, bytes_accessed=cost, transcendentals=0)
     return pl.pallas_call(
         kernel,
-        out_shape=[
-            pltpu.VMEM(shape, jnp.float32)
-            if number in in_vmem
-            else jax.ShapeDtypeStruct(shape, jnp.float32)
-            for number, shape in enumerate(outs)
-        ],
+        out_shape=[jax.ShapeDtypeStruct(shape, jnp.float32) for shape in outs],
         in_specs=specs,
         scratch_shapes=list(scratch),
         cost_estimate=estimate,
@@ -827,7 +822,6 @@
         cell_ids,
         weights,
         ocean,
-        send_list,
         point_ids,
         jacobian,
         land_area,
@@ -836,17 +830,19 @@
     )
     slab, moved = call(
         functools.partial(start_kernel, planes, len(first_inputs)),
-        [(blocks, IDS_AT + blocks + ocean_planes, LANES), air.shape],
+        [(blocks, IDS_AT + blocks, LANES), air.shape],
         [HBM_SPEC] * len(first_inputs),
-        [pltpu.VMEM(array.shape, array.dtype) for array in first_inputs]
+        [
+            pltpu.VMEM((ROWS, cells) if array is ocean else array.shape, array.dtype)
+            for array in first_inputs
+        ]
         + [pltpu.SemaphoreType.DMA((len(first_inputs),))],
-        in_vmem=(0,),
     )(*(pltpu.with_memory_space_constraint(array, pltpu.HBM) for array in first_inputs))
     recv = lax.all_to_all(slab, "blk", split_axis=0, concat_axis=0, tiled=True)
 
     chunks = cells // LANES
     reads_per_chunk = edge_coef.shape[0] * chunks * (ocean_planes // ROWS)
-    starts = (0, chunks * 11 // 16)
+    starts = (0, chunks * 5 // 16, chunks * 11 // 16)
 
     def ocean_part(start, end, after):
         (result,) = call(
@@ -857,17 +853,37 @@
         )(ocean, edge_coef, neighbours, rate, after)
         return result
 
-    first_part = ocean_part(starts[0], starts[1], moved)
+    to_before, to_after = call(
+        send_kernel,
+        [(ocean_planes, LANES)] * 2,
+        [VMEM_SPEC] * 2 + [ANY_SPEC],
+        cost=reads_per_chunk * ROWS * LANES,
+    )(ocean, send_list, moved)
+    onward = [(i, (i + 1) % blocks) for i in range(blocks)]
+    rim_before = lax.ppermute(to_after, "blk", onward)
+    rim_after = lax.ppermute(to_before, "blk", [(to, source) for source, to in onward])
+    first_part = ocean_part(starts[0], starts[1], to_before)
     side_rows = 2 * planes + 2 * levels + 2 * SURF_ARRAYS + 4
     avg, down, up, surf = call(
         functools.partial(panel_kernel, planes),
         [air.shape, (side_rows, LANES), (side_rows, LANES), (4 * ROWS * SURF_ARRAYS, LANES)],
-        [VMEM_SPEC] * 7 + [ANY_SPEC],
-    )(moved, recv, air, wind, jacobian, land_area, point_ids, first_part)
+        [VMEM_SPEC] * 7 + [ANY_SPEC] * 3,
+    )(
+        moved,
+        recv,
+        air,
+        wind,
+        jacobian,
+        land_area,
+        point_ids,
+        first_part,
+        rim_before,
+        rim_after,
+    )
     after_me = [(i, (i + 1) % faces) for i in range(faces)]
     low = lax.ppermute(up, "face", after_me)
     high = lax.ppermute(down, "face", [(to, source) for source, to in after_me])
-    second_part = ocean_part(starts[1], chunks, surf)
+    second_part = ocean_part(starts[1], starts[2], surf)
 
     slab, sums, final, inverse = call(
         functools.partial(second_kernel, planes),
@@ -878,15 +894,15 @@
             (x_points, y_points),
         ],
         [VMEM_SPEC] * 6 + [ANY_SPEC],
-        in_vmem=(0,),
     )(avg, surf, low, high, wind, point_ids, second_part)
     arrived = lax.all_to_all(slab, "blk", split_axis=0, concat_axis=0, tiled=True)
+    third_part = ocean_part(starts[2], chunks, final)
     partial, gain = call(
         functools.partial(rim_kernel, starts),
         [ocean.shape, area.shape],
-        [VMEM_SPEC] * 4 + [ANY_SPEC] + [VMEM_SPEC] * len(starts),
+        [VMEM_SPEC] * (5 + len(starts)),
         cost=chunks * reads_per_chunk // 8 * ROWS * LANES * 4,
-    )(recv, edge_coef, neighbours, area, final, first_part, second_part)
+    )(rim_before, rim_after, edge_coef, neighbours, area, first_part, second_part, third_part)
     air_final, ocean_final = call(
         functools.partial(end_kernel, planes),
         [air.shape, ocean.shape],

time: 37.7 us -> 34.6 us (0.918)
  waiting for transfers between devices: 5.54 us -> 1.49 us
  starting transfers between devices: 12.7 us -> 15.5 us
  Pallas kernels: 18.2 us -> 15.7 us
  local copies, waits for them, and re-layouts: 0.07 us -> 0.73 us
    ppermute x0 -> x2, starting transfers between devices: none -> 2.79 us  [the longest x1 2.24 us: body(): lax.ppermute(to_before, 'blk', [(to, source) for source, to in onward])]
    all_to_all x1, waiting for transfers between devices: 3.73 us -> 1.29 us  [body(): lax.all_to_all(slab, 'blk', split_axis=0, concat_axis=0, tiled=True)]
    pallas_call x1, Pallas kernels: 4.29 us -> 2.9 us  [body(): call(functools.partial(start_kernel, planes, len(first_inputs)), [(blocks...]
    pallas_call x1, Pallas kernels: 3.08 us -> 1.73 us  [body(): call(functools.partial(second_kernel, planes), [(blocks, EDGE_AT + ROWS,...]
    all_to_all x1, waiting for transfers between devices: 1.35 us -> 0.01 us  [body(): recv = lax.all_to_all(slab, 'blk', split_axis=0, concat_axis=0, tiled=True)]
    unnamed x24 -> x26, local copies, waits for them, and re-layouts: 0.07 us -> 0.73 us
    ppermute x1, waiting for transfers between devices: 0.46 us -> 0.01 us  [body(): low = lax.ppermute(up, 'face', after_me)]
    pallas_call x2 -> x3, Pallas kernels: 7.97 us -> 7.98 us  [ocean_part(): call(functools.partial(ocean_kernel, ocean_levels, start), [(ocean_planes...]
  transfers between devices with their start and end apart: 4 -> 6, of which waited for: 3 -> 2; matrix products, arithmetic and copies ran while one was open for 0% -> 0% of each run, Pallas kernels for 25% -> 27%
where the time goes in v6:
time: 34.6 us; the launch traced here: 34.2 us
  Pallas kernels  15.7 us (45%)
  starting transfers between devices  15.5 us (45%)
  waiting for transfers between devices  1.49 us (4%)
  between operations  0.83 us (2%)
  local copies, waits for them, and re-layouts  0.73 us (2%)
    pallas_call x3, Pallas kernels, ocean_part(): call(functools.partial(ocean_kernel, ocean_levels, start), [(ocean_planes...  7.98 us
    all_to_all x1, starting transfers between devices, body(): recv = lax.all_to_all(slab, 'blk', split_axis=0, concat_axis=0, tiled=True)  5.31 us
    all_to_all x1, starting transfers between devices, body(): lax.all_to_all(slab, 'blk', split_axis=0, concat_axis=0, tiled=True)  3.5 us
    pallas_call x1, Pallas kernels, body(): call(functools.partial(start_kernel, planes, len(first_inputs)), [(blocks...  2.9 us
    ppermute x1, starting transfers between devices, body(): high = lax.ppermute(down, 'face', [(to, source) for source, to in after_me])  2.25 us
    ppermute x1, starting transfers between devices, body(): lax.ppermute(to_before, 'blk', [(to, source) for source, to in onward])  2.24 us
    pallas_call x1, Pallas kernels, body(): call(functools.partial(second_kernel, planes), [(blocks, EDGE_AT + ROWS,...  1.73 us
    ppermute x1, starting transfers between devices, body(): low = lax.ppermute(up, 'face', after_me)  1.63 us
  transfers between devices with their start and end apart: 6, of which 2 were waited for; matrix products, arithmetic and copies ran while one was open for 0% of the time, Pallas kernels for 27%

profile of v6, /device:TPU:0, one launch (start us, length us, event | category | flops | bytes accessed | tf_op | source)
XLA Modules:
  0.0 34.2 jit_solution(15228538003028029755)
XLA Ops:
  0.6 2.9 %start_kernel.1 = (f32[8,32,128]{2,1,0:T(8,128)}, f32[768,128]{1,0:T(8,128)S(1)}) custom-call(s32[8,128]{1,0:T(8,128)} %bitcast.26, f32[8,128]{1,0:T(8,128)} %bitcast.28, f32[32,2048]{1,0:T(8,128)} %bitcast.10, s32[8,128]{1,0:T(8,128)} %bitcast.23, f32[16,128]{1,0:T(8,128)} %jac_ref.1, f32[16,128]{1,0:T(8,128)} %land_ref.1, f32[512,128]{1,0:T(8,128)} %bitcast.15, ...), custom_call_target="tpu_custom_call" | custom-call | tf_op jit(solution)/shard_map/start_kernel/pallas_call | solution.py:831
  3.5 0.0 copy-start
  3.5 5.3 %all-to-all-start = ((f32[8,32,128]{2,1,0:T(8,128)}), f32[8,32,128]{2,1,0:T(8,128)S(1)}, u32[]{:S(2)}, u32[]{:S(2)}) async-start(f32[8,32,128]{2,1,0:T(8,128)} %get-tuple-element.19), calls=%async_computation | async-start | bytes 262144 | tf_op jit(solution)/shard_map/all_to_all | solution.py:841
  8.9 0.0 copy-start.12
  8.9 0.0 copy-done
  8.9 0.7 %copy-done.12 = s32[1,256]{1,0:T(1,128)S(1)} copy-done((s32[1,256]{1,0:T(1,128)S(1)}, s32[1,256]{1,0:T(1,128)}, u32[]{:S(2)}) %copy-start.12) | copy-done | bytes 1048
  9.5 0.0 copy-start.3
  9.5 0.0 copy-start.4
  9.5 0.0 copy-start.5
  9.5 0.0 copy-start.2
  9.6 0.2 send_kernel.1
  9.8 0.0 copy-start.1
  9.8 0.6 %collective-permute-start = (f32[32,128]{1,0:T(8,128)S(1)}, f32[32,128]{1,0:T(8,128)S(1)}, u32[]{:S(2)}, u32[]{:S(2)}) collective-permute-start(f32[32,128]{1,0:T(8,128)S(1)} %get-tuple-element.21), channel_id=1, source_target_pairs={{0,1},{1,2},{2,3},{3,4},{4,5},{5,6},{6,7},{7,0},{8,9},{9,10},{10,1... | collective-permute-start | bytes 49160 | tf_op jit(solution)/shard_map/ppermute | solution.py:863
  10.3 2.2 %collective-permute-start.1 = (f32[32,128]{1,0:T(8,128)S(1)}, f32[32,128]{1,0:T(8,128)S(1)}, u32[]{:S(2)}, u32[]{:S(2)}) collective-permute-start(f32[32,128]{1,0:T(8,128)S(1)} %get-tuple-element.20.after_ref), channel_id=1, source_target_pairs={{1,0},{2,1},{3,2},{4,3},{5,4},{6,5},{7,6},{0,7},{9,8},{10,9},{11,1... | collective-permute-start | bytes 49160 | tf_op jit(solution)/shard_map/ppermute | solution.py:864
  12.6 0.0 copy-done.3
  12.6 0.0 copy-done.4
  12.6 0.0 copy-done.5
  12.6 0.0 copy-start.6
  12.6 0.0 copy-start.7
  12.6 0.0 copy-start.8
  12.6 2.5 %ocean_kernel.3.after_ref.refs_0_ = f32[32,640]{1,0:T(8,128)S(1)} custom-call(f32[32,2048]{1,0:T(8,128)S(1)} %bitcast.12, f32[6,2048]{1,0:T(8,128)S(1)} %copy-done.3, s32[6,2048]{1,0:T(8,128)S(1)} %copy-done.4, f32[16,128]{1,0:T(8,128)S(1)} %bitcast.20, f32[32,128]{1,0:T(8,128)S(1)} %get-tuple-element.20.after_ref), custom_call_target="tpu_custom_call" | custom-call | bytes 7864320 | tf_op jit(solution)/shard_map/ocean_kernel/pallas_call | solution.py:848
  15.1 0.0 collective-permute-done.rim_before_ref.before_ref
  15.1 0.0 collective-permute-done.1.rim_after_ref.after_ref
  15.1 0.0 all-to-all-done.recv_ref
  15.1 0.0 copy-done.2
  15.1 0.0 copy-done.1
  15.2 0.0 copy-done.6
  15.2 0.0 copy-done.7
  15.2 0.0 copy-done.8
  15.2 0.5 %panel_kernel.1 = (f32[768,128]{1,0:T(8,128)S(1)}, f32[144,128]{1,0:T(8,128)S(1)}, f32[144,128]{1,0:T(8,128)S(1)}, f32[192,128]{1,0:T(8,128)S(1)}) custom-call(f32[768,128]{1,0:T(8,128)S(1)} %get-tuple-element.18.after_ref.moved_ref, f32[8,32,128]{2,1,0:T(8,128)S(1)} %all-to-all-done.recv_ref, f32[768,128]{1,0:T(8,128)S(1)} %bitcast.19, ...), custom_call_target="tpu_custom_call" | custom-call | tf_op jit(solution)/shard_map/panel_kernel/pallas_call | solution.py:867
  15.7 1.6 %collective-permute-start.2 = (f32[144,128]{1,0:T(8,128)S(1)}, f32[144,128]{1,0:T(8,128)S(1)}, u32[]{:S(2)}, u32[]{:S(2)}) collective-permute-start(f32[144,128]{1,0:T(8,128)S(1)} %get-tuple-element.24), channel_id=1, source_target_pairs={{0,8},{8,16},{16,24},{24,0},{1,9},{9,17},{17,25},{25,1},{2,10},{10... | collective-permute-start | bytes 221192 | tf_op jit(solution)/shard_map/ppermute | solution.py:884
  17.3 2.2 %collective-permute-start.3 = (f32[144,128]{1,0:T(8,128)S(1)}, f32[144,128]{1,0:T(8,128)S(1)}, u32[]{:S(2)}, u32[]{:S(2)}) collective-permute-start(f32[144,128]{1,0:T(8,128)S(1)} %get-tuple-element.25), channel_id=1, source_target_pairs={{8,0},{16,8},{24,16},{0,24},{9,1},{17,9},{25,17},{1,25},{10,2},{18... | collective-permute-start | bytes 221192 | tf_op jit(solution)/shard_map/ppermute | solution.py:885
  19.6 3.0 %ocean_kernel.4.after_ref.refs_1_ = f32[32,768]{1,0:T(8,128)S(1)} custom-call(f32[32,2048]{1,0:T(8,128)S(1)} %bitcast.13, f32[6,2048]{1,0:T(8,128)S(1)} %copy-done.3, s32[6,2048]{1,0:T(8,128)S(1)} %copy-done.4, f32[16,128]{1,0:T(8,128)S(1)} %bitcast.21, f32[192,128]{1,0:T(8,128)S(1)} %get-tuple-element.23.after_ref.surf_ref), custom_call_target="tpu_custom_call" | custom-call | bytes 9437184 | tf_op jit(solution)/shard_map/ocean_kernel/pallas_call | solution.py:848
  22.6 0.0 collective-permute-done.2.low_ref
  22.6 0.2 collective-permute-done.3.high_ref
  22.8 1.7 %second_kernel.1 = (f32[8,16,128]{2,1,0:T(8,128)}, f32[768,128]{1,0:T(8,128)S(1)}, f32[16,128]{1,0:T(8,128)S(1)}, f32[16,128]{1,0:T(8,128)S(1)}) custom-call(f32[768,128]{1,0:T(8,128)S(1)} %get-tuple-element.22.avg_ref, f32[192,128]{1,0:T(8,128)S(1)} %get-tuple-element.23.after_ref.surf_ref, f32[144,128]{1,0:T(8,128)S(1)} %collective-permute-done.2.low_ref, ...), custom_call_target="tpu_custom_call" | custom-call | tf_op jit(solution)/shard_map/second_kernel/pallas_call | solution.py:888
  24.5 3.5 %all-to-all-start.1 = ((f32[8,16,128]{2,1,0:T(8,128)}), f32[8,16,128]{2,1,0:T(8,128)S(1)}, u32[]{:S(2)}, u32[]{:S(2)}) async-start(f32[8,16,128]{2,1,0:T(8,128)} %get-tuple-element.27), calls=%async_computation.1 | async-start | bytes 131072 | tf_op jit(solution)/shard_map/all_to_all | solution.py:898
  28.0 0.0 copy-start.11
  28.0 2.5 %ocean_kernel.5.refs_2_ = f32[32,640]{1,0:T(8,128)S(1)} custom-call(f32[32,2048]{1,0:T(8,128)S(1)} %bitcast.14, f32[6,2048]{1,0:T(8,128)S(1)} %copy-done.3, s32[6,2048]{1,0:T(8,128)S(1)} %copy-done.4, f32[16,128]{1,0:T(8,128)S(1)} %bitcast.22, f32[16,128]{1,0:T(8,128)S(1)} %get-tuple-element.28.after_ref.final_ref), custom_call_target="tpu_custom_call" | custom-call | bytes 7864320 | tf_op jit(solution)/shard_map/ocean_kernel/pallas_call | solution.py:848
  30.5 0.0 copy-done.11
  30.5 0.0 copy-start.10
  30.5 1.2 %rim_kernel.1 = (f32[32,2048]{1,0:T(8,128)S(1)}, f32[16,128]{1,0:T(8,128)S(1)}) custom-call(f32[32,128]{1,0:T(8,128)S(1)} %collective-permute-done.rim_before_ref.before_ref, f32[32,128]{1,0:T(8,128)S(1)} %collective-permute-done.1.rim_after_ref.after_ref, f32[6,2048]{1,0:T(8,128)S(1)} %copy-done.3, s32[6,2048]{1,0:T(8,128)S(1)} %copy-done.4, ...), custom_call_target="tpu_custom_call" | custom-call | bytes 3145728 | tf_op jit(solution)/shard_map/rim_kernel/pallas_call | solution.py:900
  31.7 0.0 copy-start.9
  31.7 1.3 %all-to-all-done.1.recv_ref = f32[8,16,128]{2,1,0:T(8,128)S(1)} async-done(((f32[8,16,128]{2,1,0:T(8,128)}), f32[8,16,128]{2,1,0:T(8,128)S(1)}, u32[]{:S(2)}, u32[]{:S(2)}) %all-to-all-start.1) | async-done | bytes 65568 | tf_op jit(solution)/shard_map/all_to_all | solution.py:898
  33.0 0.0 copy-done.10
  33.0 0.0 copy-done.9
  33.0 1.2 %end_kernel.1 = (f32[768,128]{1,0:T(8,128)}, f32[32,2048]{1,0:T(8,128)}) custom-call(f32[768,128]{1,0:T(8,128)S(1)} %get-tuple-element.26.sums_ref, f32[8,16,128]{2,1,0:T(8,128)S(1)} %all-to-all-done.1.recv_ref, f32[16,128]{1,0:T(8,128)S(1)} %get-tuple-element.28.after_ref.final_ref, f32[16,128]{1,0:T(8,128)S(1)} %get-tuple-element.29.inverse_ref, ...), custom_call_target="tpu_custom_call" | custom-call | tf_op jit(solution)/shard_map/end_kernel/pallas_call | solution.py:906
Async XLA Ops:
  3.5 5.3 %copy-start = (f32[2,16,2048]{2,1,0:T(8,128)S(1)}, f32[2,16,2048]{2,1,0:T(8,128)}, u32[]{:S(2)}) copy-start(f32[2,16,2048]{2,1,0:T(8,128)} %param.18) | copy-start | bytes 786436
  3.5 11.6 %all-to-all-start = ((f32[8,32,128]{2,1,0:T(8,128)}), f32[8,32,128]{2,1,0:T(8,128)S(1)}, u32[]{:S(2)}, u32[]{:S(2)}) async-start(f32[8,32,128]{2,1,0:T(8,128)} %get-tuple-element.19), calls=%async_computation | async-start | bytes 262144 | tf_op jit(solution)/shard_map/all_to_all | solution.py:841
  8.9 0.7 %copy-start.12 = (s32[1,256]{1,0:T(1,128)S(1)}, s32[1,256]{1,0:T(1,128)}, u32[]{:S(2)}) copy-start(s32[1,256]{1,0:T(1,128)} %send_ref.1) | copy-start | bytes 3076
  9.5 3.0 %copy-start.3 = (f32[6,2048]{1,0:T(8,128)S(1)}, f32[6,2048]{1,0:T(8,128)}, u32[]{:S(2)}) copy-start(f32[6,2048]{1,0:T(8,128)} %coef_ref.7) | copy-start | bytes 147460
  9.5 3.0 %copy-start.4 = (s32[6,2048]{1,0:T(8,128)S(1)}, s32[6,2048]{1,0:T(8,128)}, u32[]{:S(2)}) copy-start(s32[6,2048]{1,0:T(8,128)} %near_ref.7) | copy-start | bytes 147460
  9.5 3.0 %copy-start.5 = (f32[2048]{0:T(1024)S(1)}, f32[2048]{0:T(1024)}, u32[]{:S(2)}) copy-start(f32[2048]{0:T(1024)} %param.21) | copy-start | bytes 24580
  9.5 5.6 %copy-start.2 = (f32[3,16,16,128]{3,2,1,0:T(8,128)S(1)}, f32[3,16,16,128]{3,2,1,0:T(8,128)}, u32[]{:S(2)}) copy-start(f32[3,16,16,128]{3,2,1,0:T(8,128)} %param.13) | copy-start | bytes 1179652
  9.8 5.4 %copy-start.1 = (f32[2,16,16,128]{3,2,1,0:T(8,128)S(1)}, f32[2,16,16,128]{3,2,1,0:T(8,128)}, u32[]{:S(2)}) copy-start(f32[2,16,16,128]{3,2,1,0:T(8,128)} %param.14) | copy-start | bytes 786436
  9.8 5.3 %collective-permute-start = (f32[32,128]{1,0:T(8,128)S(1)}, f32[32,128]{1,0:T(8,128)S(1)}, u32[]{:S(2)}, u32[]{:S(2)}) collective-permute-start(f32[32,128]{1,0:T(8,128)S(1)} %get-tuple-element.21), channel_id=1, source_target_pairs={{0,1},{1,2},{2,3},{3,4},{4,5},{5,6},{6,7},{7,0},{8,9},{9,10},{10,1... | collective-permute-start | bytes 49160 | tf_op jit(solution)/shard_map/ppermute | solution.py:863
  10.3 4.8 %collective-permute-start.1 = (f32[32,128]{1,0:T(8,128)S(1)}, f32[32,128]{1,0:T(8,128)S(1)}, u32[]{:S(2)}, u32[]{:S(2)}) collective-permute-start(f32[32,128]{1,0:T(8,128)S(1)} %get-tuple-element.20.after_ref), channel_id=1, source_target_pairs={{1,0},{2,1},{3,2},{4,3},{5,4},{6,5},{7,6},{0,7},{9,8},{10,9},{11,1... | collective-permute-start | bytes 49160 | tf_op jit(solution)/shard_map/ppermute | solution.py:864
  12.6 2.6 %copy-start.6 = (s32[1,8,128]{2,1,0:T(8,128)S(1)}, s32[1,8,128]{2,1,0:T(8,128)}, u32[]{:S(2)}) copy-start(s32[1,8,128]{2,1,0:T(8,128)} %param.17) | copy-start | bytes 12292
  12.6 2.6 %copy-start.7 = (f32[16,128]{1,0:T(8,128)S(1)}, f32[16,128]{1,0:T(8,128)}, u32[]{:S(2)}) copy-start(f32[16,128]{1,0:T(8,128)} %jac_ref.1) | copy-start | bytes 24580
  12.6 2.6 %copy-start.8 = (f32[16,128]{1,0:T(8,128)S(1)}, f32[16,128]{1,0:T(8,128)}, u32[]{:S(2)}) copy-start(f32[16,128]{1,0:T(8,128)} %land_ref.1) | copy-start | bytes 24580
  15.7 6.9 %collective-permute-start.2 = (f32[144,128]{1,0:T(8,128)S(1)}, f32[144,128]{1,0:T(8,128)S(1)}, u32[]{:S(2)}, u32[]{:S(2)}) collective-permute-start(f32[144,128]{1,0:T(8,128)S(1)} %get-tuple-element.24), channel_id=1, source_target_pairs={{0,8},{8,16},{16,24},{24,0},{1,9},{9,17},{17,25},{25,1},{2,10},{10... | collective-permute-start | bytes 221192 | tf_op jit(solution)/shard_map/ppermute | solution.py:884
  17.3 5.5 %collective-permute-start.3 = (f32[144,128]{1,0:T(8,128)S(1)}, f32[144,128]{1,0:T(8,128)S(1)}, u32[]{:S(2)}, u32[]{:S(2)}) collective-permute-start(f32[144,128]{1,0:T(8,128)S(1)} %get-tuple-element.25), channel_id=1, source_target_pairs={{8,0},{16,8},{24,16},{0,24},{9,1},{17,9},{25,17},{1,25},{10,2},{18... | collective-permute-start | bytes 221192 | tf_op jit(solution)/shard_map/ppermute | solution.py:885
  24.5 8.5 %all-to-all-start.1 = ((f32[8,16,128]{2,1,0:T(8,128)}), f32[8,16,128]{2,1,0:T(8,128)S(1)}, u32[]{:S(2)}, u32[]{:S(2)}) async-start(f32[8,16,128]{2,1,0:T(8,128)} %get-tuple-element.27), calls=%async_computation.1 | async-start | bytes 131072 | tf_op jit(solution)/shard_map/all_to_all | solution.py:898
  28.0 2.5 %copy-start.11 = (f32[2048]{0:T(1024)S(1)}, f32[2048]{0:T(1024)}, u32[]{:S(2)}) copy-start(f32[2048]{0:T(1024)} %param.22) | copy-start | bytes 24580
  30.5 2.5 %copy-start.10 = (f32[1,8,128]{2,1,0:T(8,128)S(1)}, f32[1,8,128]{2,1,0:T(8,128)}, u32[]{:S(2)}) copy-start(f32[1,8,128]{2,1,0:T(8,128)} %param.25) | copy-start | bytes 12292
  31.7 1.3 %copy-start.9 = (s32[1,8,128]{2,1,0:T(8,128)S(1)}, s32[1,8,128]{2,1,0:T(8,128)}, u32[]{:S(2)}) copy-start(s32[1,8,128]{2,1,0:T(8,128)} %param.24) | copy-start | bytes 12292

commit v7 on v6

--- a/solution.py
+++ b/solution.py
@@ -21,7 +21,8 @@
 relax_rate = 0.3
 flux_gain = 0.2
 
-HEAD, EDGE_AT, STRIP_AT, IDS_AT = 8, 8, 16, 24
+HEAD, EDGE_AT = 8, 8
+SIDE_EDGE, SIDE_STRIP, SIDE_IDS = 0, 8, 16
 AVG, MASS_SUM, MASS, COEF_X, COEF_Y, SURF = range(6)
 SURF_ARRAYS = 6
 
@@ -224,32 +225,54 @@
     ]
 
 
-def start_kernel(planes, inputs, *refs):
-    sources, (slab_ref, moved_ref), held = (
-        refs[:inputs],
-        refs[inputs : inputs + 2],
-        refs[inputs + 2 : -1],
-    )
+def start_kernel(
+    planes,
+    cols_in,
+    weights_in,
+    tracers_in,
+    rows_in,
+    jac_in,
+    land_in,
+    wind_in,
+    air_in,
+    send_in,
+    slab_out,
+    moved_ref,
+    before_ref,
+    after_ref,
+    cols_ref,
+    weights_ref,
+    rows_ref,
+    send_ref,
+    slab_ref,
+    tracers_ref,
+    jac_ref,
+    land_ref,
+    wind_ref,
+    air_ref,
+    semaphores,
+):
     copies = [
-        pltpu.make_async_copy(source.at[: target.shape[0]], target, refs[-1].at[i])
-        for i, (source, target) in enumerate(zip(sources, held))
+        pltpu.make_async_copy(source, target, semaphores.at[i])
+        for i, (source, target) in enumerate(
+            (
+                (cols_in, cols_ref),
+                (tracers_in.at[:ROWS], tracers_ref),
+                (weights_in, weights_ref),
+                (rows_in, rows_ref),
+                (air_in, air_ref),
+                (wind_in, wind_ref),
+                (jac_in, jac_ref),
+                (land_in, land_ref),
+                (send_in, send_ref),
+            )
+        )
     ]
     for copy in copies:
         copy.start()
-    (
-        cols_ref,
-        weights_ref,
-        tracers_ref,
-        rows_ref,
-        jac_ref,
-        land_ref,
-        wind_ref,
-        air_ref,
-    ) = held
     geo = Geometry()
     blocks = cols_ref.shape[0]
     x_points = jac_ref.shape[0]
-    left, right = neighbours_of(blocks)
     levels = wind_ref.shape[0] // (2 * x_points)
     chunks = tracers_ref.shape[1] // LANES
     for copy in copies[:4]:
@@ -272,9 +295,12 @@
                 slab_ref[to, 2 * place : 2 * place + 1, :] = heat[c : c + 1]
                 slab_ref[to, 2 * place + 1 : 2 * place + 2, :] = area[c : c + 1]
 
+    out = pltpu.make_async_copy(slab_ref, slab_out, semaphores.at[len(copies)])
+    out.start()
     ids = rows_ref[...].astype(jnp.float32)
-    for to in (left, right):
-        slab_ref[to, IDS_AT : IDS_AT + blocks, :] = ids
+    for side_ref in (before_ref, after_ref):
+        side_ref[SIDE_IDS : SIDE_IDS + blocks, :] = ids
+
     for copy in copies[4:]:
         copy.wait()
     strips = []
@@ -296,8 +322,8 @@
             )
         strips.append(pack)
     to_right, to_left = split_sides(geo, strips[0], strips[1], ROWS)
-    slab_ref[right, STRIP_AT : STRIP_AT + ROWS, :] = to_right
-    slab_ref[left, STRIP_AT : STRIP_AT + ROWS, :] = to_left
+    after_ref[SIDE_STRIP : SIDE_STRIP + ROWS, :] = to_right
+    before_ref[SIDE_STRIP : SIDE_STRIP + ROWS, :] = to_left
 
     y_weight = jnp.where(geo.y_edge, 1.0 / 6.0, 5.0 / 6.0)
     for element in range(x_points // GLL):
@@ -324,22 +350,23 @@
                     moved_ref[planes * x + plane : planes * x + plane + ROWS, :] = moved
     packs = all_edges(geo, moved_ref, planes, x_points)
     to_right, to_left = split_sides(geo, packs[0], packs[1], 1)
-    slab_ref[right, EDGE_AT : EDGE_AT + ROWS, :] = to_right
-    slab_ref[left, EDGE_AT : EDGE_AT + ROWS, :] = to_left
+    after_ref[SIDE_EDGE : SIDE_EDGE + ROWS, :] = to_right
+    before_ref[SIDE_EDGE : SIDE_EDGE + ROWS, :] = to_left
+    out.wait()
 
 
 def panel_kernel(
     planes,
     moved_ref,
     recv_ref,
+    before_ref,
+    after_ref,
     air_ref,
     wind_ref,
     jac_ref,
     land_ref,
     rows_ref,
-    after_ref,
-    rim_before_ref,
-    rim_after_ref,
+    ocean_ref,
     avg_ref,
     down_ref,
     up_ref,
@@ -347,13 +374,12 @@
 ):
     geo = Geometry()
     blocks = rows_ref.shape[0]
-    left, right = neighbours_of(blocks)
     x_points = jac_ref.shape[0]
     levels = wind_ref.shape[0] // (2 * x_points)
 
     own_ids = rows_ref[...]
-    left_ids = recv_ref[left, IDS_AT : IDS_AT + blocks, :].astype(jnp.int32)
-    right_ids = recv_ref[right, IDS_AT : IDS_AT + blocks, :].astype(jnp.int32)
+    left_ids = before_ref[SIDE_IDS : SIDE_IDS + blocks, :].astype(jnp.int32)
+    right_ids = after_ref[SIDE_IDS : SIDE_IDS + blocks, :].astype(jnp.int32)
     head = [
         jnp.concatenate([recv_ref[c, i : i + 1, :] for c in range(blocks)], axis=0)
         for i in range(6)
@@ -369,8 +395,8 @@
     in_strip = (geo.lane < ROWS) | (geo.lane >= LANES - ROWS)
     packs = join_sides(
         geo,
-        recv_ref[left, STRIP_AT : STRIP_AT + ROWS, :],
-        recv_ref[right, STRIP_AT : STRIP_AT + ROWS, :],
+        before_ref[SIDE_STRIP : SIDE_STRIP + ROWS, :],
+        after_ref[SIDE_STRIP : SIDE_STRIP + ROWS, :],
         ROWS,
     )
     own, strip = [], []
@@ -428,8 +454,8 @@
 
     joined = join_edges(
         geo,
-        recv_ref[left, EDGE_AT : EDGE_AT + ROWS, :],
-        recv_ref[right, EDGE_AT : EDGE_AT + ROWS, :],
+        before_ref[SIDE_EDGE : SIDE_EDGE + ROWS, :],
+        after_ref[SIDE_EDGE : SIDE_EDGE + ROWS, :],
     )
     for x in range(x_points):
         for group in range(planes // ROWS):
@@ -493,11 +519,14 @@
     high_ref,
     wind_ref,
     rows_ref,
-    after_ref,
-    slab_ref,
+    ocean_ref,
+    slab_out,
     sums_ref,
     final_ref,
     inverse_ref,
+    flux_ref,
+    edges_ref,
+    semaphores,
 ):
     geo = Geometry()
     blocks = rows_ref.shape[0]
@@ -568,7 +597,12 @@
             line = spread(flux[x // ROWS][x % ROWS : x % ROWS + 1])
             picked = jnp.where(high == x, take(line, low, 1), picked)
         for c in range(ROWS):
-            slab_ref[ROWS * group + c, 0:1, :] = picked[c : c + 1]
+            flux_ref[ROWS * group + c, 0:1, :] = picked[c : c + 1]
+
+    copies = [
+        pltpu.make_async_copy(flux_ref, slab_out.at[:, :HEAD], semaphores.at[0])
+    ]
+    copies[0].start()
 
     def put(x, plane, value):
         sums_ref[planes * x + plane : planes * x + plane + ROWS, :] = value
@@ -632,8 +666,18 @@
                     put(last, plane, held[plane] + after)
     packs = all_edges(geo, sums_ref, planes, x_points)
     to_right, to_left = split_sides(geo, packs[0], packs[1], 1)
-    slab_ref[right, EDGE_AT : EDGE_AT + ROWS, :] = to_right
-    slab_ref[left, EDGE_AT : EDGE_AT + ROWS, :] = to_left
+    for i, (to, edges) in enumerate(((right, to_right), (left, to_left))):
+        edges_ref[i] = edges
+        copies.append(
+            pltpu.make_async_copy(
+                edges_ref.at[i],
+                slab_out.at[to, EDGE_AT : EDGE_AT + ROWS],
+                semaphores.at[1 + i],
+            )
+        )
+        copies[-1].start()
+    for copy in copies:
+        copy.wait()
 
 
 def end_kernel(
@@ -730,9 +774,11 @@
     lax.fori_loop(0, out_ref.shape[1] // LANES, one_chunk, 0)
 
 
-def send_kernel(tracers_ref, send_ref, after_ref, *rim_refs):
+def send_kernel(tracers_ref, send_ref, before_ref, after_ref, *out_refs):
     chunks = tracers_ref.shape[1] // LANES
-    for part, rim_ref in enumerate(rim_refs):
+    for part, (side_ref, out_ref) in enumerate(zip((before_ref, after_ref), out_refs)):
+        base = side_ref.shape[0]
+        out_ref[:base, :] = side_ref[...]
         cells = spread(send_ref[0:1, LANES * part : LANES * (part + 1)])
         high, low = cells >> 7, cells & (LANES - 1)
         for group in range(tracers_ref.shape[0] // ROWS):
@@ -741,7 +787,7 @@
             for k in range(chunks):
                 tile = tracers_ref[half, LANES * k : LANES * (k + 1)]
                 rim = jnp.where(high == k, take(tile, low, 1), rim)
-            rim_ref[half, :] = rim
+            out_ref[base + ROWS * group : base + ROWS * (group + 1), :] = rim
 
 
 def rim_kernel(
@@ -756,11 +802,13 @@
     partial_refs, (out_ref, gain_ref) = refs[: len(starts)], refs[len(starts) :]
     chunks = coef_ref.shape[1] // LANES
     groups = out_ref.shape[0] // ROWS
+    rim_at = before_ref.shape[0] - out_ref.shape[0]
     sides = before_ref, after_ref
     gain_ref[...] = flux_gain / area_ref[...]
 
     def source(group, s):
-        return sides[s][ROWS * group : ROWS * (group + 1), :]
+        at = rim_at + ROWS * group
+        return sides[s][at : at + ROWS, :]
 
     for k in range(chunks):
         at = slice(LANES * k, LANES * (k + 1))
@@ -777,14 +825,22 @@
 HBM_SPEC = pl.BlockSpec(memory_space=pltpu.HBM)
 
 
-def call(kernel, outs, specs, scratch=(), cost=0):
+def call(kernel, outs, specs, scratch=(), cost=0, hbm_out=False):
     estimate = None
     if cost:
         estimate = pl.CostEstimate(flops=0, bytes_accessed=cost, transcendentals=0)
+    outs = [
+        out if isinstance(out, jax.ShapeDtypeStruct) else jax.ShapeDtypeStruct(out, jnp.float32)
+        for out in outs
+    ]
+    out_specs = [VMEM_SPEC] * len(outs)
+    if hbm_out:
+        out_specs[0] = HBM_SPEC
     return pl.pallas_call(
         kernel,
-        out_shape=[jax.ShapeDtypeStruct(shape, jnp.float32) for shape in outs],
+        out_shape=outs,
         in_specs=specs,
+        out_specs=out_specs,
         scratch_shapes=list(scratch),
         cost_estimate=estimate,
         compiler_params=pltpu.CompilerParams(vmem_limit_bytes=32 * 2**20),
@@ -827,22 +883,34 @@
         land_area,
         wind,
         air,
-    )
-    slab, moved = call(
-        functools.partial(start_kernel, planes, len(first_inputs)),
-        [(blocks, IDS_AT + blocks, LANES), air.shape],
+        send_list,
+    )
+    kept = (cell_ids, weights, point_ids, send_list)
+    slab, moved, to_before, to_after, cell_ids, weights, point_ids, send_list = call(
+        functools.partial(start_kernel, planes),
+        [(blocks, HEAD, LANES), air.shape]
+        + [(SIDE_IDS + blocks, LANES)] * 2
+        + [jax.ShapeDtypeStruct(array.shape, array.dtype) for array in kept],
         [HBM_SPEC] * len(first_inputs),
         [
-            pltpu.VMEM((ROWS, cells) if array is ocean else array.shape, array.dtype)
-            for array in first_inputs
+            pltpu.VMEM(shape, jnp.float32)
+            for shape in (
+                (blocks, HEAD, LANES),
+                (ROWS, cells),
+                jacobian.shape,
+                land_area.shape,
+                wind.shape,
+                air.shape,
+            )
         ]
-        + [pltpu.SemaphoreType.DMA((len(first_inputs),))],
+        + [pltpu.SemaphoreType.DMA((len(first_inputs) + 1,))],
+        hbm_out=True,
     )(*(pltpu.with_memory_space_constraint(array, pltpu.HBM) for array in first_inputs))
     recv = lax.all_to_all(slab, "blk", split_axis=0, concat_axis=0, tiled=True)
 
     chunks = cells // LANES
     reads_per_chunk = edge_coef.shape[0] * chunks * (ocean_planes // ROWS)
-    starts = (0, chunks * 5 // 16, chunks * 11 // 16)
+    starts = (0, chunks * 3 // 16, chunks * 10 // 16)
 
     def ocean_part(start, end, after):
         (result,) = call(
@@ -855,30 +923,30 @@
 
     to_before, to_after = call(
         send_kernel,
-        [(ocean_planes, LANES)] * 2,
-        [VMEM_SPEC] * 2 + [ANY_SPEC],
+        [(SIDE_IDS + blocks + ocean_planes, LANES)] * 2,
+        [VMEM_SPEC] * 4,
         cost=reads_per_chunk * ROWS * LANES,
-    )(ocean, send_list, moved)
+    )(ocean, send_list, to_before, to_after)
     onward = [(i, (i + 1) % blocks) for i in range(blocks)]
-    rim_before = lax.ppermute(to_after, "blk", onward)
-    rim_after = lax.ppermute(to_before, "blk", [(to, source) for source, to in onward])
+    before = lax.ppermute(to_after, "blk", onward)
+    after = lax.ppermute(to_before, "blk", [(to, source) for source, to in onward])
     first_part = ocean_part(starts[0], starts[1], to_before)
     side_rows = 2 * planes + 2 * levels + 2 * SURF_ARRAYS + 4
     avg, down, up, surf = call(
         functools.partial(panel_kernel, planes),
         [air.shape, (side_rows, LANES), (side_rows, LANES), (4 * ROWS * SURF_ARRAYS, LANES)],
-        [VMEM_SPEC] * 7 + [ANY_SPEC] * 3,
+        [VMEM_SPEC] * 9 + [ANY_SPEC],
     )(
         moved,
         recv,
+        before,
+        after,
         air,
         wind,
         jacobian,
         land_area,
         point_ids,
         first_part,
-        rim_before,
-        rim_after,
     )
     after_me = [(i, (i + 1) % faces) for i in range(faces)]
     low = lax.ppermute(up, "face", after_me)
@@ -894,6 +962,12 @@
             (x_points, y_points),
         ],
         [VMEM_SPEC] * 6 + [ANY_SPEC],
+        [
+            pltpu.VMEM((blocks, HEAD, LANES), jnp.float32),
+            pltpu.VMEM((2, ROWS, LANES), jnp.float32),
+            pltpu.SemaphoreType.DMA((3,)),
+        ],
+        hbm_out=True,
     )(avg, surf, low, high, wind, point_ids, second_part)
     arrived = lax.all_to_all(slab, "blk", split_axis=0, concat_axis=0, tiled=True)
     third_part = ocean_part(starts[2], chunks, final)
@@ -902,7 +976,7 @@
         [ocean.shape, area.shape],
         [VMEM_SPEC] * (5 + len(starts)),
         cost=chunks * reads_per_chunk // 8 * ROWS * LANES * 4,
-    )(rim_before, rim_after, edge_coef, neighbours, area, first_part, second_part, third_part)
+    )(before, after, edge_coef, neighbours, area, first_part, second_part, third_part)
     air_final, ocean_final = call(
         functools.partial(end_kernel, planes),
         [air.shape, ocean.shape],

time: 34.6 us -> 33.1 us (0.957)
  Pallas kernels: 15.7 us -> 15 us
  local copies, waits for them, and re-layouts: 0.73 us -> 0.05 us
    unnamed x26 -> x18, local copies, waits for them, and re-layouts: 0.73 us -> 0.05 us
    pallas_call x2, Pallas kernels: 3.1 us -> 2.47 us  [the longest x1 2.27 us: body(): call(functools.partial(start_kernel, planes), [(blocks, HEAD, LANES), air...]
    all_to_all x1, waiting for transfers between devices: 1.29 us -> 0.74 us  [body(): lax.all_to_all(slab, 'blk', split_axis=0, concat_axis=0, tiled=True)]
    ppermute x1, waiting for transfers between devices: 0.2 us -> 0.57 us  [body(): high = lax.ppermute(down, 'face', [(to, source) for source, to in after_me])]
  transfers between devices with their start and end apart: 6 -> 6, of which waited for: 2 -> 3; matrix products, arithmetic and copies ran while one was open for 0% -> 0% of each run, Pallas kernels for 27% -> 29%
where the time goes in v7:
time: 33.1 us; the launch traced here: 32.8 us
  starting transfers between devices  15.3 us (46%)
  Pallas kernels  15 us (45%)
  waiting for transfers between devices  1.6 us (5%)
  between operations  0.81 us (2%)
    pallas_call x3, Pallas kernels, ocean_part(): call(functools.partial(ocean_kernel, ocean_levels, start), [(ocean_planes...  7.98 us
    all_to_all x1, starting transfers between devices, body(): recv = lax.all_to_all(slab, 'blk', split_axis=0, concat_axis=0, tiled=True)  5.31 us
    all_to_all x1, starting transfers between devices, body(): lax.all_to_all(slab, 'blk', split_axis=0, concat_axis=0, tiled=True)  3.36 us
    pallas_call x1, Pallas kernels, body(): call(functools.partial(start_kernel, planes), [(blocks, HEAD, LANES), air...  2.27 us
    ppermute x1, starting transfers between devices, body(): high = lax.ppermute(down, 'face', [(to, source) for source, to in after_me])  2.25 us
    ppermute x1, starting transfers between devices, body(): lax.ppermute(to_before, 'blk', [(to, source) for source, to in onward])  2.24 us
    pallas_call x1, Pallas kernels, body(): call(functools.partial(second_kernel, planes), [(blocks, EDGE_AT + ROWS,...  1.72 us
    ppermute x1, starting transfers between devices, body(): low = lax.ppermute(up, 'face', after_me)  1.63 us
  transfers between devices with their start and end apart: 6, of which 3 were waited for; matrix products, arithmetic and copies ran while one was open for 0% of the time, Pallas kernels for 29%

profile of v7, /device:TPU:0, one launch (start us, length us, event | category | flops | bytes accessed | tf_op | source)
XLA Modules:
  0.0 32.8 jit_solution(6761073289975880805)
XLA Ops:
  0.6 0.0 copy-start
  0.6 2.3 %start_kernel.1 = (f32[8,8,128]{2,1,0:T(8,128)}, f32[768,128]{1,0:T(8,128)S(1)}, f32[24,128]{1,0:T(8,128)S(1)}, f32[24,128]{1,0:T(8,128)S(1)}, s32[8,128]{1,0:T(...) custom-call(s32[8,128]{1,0:T(8,128)} %bitcast.24, f32[8,128]{1,0:T(8,128)} %bitcast.25, ...), custom_call_target="tpu_custom_call" | custom-call | tf_op jit(solution)/shard_map/start_kernel/pallas_call | solution.py:889
  2.9 0.0 copy-start.3
  2.9 0.0 copy-start.4
  2.9 0.0 copy-start.5
  3.0 5.3 %all-to-all-start = ((f32[8,8,128]{2,1,0:T(8,128)}), f32[8,8,128]{2,1,0:T(8,128)S(1)}, u32[]{:S(2)}, u32[]{:S(2)}) async-start(f32[8,8,128]{2,1,0:T(8,128)} %get-tuple-element.25), calls=%async_computation | async-start | bytes 65536 | tf_op jit(solution)/shard_map/all_to_all | solution.py:909
  8.3 0.0 copy-start.2
  8.3 0.0 copy-done
  8.3 0.2 send_kernel.1
  8.5 0.0 copy-start.1
  8.5 0.5 %collective-permute-start = (f32[56,128]{1,0:T(8,128)S(1)}, f32[56,128]{1,0:T(8,128)S(1)}, u32[]{:S(2)}, u32[]{:S(2)}) collective-permute-start(f32[56,128]{1,0:T(8,128)S(1)} %get-tuple-element.29), channel_id=1, source_target_pairs={{0,1},{1,2},{2,3},{3,4},{4,5},{5,6},{6,7},{7,0},{8,9},{9,10},{10,1... | collective-permute-start | bytes 86024 | tf_op jit(solution)/shard_map/ppermute | solution.py:931
  9.1 2.2 %collective-permute-start.1 = (f32[56,128]{1,0:T(8,128)S(1)}, f32[56,128]{1,0:T(8,128)S(1)}, u32[]{:S(2)}, u32[]{:S(2)}) collective-permute-start(f32[56,128]{1,0:T(8,128)S(1)} %get-tuple-element.30.after_ref), channel_id=1, source_target_pairs={{1,0},{2,1},{3,2},{4,3},{5,4},{6,5},{7,6},{0,7},{9,8},{10,9},{11,1... | collective-permute-start | bytes 86024 | tf_op jit(solution)/shard_map/ppermute | solution.py:932
  11.3 0.0 copy-done.3
  11.3 0.0 copy-done.4
  11.3 0.0 copy-done.5
  11.3 0.0 copy-start.6
  11.3 0.0 copy-start.7
  11.3 1.5 %ocean_kernel.3.ocean_ref.refs_0_ = f32[32,384]{1,0:T(8,128)S(1)} custom-call(f32[32,2048]{1,0:T(8,128)S(1)} %bitcast.12, f32[6,2048]{1,0:T(8,128)S(1)} %copy-done.3, s32[6,2048]{1,0:T(8,128)S(1)} %copy-done.4, f32[16,128]{1,0:T(8,128)S(1)} %bitcast.20, f32[56,128]{1,0:T(8,128)S(1)} %get-tuple-element.30.after_ref), custom_call_target="tpu_custom_call" | custom-call | bytes 4718592 | tf_op jit(solution)/shard_map/ocean_kernel/pallas_call | solution.py:916
  12.8 0.3 all-to-all-done.recv_ref
  13.1 0.0 collective-permute-done.before_ref
  13.1 0.0 collective-permute-done.1.after_ref
  13.1 0.0 copy-done.2
  13.1 0.0 copy-done.1
  13.1 0.0 copy-done.6
  13.1 0.0 copy-done.7
  13.2 0.5 %panel_kernel.1 = (f32[768,128]{1,0:T(8,128)S(1)}, f32[144,128]{1,0:T(8,128)S(1)}, f32[144,128]{1,0:T(8,128)S(1)}, f32[192,128]{1,0:T(8,128)S(1)}) custom-call(f32[768,128]{1,0:T(8,128)S(1)} %get-tuple-element.24.moved_ref, f32[8,8,128]{2,1,0:T(8,128)S(1)} %all-to-all-done.recv_ref, f32[56,128]{1,0:T(8,128)S(1)} %collective-permute-done.before_ref, ...), custom_call_target="tpu_custom_call" | custom-call | tf_op jit(solution)/shard_map/panel_kernel/pallas_call | solution.py:935
  13.6 1.6 %collective-permute-start.2 = (f32[144,128]{1,0:T(8,128)S(1)}, f32[144,128]{1,0:T(8,128)S(1)}, u32[]{:S(2)}, u32[]{:S(2)}) collective-permute-start(f32[144,128]{1,0:T(8,128)S(1)} %get-tuple-element.34), channel_id=1, source_target_pairs={{0,8},{8,16},{16,24},{24,0},{1,9},{9,17},{17,25},{25,1},{2,10},{10... | collective-permute-start | bytes 221192 | tf_op jit(solution)/shard_map/ppermute | solution.py:952
  15.3 2.2 %collective-permute-start.3 = (f32[144,128]{1,0:T(8,128)S(1)}, f32[144,128]{1,0:T(8,128)S(1)}, u32[]{:S(2)}, u32[]{:S(2)}) collective-permute-start(f32[144,128]{1,0:T(8,128)S(1)} %get-tuple-element.35), channel_id=1, source_target_pairs={{8,0},{16,8},{24,16},{0,24},{9,1},{17,9},{25,17},{1,25},{10,2},{18... | collective-permute-start | bytes 221192 | tf_op jit(solution)/shard_map/ppermute | solution.py:953
  17.5 3.5 %ocean_kernel.4.ocean_ref.refs_1_ = f32[32,896]{1,0:T(8,128)S(1)} custom-call(f32[32,2048]{1,0:T(8,128)S(1)} %bitcast.13, f32[6,2048]{1,0:T(8,128)S(1)} %copy-done.3, s32[6,2048]{1,0:T(8,128)S(1)} %copy-done.4, f32[16,128]{1,0:T(8,128)S(1)} %bitcast.21, f32[192,128]{1,0:T(8,128)S(1)} %get-tuple-element.33.after_ref.surf_ref), custom_call_target="tpu_custom_call" | custom-call | bytes 11010048 | tf_op jit(solution)/shard_map/ocean_kernel/pallas_call | solution.py:916
  21.0 0.0 collective-permute-done.2.low_ref
  21.0 0.6 %collective-permute-done.3.high_ref = f32[144,128]{1,0:T(8,128)S(1)} collective-permute-done((f32[144,128]{1,0:T(8,128)S(1)}, f32[144,128]{1,0:T(8,128)S(1)}, u32[]{:S(2)}, u32[]{:S(2)}) %collective-permute-start.3) | collective-permute-done | bytes 73760 | tf_op jit(solution)/shard_map/ppermute | solution.py:953
  21.6 1.7 %second_kernel.1 = (f32[8,16,128]{2,1,0:T(8,128)}, f32[768,128]{1,0:T(8,128)S(1)}, f32[16,128]{1,0:T(8,128)S(1)}, f32[16,128]{1,0:T(8,128)S(1)}) custom-call(f32[768,128]{1,0:T(8,128)S(1)} %get-tuple-element.32.avg_ref, f32[192,128]{1,0:T(8,128)S(1)} %get-tuple-element.33.after_ref.surf_ref, f32[144,128]{1,0:T(8,128)S(1)} %collective-permute-done.2.low_ref, ...), custom_call_target="tpu_custom_call" | custom-call | tf_op jit(solution)/shard_map/second_kernel/pallas_call | solution.py:956
  23.3 3.4 %all-to-all-start.1 = ((f32[8,16,128]{2,1,0:T(8,128)}), f32[8,16,128]{2,1,0:T(8,128)S(1)}, u32[]{:S(2)}, u32[]{:S(2)}) async-start(f32[8,16,128]{2,1,0:T(8,128)} %get-tuple-element.37), calls=%async_computation.1 | async-start | bytes 131072 | tf_op jit(solution)/shard_map/all_to_all | solution.py:972
  26.7 0.0 copy-start.8
  26.7 3.0 %ocean_kernel.5.refs_2_ = f32[32,768]{1,0:T(8,128)S(1)} custom-call(f32[32,2048]{1,0:T(8,128)S(1)} %bitcast.14, f32[6,2048]{1,0:T(8,128)S(1)} %copy-done.3, s32[6,2048]{1,0:T(8,128)S(1)} %copy-done.4, f32[16,128]{1,0:T(8,128)S(1)} %bitcast.22, f32[16,128]{1,0:T(8,128)S(1)} %get-tuple-element.38.after_ref.final_ref), custom_call_target="tpu_custom_call" | custom-call | bytes 9437184 | tf_op jit(solution)/shard_map/ocean_kernel/pallas_call | solution.py:916
  29.7 0.0 copy-done.8
  29.7 1.2 %rim_kernel.1 = (f32[32,2048]{1,0:T(8,128)S(1)}, f32[16,128]{1,0:T(8,128)S(1)}) custom-call(f32[56,128]{1,0:T(8,128)S(1)} %collective-permute-done.before_ref, f32[56,128]{1,0:T(8,128)S(1)} %collective-permute-done.1.after_ref, f32[6,2048]{1,0:T(8,128)S(1)} %copy-done.3, s32[6,2048]{1,0:T(8,128)S(1)} %copy-done.4, f32[16,128]{1,0:T(8,128)S(1)} %bitcast.23, ...), custom_call_target="tpu_custom_call" | custom-call | bytes 3145728 | tf_op jit(solution)/shard_map/rim_kernel/pallas_call | solution.py:974
  30.9 0.7 %all-to-all-done.1.recv_ref = f32[8,16,128]{2,1,0:T(8,128)S(1)} async-done(((f32[8,16,128]{2,1,0:T(8,128)}), f32[8,16,128]{2,1,0:T(8,128)S(1)}, u32[]{:S(2)}, u32[]{:S(2)}) %all-to-all-start.1) | async-done | bytes 65568 | tf_op jit(solution)/shard_map/all_to_all | solution.py:972
  31.6 1.2 %end_kernel.1 = (f32[768,128]{1,0:T(8,128)}, f32[32,2048]{1,0:T(8,128)}) custom-call(f32[768,128]{1,0:T(8,128)S(1)} %get-tuple-element.36.sums_ref, f32[8,16,128]{2,1,0:T(8,128)S(1)} %all-to-all-done.1.recv_ref, f32[16,128]{1,0:T(8,128)S(1)} %get-tuple-element.38.after_ref.final_ref, f32[16,128]{1,0:T(8,128)S(1)} %get-tuple-element.39.inverse_ref, ...), custom_call_target="tpu_custom_call" | custom-call | tf_op jit(solution)/shard_map/end_kernel/pallas_call | solution.py:980
Async XLA Ops:
  0.6 7.6 %copy-start = (f32[2,16,2048]{2,1,0:T(8,128)S(1)}, f32[2,16,2048]{2,1,0:T(8,128)}, u32[]{:S(2)}) copy-start(f32[2,16,2048]{2,1,0:T(8,128)} %param.18) | copy-start | bytes 786436
  2.9 8.4 %copy-start.3 = (f32[6,2048]{1,0:T(8,128)S(1)}, f32[6,2048]{1,0:T(8,128)}, u32[]{:S(2)}) copy-start(f32[6,2048]{1,0:T(8,128)} %coef_ref.7) | copy-start | bytes 147460
  2.9 8.4 %copy-start.4 = (s32[6,2048]{1,0:T(8,128)S(1)}, s32[6,2048]{1,0:T(8,128)}, u32[]{:S(2)}) copy-start(s32[6,2048]{1,0:T(8,128)} %near_ref.7) | copy-start | bytes 147460
  2.9 8.4 %copy-start.5 = (f32[2048]{0:T(1024)S(1)}, f32[2048]{0:T(1024)}, u32[]{:S(2)}) copy-start(f32[2048]{0:T(1024)} %param.21) | copy-start | bytes 24580
  3.0 10.2 %all-to-all-start = ((f32[8,8,128]{2,1,0:T(8,128)}), f32[8,8,128]{2,1,0:T(8,128)S(1)}, u32[]{:S(2)}, u32[]{:S(2)}) async-start(f32[8,8,128]{2,1,0:T(8,128)} %get-tuple-element.25), calls=%async_computation | async-start | bytes 65536 | tf_op jit(solution)/shard_map/all_to_all | solution.py:909
  8.3 4.9 %copy-start.2 = (f32[3,16,16,128]{3,2,1,0:T(8,128)S(1)}, f32[3,16,16,128]{3,2,1,0:T(8,128)}, u32[]{:S(2)}) copy-start(f32[3,16,16,128]{3,2,1,0:T(8,128)} %param.13) | copy-start | bytes 1179652
  8.5 4.6 %copy-start.1 = (f32[2,16,16,128]{3,2,1,0:T(8,128)S(1)}, f32[2,16,16,128]{3,2,1,0:T(8,128)}, u32[]{:S(2)}) copy-start(f32[2,16,16,128]{3,2,1,0:T(8,128)} %param.14) | copy-start | bytes 786436
  8.5 4.6 %collective-permute-start = (f32[56,128]{1,0:T(8,128)S(1)}, f32[56,128]{1,0:T(8,128)S(1)}, u32[]{:S(2)}, u32[]{:S(2)}) collective-permute-start(f32[56,128]{1,0:T(8,128)S(1)} %get-tuple-element.29), channel_id=1, source_target_pairs={{0,1},{1,2},{2,3},{3,4},{4,5},{5,6},{6,7},{7,0},{8,9},{9,10},{10,1... | collective-permute-start | bytes 86024 | tf_op jit(solution)/shard_map/ppermute | solution.py:931
  9.1 4.1 %collective-permute-start.1 = (f32[56,128]{1,0:T(8,128)S(1)}, f32[56,128]{1,0:T(8,128)S(1)}, u32[]{:S(2)}, u32[]{:S(2)}) collective-permute-start(f32[56,128]{1,0:T(8,128)S(1)} %get-tuple-element.30.after_ref), channel_id=1, source_target_pairs={{1,0},{2,1},{3,2},{4,3},{5,4},{6,5},{7,6},{0,7},{9,8},{10,9},{11,1... | collective-permute-start | bytes 86024 | tf_op jit(solution)/shard_map/ppermute | solution.py:932
  11.3 1.8 %copy-start.6 = (f32[16,128]{1,0:T(8,128)S(1)}, f32[16,128]{1,0:T(8,128)}, u32[]{:S(2)}) copy-start(f32[16,128]{1,0:T(8,128)} %jac_ref.1) | copy-start | bytes 24580
  11.3 1.8 %copy-start.7 = (f32[16,128]{1,0:T(8,128)S(1)}, f32[16,128]{1,0:T(8,128)}, u32[]{:S(2)}) copy-start(f32[16,128]{1,0:T(8,128)} %land_ref.1) | copy-start | bytes 24580
  13.6 7.4 %collective-permute-start.2 = (f32[144,128]{1,0:T(8,128)S(1)}, f32[144,128]{1,0:T(8,128)S(1)}, u32[]{:S(2)}, u32[]{:S(2)}) collective-permute-start(f32[144,128]{1,0:T(8,128)S(1)} %get-tuple-element.34), channel_id=1, source_target_pairs={{0,8},{8,16},{16,24},{24,0},{1,9},{9,17},{17,25},{25,1},{2,10},{10... | collective-permute-start | bytes 221192 | tf_op jit(solution)/shard_map/ppermute | solution.py:952
  15.3 6.3 %collective-permute-start.3 = (f32[144,128]{1,0:T(8,128)S(1)}, f32[144,128]{1,0:T(8,128)S(1)}, u32[]{:S(2)}, u32[]{:S(2)}) collective-permute-start(f32[144,128]{1,0:T(8,128)S(1)} %get-tuple-element.35), channel_id=1, source_target_pairs={{8,0},{16,8},{24,16},{0,24},{9,1},{17,9},{25,17},{1,25},{10,2},{18... | collective-permute-start | bytes 221192 | tf_op jit(solution)/shard_map/ppermute | solution.py:953
  23.3 8.3 %all-to-all-start.1 = ((f32[8,16,128]{2,1,0:T(8,128)}), f32[8,16,128]{2,1,0:T(8,128)S(1)}, u32[]{:S(2)}, u32[]{:S(2)}) async-start(f32[8,16,128]{2,1,0:T(8,128)} %get-tuple-element.37), calls=%async_computation.1 | async-start | bytes 131072 | tf_op jit(solution)/shard_map/all_to_all | solution.py:972
  26.7 3.0 %copy-start.8 = (f32[2048]{0:T(1024)S(1)}, f32[2048]{0:T(1024)}, u32[]{:S(2)}) copy-start(f32[2048]{0:T(1024)} %param.22) | copy-start | bytes 24580

commit v8 on v7

--- a/solution.py
+++ b/solution.py
@@ -129,12 +129,15 @@
     return x // ROWS, LANES // 2 * (x % 2) + ROWS * group + 2 * (x % ROWS // 2)
 
 
-def all_edges(geo, ref, planes, x_points):
+def all_edges(geo, ref, planes, x_points, ends_ref=None):
     packs = [jnp.zeros((ROWS, LANES), jnp.float32) for _ in range(2)]
     for x in range(x_points):
+        rows, first = ref, planes * x
+        if ends_ref is not None and x in (0, x_points - 1):
+            rows, first = ends_ref, planes * (x // (x_points - 1))
         for group in range(planes // ROWS):
             q, at = edge_place(x, group)
-            tile = ref[planes * x + ROWS * group : planes * x + ROWS * (group + 1), :]
+            tile = rows[first + ROWS * group : first + ROWS * (group + 1), :]
             rolled = pltpu.roll(tile, (at + 1) % LANES, 1)
             packs[q] = jnp.where((geo.lane >> 1) == at // 2, rolled, packs[q])
     return packs
@@ -498,13 +501,15 @@
         mass = surf_ref[4 * ROWS * MASS + r : 4 * ROWS * MASS + r + 1, :]
         wind = time_step * mass * wind_ref[pl.ds(r, 2 * levels, stride=x_points), :]
         out_ref[0:planes, :] = line(r)
-        for first in range(0, planes, levels):
-            out_ref[planes + first : planes + first + levels, :] = (
-                wind[:levels] * slope[first : first + levels]
-            )
-        base = 2 * planes
-        out_ref[base : base + 2 * levels, :] = wind
-        base += 2 * levels
+        columns = [
+            wind[plane % levels : plane % levels + ROWS] * slope[plane : plane + ROWS]
+            for plane in range(0, planes, ROWS)
+        ] + [wind[level : level + ROWS] for level in range(0, 2 * levels, ROWS)]
+        pack = jnp.zeros((ROWS, LANES), jnp.float32)
+        for i, tile in enumerate(columns):
+            pack = jnp.where((geo.lane >> 1) == i, pltpu.roll(tile, 2 * i + 1, 1), pack)
+        out_ref[planes : planes + ROWS, :] = pack
+        base = planes + ROWS
         for number in range(SURF_ARRAYS):
             out_ref[base + 2 * number : base + 2 * number + 2, :] = surf_line(number, r)
         base += 2 * SURF_ARRAYS
@@ -526,6 +531,7 @@
     inverse_ref,
     flux_ref,
     edges_ref,
+    ends_ref,
     semaphores,
 ):
     geo = Geometry()
@@ -533,7 +539,7 @@
     left, right = neighbours_of(blocks)
     x_points = final_ref.shape[0]
     levels = wind_ref.shape[0] // (2 * x_points)
-    base = low_ref.shape[0] - 2 * SURF_ARRAYS - 4
+    base = planes + ROWS
 
     def surf_tile(number, tile, h):
         at = 4 * ROWS * number + 2 * ROWS * tile + ROWS * h
@@ -607,13 +613,16 @@
     def put(x, plane, value):
         sums_ref[planes * x + plane : planes * x + plane + ROWS, :] = value
 
+    def column(ref, number):
+        return pltpu.roll(ref[planes : planes + ROWS, :], (-(2 * number + 1)) % LANES, 1)
+
     def beyond(ref, plane, field, slope, own_coef):
-        wind_at = 2 * planes + plane % levels
+        wind_at = (planes + plane % levels) // ROWS
         return (
             beside(ref, MASS, 0) * field
-            - ref[planes + plane : planes + plane + ROWS, :]
-            - ref[wind_at : wind_at + ROWS, :] * (own_coef * field)
-            - ref[wind_at + levels : wind_at + levels + ROWS, :] * slope
+            - column(ref, plane // ROWS)
+            - column(ref, wind_at) * (own_coef * field)
+            - column(ref, wind_at + levels // ROWS) * slope
         )
 
     def row_of(tiles, x):
@@ -650,8 +659,10 @@
                         mass[i] * (fields[i] - (wind[0][i] * slope + wind[1][i] * slopes[i]))
                     )
                 if first == 0:
-                    before = beyond(low_ref, plane, fields[0], slopes[0], deriv_table[3][3])
-                    put(first, plane, before + moved[0])
+                    put(first, plane, moved[0])
+                    ends_ref[plane : plane + ROWS, :] = moved[0] + beyond(
+                        low_ref, plane, fields[0], slopes[0], deriv_table[3][3]
+                    )
                 else:
                     shared = held[plane] + moved[0]
                     put(first - 1, plane, shared)
@@ -660,11 +671,12 @@
                     put(lines[i], plane, moved[i])
                 held[plane] = moved[-1]
                 if last == x_points - 1:
-                    after = beyond(
+                    put(last, plane, moved[-1])
+                    at = planes + plane
+                    ends_ref[at : at + ROWS, :] = moved[-1] + beyond(
                         high_ref, plane, fields[-1], slopes[-1], deriv_table[0][0]
                     )
-                    put(last, plane, held[plane] + after)
-    packs = all_edges(geo, sums_ref, planes, x_points)
+    packs = all_edges(geo, sums_ref, planes, x_points, ends_ref)
     to_right, to_left = split_sides(geo, packs[0], packs[1], 1)
     for i, (to, edges) in enumerate(((right, to_right), (left, to_left))):
         edges_ref[i] = edges
@@ -680,9 +692,17 @@
         copy.wait()
 
 
+def rows_kernel(sums_ref, down_ref, up_ref):
+    planes = down_ref.shape[0]
+    down_ref[...] = sums_ref[:planes, :]
+    up_ref[...] = sums_ref[sums_ref.shape[0] - planes :, :]
+
+
 def end_kernel(
     planes,
     sums_ref,
+    low_ref,
+    high_ref,
     recv_ref,
     final_ref,
     inverse_ref,
@@ -715,9 +735,14 @@
         inverse = spread(inverse_ref[x : x + 1, :])
         for group in range(planes // ROWS):
             at = planes * x + ROWS * group
+            half = slice(ROWS * group, ROWS * (group + 1))
+            total = sums_ref[at : at + ROWS, :]
+            if x == 0:
+                total = total + low_ref[half, :]
+            elif x == x_points - 1:
+                total = total + high_ref[half, :]
             air_out[pl.ds(ROWS * group * x_points + x, ROWS, stride=x_points), :] = (
-                inverse
-                * geo.sum_y(sums_ref[at : at + ROWS, :], outer_edges(joined, x, group))
+                inverse * geo.sum_y(total, outer_edges(joined, x, group))
             )
     air_out[0:x_points, :] = final_ref[...]
 
@@ -735,8 +760,37 @@
     return totals
 
 
+def multiplied(ids, coefs, halves_ref, sources, groups):
+    lane_at = iota((LANES, LANES), 0)
+    hot = jnp.concatenate(
+        [
+            jnp.where(lane_at == (ids[edge : edge + 1] & (LANES - 1)), 1.0, 0.0).astype(
+                jnp.bfloat16
+            )
+            for edge in range(2)
+        ],
+        axis=1,
+    )
+    picked = jnp.dot(
+        halves_ref[...],
+        jnp.concatenate([hot, hot], axis=0),
+        preferred_element_type=jnp.float32,
+    )
+    totals = [jnp.zeros((ROWS, LANES), jnp.float32) for _ in range(groups)]
+    for edge in range(2):
+        high = spread(ids[edge : edge + 1]) >> 7
+        coef = spread(coefs[edge : edge + 1])
+        side = slice(LANES * edge, LANES * (edge + 1))
+        for s in range(sources):
+            scaled = jnp.where(high == s, coef, 0.0)
+            for group in range(groups):
+                at = ROWS * (groups * s + group)
+                totals[group] += scaled * picked[at : at + ROWS, side]
+    return totals
+
+
 def ocean_kernel(
-    levels, start, tracers_ref, coef_ref, near_ref, rate_ref, after_ref, out_ref
+    levels, start, tracers_ref, coef_ref, near_ref, rate_ref, after_ref, out_ref, halves_ref
 ):
     chunks = tracers_ref.shape[1] // LANES
     groups = tracers_ref.shape[0] // ROWS
@@ -746,13 +800,28 @@
         return tracers_ref[
             ROWS * group : ROWS * (group + 1), LANES * s : LANES * (s + 1)
         ]
+
+    planes = tracers_ref.shape[0]
+    for s in range(chunks):
+        values = tracers_ref[:, LANES * s : LANES * (s + 1)]
+        upper = values.astype(jnp.bfloat16)
+        at = slice(planes * s, planes * (s + 1))
+        halves_ref[at, :LANES] = upper
+        halves_ref[at, LANES:] = (values - upper.astype(jnp.float32)).astype(jnp.bfloat16)
+    edges = near_ref.shape[0]
 
     def one_chunk(number, carry):
         k = number + start
         at = pl.ds(pl.multiple_of(k * LANES, LANES), LANES)
         out_at = pl.ds(pl.multiple_of(number * LANES, LANES), LANES)
         ids, coefs = near_ref[:, at], coef_ref[:, at]
-        totals = gathered(ids, coefs, source, chunks, groups)
+        by_gather = edges - edges // 3 * 2
+        totals = gathered(ids[:by_gather], coefs[:by_gather], source, chunks, groups)
+        for edge in range(by_gather, edges, 2):
+            more = multiplied(
+                ids[edge : edge + 2], coefs[edge : edge + 2], halves_ref, chunks, groups
+            )
+            totals = [total + part for total, part in zip(totals, more)]
         coef_sum = spread(jnp.sum(coefs, axis=0, keepdims=True))
         rate = spread(rate_ref[pl.ds(k, 1), :])
         tiles = [tracers_ref[ROWS * g : ROWS * (g + 1), at] for g in range(groups)]
@@ -910,14 +979,15 @@
 
     chunks = cells // LANES
     reads_per_chunk = edge_coef.shape[0] * chunks * (ocean_planes // ROWS)
-    starts = (0, chunks * 3 // 16, chunks * 10 // 16)
+    starts = (0, chunks * 3 // 16, chunks * 11 // 16)
 
     def ocean_part(start, end, after):
         (result,) = call(
             functools.partial(ocean_kernel, ocean_levels, start),
             [(ocean_planes, (end - start) * LANES)],
             [VMEM_SPEC] * 4 + [ANY_SPEC],
-            cost=(end - start) * reads_per_chunk * ROWS * LANES * 4,
+            [pltpu.VMEM((chunks * ocean_planes, 2 * LANES), jnp.bfloat16)],
+            cost=(end - start) * reads_per_chunk * ROWS * LANES * 2,
         )(ocean, edge_coef, neighbours, rate, after)
         return result
 
@@ -931,7 +1001,7 @@
     before = lax.ppermute(to_after, "blk", onward)
     after = lax.ppermute(to_before, "blk", [(to, source) for source, to in onward])
     first_part = ocean_part(starts[0], starts[1], to_before)
-    side_rows = 2 * planes + 2 * levels + 2 * SURF_ARRAYS + 4
+    side_rows = planes + ROWS + 2 * SURF_ARRAYS + 4
     avg, down, up, surf = call(
         functools.partial(panel_kernel, planes),
         [air.shape, (side_rows, LANES), (side_rows, LANES), (4 * ROWS * SURF_ARRAYS, LANES)],
@@ -965,12 +1035,16 @@
         [
             pltpu.VMEM((blocks, HEAD, LANES), jnp.float32),
             pltpu.VMEM((2, ROWS, LANES), jnp.float32),
+            pltpu.VMEM((2 * planes, LANES), jnp.float32),
             pltpu.SemaphoreType.DMA((3,)),
         ],
         hbm_out=True,
     )(avg, surf, low, high, wind, point_ids, second_part)
     arrived = lax.all_to_all(slab, "blk", split_axis=0, concat_axis=0, tiled=True)
-    third_part = ocean_part(starts[2], chunks, final)
+    down, up = call(rows_kernel, [(planes, LANES)] * 2, [VMEM_SPEC])(sums)
+    low = lax.ppermute(up, "face", after_me)
+    high = lax.ppermute(down, "face", [(to, source) for source, to in after_me])
+    third_part = ocean_part(starts[2], chunks, down)
     partial, gain = call(
         functools.partial(rim_kernel, starts),
         [ocean.shape, area.shape],
@@ -980,8 +1054,8 @@
     air_final, ocean_final = call(
         functools.partial(end_kernel, planes),
         [air.shape, ocean.shape],
-        [VMEM_SPEC] * 8,
-    )(sums, arrived, final, inverse, cell_ids, weights, gain, partial)
+        [VMEM_SPEC] * 10,
+    )(sums, low, high, arrived, final, inverse, cell_ids, weights, gain, partial)
     return air_final.reshape(air_state.shape), ocean_final.reshape(tracers.shape)
 
 

time: 33.1 us -> 34.2 us (1.033)
  starting transfers between devices: 15.3 us -> 19.5 us
  Pallas kernels: 15 us -> 12.7 us
  waiting for transfers between devices: 1.6 us -> 0.75 us
    ppermute x1 -> x2, starting transfers between devices: 2.25 us -> 5.56 us  [body(): high = lax.ppermute(down, 'face', [(to, source) for source, to in after_me])]
    pallas_call x3, Pallas kernels: 7.98 us -> 5.64 us  [ocean_part(): call(functools.partial(ocean_kernel, ocean_levels, start), [(ocean_planes...]
    all_to_all x1, waiting for transfers between devices: 0.74 us -> 0.01 us  [body(): lax.all_to_all(slab, 'blk', split_axis=0, concat_axis=0, tiled=True)]
    ppermute x1 -> x2, starting transfers between devices: 1.63 us -> 2.2 us  [body(): low = lax.ppermute(up, 'face', after_me)]
    ppermute x1 -> x2, waiting for transfers between devices: 0.57 us -> 0.01 us  [body(): high = lax.ppermute(down, 'face', [(to, source) for source, to in after_me])]
    all_to_all x1, waiting for transfers between devices: 0.29 us -> 0.73 us  [body(): recv = lax.all_to_all(slab, 'blk', split_axis=0, concat_axis=0, tiled=True)]
  transfers between devices with their start and end apart: 6 -> 8, of which waited for: 3 -> 1; matrix products, arithmetic and copies ran while one was open for 0% -> 0% of each run, Pallas kernels for 29% -> 21%
where the time goes in v8:
time: 34.2 us; the launch traced here: 33.9 us
  starting transfers between devices  19.5 us (57%)
  Pallas kernels  12.7 us (37%)
  between operations  0.84 us (2%)
  waiting for transfers between devices  0.75 us (2%)
    pallas_call x3, Pallas kernels, ocean_part(): call(functools.partial(ocean_kernel, ocean_levels, start), [(ocean_planes...  5.64 us
    ppermute x2, starting transfers between devices, body(): high = lax.ppermute(down, 'face', [(to, source) for source, to in after_me])  5.56 us
    all_to_all x1, starting transfers between devices, body(): recv = lax.all_to_all(slab, 'blk', split_axis=0, concat_axis=0, tiled=True)  5.31 us
    all_to_all x1, starting transfers between devices, body(): lax.all_to_all(slab, 'blk', split_axis=0, concat_axis=0, tiled=True)  3.68 us
    pallas_call x1, Pallas kernels, body(): call(functools.partial(start_kernel, planes), [(blocks, HEAD, LANES), air...  2.27 us
    ppermute x1, starting transfers between devices, body(): lax.ppermute(to_before, 'blk', [(to, source) for source, to in onward])  2.24 us
    ppermute x2, starting transfers between devices, body(): low = lax.ppermute(up, 'face', after_me)  2.2 us
    pallas_call x1, Pallas kernels, body(): call(functools.partial(second_kernel, planes), [(blocks, EDGE_AT + ROWS,...  1.77 us
  transfers between devices with their start and end apart: 8, of which 1 were waited for; matrix products, arithmetic and copies ran while one was open for 0% of the time, Pallas kernels for 21%

profile of v8, /device:TPU:0, one launch (start us, length us, event | category | flops | bytes accessed | tf_op | source)
XLA Modules:
  0.0 33.9 jit_solution(1483628870489830947)
XLA Ops:
  0.6 0.0 copy-start
  0.6 2.3 %start_kernel.1 = (f32[8,8,128]{2,1,0:T(8,128)}, f32[768,128]{1,0:T(8,128)S(1)}, f32[24,128]{1,0:T(8,128)S(1)}, f32[24,128]{1,0:T(8,128)S(1)}, s32[8,128]{1,0:T(...) custom-call(s32[8,128]{1,0:T(8,128)} %bitcast.24, f32[8,128]{1,0:T(8,128)} %bitcast.25, ...), custom_call_target="tpu_custom_call" | custom-call | tf_op jit(solution)/shard_map/start_kernel/pallas_call | solution.py:958
  2.9 0.0 copy-start.3
  2.9 0.0 copy-start.4
  2.9 0.0 copy-start.5
  3.0 5.3 %all-to-all-start = ((f32[8,8,128]{2,1,0:T(8,128)}), f32[8,8,128]{2,1,0:T(8,128)S(1)}, u32[]{:S(2)}, u32[]{:S(2)}) async-start(f32[8,8,128]{2,1,0:T(8,128)} %get-tuple-element.27), calls=%async_computation | async-start | bytes 65536 | tf_op jit(solution)/shard_map/all_to_all | solution.py:978
  8.3 0.0 copy-start.2
  8.3 0.0 copy-done
  8.3 0.2 send_kernel.1
  8.5 0.0 copy-start.1
  8.5 0.5 %collective-permute-start = (f32[56,128]{1,0:T(8,128)S(1)}, f32[56,128]{1,0:T(8,128)S(1)}, u32[]{:S(2)}, u32[]{:S(2)}) collective-permute-start(f32[56,128]{1,0:T(8,128)S(1)} %get-tuple-element.31), channel_id=1, source_target_pairs={{0,1},{1,2},{2,3},{3,4},{4,5},{5,6},{6,7},{7,0},{8,9},{9,10},{10,1... | collective-permute-start | bytes 86024 | tf_op jit(solution)/shard_map/ppermute | solution.py:1001
  9.1 2.2 %collective-permute-start.1 = (f32[56,128]{1,0:T(8,128)S(1)}, f32[56,128]{1,0:T(8,128)S(1)}, u32[]{:S(2)}, u32[]{:S(2)}) collective-permute-start(f32[56,128]{1,0:T(8,128)S(1)} %get-tuple-element.32.after_ref), channel_id=1, source_target_pairs={{1,0},{2,1},{3,2},{4,3},{5,4},{6,5},{7,6},{0,7},{9,8},{10,9},{11,1... | collective-permute-start | bytes 86024 | tf_op jit(solution)/shard_map/ppermute | solution.py:1002
  11.3 0.0 copy-done.3
  11.3 0.0 copy-done.4
  11.3 0.0 copy-done.5
  11.3 0.0 copy-start.6
  11.3 0.0 copy-start.7
  11.3 1.1 %ocean_kernel.3.ocean_ref.refs_0_ = f32[32,384]{1,0:T(8,128)S(1)} custom-call(f32[32,2048]{1,0:T(8,128)S(1)} %bitcast.12, f32[6,2048]{1,0:T(8,128)S(1)} %copy-done.3, s32[6,2048]{1,0:T(8,128)S(1)} %copy-done.4, f32[16,128]{1,0:T(8,128)S(1)} %bitcast.20, f32[56,128]{1,0:T(8,128)S(1)} %get-tuple-element.32.after_ref), custom_call_target="tpu_custom_call" | custom-call | bytes 2359296 | tf_op jit(solution)/shard_map/ocean_kernel/pallas_call | solution.py:985
  12.4 0.7 %all-to-all-done.recv_ref = f32[8,8,128]{2,1,0:T(8,128)S(1)} async-done(((f32[8,8,128]{2,1,0:T(8,128)}), f32[8,8,128]{2,1,0:T(8,128)S(1)}, u32[]{:S(2)}, u32[]{:S(2)}) %all-to-all-start) | async-done | bytes 32800 | tf_op jit(solution)/shard_map/all_to_all | solution.py:978
  13.1 0.0 collective-permute-done.before_ref
  13.1 0.0 collective-permute-done.1.after_ref
  13.1 0.0 copy-done.2
  13.1 0.0 copy-done.1
  13.1 0.0 copy-done.6
  13.1 0.0 copy-done.7
  13.2 0.5 %panel_kernel.1 = (f32[768,128]{1,0:T(8,128)S(1)}, f32[72,128]{1,0:T(8,128)S(1)}, f32[72,128]{1,0:T(8,128)S(1)}, f32[192,128]{1,0:T(8,128)S(1)}) custom-call(f32[768,128]{1,0:T(8,128)S(1)} %get-tuple-element.26.moved_ref, f32[8,8,128]{2,1,0:T(8,128)S(1)} %all-to-all-done.recv_ref, f32[56,128]{1,0:T(8,128)S(1)} %collective-permute-done.before_ref, ...), custom_call_target="tpu_custom_call" | custom-call | tf_op jit(solution)/shard_map/panel_kernel/pallas_call | solution.py:1005
  13.6 1.6 %collective-permute-start.2 = (f32[72,128]{1,0:T(8,128)S(1)}, f32[72,128]{1,0:T(8,128)S(1)}, u32[]{:S(2)}, u32[]{:S(2)}) collective-permute-start(f32[72,128]{1,0:T(8,128)S(1)} %get-tuple-element.36), channel_id=1, source_target_pairs={{0,8},{8,16},{16,24},{24,0},{1,9},{9,17},{17,25},{25,1},{2,10},{10... | collective-permute-start | bytes 110600 | tf_op jit(solution)/shard_map/ppermute | solution.py:1022
  15.3 2.2 %collective-permute-start.3 = (f32[72,128]{1,0:T(8,128)S(1)}, f32[72,128]{1,0:T(8,128)S(1)}, u32[]{:S(2)}, u32[]{:S(2)}) collective-permute-start(f32[72,128]{1,0:T(8,128)S(1)} %get-tuple-element.37), channel_id=1, source_target_pairs={{8,0},{16,8},{24,16},{0,24},{9,1},{17,9},{25,17},{1,25},{10,2},{18... | collective-permute-start | bytes 110600 | tf_op jit(solution)/shard_map/ppermute | solution.py:1023
  17.5 2.8 %ocean_kernel.4.ocean_ref.refs_1_ = f32[32,1024]{1,0:T(8,128)S(1)} custom-call(f32[32,2048]{1,0:T(8,128)S(1)} %bitcast.13, f32[6,2048]{1,0:T(8,128)S(1)} %copy-done.3, s32[6,2048]{1,0:T(8,128)S(1)} %copy-done.4, f32[16,128]{1,0:T(8,128)S(1)} %bitcast.21, f32[192,128]{1,0:T(8,128)S(1)} %get-tuple-element.35.after_ref.surf_ref), custom_call_target="tpu_custom_call" | custom-call | bytes 6291456 | tf_op jit(solution)/shard_map/ocean_kernel/pallas_call | solution.py:985
  20.3 0.0 collective-permute-done.2.low_ref
  20.3 0.0 collective-permute-done.3.high_ref
  20.4 1.8 %second_kernel.1 = (f32[8,16,128]{2,1,0:T(8,128)}, f32[768,128]{1,0:T(8,128)S(1)}, f32[16,128]{1,0:T(8,128)S(1)}, f32[16,128]{1,0:T(8,128)S(1)}) custom-call(f32[768,128]{1,0:T(8,128)S(1)} %get-tuple-element.34.avg_ref, f32[192,128]{1,0:T(8,128)S(1)} %get-tuple-element.35.after_ref.surf_ref, f32[72,128]{1,0:T(8,128)S(1)} %collective-permute-done.2.low_ref, ...), custom_call_target="tpu_custom_call" | custom-call | tf_op jit(solution)/shard_map/second_kernel/pallas_call | solution.py:1026
  22.1 3.7 %all-to-all-start.1 = ((f32[8,16,128]{2,1,0:T(8,128)}), f32[8,16,128]{2,1,0:T(8,128)S(1)}, u32[]{:S(2)}, u32[]{:S(2)}) async-start(f32[8,16,128]{2,1,0:T(8,128)} %get-tuple-element.41), calls=%async_computation.1 | async-start | bytes 131072 | tf_op jit(solution)/shard_map/all_to_all | solution.py:1043
  25.8 0.6 %collective-permute-start.4 = (f32[48,128]{1,0:T(8,128)S(1)}, f32[48,128]{1,0:T(8,128)S(1)}, u32[]{:S(2)}, u32[]{:S(2)}) collective-permute-start(f32[48,128]{1,0:T(8,128)S(1)} %get-tuple-element.39), channel_id=1, source_target_pairs={{0,8},{8,16},{16,24},{24,0},{1,9},{9,17},{17,25},{25,1},{2,10},{10... | collective-permute-start | bytes 73736 | tf_op jit(solution)/shard_map/ppermute | solution.py:1045
  26.4 0.0 copy-start.8
  26.4 3.3 %collective-permute-start.5 = (f32[48,128]{1,0:T(8,128)S(1)}, f32[48,128]{1,0:T(8,128)S(1)}, u32[]{:S(2)}, u32[]{:S(2)}) collective-permute-start(f32[48,128]{1,0:T(8,128)S(1)} %get-tuple-element.40.after_ref), channel_id=1, source_target_pairs={{8,0},{16,8},{24,16},{0,24},{9,1},{17,9},{25,17},{1,25},{10,2},{18... | collective-permute-start | bytes 73736 | tf_op jit(solution)/shard_map/ppermute | solution.py:1046
  29.7 1.8 %ocean_kernel.5.refs_2_ = f32[32,640]{1,0:T(8,128)S(1)} custom-call(f32[32,2048]{1,0:T(8,128)S(1)} %bitcast.14, f32[6,2048]{1,0:T(8,128)S(1)} %copy-done.3, s32[6,2048]{1,0:T(8,128)S(1)} %copy-done.4, f32[16,128]{1,0:T(8,128)S(1)} %bitcast.22, f32[48,128]{1,0:T(8,128)S(1)} %get-tuple-element.40.after_ref), custom_call_target="tpu_custom_call" | custom-call | bytes 3932160 | tf_op jit(solution)/shard_map/ocean_kernel/pallas_call | solution.py:985
  31.5 0.0 copy-done.8
  31.5 1.2 %rim_kernel.1 = (f32[32,2048]{1,0:T(8,128)S(1)}, f32[16,128]{1,0:T(8,128)S(1)}) custom-call(f32[56,128]{1,0:T(8,128)S(1)} %collective-permute-done.before_ref, f32[56,128]{1,0:T(8,128)S(1)} %collective-permute-done.1.after_ref, f32[6,2048]{1,0:T(8,128)S(1)} %copy-done.3, s32[6,2048]{1,0:T(8,128)S(1)} %copy-done.4, f32[16,128]{1,0:T(8,128)S(1)} %bitcast.23, ...), custom_call_target="tpu_custom_call" | custom-call | bytes 3145728 | tf_op jit(solution)/shard_map/rim_kernel/pallas_call | solution.py:1048
  32.7 0.0 collective-permute-done.4.low_ref
  32.7 0.0 collective-permute-done.5.high_ref
  32.7 0.0 all-to-all-done.1.recv_ref
  32.7 1.2 %end_kernel.1 = (f32[768,128]{1,0:T(8,128)}, f32[32,2048]{1,0:T(8,128)}) custom-call(f32[768,128]{1,0:T(8,128)S(1)} %get-tuple-element.38.sums_ref, f32[48,128]{1,0:T(8,128)S(1)} %collective-permute-done.4.low_ref, f32[48,128]{1,0:T(8,128)S(1)} %collective-permute-done.5.high_ref, f32[8,16,128]{2,1,0:T(8,128)S(1)} %all-to-all-done.1.recv_ref, ...), custom_call_target="tpu_custom_call" | custom-call | tf_op jit(solution)/shard_map/end_kernel/pallas_call | solution.py:1054
  (1 shorter events, 0.0 us)
Async XLA Ops:
  0.6 7.6 %copy-start = (f32[2,16,2048]{2,1,0:T(8,128)S(1)}, f32[2,16,2048]{2,1,0:T(8,128)}, u32[]{:S(2)}) copy-start(f32[2,16,2048]{2,1,0:T(8,128)} %param.18) | copy-start | bytes 786436
  2.9 8.4 %copy-start.3 = (f32[6,2048]{1,0:T(8,128)S(1)}, f32[6,2048]{1,0:T(8,128)}, u32[]{:S(2)}) copy-start(f32[6,2048]{1,0:T(8,128)} %coef_ref.7) | copy-start | bytes 147460
  2.9 8.4 %copy-start.4 = (s32[6,2048]{1,0:T(8,128)S(1)}, s32[6,2048]{1,0:T(8,128)}, u32[]{:S(2)}) copy-start(s32[6,2048]{1,0:T(8,128)} %near_ref.7) | copy-start | bytes 147460
  2.9 8.4 %copy-start.5 = (f32[2048]{0:T(1024)S(1)}, f32[2048]{0:T(1024)}, u32[]{:S(2)}) copy-start(f32[2048]{0:T(1024)} %param.21) | copy-start | bytes 24580
  3.0 10.2 %all-to-all-start = ((f32[8,8,128]{2,1,0:T(8,128)}), f32[8,8,128]{2,1,0:T(8,128)S(1)}, u32[]{:S(2)}, u32[]{:S(2)}) async-start(f32[8,8,128]{2,1,0:T(8,128)} %get-tuple-element.27), calls=%async_computation | async-start | bytes 65536 | tf_op jit(solution)/shard_map/all_to_all | solution.py:978
  8.3 4.9 %copy-start.2 = (f32[3,16,16,128]{3,2,1,0:T(8,128)S(1)}, f32[3,16,16,128]{3,2,1,0:T(8,128)}, u32[]{:S(2)}) copy-start(f32[3,16,16,128]{3,2,1,0:T(8,128)} %param.13) | copy-start | bytes 1179652
  8.5 4.6 %copy-start.1 = (f32[2,16,16,128]{3,2,1,0:T(8,128)S(1)}, f32[2,16,16,128]{3,2,1,0:T(8,128)}, u32[]{:S(2)}) copy-start(f32[2,16,16,128]{3,2,1,0:T(8,128)} %param.14) | copy-start | bytes 786436
  8.5 4.6 %collective-permute-start = (f32[56,128]{1,0:T(8,128)S(1)}, f32[56,128]{1,0:T(8,128)S(1)}, u32[]{:S(2)}, u32[]{:S(2)}) collective-permute-start(f32[56,128]{1,0:T(8,128)S(1)} %get-tuple-element.31), channel_id=1, source_target_pairs={{0,1},{1,2},{2,3},{3,4},{4,5},{5,6},{6,7},{7,0},{8,9},{9,10},{10,1... | collective-permute-start | bytes 86024 | tf_op jit(solution)/shard_map/ppermute | solution.py:1001
  9.1 4.1 %collective-permute-start.1 = (f32[56,128]{1,0:T(8,128)S(1)}, f32[56,128]{1,0:T(8,128)S(1)}, u32[]{:S(2)}, u32[]{:S(2)}) collective-permute-start(f32[56,128]{1,0:T(8,128)S(1)} %get-tuple-element.32.after_ref), channel_id=1, source_target_pairs={{1,0},{2,1},{3,2},{4,3},{5,4},{6,5},{7,6},{0,7},{9,8},{10,9},{11,1... | collective-permute-start | bytes 86024 | tf_op jit(solution)/shard_map/ppermute | solution.py:1002
  11.3 1.8 %copy-start.6 = (f32[16,128]{1,0:T(8,128)S(1)}, f32[16,128]{1,0:T(8,128)}, u32[]{:S(2)}) copy-start(f32[16,128]{1,0:T(8,128)} %jac_ref.1) | copy-start | bytes 24580
  11.3 1.8 %copy-start.7 = (f32[16,128]{1,0:T(8,128)S(1)}, f32[16,128]{1,0:T(8,128)}, u32[]{:S(2)}) copy-start(f32[16,128]{1,0:T(8,128)} %land_ref.1) | copy-start | bytes 24580
  13.6 6.7 %collective-permute-start.2 = (f32[72,128]{1,0:T(8,128)S(1)}, f32[72,128]{1,0:T(8,128)S(1)}, u32[]{:S(2)}, u32[]{:S(2)}) collective-permute-start(f32[72,128]{1,0:T(8,128)S(1)} %get-tuple-element.36), channel_id=1, source_target_pairs={{0,8},{8,16},{16,24},{24,0},{1,9},{9,17},{17,25},{25,1},{2,10},{10... | collective-permute-start | bytes 110600 | tf_op jit(solution)/shard_map/ppermute | solution.py:1022
  15.3 5.1 %collective-permute-start.3 = (f32[72,128]{1,0:T(8,128)S(1)}, f32[72,128]{1,0:T(8,128)S(1)}, u32[]{:S(2)}, u32[]{:S(2)}) collective-permute-start(f32[72,128]{1,0:T(8,128)S(1)} %get-tuple-element.37), channel_id=1, source_target_pairs={{8,0},{16,8},{24,16},{0,24},{9,1},{17,9},{25,17},{1,25},{10,2},{18... | collective-permute-start | bytes 110600 | tf_op jit(solution)/shard_map/ppermute | solution.py:1023
  22.1 10.6 %all-to-all-start.1 = ((f32[8,16,128]{2,1,0:T(8,128)}), f32[8,16,128]{2,1,0:T(8,128)S(1)}, u32[]{:S(2)}, u32[]{:S(2)}) async-start(f32[8,16,128]{2,1,0:T(8,128)} %get-tuple-element.41), calls=%async_computation.1 | async-start | bytes 131072 | tf_op jit(solution)/shard_map/all_to_all | solution.py:1043
  25.8 6.9 %collective-permute-start.4 = (f32[48,128]{1,0:T(8,128)S(1)}, f32[48,128]{1,0:T(8,128)S(1)}, u32[]{:S(2)}, u32[]{:S(2)}) collective-permute-start(f32[48,128]{1,0:T(8,128)S(1)} %get-tuple-element.39), channel_id=1, source_target_pairs={{0,8},{8,16},{16,24},{24,0},{1,9},{9,17},{17,25},{25,1},{2,10},{10... | collective-permute-start | bytes 73736 | tf_op jit(solution)/shard_map/ppermute | solution.py:1045
  26.4 5.1 %copy-start.8 = (f32[2048]{0:T(1024)S(1)}, f32[2048]{0:T(1024)}, u32[]{:S(2)}) copy-start(f32[2048]{0:T(1024)} %param.22) | copy-start | bytes 24580
  26.4 6.3 %collective-permute-start.5 = (f32[48,128]{1,0:T(8,128)S(1)}, f32[48,128]{1,0:T(8,128)S(1)}, u32[]{:S(2)}, u32[]{:S(2)}) collective-permute-start(f32[48,128]{1,0:T(8,128)S(1)} %get-tuple-element.40.after_ref), channel_id=1, source_target_pairs={{8,0},{16,8},{24,16},{0,24},{9,1},{17,9},{25,17},{1,25},{10,2},{18... | collective-permute-start | bytes 73736 | tf_op jit(solution)/shard_map/ppermute | solution.py:1046

commit v9 on v8

--- a/solution.py
+++ b/solution.py
@@ -255,27 +255,32 @@
     air_ref,
     semaphores,
 ):
+    x_points = jac_ref.shape[0]
+    field_rows = wind_ref.shape[0] // 2
+    field_count = air_ref.shape[0] // field_rows
+    fields_at = [
+        slice(field_rows * field, field_rows * (field + 1)) for field in range(field_count)
+    ]
     copies = [
         pltpu.make_async_copy(source, target, semaphores.at[i])
         for i, (source, target) in enumerate(
-            (
+            [
                 (cols_in, cols_ref),
                 (tracers_in.at[:ROWS], tracers_ref),
                 (weights_in, weights_ref),
                 (rows_in, rows_ref),
-                (air_in, air_ref),
+                (jac_in, jac_ref),
                 (wind_in, wind_ref),
-                (jac_in, jac_ref),
                 (land_in, land_ref),
-                (send_in, send_ref),
-            )
+            ]
+            + [(air_in.at[at], air_ref.at[at]) for at in fields_at]
+            + [(send_in, send_ref)]
         )
     ]
     for copy in copies:
         copy.start()
     geo = Geometry()
     blocks = cols_ref.shape[0]
-    x_points = jac_ref.shape[0]
     levels = wind_ref.shape[0] // (2 * x_points)
     chunks = tracers_ref.shape[1] // LANES
     for copy in copies[:4]:
@@ -304,7 +309,7 @@
     for side_ref in (before_ref, after_ref):
         side_ref[SIDE_IDS : SIDE_IDS + blocks, :] = ids
 
-    for copy in copies[4:]:
+    for copy in copies[4:8]:
         copy.wait()
     strips = []
     for h in range(2):
@@ -329,28 +334,31 @@
     before_ref[SIDE_STRIP : SIDE_STRIP + ROWS, :] = to_left
 
     y_weight = jnp.where(geo.y_edge, 1.0 / 6.0, 5.0 / 6.0)
-    for element in range(x_points // GLL):
-        lines = [GLL * element + i for i in range(GLL)]
-        mass = [
-            (1.0 / 6.0 if i in (0, GLL - 1) else 5.0 / 6.0)
-            * y_weight
-            * spread(jac_ref[x : x + 1, :])
-            for i, x in enumerate(lines)
-        ]
-        for level in range(0, levels, ROWS):
-            wind = wind_tiles(wind_ref, x_points, level, lines)
-            for plane in range(level, planes, levels):
-                fields = [
+    for field in range(field_count):
+        if field:
+            copies[7 + field].wait()
+        for element in range(x_points // GLL):
+            lines = [GLL * element + i for i in range(GLL)]
+            mass = [
+                (1.0 / 6.0 if i in (0, GLL - 1) else 5.0 / 6.0)
+                * y_weight
+                * spread(jac_ref[x : x + 1, :])
+                for i, x in enumerate(lines)
+            ]
+            for level in range(0, levels, ROWS):
+                plane = levels * field + level
+                wind = wind_tiles(wind_ref, x_points, level, lines)
+                values = [
                     air_ref[pl.ds(plane * x_points + x, ROWS, stride=x_points), :]
                     for x in lines
                 ]
-                slopes = geo.d_y(*fields)
+                slopes = geo.d_y(*values)
                 for i, x in enumerate(lines):
-                    slope = sum(deriv_table[i][j] * fields[j] for j in range(GLL))
-                    moved = mass[i] * (
-                        fields[i] - (wind[0][i] * slope + wind[1][i] * slopes[i])
-                    )
-                    moved_ref[planes * x + plane : planes * x + plane + ROWS, :] = moved
+                    slope = sum(deriv_table[i][j] * values[j] for j in range(GLL))
+                    moved_ref[planes * x + plane : planes * x + plane + ROWS, :] = mass[
+                        i
+                    ] * (values[i] - (wind[0][i] * slope + wind[1][i] * slopes[i]))
+    copies[-1].wait()
     packs = all_edges(geo, moved_ref, planes, x_points)
     to_right, to_left = split_sides(geo, packs[0], packs[1], 1)
     after_ref[SIDE_EDGE : SIDE_EDGE + ROWS, :] = to_right
@@ -692,7 +700,7 @@
         copy.wait()
 
 
-def rows_kernel(sums_ref, down_ref, up_ref):
+def rows_kernel(sums_ref, ocean_ref, down_ref, up_ref):
     planes = down_ref.shape[0]
     down_ref[...] = sums_ref[:planes, :]
     up_ref[...] = sums_ref[sums_ref.shape[0] - planes :, :]
@@ -712,39 +720,56 @@
     ocean_ref,
     air_out,
     ocean_out,
+    air_ref,
+    first_ref,
+    semaphores,
 ):
     geo = Geometry()
     blocks = cols_ref.shape[0]
     left, right = neighbours_of(blocks)
     chunks = gain_ref.shape[0]
+    x_points = inverse_ref.shape[0]
+    copies = []
+
+    def send(source, target):
+        copies.append(
+            pltpu.make_async_copy(source, target, semaphores.at[len(copies)])
+        )
+        copies[-1].start()
+
+    send(ocean_ref.at[ROWS:], ocean_out.at[ROWS:])
     arrived = jnp.concatenate([recv_ref[c, 0:1, :] for c in range(blocks)], axis=0)
     (inflow,) = scatter_sum([weights_ref[...] * arrived], cols_ref[...], chunks)
     gain = inflow * gain_ref[...]
-    ocean_out[...] = ocean_ref[...]
+    first_ref[...] = ocean_ref[:ROWS, :]
     for k in range(chunks):
         at = slice(LANES * k, LANES * (k + 1))
-        ocean_out[0:1, at] = ocean_ref[0:1, at] + gain[k : k + 1]
-
-    x_points = inverse_ref.shape[0]
+        first_ref[0:1, at] = ocean_ref[0:1, at] + gain[k : k + 1]
+    send(first_ref, ocean_out.at[:ROWS])
+
     joined = join_edges(
         geo,
         recv_ref[left, EDGE_AT : EDGE_AT + ROWS, :],
         recv_ref[right, EDGE_AT : EDGE_AT + ROWS, :],
     )
-    for x in range(x_points):
-        inverse = spread(inverse_ref[x : x + 1, :])
-        for group in range(planes // ROWS):
+    for group in range(planes // ROWS):
+        half = slice(ROWS * group, ROWS * (group + 1))
+        for x in range(x_points):
             at = planes * x + ROWS * group
-            half = slice(ROWS * group, ROWS * (group + 1))
             total = sums_ref[at : at + ROWS, :]
             if x == 0:
                 total = total + low_ref[half, :]
             elif x == x_points - 1:
                 total = total + high_ref[half, :]
-            air_out[pl.ds(ROWS * group * x_points + x, ROWS, stride=x_points), :] = (
-                inverse * geo.sum_y(total, outer_edges(joined, x, group))
-            )
-    air_out[0:x_points, :] = final_ref[...]
+            air_ref[pl.ds(ROWS * group * x_points + x, ROWS, stride=x_points), :] = spread(
+                inverse_ref[x : x + 1, :]
+            ) * geo.sum_y(total, outer_edges(joined, x, group))
+        if group == 0:
+            air_ref[0:x_points, :] = final_ref[...]
+        rows = slice(ROWS * group * x_points, ROWS * (group + 1) * x_points)
+        send(air_ref.at[rows], air_out.at[rows])
+    for copy in copies:
+        copy.wait()
 
 
 def gathered(ids, coefs, source, sources, groups, first=0):
@@ -840,7 +865,15 @@
             )
         return carry
 
-    lax.fori_loop(0, out_ref.shape[1] // LANES, one_chunk, 0)
+    count = out_ref.shape[1] // LANES
+    step = 2 if count % 2 == 0 else 1
+
+    def some_chunks(number, carry):
+        for i in range(step):
+            one_chunk(step * number + i, carry)
+        return carry
+
+    lax.fori_loop(0, count // step, some_chunks, 0)
 
 
 def send_kernel(tracers_ref, send_ref, before_ref, after_ref, *out_refs):
@@ -866,6 +899,7 @@
     coef_ref,
     near_ref,
     area_ref,
+    rows_ref,
     *refs,
 ):
     partial_refs, (out_ref, gain_ref) = refs[: len(starts)], refs[len(starts) :]
@@ -894,7 +928,7 @@
 HBM_SPEC = pl.BlockSpec(memory_space=pltpu.HBM)
 
 
-def call(kernel, outs, specs, scratch=(), cost=0, hbm_out=False):
+def call(kernel, outs, specs, scratch=(), cost=0, hbm_outs=0):
     estimate = None
     if cost:
         estimate = pl.CostEstimate(flops=0, bytes_accessed=cost, transcendentals=0)
@@ -903,8 +937,7 @@
         for out in outs
     ]
     out_specs = [VMEM_SPEC] * len(outs)
-    if hbm_out:
-        out_specs[0] = HBM_SPEC
+    out_specs[:hbm_outs] = [HBM_SPEC] * hbm_outs
     return pl.pallas_call(
         kernel,
         out_shape=outs,
@@ -972,14 +1005,14 @@
                 air.shape,
             )
         ]
-        + [pltpu.SemaphoreType.DMA((len(first_inputs) + 1,))],
-        hbm_out=True,
+        + [pltpu.SemaphoreType.DMA((len(first_inputs) + field_count,))],
+        hbm_outs=1,
     )(*(pltpu.with_memory_space_constraint(array, pltpu.HBM) for array in first_inputs))
     recv = lax.all_to_all(slab, "blk", split_axis=0, concat_axis=0, tiled=True)
 
     chunks = cells // LANES
     reads_per_chunk = edge_coef.shape[0] * chunks * (ocean_planes // ROWS)
-    starts = (0, chunks * 3 // 16, chunks * 11 // 16)
+    starts = (0, chunks // 4, chunks * 3 // 4)
 
     def ocean_part(start, end, after):
         (result,) = call(
@@ -1038,23 +1071,41 @@
             pltpu.VMEM((2 * planes, LANES), jnp.float32),
             pltpu.SemaphoreType.DMA((3,)),
         ],
-        hbm_out=True,
+        hbm_outs=1,
     )(avg, surf, low, high, wind, point_ids, second_part)
     arrived = lax.all_to_all(slab, "blk", split_axis=0, concat_axis=0, tiled=True)
-    down, up = call(rows_kernel, [(planes, LANES)] * 2, [VMEM_SPEC])(sums)
+    third_part = ocean_part(starts[2], chunks, final)
+    down, up = call(rows_kernel, [(planes, LANES)] * 2, [VMEM_SPEC, ANY_SPEC])(
+        sums, third_part
+    )
     low = lax.ppermute(up, "face", after_me)
     high = lax.ppermute(down, "face", [(to, source) for source, to in after_me])
-    third_part = ocean_part(starts[2], chunks, down)
     partial, gain = call(
         functools.partial(rim_kernel, starts),
         [ocean.shape, area.shape],
-        [VMEM_SPEC] * (5 + len(starts)),
+        [VMEM_SPEC] * 5 + [ANY_SPEC] + [VMEM_SPEC] * len(starts),
         cost=chunks * reads_per_chunk // 8 * ROWS * LANES * 4,
-    )(before, after, edge_coef, neighbours, area, first_part, second_part, third_part)
+    )(
+        before,
+        after,
+        edge_coef,
+        neighbours,
+        area,
+        down,
+        first_part,
+        second_part,
+        third_part,
+    )
     air_final, ocean_final = call(
         functools.partial(end_kernel, planes),
         [air.shape, ocean.shape],
         [VMEM_SPEC] * 10,
+        [
+            pltpu.VMEM(air.shape, jnp.float32),
+            pltpu.VMEM((ROWS, cells), jnp.float32),
+            pltpu.SemaphoreType.DMA((2 + planes // ROWS,)),
+        ],
+        hbm_outs=2,
     )(sums, low, high, arrived, final, inverse, cell_ids, weights, gain, partial)
     return air_final.reshape(air_state.shape), ocean_final.reshape(tracers.shape)
 

time: 34.2 us -> 33.6 us (0.982)
  Pallas kernels: 12.7 us -> 11.5 us
  waiting for transfers between devices: 0.75 us -> 1.72 us
    pallas_call x3, Pallas kernels: 5.64 us -> 4.29 us  [ocean_part(): call(functools.partial(ocean_kernel, ocean_levels, start), [(ocean_planes...]
    ppermute x2, waiting for transfers between devices: 0.01 us -> 0.9 us  [body(): low = lax.ppermute(up, 'face', after_me)]
    ppermute x2, starting transfers between devices: 2.2 us -> 2.81 us  [body(): low = lax.ppermute(up, 'face', after_me)]
    ppermute x2, starting transfers between devices: 5.56 us -> 4.94 us  [body(): high = lax.ppermute(down, 'face', [(to, source) for source, to in after_me])]
  transfers between devices with their start and end apart: 8 -> 8, of which waited for: 1 -> 4; matrix products, arithmetic and copies ran while one was open for 0% -> 0% of each run, Pallas kernels for 21% -> 17%
where the time goes in v9:
time: 33.6 us; the launch traced here: 33.2 us
  starting transfers between devices  19.2 us (57%)
  Pallas kernels  11.5 us (34%)
  waiting for transfers between devices  1.72 us (5%)
  between operations  0.81 us (2%)
    all_to_all x1, starting transfers between devices, body(): recv = lax.all_to_all(slab, 'blk', split_axis=0, concat_axis=0, tiled=True)  5.31 us
    ppermute x2, starting transfers between devices, body(): high = lax.ppermute(down, 'face', [(to, source) for source, to in after_me])  4.94 us
    pallas_call x3, Pallas kernels, ocean_part(): call(functools.partial(ocean_kernel, ocean_levels, start), [(ocean_planes...  4.29 us
    all_to_all x1, starting transfers between devices, body(): lax.all_to_all(slab, 'blk', split_axis=0, concat_axis=0, tiled=True)  3.36 us
    ppermute x2, starting transfers between devices, body(): low = lax.ppermute(up, 'face', after_me)  2.81 us
    pallas_call x1, Pallas kernels, body(): call(functools.partial(start_kernel, planes), [(blocks, HEAD, LANES), air...  2.43 us
    ppermute x1, starting transfers between devices, body(): lax.ppermute(to_before, 'blk', [(to, source) for source, to in onward])  2.24 us
    pallas_call x1, Pallas kernels, body(): call(functools.partial(second_kernel, planes), [(blocks, EDGE_AT + ROWS,...  1.76 us
  transfers between devices with their start and end apart: 8, of which 4 were waited for; matrix products, arithmetic and copies ran while one was open for 0% of the time, Pallas kernels for 17%

profile of v9, /device:TPU:0, one launch (start us, length us, event | category | flops | bytes accessed | tf_op | source)
XLA Modules:
  0.0 33.2 jit_solution(16663949710597391409)
XLA Ops:
  0.6 0.0 copy-start
  0.6 2.4 %start_kernel.1 = (f32[8,8,128]{2,1,0:T(8,128)}, f32[768,128]{1,0:T(8,128)S(1)}, f32[24,128]{1,0:T(8,128)S(1)}, f32[24,128]{1,0:T(8,128)S(1)}, s32[8,128]{1,0:T(...) custom-call(s32[8,128]{1,0:T(8,128)} %bitcast.24, f32[8,128]{1,0:T(8,128)} %bitcast.25, ...), custom_call_target="tpu_custom_call" | custom-call | tf_op jit(solution)/shard_map/start_kernel/pallas_call | solution.py:991
  3.1 0.0 copy-start.3
  3.1 0.0 copy-start.4
  3.1 5.3 %all-to-all-start = ((f32[8,8,128]{2,1,0:T(8,128)}), f32[8,8,128]{2,1,0:T(8,128)S(1)}, u32[]{:S(2)}, u32[]{:S(2)}) async-start(f32[8,8,128]{2,1,0:T(8,128)} %get-tuple-element.27), calls=%async_computation | async-start | bytes 65536 | tf_op jit(solution)/shard_map/all_to_all | solution.py:1011
  8.4 0.0 copy-start.5
  8.4 0.0 copy-done
  8.4 0.0 copy-start.2
  8.4 0.2 send_kernel.1
  8.7 0.0 copy-start.1
  8.7 0.5 %collective-permute-start = (f32[56,128]{1,0:T(8,128)S(1)}, f32[56,128]{1,0:T(8,128)S(1)}, u32[]{:S(2)}, u32[]{:S(2)}) collective-permute-start(f32[56,128]{1,0:T(8,128)S(1)} %get-tuple-element.31), channel_id=1, source_target_pairs={{0,1},{1,2},{2,3},{3,4},{4,5},{5,6},{6,7},{7,0},{8,9},{9,10},{10,1... | collective-permute-start | bytes 86024 | tf_op jit(solution)/shard_map/ppermute | solution.py:1034
  9.2 2.2 %collective-permute-start.1 = (f32[56,128]{1,0:T(8,128)S(1)}, f32[56,128]{1,0:T(8,128)S(1)}, u32[]{:S(2)}, u32[]{:S(2)}) collective-permute-start(f32[56,128]{1,0:T(8,128)S(1)} %get-tuple-element.32.after_ref), channel_id=1, source_target_pairs={{1,0},{2,1},{3,2},{4,3},{5,4},{6,5},{7,6},{0,7},{9,8},{10,9},{11,1... | collective-permute-start | bytes 86024 | tf_op jit(solution)/shard_map/ppermute | solution.py:1035
  11.4 0.0 copy-done.3
  11.4 0.0 copy-done.4
  11.5 0.0 copy-done.5
  11.5 0.0 copy-start.6
  11.5 0.0 copy-start.7
  11.5 1.1 %ocean_kernel.3.ocean_ref.refs_0_ = f32[32,512]{1,0:T(8,128)S(1)} custom-call(f32[32,2048]{1,0:T(8,128)S(1)} %bitcast.12, f32[6,2048]{1,0:T(8,128)S(1)} %copy-done.3, s32[6,2048]{1,0:T(8,128)S(1)} %copy-done.4, f32[16,128]{1,0:T(8,128)S(1)} %bitcast.20, f32[56,128]{1,0:T(8,128)S(1)} %get-tuple-element.32.after_ref), custom_call_target="tpu_custom_call" | custom-call | bytes 3145728 | tf_op jit(solution)/shard_map/ocean_kernel/pallas_call | solution.py:1018
  12.6 0.7 %all-to-all-done.recv_ref = f32[8,8,128]{2,1,0:T(8,128)S(1)} async-done(((f32[8,8,128]{2,1,0:T(8,128)}), f32[8,8,128]{2,1,0:T(8,128)S(1)}, u32[]{:S(2)}, u32[]{:S(2)}) %all-to-all-start) | async-done | bytes 32800 | tf_op jit(solution)/shard_map/all_to_all | solution.py:1011
  13.3 0.0 collective-permute-done.before_ref
  13.3 0.0 collective-permute-done.1.after_ref
  13.3 0.0 copy-done.2
  13.3 0.0 copy-done.1
  13.3 0.0 copy-done.6
  13.3 0.0 copy-done.7
  13.3 0.5 %panel_kernel.1 = (f32[768,128]{1,0:T(8,128)S(1)}, f32[72,128]{1,0:T(8,128)S(1)}, f32[72,128]{1,0:T(8,128)S(1)}, f32[192,128]{1,0:T(8,128)S(1)}) custom-call(f32[768,128]{1,0:T(8,128)S(1)} %get-tuple-element.26.moved_ref, f32[8,8,128]{2,1,0:T(8,128)S(1)} %all-to-all-done.recv_ref, f32[56,128]{1,0:T(8,128)S(1)} %collective-permute-done.before_ref, ...), custom_call_target="tpu_custom_call" | custom-call | tf_op jit(solution)/shard_map/panel_kernel/pallas_call | solution.py:1038
  13.8 1.6 %collective-permute-start.2 = (f32[72,128]{1,0:T(8,128)S(1)}, f32[72,128]{1,0:T(8,128)S(1)}, u32[]{:S(2)}, u32[]{:S(2)}) collective-permute-start(f32[72,128]{1,0:T(8,128)S(1)} %get-tuple-element.36), channel_id=1, source_target_pairs={{0,8},{8,16},{16,24},{24,0},{1,9},{9,17},{17,25},{25,1},{2,10},{10... | collective-permute-start | bytes 110600 | tf_op jit(solution)/shard_map/ppermute | solution.py:1055
  15.4 2.2 %collective-permute-start.3 = (f32[72,128]{1,0:T(8,128)S(1)}, f32[72,128]{1,0:T(8,128)S(1)}, u32[]{:S(2)}, u32[]{:S(2)}) collective-permute-start(f32[72,128]{1,0:T(8,128)S(1)} %get-tuple-element.37), channel_id=1, source_target_pairs={{8,0},{16,8},{24,16},{0,24},{9,1},{17,9},{25,17},{1,25},{10,2},{18... | collective-permute-start | bytes 110600 | tf_op jit(solution)/shard_map/ppermute | solution.py:1056
  17.7 2.1 %ocean_kernel.4.ocean_ref.refs_1_ = f32[32,1024]{1,0:T(8,128)S(1)} custom-call(f32[32,2048]{1,0:T(8,128)S(1)} %bitcast.13, f32[6,2048]{1,0:T(8,128)S(1)} %copy-done.3, s32[6,2048]{1,0:T(8,128)S(1)} %copy-done.4, f32[16,128]{1,0:T(8,128)S(1)} %bitcast.21, f32[192,128]{1,0:T(8,128)S(1)} %get-tuple-element.35.after_ref.surf_ref), custom_call_target="tpu_custom_call" | custom-call | bytes 6291456 | tf_op jit(solution)/shard_map/ocean_kernel/pallas_call | solution.py:1018
  19.8 0.3 collective-permute-done.2.low_ref
  20.1 0.1 collective-permute-done.3.high_ref
  20.2 1.8 %second_kernel.1 = (f32[8,16,128]{2,1,0:T(8,128)}, f32[768,128]{1,0:T(8,128)S(1)}, f32[16,128]{1,0:T(8,128)S(1)}, f32[16,128]{1,0:T(8,128)S(1)}) custom-call(f32[768,128]{1,0:T(8,128)S(1)} %get-tuple-element.34.avg_ref, f32[192,128]{1,0:T(8,128)S(1)} %get-tuple-element.35.after_ref.surf_ref, f32[72,128]{1,0:T(8,128)S(1)} %collective-permute-done.2.low_ref, ...), custom_call_target="tpu_custom_call" | custom-call | tf_op jit(solution)/shard_map/second_kernel/pallas_call | solution.py:1059
  21.9 3.4 %all-to-all-start.1 = ((f32[8,16,128]{2,1,0:T(8,128)}), f32[8,16,128]{2,1,0:T(8,128)S(1)}, u32[]{:S(2)}, u32[]{:S(2)}) async-start(f32[8,16,128]{2,1,0:T(8,128)} %get-tuple-element.42), calls=%async_computation.1 | async-start | bytes 131072 | tf_op jit(solution)/shard_map/all_to_all | solution.py:1076
  25.3 1.1 %ocean_kernel.5.ocean_ref.refs_2_ = f32[32,512]{1,0:T(8,128)S(1)} custom-call(f32[32,2048]{1,0:T(8,128)S(1)} %bitcast.14, f32[6,2048]{1,0:T(8,128)S(1)} %copy-done.3, s32[6,2048]{1,0:T(8,128)S(1)} %copy-done.4, f32[16,128]{1,0:T(8,128)S(1)} %bitcast.22, f32[16,128]{1,0:T(8,128)S(1)} %get-tuple-element.39.after_ref.final_ref), custom_call_target="tpu_custom_call" | custom-call | bytes 3145728 | tf_op jit(solution)/shard_map/ocean_kernel/pallas_call | solution.py:1018
  26.4 0.0 copy-start.8
  26.4 1.2 %collective-permute-start.4 = (f32[48,128]{1,0:T(8,128)S(1)}, f32[48,128]{1,0:T(8,128)S(1)}, u32[]{:S(2)}, u32[]{:S(2)}) collective-permute-start(f32[48,128]{1,0:T(8,128)S(1)} %get-tuple-element.40), channel_id=1, source_target_pairs={{0,8},{8,16},{16,24},{24,0},{1,9},{9,17},{17,25},{25,1},{2,10},{10... | collective-permute-start | bytes 73736 | tf_op jit(solution)/shard_map/ppermute | solution.py:1081
  27.6 2.7 %collective-permute-start.5 = (f32[48,128]{1,0:T(8,128)S(1)}, f32[48,128]{1,0:T(8,128)S(1)}, u32[]{:S(2)}, u32[]{:S(2)}) collective-permute-start(f32[48,128]{1,0:T(8,128)S(1)} %get-tuple-element.41.rows_ref), channel_id=1, source_target_pairs={{8,0},{16,8},{24,16},{0,24},{9,1},{17,9},{25,17},{1,25},{10,2},{18... | collective-permute-start | bytes 73736 | tf_op jit(solution)/shard_map/ppermute | solution.py:1082
  30.3 0.0 copy-done.8
  30.3 1.2 %rim_kernel.1 = (f32[32,2048]{1,0:T(8,128)S(1)}, f32[16,128]{1,0:T(8,128)S(1)}) custom-call(f32[56,128]{1,0:T(8,128)S(1)} %collective-permute-done.before_ref, f32[56,128]{1,0:T(8,128)S(1)} %collective-permute-done.1.after_ref, f32[6,2048]{1,0:T(8,128)S(1)} %copy-done.3, s32[6,2048]{1,0:T(8,128)S(1)} %copy-done.4, f32[16,128]{1,0:T(8,128)S(1)} %bitcast.23, ...), custom_call_target="tpu_custom_call" | custom-call | bytes 3145728 | tf_op jit(solution)/shard_map/rim_kernel/pallas_call | solution.py:1083
  31.5 0.6 %collective-permute-done.4.low_ref = f32[48,128]{1,0:T(8,128)S(1)} collective-permute-done((f32[48,128]{1,0:T(8,128)S(1)}, f32[48,128]{1,0:T(8,128)S(1)}, u32[]{:S(2)}, u32[]{:S(2)}) %collective-permute-start.4) | collective-permute-done | bytes 24608 | tf_op jit(solution)/shard_map/ppermute | solution.py:1081
  32.1 0.0 collective-permute-done.5.high_ref
  32.1 0.0 all-to-all-done.1.recv_ref
  32.1 1.1 %end_kernel.1 = (f32[768,128]{1,0:T(8,128)}, f32[32,2048]{1,0:T(8,128)}) custom-call(f32[768,128]{1,0:T(8,128)S(1)} %get-tuple-element.38.sums_ref, f32[48,128]{1,0:T(8,128)S(1)} %collective-permute-done.4.low_ref, f32[48,128]{1,0:T(8,128)S(1)} %collective-permute-done.5.high_ref, f32[8,16,128]{2,1,0:T(8,128)S(1)} %all-to-all-done.1.recv_ref, ...), custom_call_target="tpu_custom_call" | custom-call | tf_op jit(solution)/shard_map/end_kernel/pallas_call | solution.py:1099
  (1 shorter events, 0.0 us)
Async XLA Ops:
  0.6 7.8 %copy-start = (f32[2,16,2048]{2,1,0:T(8,128)S(1)}, f32[2,16,2048]{2,1,0:T(8,128)}, u32[]{:S(2)}) copy-start(f32[2,16,2048]{2,1,0:T(8,128)} %param.18) | copy-start | bytes 786436
  3.1 8.4 %copy-start.3 = (f32[6,2048]{1,0:T(8,128)S(1)}, f32[6,2048]{1,0:T(8,128)}, u32[]{:S(2)}) copy-start(f32[6,2048]{1,0:T(8,128)} %coef_ref.7) | copy-start | bytes 147460
  3.1 8.4 %copy-start.4 = (s32[6,2048]{1,0:T(8,128)S(1)}, s32[6,2048]{1,0:T(8,128)}, u32[]{:S(2)}) copy-start(s32[6,2048]{1,0:T(8,128)} %near_ref.7) | copy-start | bytes 147460
  3.1 10.2 %all-to-all-start = ((f32[8,8,128]{2,1,0:T(8,128)}), f32[8,8,128]{2,1,0:T(8,128)S(1)}, u32[]{:S(2)}, u32[]{:S(2)}) async-start(f32[8,8,128]{2,1,0:T(8,128)} %get-tuple-element.27), calls=%async_computation | async-start | bytes 65536 | tf_op jit(solution)/shard_map/all_to_all | solution.py:1011
  8.4 3.0 %copy-start.5 = (f32[2048]{0:T(1024)S(1)}, f32[2048]{0:T(1024)}, u32[]{:S(2)}) copy-start(f32[2048]{0:T(1024)} %param.21) | copy-start | bytes 24580
  8.4 4.8 %copy-start.2 = (f32[3,16,16,128]{3,2,1,0:T(8,128)S(1)}, f32[3,16,16,128]{3,2,1,0:T(8,128)}, u32[]{:S(2)}) copy-start(f32[3,16,16,128]{3,2,1,0:T(8,128)} %param.13) | copy-start | bytes 1179652
  8.7 4.6 %copy-start.1 = (f32[2,16,16,128]{3,2,1,0:T(8,128)S(1)}, f32[2,16,16,128]{3,2,1,0:T(8,128)}, u32[]{:S(2)}) copy-start(f32[2,16,16,128]{3,2,1,0:T(8,128)} %param.14) | copy-start | bytes 786436
  8.7 4.6 %collective-permute-start = (f32[56,128]{1,0:T(8,128)S(1)}, f32[56,128]{1,0:T(8,128)S(1)}, u32[]{:S(2)}, u32[]{:S(2)}) collective-permute-start(f32[56,128]{1,0:T(8,128)S(1)} %get-tuple-element.31), channel_id=1, source_target_pairs={{0,1},{1,2},{2,3},{3,4},{4,5},{5,6},{6,7},{7,0},{8,9},{9,10},{10,1... | collective-permute-start | bytes 86024 | tf_op jit(solution)/shard_map/ppermute | solution.py:1034
  9.2 4.1 %collective-permute-start.1 = (f32[56,128]{1,0:T(8,128)S(1)}, f32[56,128]{1,0:T(8,128)S(1)}, u32[]{:S(2)}, u32[]{:S(2)}) collective-permute-start(f32[56,128]{1,0:T(8,128)S(1)} %get-tuple-element.32.after_ref), channel_id=1, source_target_pairs={{1,0},{2,1},{3,2},{4,3},{5,4},{6,5},{7,6},{0,7},{9,8},{10,9},{11,1... | collective-permute-start | bytes 86024 | tf_op jit(solution)/shard_map/ppermute | solution.py:1035
  11.5 1.8 %copy-start.6 = (f32[16,128]{1,0:T(8,128)S(1)}, f32[16,128]{1,0:T(8,128)}, u32[]{:S(2)}) copy-start(f32[16,128]{1,0:T(8,128)} %jac_ref.1) | copy-start | bytes 24580
  11.5 1.8 %copy-start.7 = (f32[16,128]{1,0:T(8,128)S(1)}, f32[16,128]{1,0:T(8,128)}, u32[]{:S(2)}) copy-start(f32[16,128]{1,0:T(8,128)} %land_ref.1) | copy-start | bytes 24580
  13.8 6.3 %collective-permute-start.2 = (f32[72,128]{1,0:T(8,128)S(1)}, f32[72,128]{1,0:T(8,128)S(1)}, u32[]{:S(2)}, u32[]{:S(2)}) collective-permute-start(f32[72,128]{1,0:T(8,128)S(1)} %get-tuple-element.36), channel_id=1, source_target_pairs={{0,8},{8,16},{16,24},{24,0},{1,9},{9,17},{17,25},{25,1},{2,10},{10... | collective-permute-start | bytes 110600 | tf_op jit(solution)/shard_map/ppermute | solution.py:1055
  15.4 4.7 %collective-permute-start.3 = (f32[72,128]{1,0:T(8,128)S(1)}, f32[72,128]{1,0:T(8,128)S(1)}, u32[]{:S(2)}, u32[]{:S(2)}) collective-permute-start(f32[72,128]{1,0:T(8,128)S(1)} %get-tuple-element.37), channel_id=1, source_target_pairs={{8,0},{16,8},{24,16},{0,24},{9,1},{17,9},{25,17},{1,25},{10,2},{18... | collective-permute-start | bytes 110600 | tf_op jit(solution)/shard_map/ppermute | solution.py:1056
  21.9 10.2 %all-to-all-start.1 = ((f32[8,16,128]{2,1,0:T(8,128)}), f32[8,16,128]{2,1,0:T(8,128)S(1)}, u32[]{:S(2)}, u32[]{:S(2)}) async-start(f32[8,16,128]{2,1,0:T(8,128)} %get-tuple-element.42), calls=%async_computation.1 | async-start | bytes 131072 | tf_op jit(solution)/shard_map/all_to_all | solution.py:1076
  26.4 3.9 %copy-start.8 = (f32[2048]{0:T(1024)S(1)}, f32[2048]{0:T(1024)}, u32[]{:S(2)}) copy-start(f32[2048]{0:T(1024)} %param.22) | copy-start | bytes 24580
  26.4 5.7 %collective-permute-start.4 = (f32[48,128]{1,0:T(8,128)S(1)}, f32[48,128]{1,0:T(8,128)S(1)}, u32[]{:S(2)}, u32[]{:S(2)}) collective-permute-start(f32[48,128]{1,0:T(8,128)S(1)} %get-tuple-element.40), channel_id=1, source_target_pairs={{0,8},{8,16},{16,24},{24,0},{1,9},{9,17},{17,25},{25,1},{2,10},{10... | collective-permute-start | bytes 73736 | tf_op jit(solution)/shard_map/ppermute | solution.py:1081
  27.6 4.5 %collective-permute-start.5 = (f32[48,128]{1,0:T(8,128)S(1)}, f32[48,128]{1,0:T(8,128)S(1)}, u32[]{:S(2)}, u32[]{:S(2)}) collective-permute-start(f32[48,128]{1,0:T(8,128)S(1)} %get-tuple-element.41.rows_ref), channel_id=1, source_target_pairs={{8,0},{16,8},{24,16},{0,24},{9,1},{17,9},{25,17},{1,25},{10,2},{18... | collective-permute-start | bytes 73736 | tf_op jit(solution)/shard_map/ppermute | solution.py:1082

commit v10 on v7

--- a/solution.py
+++ b/solution.py
@@ -129,12 +129,13 @@
     return x // ROWS, LANES // 2 * (x % 2) + ROWS * group + 2 * (x % ROWS // 2)
 
 
-def all_edges(geo, ref, planes, x_points):
-    packs = [jnp.zeros((ROWS, LANES), jnp.float32) for _ in range(2)]
-    for x in range(x_points):
+def edges_of(geo, packs, ref, planes, lines, first=None):
+    packs = list(packs)
+    for number, x in enumerate(lines):
+        base = planes * (number if first is None else x - first)
         for group in range(planes // ROWS):
             q, at = edge_place(x, group)
-            tile = ref[planes * x + ROWS * group : planes * x + ROWS * (group + 1), :]
+            tile = ref[base + ROWS * group : base + ROWS * (group + 1), :]
             rolled = pltpu.roll(tile, (at + 1) % LANES, 1)
             packs[q] = jnp.where((geo.lane >> 1) == at // 2, rolled, packs[q])
     return packs
@@ -348,7 +349,8 @@
                         fields[i] - (wind[0][i] * slope + wind[1][i] * slopes[i])
                     )
                     moved_ref[planes * x + plane : planes * x + plane + ROWS, :] = moved
-    packs = all_edges(geo, moved_ref, planes, x_points)
+    packs = [jnp.zeros((ROWS, LANES), jnp.float32) for _ in range(2)]
+    packs = edges_of(geo, packs, moved_ref, planes, range(x_points))
     to_right, to_left = split_sides(geo, packs[0], packs[1], 1)
     after_ref[SIDE_EDGE : SIDE_EDGE + ROWS, :] = to_right
     before_ref[SIDE_EDGE : SIDE_EDGE + ROWS, :] = to_left
@@ -457,7 +459,7 @@
         before_ref[SIDE_EDGE : SIDE_EDGE + ROWS, :],
         after_ref[SIDE_EDGE : SIDE_EDGE + ROWS, :],
     )
-    for x in range(x_points):
+    for x in outer_rows(x_points):
         for group in range(planes // ROWS):
             at = slice(planes * x + ROWS * group, planes * x + ROWS * (group + 1))
             avg_ref[at, :] = geo.sum_y(moved_ref[at, :], outer_edges(joined, x, group))
@@ -511,9 +513,91 @@
         out_ref[base : base + 2, :] = surf_line(COEF_X, r) * surf_slope
 
 
+def outer_rows(x_points):
+    return [x for x in range(x_points) if x <= GLL or x >= x_points - GLL - 1]
+
+
+def advance(geo, fields, wind, mass):
+    slopes = geo.d_y(*fields)
+    moved = []
+    for i in range(GLL):
+        slope = sum(deriv_table[i][j] * fields[j] for j in range(GLL))
+        moved.append(mass[i] * (fields[i] - (wind[0][i] * slope + wind[1][i] * slopes[i])))
+    return moved, slopes
+
+
+def inner_kernel(
+    planes, avg_ref, moved_ref, before_ref, after_ref, surf_ref, wind_ref, out_ref, packs_ref
+):
+    geo = Geometry()
+    x_points = avg_ref.shape[0] // planes
+    levels = wind_ref.shape[0] // (2 * x_points)
+    joined = join_edges(
+        geo,
+        before_ref[SIDE_EDGE : SIDE_EDGE + ROWS, :],
+        after_ref[SIDE_EDGE : SIDE_EDGE + ROWS, :],
+    )
+    outer = outer_rows(x_points)
+
+    def average(x, plane):
+        at = slice(planes * x + plane, planes * x + plane + ROWS)
+        if x in outer:
+            return avg_ref[at, :]
+        return geo.sum_y(moved_ref[at, :], outer_edges(joined, x, plane // ROWS))
+
+    def surf_row(number, x):
+        at = 4 * ROWS * number + x
+        return spread(surf_ref[at : at + 1, :])
+
+    def put(x, plane, value):
+        at = planes * (x - GLL) + plane
+        out_ref[at : at + ROWS, :] = value
+
+    held = {}
+    carried = {}
+    for element in range(1, x_points // GLL - 1):
+        lines = [GLL * element + i for i in range(GLL)]
+        totals = [surf_row(MASS_SUM, x) for x in lines]
+        totals[0] = totals[0] + surf_row(MASS_SUM, lines[0] - 1)
+        totals[-1] = totals[-1] + surf_row(MASS_SUM, lines[-1] + 1)
+        scale = [1.0 / total for total in totals]
+        mass = [surf_row(MASS, x) for x in lines]
+        for level in range(0, levels, ROWS):
+            wind = wind_tiles(wind_ref, x_points, level, lines)
+            for plane in range(level, planes, levels):
+                if element == 1:
+                    first = average(lines[0], plane) + average(lines[0] - 1, plane)
+                else:
+                    first = carried[plane]
+                last = average(lines[-1], plane) + average(lines[-1] + 1, plane)
+                carried[plane] = last
+                totals = (
+                    [first] + [average(x, plane) for x in lines[1:-1]] + [last]
+                )
+                fields = [total * factor for total, factor in zip(totals, scale)]
+                moved, _ = advance(geo, fields, wind, mass)
+                if element == 1:
+                    put(lines[0], plane, moved[0])
+                else:
+                    shared = held[plane] + moved[0]
+                    put(lines[0] - 1, plane, shared)
+                    put(lines[0], plane, shared)
+                for i in range(1, GLL - 1):
+                    put(lines[i], plane, moved[i])
+                held[plane] = moved[-1]
+                if lines[-1] == x_points - GLL - 1:
+                    put(lines[-1], plane, moved[-1])
+    packs = [jnp.zeros((ROWS, LANES), jnp.float32) for _ in range(2)]
+    inner = [x for x in range(x_points) if x not in outer]
+    for q, pack in enumerate(edges_of(geo, packs, out_ref, planes, inner, GLL)):
+        packs_ref[ROWS * q : ROWS * (q + 1), :] = pack
+
+
 def second_kernel(
     planes,
     avg_ref,
+    inner_ref,
+    packs_ref,
     surf_ref,
     low_ref,
     high_ref,
@@ -604,8 +688,11 @@
     ]
     copies[0].start()
 
+    kept = outer_rows(x_points)
+
     def put(x, plane, value):
-        sums_ref[planes * x + plane : planes * x + plane + ROWS, :] = value
+        at = planes * kept.index(x) + plane
+        sums_ref[at : at + ROWS, :] = value
 
     def beyond(ref, plane, field, slope, own_coef):
         wind_at = 2 * planes + plane % levels
@@ -620,10 +707,9 @@
         return spread(tiles[x // ROWS][x % ROWS : x % ROWS + 1])
 
     masses = [surf_tile(MASS, 0, h) for h in range(2)]
-    held = {}
-    for element in range(x_points // GLL):
+    last_element = x_points // GLL - 1
+    for element in (0, last_element):
         lines = [GLL * element + i for i in range(GLL)]
-        first, last = lines[0], lines[-1]
         scale = [row_of(inverse[0], x) for x in lines]
         mass = [row_of(masses, x) for x in lines]
         for level in range(0, levels, ROWS):
@@ -642,29 +728,26 @@
                         at = planes * other + plane
                         total = total + avg_ref[at : at + ROWS, :]
                     fields.append(total * scale[i])
-                slopes = geo.d_y(*fields)
-                moved = []
-                for i, x in enumerate(lines):
-                    slope = sum(deriv_table[i][j] * fields[j] for j in range(GLL))
-                    moved.append(
-                        mass[i] * (fields[i] - (wind[0][i] * slope + wind[1][i] * slopes[i]))
-                    )
-                if first == 0:
+                moved, slopes = advance(geo, fields, wind, mass)
+                if element == 0:
                     before = beyond(low_ref, plane, fields[0], slopes[0], deriv_table[3][3])
-                    put(first, plane, before + moved[0])
+                    put(lines[0], plane, before + moved[0])
+                    shared = moved[-1] + inner_ref[here, :]
+                    put(lines[-1], plane, shared)
+                    put(lines[-1] + 1, plane, shared)
                 else:
-                    shared = held[plane] + moved[0]
-                    put(first - 1, plane, shared)
-                    put(first, plane, shared)
-                for i in range(1, GLL - 1):
-                    put(lines[i], plane, moved[i])
-                held[plane] = moved[-1]
-                if last == x_points - 1:
+                    at = inner_ref.shape[0] - planes + plane
+                    shared = moved[0] + inner_ref[at : at + ROWS, :]
+                    put(lines[0] - 1, plane, shared)
+                    put(lines[0], plane, shared)
                     after = beyond(
                         high_ref, plane, fields[-1], slopes[-1], deriv_table[0][0]
                     )
-                    put(last, plane, held[plane] + after)
-    packs = all_edges(geo, sums_ref, planes, x_points)
+                    put(lines[-1], plane, moved[-1] + after)
+                for i in range(1, GLL - 1):
+                    put(lines[i], plane, moved[i])
+    packs = [packs_ref[:ROWS, :], packs_ref[ROWS:, :]]
+    packs = edges_of(geo, packs, sums_ref, planes, kept)
     to_right, to_left = split_sides(geo, packs[0], packs[1], 1)
     for i, (to, edges) in enumerate(((right, to_right), (left, to_left))):
         edges_ref[i] = edges
@@ -680,9 +763,24 @@
         copy.wait()
 
 
+def last_kernel(planes, inner_ref, outer_ref, inverse_ref, out_ref):
+    geo = Geometry()
+    x_points = inverse_ref.shape[0]
+    kept = outer_rows(x_points)
+    for x in range(x_points):
+        inverse = spread(inverse_ref[x : x + 1, :])
+        ref, first = inner_ref, planes * (x - GLL)
+        if x in kept:
+            ref, first = outer_ref, planes * kept.index(x)
+        for group in range(planes // ROWS):
+            tile = ref[first + ROWS * group : first + ROWS * (group + 1), :]
+            at = planes * x + ROWS * group
+            out_ref[at : at + ROWS, :] = inverse * geo.sum_y(tile, 0.0)
+
+
 def end_kernel(
     planes,
-    sums_ref,
+    last_ref,
     recv_ref,
     final_ref,
     inverse_ref,
@@ -692,34 +790,51 @@
     ocean_ref,
     air_out,
     ocean_out,
+    air_ref,
+    first_ref,
+    semaphores,
 ):
     geo = Geometry()
     blocks = cols_ref.shape[0]
     left, right = neighbours_of(blocks)
     chunks = gain_ref.shape[0]
+    x_points = inverse_ref.shape[0]
+    copies = []
+
+    def send(source, target):
+        copies.append(
+            pltpu.make_async_copy(source, target, semaphores.at[len(copies)])
+        )
+        copies[-1].start()
+
+    send(ocean_ref.at[ROWS:], ocean_out.at[ROWS:])
     arrived = jnp.concatenate([recv_ref[c, 0:1, :] for c in range(blocks)], axis=0)
     (inflow,) = scatter_sum([weights_ref[...] * arrived], cols_ref[...], chunks)
     gain = inflow * gain_ref[...]
-    ocean_out[...] = ocean_ref[...]
+    first_ref[...] = ocean_ref[:ROWS, :]
     for k in range(chunks):
         at = slice(LANES * k, LANES * (k + 1))
-        ocean_out[0:1, at] = ocean_ref[0:1, at] + gain[k : k + 1]
-
-    x_points = inverse_ref.shape[0]
+        first_ref[0:1, at] = ocean_ref[0:1, at] + gain[k : k + 1]
+    send(first_ref, ocean_out.at[:ROWS])
+
     joined = join_edges(
         geo,
         recv_ref[left, EDGE_AT : EDGE_AT + ROWS, :],
         recv_ref[right, EDGE_AT : EDGE_AT + ROWS, :],
     )
-    for x in range(x_points):
-        inverse = spread(inverse_ref[x : x + 1, :])
-        for group in range(planes // ROWS):
+    for group in range(planes // ROWS):
+        for x in range(x_points):
             at = planes * x + ROWS * group
-            air_out[pl.ds(ROWS * group * x_points + x, ROWS, stride=x_points), :] = (
-                inverse
-                * geo.sum_y(sums_ref[at : at + ROWS, :], outer_edges(joined, x, group))
-            )
-    air_out[0:x_points, :] = final_ref[...]
+            beside = spread(inverse_ref[x : x + 1, :]) * outer_edges(joined, x, group)
+            air_ref[pl.ds(ROWS * group * x_points + x, ROWS, stride=x_points), :] = last_ref[
+                at : at + ROWS, :
+            ] + jnp.where(geo.outer_lane, beside, 0.0)
+        if group == 0:
+            air_ref[0:x_points, :] = final_ref[...]
+        rows = slice(ROWS * group * x_points, ROWS * (group + 1) * x_points)
+        send(air_ref.at[rows], air_out.at[rows])
+    for copy in copies:
+        copy.wait()
 
 
 def gathered(ids, coefs, source, sources, groups, first=0):
@@ -735,8 +850,37 @@
     return totals
 
 
+def multiplied(ids, coefs, halves_ref, sources, groups):
+    lane_at = iota((LANES, LANES), 0)
+    hot = jnp.concatenate(
+        [
+            jnp.where(lane_at == (ids[edge : edge + 1] & (LANES - 1)), 1.0, 0.0).astype(
+                jnp.bfloat16
+            )
+            for edge in range(2)
+        ],
+        axis=1,
+    )
+    picked = jnp.dot(
+        halves_ref[...],
+        jnp.concatenate([hot, hot], axis=0),
+        preferred_element_type=jnp.float32,
+    )
+    totals = [jnp.zeros((ROWS, LANES), jnp.float32) for _ in range(groups)]
+    for edge in range(2):
+        high = spread(ids[edge : edge + 1]) >> 7
+        coef = spread(coefs[edge : edge + 1])
+        side = slice(LANES * edge, LANES * (edge + 1))
+        for s in range(sources):
+            scaled = jnp.where(high == s, coef, 0.0)
+            for group in range(groups):
+                at = ROWS * (groups * s + group)
+                totals[group] += scaled * picked[at : at + ROWS, side]
+    return totals
+
+
 def ocean_kernel(
-    levels, start, tracers_ref, coef_ref, near_ref, rate_ref, after_ref, out_ref
+    levels, start, tracers_ref, coef_ref, near_ref, rate_ref, after_ref, out_ref, halves_ref
 ):
     chunks = tracers_ref.shape[1] // LANES
     groups = tracers_ref.shape[0] // ROWS
@@ -746,13 +890,28 @@
         return tracers_ref[
             ROWS * group : ROWS * (group + 1), LANES * s : LANES * (s + 1)
         ]
+
+    planes = tracers_ref.shape[0]
+    for s in range(chunks):
+        values = tracers_ref[:, LANES * s : LANES * (s + 1)]
+        upper = values.astype(jnp.bfloat16)
+        at = slice(planes * s, planes * (s + 1))
+        halves_ref[at, :LANES] = upper
+        halves_ref[at, LANES:] = (values - upper.astype(jnp.float32)).astype(jnp.bfloat16)
+    edges = near_ref.shape[0]
 
     def one_chunk(number, carry):
         k = number + start
         at = pl.ds(pl.multiple_of(k * LANES, LANES), LANES)
         out_at = pl.ds(pl.multiple_of(number * LANES, LANES), LANES)
         ids, coefs = near_ref[:, at], coef_ref[:, at]
-        totals = gathered(ids, coefs, source, chunks, groups)
+        by_gather = edges - edges // 3 * 2
+        totals = gathered(ids[:by_gather], coefs[:by_gather], source, chunks, groups)
+        for edge in range(by_gather, edges, 2):
+            more = multiplied(
+                ids[edge : edge + 2], coefs[edge : edge + 2], halves_ref, chunks, groups
+            )
+            totals = [total + part for total, part in zip(totals, more)]
         coef_sum = spread(jnp.sum(coefs, axis=0, keepdims=True))
         rate = spread(rate_ref[pl.ds(k, 1), :])
         tiles = [tracers_ref[ROWS * g : ROWS * (g + 1), at] for g in range(groups)]
@@ -771,7 +930,15 @@
             )
         return carry
 
-    lax.fori_loop(0, out_ref.shape[1] // LANES, one_chunk, 0)
+    count = out_ref.shape[1] // LANES
+    step = 2 if count % 2 == 0 else 1
+
+    def some_chunks(number, carry):
+        for i in range(step):
+            one_chunk(step * number + i, carry)
+        return carry
+
+    lax.fori_loop(0, count // step, some_chunks, 0)
 
 
 def send_kernel(tracers_ref, send_ref, before_ref, after_ref, *out_refs):
@@ -797,6 +964,7 @@
     coef_ref,
     near_ref,
     area_ref,
+    rows_ref,
     *refs,
 ):
     partial_refs, (out_ref, gain_ref) = refs[: len(starts)], refs[len(starts) :]
@@ -825,7 +993,7 @@
 HBM_SPEC = pl.BlockSpec(memory_space=pltpu.HBM)
 
 
-def call(kernel, outs, specs, scratch=(), cost=0, hbm_out=False):
+def call(kernel, outs, specs, scratch=(), cost=0, hbm_outs=0):
     estimate = None
     if cost:
         estimate = pl.CostEstimate(flops=0, bytes_accessed=cost, transcendentals=0)
@@ -834,8 +1002,7 @@
         for out in outs
     ]
     out_specs = [VMEM_SPEC] * len(outs)
-    if hbm_out:
-        out_specs[0] = HBM_SPEC
+    out_specs[:hbm_outs] = [HBM_SPEC] * hbm_outs
     return pl.pallas_call(
         kernel,
         out_shape=outs,
@@ -904,20 +1071,21 @@
             )
         ]
         + [pltpu.SemaphoreType.DMA((len(first_inputs) + 1,))],
-        hbm_out=True,
+        hbm_outs=1,
     )(*(pltpu.with_memory_space_constraint(array, pltpu.HBM) for array in first_inputs))
     recv = lax.all_to_all(slab, "blk", split_axis=0, concat_axis=0, tiled=True)
 
     chunks = cells // LANES
     reads_per_chunk = edge_coef.shape[0] * chunks * (ocean_planes // ROWS)
-    starts = (0, chunks * 3 // 16, chunks * 10 // 16)
+    starts = (0, chunks // 4, chunks * 3 // 4)
 
     def ocean_part(start, end, after):
         (result,) = call(
             functools.partial(ocean_kernel, ocean_levels, start),
             [(ocean_planes, (end - start) * LANES)],
             [VMEM_SPEC] * 4 + [ANY_SPEC],
-            cost=(end - start) * reads_per_chunk * ROWS * LANES * 4,
+            [pltpu.VMEM((chunks * ocean_planes, 2 * LANES), jnp.bfloat16)],
+            cost=(end - start) * reads_per_chunk * ROWS * LANES * 2,
         )(ocean, edge_coef, neighbours, rate, after)
         return result
 
@@ -951,37 +1119,65 @@
     after_me = [(i, (i + 1) % faces) for i in range(faces)]
     low = lax.ppermute(up, "face", after_me)
     high = lax.ppermute(down, "face", [(to, source) for source, to in after_me])
+    inner, packs = call(
+        functools.partial(inner_kernel, planes),
+        [((x_points - 2 * GLL) * planes, LANES), (2 * ROWS, LANES)],
+        [VMEM_SPEC] * 6,
+        cost=2 * air.size * 4,
+    )(avg, moved, before, after, surf, wind)
     second_part = ocean_part(starts[1], starts[2], surf)
 
-    slab, sums, final, inverse = call(
+    slab, outer, final, inverse = call(
         functools.partial(second_kernel, planes),
         [
             (blocks, EDGE_AT + ROWS, LANES),
-            air.shape,
+            (len(outer_rows(x_points)) * planes, LANES),
             (x_points, y_points),
             (x_points, y_points),
         ],
-        [VMEM_SPEC] * 6 + [ANY_SPEC],
+        [VMEM_SPEC] * 8 + [ANY_SPEC],
         [
             pltpu.VMEM((blocks, HEAD, LANES), jnp.float32),
             pltpu.VMEM((2, ROWS, LANES), jnp.float32),
             pltpu.SemaphoreType.DMA((3,)),
         ],
-        hbm_out=True,
-    )(avg, surf, low, high, wind, point_ids, second_part)
+        hbm_outs=1,
+    )(avg, inner, packs, surf, low, high, wind, point_ids, second_part)
     arrived = lax.all_to_all(slab, "blk", split_axis=0, concat_axis=0, tiled=True)
+    (last,) = call(
+        functools.partial(last_kernel, planes),
+        [air.shape],
+        [VMEM_SPEC] * 3,
+        cost=2 * air.size * 4,
+    )(inner, outer, inverse)
     third_part = ocean_part(starts[2], chunks, final)
     partial, gain = call(
         functools.partial(rim_kernel, starts),
         [ocean.shape, area.shape],
-        [VMEM_SPEC] * (5 + len(starts)),
+        [VMEM_SPEC] * 5 + [ANY_SPEC] + [VMEM_SPEC] * len(starts),
         cost=chunks * reads_per_chunk // 8 * ROWS * LANES * 4,
-    )(before, after, edge_coef, neighbours, area, first_part, second_part, third_part)
+    )(
+        before,
+        after,
+        edge_coef,
+        neighbours,
+        area,
+        final,
+        first_part,
+        second_part,
+        third_part,
+    )
     air_final, ocean_final = call(
         functools.partial(end_kernel, planes),
         [air.shape, ocean.shape],
         [VMEM_SPEC] * 8,
-    )(sums, arrived, final, inverse, cell_ids, weights, gain, partial)
+        [
+            pltpu.VMEM(air.shape, jnp.float32),
+            pltpu.VMEM((ROWS, cells), jnp.float32),
+            pltpu.SemaphoreType.DMA((2 + planes // ROWS,)),
+        ],
+        hbm_outs=2,
+    )(last, arrived, final, inverse, cell_ids, weights, gain, partial)
     return air_final.reshape(air_state.shape), ocean_final.reshape(tracers.shape)
 
 

time: 33.1 us -> 32.7 us (0.988)
  Pallas kernels: 15 us -> 12.2 us
  waiting for transfers between devices: 1.6 us -> 3.49 us
  local copies, waits for them, and re-layouts: 0.05 us -> 0.55 us
    pallas_call x3, Pallas kernels: 7.98 us -> 4.29 us  [ocean_part(): call(functools.partial(ocean_kernel, ocean_levels, start), [(ocean_planes...]
    pallas_call x0 -> x2, Pallas kernels: none -> 1.3 us  [the longest x1 1.12 us: body(): call(functools.partial(inner_kernel, planes), [((x_points - 2 * GLL) * pl...]
    all_to_all x1, waiting for transfers between devices: 0.74 us -> 1.97 us  [body(): lax.all_to_all(slab, 'blk', split_axis=0, concat_axis=0, tiled=True)]
    unnamed x18, local copies, waits for them, and re-layouts: 0.05 us -> 0.55 us
    all_to_all x1, waiting for transfers between devices: 0.29 us -> 0.69 us  [body(): recv = lax.all_to_all(slab, 'blk', split_axis=0, concat_axis=0, tiled=True)]
    pallas_call x1, Pallas kernels: 1.72 us -> 1.35 us  [body(): call(functools.partial(second_kernel, planes), [(blocks, EDGE_AT + ROWS,...]
  transfers between devices with their start and end apart: 6 -> 6, of which waited for: 3 -> 3; matrix products, arithmetic and copies ran while one was open for 0% -> 0% of each run, Pallas kernels for 29% -> 22%
where the time goes in v10:
time: 32.7 us; the launch traced here: 32.3 us
  starting transfers between devices  15.3 us (47%)
  Pallas kernels  12.2 us (37%)
  waiting for transfers between devices  3.49 us (11%)
  between operations  0.82 us (3%)
  local copies, waits for them, and re-layouts  0.55 us (2%)
    all_to_all x1, starting transfers between devices, body(): recv = lax.all_to_all(slab, 'blk', split_axis=0, concat_axis=0, tiled=True)  5.31 us
    pallas_call x3, Pallas kernels, ocean_part(): call(functools.partial(ocean_kernel, ocean_levels, start), [(ocean_planes...  4.29 us
    all_to_all x1, starting transfers between devices, body(): lax.all_to_all(slab, 'blk', split_axis=0, concat_axis=0, tiled=True)  3.36 us
    pallas_call x1, Pallas kernels, body(): call(functools.partial(start_kernel, planes), [(blocks, HEAD, LANES), air...  2.27 us
    ppermute x1, starting transfers between devices, body(): high = lax.ppermute(down, 'face', [(to, source) for source, to in after_me])  2.25 us
    ppermute x1, starting transfers between devices, body(): lax.ppermute(to_before, 'blk', [(to, source) for source, to in onward])  2.24 us
    all_to_all x1, waiting for transfers between devices, body(): lax.all_to_all(slab, 'blk', split_axis=0, concat_axis=0, tiled=True)  1.97 us
    ppermute x1, starting transfers between devices, body(): low = lax.ppermute(up, 'face', after_me)  1.63 us
  transfers between devices with their start and end apart: 6, of which 3 were waited for; matrix products, arithmetic and copies ran while one was open for 0% of the time, Pallas kernels for 22%

profile of v10, /device:TPU:0, one launch (start us, length us, event | category | flops | bytes accessed | tf_op | source)
XLA Modules:
  0.0 32.3 jit_solution(2569770362395736907)
XLA Ops:
  0.6 0.0 copy-start
  0.6 2.3 %start_kernel.1 = (f32[8,8,128]{2,1,0:T(8,128)}, f32[768,128]{1,0:T(8,128)S(1)}, f32[24,128]{1,0:T(8,128)S(1)}, f32[24,128]{1,0:T(8,128)S(1)}, s32[8,128]{1,0:T(...) custom-call(s32[8,128]{1,0:T(8,128)} %bitcast.25, f32[8,128]{1,0:T(8,128)} %bitcast.26, ...), custom_call_target="tpu_custom_call" | custom-call | tf_op jit(solution)/shard_map/start_kernel/pallas_call | solution.py:1056
  2.9 0.0 copy-start.3
  2.9 0.0 copy-start.4
  2.9 5.3 %all-to-all-start = ((f32[8,8,128]{2,1,0:T(8,128)}), f32[8,8,128]{2,1,0:T(8,128)S(1)}, u32[]{:S(2)}, u32[]{:S(2)}) async-start(f32[8,8,128]{2,1,0:T(8,128)} %get-tuple-element.27), calls=%async_computation | async-start | bytes 65536 | tf_op jit(solution)/shard_map/all_to_all | solution.py:1076
  8.3 0.0 copy-start.5
  8.3 0.0 copy-done
  8.3 0.0 copy-start.2
  8.3 0.2 send_kernel.1
  8.5 0.0 copy-start.1
  8.5 0.5 %collective-permute-start = (f32[56,128]{1,0:T(8,128)S(1)}, f32[56,128]{1,0:T(8,128)S(1)}, u32[]{:S(2)}, u32[]{:S(2)}) collective-permute-start(f32[56,128]{1,0:T(8,128)S(1)} %get-tuple-element.31), channel_id=1, source_target_pairs={{0,1},{1,2},{2,3},{3,4},{4,5},{5,6},{6,7},{7,0},{8,9},{9,10},{10,1... | collective-permute-start | bytes 86024 | tf_op jit(solution)/shard_map/ppermute | solution.py:1099
  9.0 2.2 %collective-permute-start.1 = (f32[56,128]{1,0:T(8,128)S(1)}, f32[56,128]{1,0:T(8,128)S(1)}, u32[]{:S(2)}, u32[]{:S(2)}) collective-permute-start(f32[56,128]{1,0:T(8,128)S(1)} %get-tuple-element.32.after_ref), channel_id=1, source_target_pairs={{1,0},{2,1},{3,2},{4,3},{5,4},{6,5},{7,6},{0,7},{9,8},{10,9},{11,1... | collective-permute-start | bytes 86024 | tf_op jit(solution)/shard_map/ppermute | solution.py:1100
  11.3 0.0 copy-done.3
  11.3 0.0 copy-done.4
  11.3 0.0 copy-done.5
  11.3 0.0 copy-start.6
  11.3 0.0 copy-start.7
  11.3 1.1 %ocean_kernel.3.ocean_ref.refs_0_ = f32[32,512]{1,0:T(8,128)S(1)} custom-call(f32[32,2048]{1,0:T(8,128)S(1)} %bitcast.12, f32[6,2048]{1,0:T(8,128)S(1)} %copy-done.3, s32[6,2048]{1,0:T(8,128)S(1)} %copy-done.4, f32[16,128]{1,0:T(8,128)S(1)} %bitcast.21, f32[56,128]{1,0:T(8,128)S(1)} %get-tuple-element.32.after_ref), custom_call_target="tpu_custom_call" | custom-call | bytes 3145728 | tf_op jit(solution)/shard_map/ocean_kernel/pallas_call | solution.py:1083
  12.4 0.7 %all-to-all-done.recv_ref = f32[8,8,128]{2,1,0:T(8,128)S(1)} async-done(((f32[8,8,128]{2,1,0:T(8,128)}), f32[8,8,128]{2,1,0:T(8,128)S(1)}, u32[]{:S(2)}, u32[]{:S(2)}) %all-to-all-start) | async-done | bytes 32800 | tf_op jit(solution)/shard_map/all_to_all | solution.py:1076
  13.1 0.0 collective-permute-done.before_ref
  13.1 0.0 collective-permute-done.1.after_ref
  13.1 0.0 copy-done.2
  13.1 0.0 copy-done.1
  13.1 0.0 copy-done.6
  13.1 0.0 copy-done.7
  13.1 0.5 %panel_kernel.1 = (f32[768,128]{1,0:T(8,128)S(1)}, f32[144,128]{1,0:T(8,128)S(1)}, f32[144,128]{1,0:T(8,128)S(1)}, f32[192,128]{1,0:T(8,128)S(1)}) custom-call(f32[768,128]{1,0:T(8,128)S(1)} %get-tuple-element.26.moved_ref, f32[8,8,128]{2,1,0:T(8,128)S(1)} %all-to-all-done.recv_ref, f32[56,128]{1,0:T(8,128)S(1)} %collective-permute-done.before_ref, ...), custom_call_target="tpu_custom_call" | custom-call | tf_op jit(solution)/shard_map/panel_kernel/pallas_call | solution.py:1103
  13.6 1.6 %collective-permute-start.2 = (f32[144,128]{1,0:T(8,128)S(1)}, f32[144,128]{1,0:T(8,128)S(1)}, u32[]{:S(2)}, u32[]{:S(2)}) collective-permute-start(f32[144,128]{1,0:T(8,128)S(1)} %get-tuple-element.38), channel_id=1, source_target_pairs={{0,8},{8,16},{16,24},{24,0},{1,9},{9,17},{17,25},{25,1},{2,10},{10... | collective-permute-start | bytes 221192 | tf_op jit(solution)/shard_map/ppermute | solution.py:1120
  15.3 2.2 %collective-permute-start.3 = (f32[144,128]{1,0:T(8,128)S(1)}, f32[144,128]{1,0:T(8,128)S(1)}, u32[]{:S(2)}, u32[]{:S(2)}) collective-permute-start(f32[144,128]{1,0:T(8,128)S(1)} %get-tuple-element.39), channel_id=1, source_target_pairs={{8,0},{16,8},{24,16},{0,24},{9,1},{17,9},{25,17},{1,25},{10,2},{18... | collective-permute-start | bytes 221192 | tf_op jit(solution)/shard_map/ppermute | solution.py:1121
  17.5 2.1 %ocean_kernel.4.ocean_ref.refs_1_ = f32[32,1024]{1,0:T(8,128)S(1)} custom-call(f32[32,2048]{1,0:T(8,128)S(1)} %bitcast.13, f32[6,2048]{1,0:T(8,128)S(1)} %copy-done.3, s32[6,2048]{1,0:T(8,128)S(1)} %copy-done.4, f32[16,128]{1,0:T(8,128)S(1)} %bitcast.22, f32[192,128]{1,0:T(8,128)S(1)} %get-tuple-element.35.surf_ref.after_ref), custom_call_target="tpu_custom_call" | custom-call | bytes 6291456 | tf_op jit(solution)/shard_map/ocean_kernel/pallas_call | solution.py:1083
  19.6 1.1 %inner_kernel.1 = (f32[384,128]{1,0:T(8,128)S(1)}, f32[16,128]{1,0:T(8,128)S(1)}) custom-call(f32[768,128]{1,0:T(8,128)S(1)} %get-tuple-element.34.avg_ref, f32[768,128]{1,0:T(8,128)S(1)} %get-tuple-element.26.moved_ref, f32[56,128]{1,0:T(8,128)S(1)} %collective-permute-done.before_ref, f32[56,128]{1,0:T(8,128)S(1)} %collective-permute-done.1.after_ref, ...), custom_call_target="tpu_custom_call" | custom-call | bytes 786432 | tf_op jit(solution)/shard_map/inner_kernel/pallas_call | solution.py:1122
  20.8 0.0 collective-permute-done.2.low_ref
  20.8 0.8 %collective-permute-done.3.high_ref = f32[144,128]{1,0:T(8,128)S(1)} collective-permute-done((f32[144,128]{1,0:T(8,128)S(1)}, f32[144,128]{1,0:T(8,128)S(1)}, u32[]{:S(2)}, u32[]{:S(2)}) %collective-permute-start.3) | collective-permute-done | bytes 73760 | tf_op jit(solution)/shard_map/ppermute | solution.py:1121
  21.6 1.4 %second_kernel.1 = (f32[8,16,128]{2,1,0:T(8,128)}, f32[480,128]{1,0:T(8,128)S(1)}, f32[16,128]{1,0:T(8,128)S(1)}, f32[16,128]{1,0:T(8,128)S(1)}) custom-call(f32[768,128]{1,0:T(8,128)S(1)} %get-tuple-element.34.avg_ref, f32[384,128]{1,0:T(8,128)S(1)} %get-tuple-element.36.inner_ref, f32[16,128]{1,0:T(8,128)S(1)} %get-tuple-element.37.packs_ref, ...), custom_call_target="tpu_custom_call" | custom-call | tf_op jit(solution)/shard_map/second_kernel/pallas_call | solution.py:1130
  23.0 3.4 %all-to-all-start.1 = ((f32[8,16,128]{2,1,0:T(8,128)}), f32[8,16,128]{2,1,0:T(8,128)S(1)}, u32[]{:S(2)}, u32[]{:S(2)}) async-start(f32[8,16,128]{2,1,0:T(8,128)} %get-tuple-element.42), calls=%async_computation.1 | async-start | bytes 131072 | tf_op jit(solution)/shard_map/all_to_all | solution.py:1146
  26.3 1.1 %ocean_kernel.5.refs_2_ = f32[32,512]{1,0:T(8,128)S(1)} custom-call(f32[32,2048]{1,0:T(8,128)S(1)} %bitcast.14, f32[6,2048]{1,0:T(8,128)S(1)} %copy-done.3, s32[6,2048]{1,0:T(8,128)S(1)} %copy-done.4, f32[16,128]{1,0:T(8,128)S(1)} %bitcast.23, f32[16,128]{1,0:T(8,128)S(1)} %get-tuple-element.43.after_ref.rows_ref.final_ref), custom_call_target="tpu_custom_call" | custom-call | bytes 3145728 | tf_op jit(solution)/shard_map/ocean_kernel/pallas_call | solution.py:1083
  27.4 0.0 copy-start.8
  27.4 0.2 last_kernel.1.last_ref
  27.6 0.5 %copy-done.8 = f32[2048]{0:T(1024)S(1)} copy-done((f32[2048]{0:T(1024)S(1)}, f32[2048]{0:T(1024)}, u32[]{:S(2)}) %copy-start.8) | copy-done | bytes 8216
  28.1 1.2 %rim_kernel.1 = (f32[32,2048]{1,0:T(8,128)S(1)}, f32[16,128]{1,0:T(8,128)S(1)}) custom-call(f32[56,128]{1,0:T(8,128)S(1)} %collective-permute-done.before_ref, f32[56,128]{1,0:T(8,128)S(1)} %collective-permute-done.1.after_ref, f32[6,2048]{1,0:T(8,128)S(1)} %copy-done.3, s32[6,2048]{1,0:T(8,128)S(1)} %copy-done.4, f32[16,128]{1,0:T(8,128)S(1)} %bitcast.24, ...), custom_call_target="tpu_custom_call" | custom-call | bytes 3145728 | tf_op jit(solution)/shard_map/rim_kernel/pallas_call | solution.py:1154
  29.3 2.0 %all-to-all-done.1.recv_ref = f32[8,16,128]{2,1,0:T(8,128)S(1)} async-done(((f32[8,16,128]{2,1,0:T(8,128)}), f32[8,16,128]{2,1,0:T(8,128)S(1)}, u32[]{:S(2)}, u32[]{:S(2)}) %all-to-all-start.1) | async-done | bytes 65568 | tf_op jit(solution)/shard_map/all_to_all | solution.py:1146
  31.3 1.1 %end_kernel.1 = (f32[768,128]{1,0:T(8,128)}, f32[32,2048]{1,0:T(8,128)}) custom-call(f32[768,128]{1,0:T(8,128)S(1)} %last_kernel.1.last_ref, f32[8,16,128]{2,1,0:T(8,128)S(1)} %all-to-all-done.1.recv_ref, f32[16,128]{1,0:T(8,128)S(1)} %get-tuple-element.43.after_ref.rows_ref.final_ref, f32[16,128]{1,0:T(8,128)S(1)} %get-tuple-element.41.inverse_ref, ...), custom_call_target="tpu_custom_call" | custom-call | tf_op jit(solution)/shard_map/end_kernel/pallas_call | solution.py:1170
Async XLA Ops:
  0.6 7.6 %copy-start = (f32[2,16,2048]{2,1,0:T(8,128)S(1)}, f32[2,16,2048]{2,1,0:T(8,128)}, u32[]{:S(2)}) copy-start(f32[2,16,2048]{2,1,0:T(8,128)} %param.18) | copy-start | bytes 786436
  2.9 8.4 %copy-start.3 = (f32[6,2048]{1,0:T(8,128)S(1)}, f32[6,2048]{1,0:T(8,128)}, u32[]{:S(2)}) copy-start(f32[6,2048]{1,0:T(8,128)} %coef_ref.7) | copy-start | bytes 147460
  2.9 8.4 %copy-start.4 = (s32[6,2048]{1,0:T(8,128)S(1)}, s32[6,2048]{1,0:T(8,128)}, u32[]{:S(2)}) copy-start(s32[6,2048]{1,0:T(8,128)} %near_ref.7) | copy-start | bytes 147460
  2.9 10.2 %all-to-all-start = ((f32[8,8,128]{2,1,0:T(8,128)}), f32[8,8,128]{2,1,0:T(8,128)S(1)}, u32[]{:S(2)}, u32[]{:S(2)}) async-start(f32[8,8,128]{2,1,0:T(8,128)} %get-tuple-element.27), calls=%async_computation | async-start | bytes 65536 | tf_op jit(solution)/shard_map/all_to_all | solution.py:1076
  8.3 3.0 %copy-start.5 = (f32[2048]{0:T(1024)S(1)}, f32[2048]{0:T(1024)}, u32[]{:S(2)}) copy-start(f32[2048]{0:T(1024)} %param.21) | copy-start | bytes 24580
  8.3 4.8 %copy-start.2 = (f32[3,16,16,128]{3,2,1,0:T(8,128)S(1)}, f32[3,16,16,128]{3,2,1,0:T(8,128)}, u32[]{:S(2)}) copy-start(f32[3,16,16,128]{3,2,1,0:T(8,128)} %param.13) | copy-start | bytes 1179652
  8.5 4.6 %copy-start.1 = (f32[2,16,16,128]{3,2,1,0:T(8,128)S(1)}, f32[2,16,16,128]{3,2,1,0:T(8,128)}, u32[]{:S(2)}) copy-start(f32[2,16,16,128]{3,2,1,0:T(8,128)} %param.14) | copy-start | bytes 786436
  8.5 4.6 %collective-permute-start = (f32[56,128]{1,0:T(8,128)S(1)}, f32[56,128]{1,0:T(8,128)S(1)}, u32[]{:S(2)}, u32[]{:S(2)}) collective-permute-start(f32[56,128]{1,0:T(8,128)S(1)} %get-tuple-element.31), channel_id=1, source_target_pairs={{0,1},{1,2},{2,3},{3,4},{4,5},{5,6},{6,7},{7,0},{8,9},{9,10},{10,1... | collective-permute-start | bytes 86024 | tf_op jit(solution)/shard_map/ppermute | solution.py:1099
  9.0 4.1 %collective-permute-start.1 = (f32[56,128]{1,0:T(8,128)S(1)}, f32[56,128]{1,0:T(8,128)S(1)}, u32[]{:S(2)}, u32[]{:S(2)}) collective-permute-start(f32[56,128]{1,0:T(8,128)S(1)} %get-tuple-element.32.after_ref), channel_id=1, source_target_pairs={{1,0},{2,1},{3,2},{4,3},{5,4},{6,5},{7,6},{0,7},{9,8},{10,9},{11,1... | collective-permute-start | bytes 86024 | tf_op jit(solution)/shard_map/ppermute | solution.py:1100
  11.3 1.8 %copy-start.6 = (f32[16,128]{1,0:T(8,128)S(1)}, f32[16,128]{1,0:T(8,128)}, u32[]{:S(2)}) copy-start(f32[16,128]{1,0:T(8,128)} %jac_ref.1) | copy-start | bytes 24580
  11.3 1.8 %copy-start.7 = (f32[16,128]{1,0:T(8,128)S(1)}, f32[16,128]{1,0:T(8,128)}, u32[]{:S(2)}) copy-start(f32[16,128]{1,0:T(8,128)} %land_ref.1) | copy-start | bytes 24580
  13.6 7.1 %collective-permute-start.2 = (f32[144,128]{1,0:T(8,128)S(1)}, f32[144,128]{1,0:T(8,128)S(1)}, u32[]{:S(2)}, u32[]{:S(2)}) collective-permute-start(f32[144,128]{1,0:T(8,128)S(1)} %get-tuple-element.38), channel_id=1, source_target_pairs={{0,8},{8,16},{16,24},{24,0},{1,9},{9,17},{17,25},{25,1},{2,10},{10... | collective-permute-start | bytes 221192 | tf_op jit(solution)/shard_map/ppermute | solution.py:1120
  15.3 6.3 %collective-permute-start.3 = (f32[144,128]{1,0:T(8,128)S(1)}, f32[144,128]{1,0:T(8,128)S(1)}, u32[]{:S(2)}, u32[]{:S(2)}) collective-permute-start(f32[144,128]{1,0:T(8,128)S(1)} %get-tuple-element.39), channel_id=1, source_target_pairs={{8,0},{16,8},{24,16},{0,24},{9,1},{17,9},{25,17},{1,25},{10,2},{18... | collective-permute-start | bytes 221192 | tf_op jit(solution)/shard_map/ppermute | solution.py:1121
  23.0 8.3 %all-to-all-start.1 = ((f32[8,16,128]{2,1,0:T(8,128)}), f32[8,16,128]{2,1,0:T(8,128)S(1)}, u32[]{:S(2)}, u32[]{:S(2)}) async-start(f32[8,16,128]{2,1,0:T(8,128)} %get-tuple-element.42), calls=%async_computation.1 | async-start | bytes 131072 | tf_op jit(solution)/shard_map/all_to_all | solution.py:1146
  27.4 0.7 %copy-start.8 = (f32[2048]{0:T(1024)S(1)}, f32[2048]{0:T(1024)}, u32[]{:S(2)}) copy-start(f32[2048]{0:T(1024)} %param.22) | copy-start | bytes 24580

commit v11 on v10

--- a/solution.py
+++ b/solution.py
@@ -175,33 +175,40 @@
     return lax.rem(here + blocks - 1, blocks), lax.rem(here + 1, blocks)
 
 
-def scatter_sum(lines, index, bins, allowed=None):
-    count = index.shape[0]
+def one_hot(index, allowed=None):
+    low = index & (LANES - 1)
+    lane_at = iota((LANES, LANES), 0)
+    if allowed is not None:
+        lane_at = jnp.where(allowed(lane_at), lane_at, -1)
+    return jnp.concatenate(
+        [
+            jnp.where(lane_at == low[c : c + 1], 1.0, 0.0).astype(jnp.bfloat16)
+            for c in range(index.shape[0])
+        ],
+        axis=1,
+    )
+
+
+def scatter_sum(lines, index, bins, lanes_hot):
     split = []
     for values in lines:
         for part in range(3):
             short = values.astype(jnp.bfloat16).astype(jnp.float32)
             split.append(short)
             values = values - short
-    high, low = index >> 7, index & (LANES - 1)
+    high = index >> 7
     bin_at = iota((bins, LANES), 0)
-    lane_at = iota((LANES, LANES), 0)
-    if allowed is not None:
-        lane_at = jnp.where(allowed(lane_at), lane_at, -1)
-    left, right = [], []
-    for c in range(count):
+    left = []
+    for c in range(index.shape[0]):
         hit = bin_at == high[c : c + 1]
         left.append(
             jnp.concatenate(
                 [jnp.where(hit, part[c : c + 1], 0.0) for part in split], axis=0
             ).astype(jnp.bfloat16)
         )
-        right.append(
-            jnp.where(lane_at == low[c : c + 1], 1.0, 0.0).astype(jnp.bfloat16)
-        )
     total = lax.dot_general(
         jnp.concatenate(left, axis=1),
-        jnp.concatenate(right, axis=1),
+        lanes_hot,
         (((1,), (1,)), ((), ())),
         preferred_element_type=jnp.float32,
     )
@@ -386,11 +393,13 @@
         jnp.concatenate([recv_ref[c, i : i + 1, :] for c in range(blocks)], axis=0)
         for i in range(6)
     ]
-    heat, frac = scatter_sum(head[2:4], own_ids, 2 * ROWS)
+    heat, frac = scatter_sum(head[2:4], own_ids, 2 * ROWS, one_hot(own_ids))
     from_left = scatter_sum(
-        head[0:2], left_ids, 2 * ROWS, lambda lane: lane >= LANES - ROWS
-    )
-    from_right = scatter_sum(head[4:6], right_ids, 2 * ROWS, lambda lane: lane < ROWS)
+        head[0:2], left_ids, 2 * ROWS, one_hot(left_ids, lambda lane: lane >= LANES - ROWS)
+    )
+    from_right = scatter_sum(
+        head[4:6], right_ids, 2 * ROWS, one_hot(right_ids, lambda lane: lane < ROWS)
+    )
     strip_heat = from_left[0] + from_right[0]
     strip_frac = from_left[1] + from_right[1]
 
@@ -682,11 +691,6 @@
             picked = jnp.where(high == x, take(line, low, 1), picked)
         for c in range(ROWS):
             flux_ref[ROWS * group + c, 0:1, :] = picked[c : c + 1]
-
-    copies = [
-        pltpu.make_async_copy(flux_ref, slab_out.at[:, :HEAD], semaphores.at[0])
-    ]
-    copies[0].start()
 
     kept = outer_rows(x_points)
 
@@ -749,24 +753,28 @@
     packs = [packs_ref[:ROWS, :], packs_ref[ROWS:, :]]
     packs = edges_of(geo, packs, sums_ref, planes, kept)
     to_right, to_left = split_sides(geo, packs[0], packs[1], 1)
-    for i, (to, edges) in enumerate(((right, to_right), (left, to_left))):
-        edges_ref[i] = edges
-        copies.append(
-            pltpu.make_async_copy(
-                edges_ref.at[i],
-                slab_out.at[to, EDGE_AT : EDGE_AT + ROWS],
-                semaphores.at[1 + i],
-            )
-        )
-        copies[-1].start()
+    edges_ref[0] = to_right
+    edges_ref[1] = to_left
+    copies = [
+        pltpu.make_async_copy(
+            edges_ref.at[i], slab_out.at[to, EDGE_AT : EDGE_AT + ROWS], semaphores.at[i]
+        )
+        for i, to in enumerate((right, left))
+    ]
+    copies.append(
+        pltpu.make_async_copy(flux_ref, slab_out.at[:, :HEAD], semaphores.at[2])
+    )
+    for copy in copies:
+        copy.start()
     for copy in copies:
         copy.wait()
 
 
-def last_kernel(planes, inner_ref, outer_ref, inverse_ref, out_ref):
+def last_kernel(planes, inner_ref, outer_ref, inverse_ref, cols_ref, out_ref, hot_ref):
     geo = Geometry()
     x_points = inverse_ref.shape[0]
     kept = outer_rows(x_points)
+    hot_ref[...] = one_hot(cols_ref[...])
     for x in range(x_points):
         inverse = spread(inverse_ref[x : x + 1, :])
         ref, first = inner_ref, planes * (x - GLL)
@@ -785,13 +793,15 @@
     final_ref,
     inverse_ref,
     cols_ref,
+    hot_ref,
     weights_ref,
     gain_ref,
-    ocean_ref,
+    first_ref,
+    ocean_in,
+    ocean_out,
     air_out,
-    ocean_out,
     air_ref,
-    first_ref,
+    row_ref,
     semaphores,
 ):
     geo = Geometry()
@@ -807,22 +817,13 @@
         )
         copies[-1].start()
 
-    send(ocean_ref.at[ROWS:], ocean_out.at[ROWS:])
-    arrived = jnp.concatenate([recv_ref[c, 0:1, :] for c in range(blocks)], axis=0)
-    (inflow,) = scatter_sum([weights_ref[...] * arrived], cols_ref[...], chunks)
-    gain = inflow * gain_ref[...]
-    first_ref[...] = ocean_ref[:ROWS, :]
-    for k in range(chunks):
-        at = slice(LANES * k, LANES * (k + 1))
-        first_ref[0:1, at] = ocean_ref[0:1, at] + gain[k : k + 1]
-    send(first_ref, ocean_out.at[:ROWS])
-
     joined = join_edges(
         geo,
         recv_ref[left, EDGE_AT : EDGE_AT + ROWS, :],
         recv_ref[right, EDGE_AT : EDGE_AT + ROWS, :],
     )
-    for group in range(planes // ROWS):
+    groups = planes // ROWS
+    for group in range(groups):
         for x in range(x_points):
             at = planes * x + ROWS * group
             beside = spread(inverse_ref[x : x + 1, :]) * outer_edges(joined, x, group)
@@ -831,8 +832,25 @@
             ] + jnp.where(geo.outer_lane, beside, 0.0)
         if group == 0:
             air_ref[0:x_points, :] = final_ref[...]
-        rows = slice(ROWS * group * x_points, ROWS * (group + 1) * x_points)
+        if group % 2:
+            rows = slice(
+                ROWS * (group - 1) * x_points, ROWS * (group + 1) * x_points
+            )
+            send(air_ref.at[rows], air_out.at[rows])
+    if groups % 2:
+        rows = slice(ROWS * (groups - 1) * x_points, planes * x_points)
         send(air_ref.at[rows], air_out.at[rows])
+
+    arrived = jnp.concatenate([recv_ref[c, 0:1, :] for c in range(blocks)], axis=0)
+    (inflow,) = scatter_sum(
+        [weights_ref[...] * arrived], cols_ref[...], chunks, hot_ref[...]
+    )
+    gain = inflow * gain_ref[...]
+    row_ref[...] = first_ref[...]
+    for k in range(chunks):
+        at = slice(LANES * k, LANES * (k + 1))
+        row_ref[0:1, at] = first_ref[0:1, at] + gain[k : k + 1]
+    send(row_ref, ocean_out.at[:ROWS])
     for copy in copies:
         copy.wait()
 
@@ -967,7 +985,7 @@
     rows_ref,
     *refs,
 ):
-    partial_refs, (out_ref, gain_ref) = refs[: len(starts)], refs[len(starts) :]
+    partial_refs, (out_ref, gain_ref, first_ref) = refs[: len(starts)], refs[len(starts) :]
     chunks = coef_ref.shape[1] // LANES
     groups = out_ref.shape[0] // ROWS
     rim_at = before_ref.shape[0] - out_ref.shape[0]
@@ -986,6 +1004,7 @@
         for g in range(groups):
             half = slice(ROWS * g, ROWS * (g + 1))
             out_ref[half, at] = partial_refs[part][half, place] + totals[g]
+    first_ref[...] = out_ref[:ROWS, :]
 
 
 VMEM_SPEC = pl.BlockSpec(memory_space=pltpu.VMEM)
@@ -993,7 +1012,7 @@
 HBM_SPEC = pl.BlockSpec(memory_space=pltpu.HBM)
 
 
-def call(kernel, outs, specs, scratch=(), cost=0, hbm_outs=0):
+def call(kernel, outs, specs, scratch=(), cost=0, hbm_outs=0, aliases=None):
     estimate = None
     if cost:
         estimate = pl.CostEstimate(flops=0, bytes_accessed=cost, transcendentals=0)
@@ -1009,6 +1028,7 @@
         in_specs=specs,
         out_specs=out_specs,
         scratch_shapes=list(scratch),
+        input_output_aliases=aliases or {},
         cost_estimate=estimate,
         compiler_params=pltpu.CompilerParams(vmem_limit_bytes=32 * 2**20),
         name=getattr(kernel, "func", kernel).__name__,
@@ -1144,16 +1164,16 @@
         hbm_outs=1,
     )(avg, inner, packs, surf, low, high, wind, point_ids, second_part)
     arrived = lax.all_to_all(slab, "blk", split_axis=0, concat_axis=0, tiled=True)
-    (last,) = call(
+    last, hot = call(
         functools.partial(last_kernel, planes),
-        [air.shape],
-        [VMEM_SPEC] * 3,
+        [air.shape, jax.ShapeDtypeStruct((LANES, blocks * LANES), jnp.bfloat16)],
+        [VMEM_SPEC] * 4,
         cost=2 * air.size * 4,
-    )(inner, outer, inverse)
+    )(inner, outer, inverse, cell_ids)
     third_part = ocean_part(starts[2], chunks, final)
-    partial, gain = call(
+    partial, gain, first_rows = call(
         functools.partial(rim_kernel, starts),
-        [ocean.shape, area.shape],
+        [ocean.shape, area.shape, (ROWS, cells)],
         [VMEM_SPEC] * 5 + [ANY_SPEC] + [VMEM_SPEC] * len(starts),
         cost=chunks * reads_per_chunk // 8 * ROWS * LANES * 4,
     )(
@@ -1167,17 +1187,29 @@
         second_part,
         third_part,
     )
-    air_final, ocean_final = call(
+    ocean_final, air_final = call(
         functools.partial(end_kernel, planes),
-        [air.shape, ocean.shape],
-        [VMEM_SPEC] * 8,
+        [ocean.shape, air.shape],
+        [VMEM_SPEC] * 9 + [HBM_SPEC],
         [
             pltpu.VMEM(air.shape, jnp.float32),
             pltpu.VMEM((ROWS, cells), jnp.float32),
-            pltpu.SemaphoreType.DMA((2 + planes // ROWS,)),
+            pltpu.SemaphoreType.DMA((1 + planes // ROWS,)),
         ],
         hbm_outs=2,
-    )(last, arrived, final, inverse, cell_ids, weights, gain, partial)
+        aliases={9: 0},
+    )(
+        last,
+        arrived,
+        final,
+        inverse,
+        cell_ids,
+        hot,
+        weights,
+        gain,
+        first_rows,
+        pltpu.with_memory_space_constraint(partial, pltpu.HBM),
+    )
     return air_final.reshape(air_state.shape), ocean_final.reshape(tracers.shape)
 
 

time: 32.7 us -> 32.7 us (level)
  waiting for transfers between devices: 3.49 us -> 2.77 us
  Pallas kernels: 12.2 us -> 12.9 us
    all_to_all x1, waiting for transfers between devices: 1.97 us -> 1.26 us  [body(): lax.all_to_all(slab, 'blk', split_axis=0, concat_axis=0, tiled=True)]
    pallas_call x3, Pallas kernels: 2.43 us -> 3.13 us  [the longest x1 1.9 us: body(): call(functools.partial(rim_kernel, starts), [ocean.shape, area.shape, (RO...]
  transfers between devices with their start and end apart: 6 -> 6, of which waited for: 3 -> 3; matrix products, arithmetic and copies ran while one was open for 0% -> 0% of each run, Pallas kernels for 22% -> 24%
where the time goes in v11:
time: 32.7 us; the launch traced here: 32.3 us
  starting transfers between devices  15.3 us (47%)
  Pallas kernels  12.9 us (39%)
  waiting for transfers between devices  2.77 us (8%)
  between operations  0.82 us (3%)
  local copies, waits for them, and re-layouts  0.53 us (2%)
    all_to_all x1, starting transfers between devices, body(): recv = lax.all_to_all(slab, 'blk', split_axis=0, concat_axis=0, tiled=True)  5.31 us
    pallas_call x3, Pallas kernels, ocean_part(): call(functools.partial(ocean_kernel, ocean_levels, start), [(ocean_planes...  4.29 us
    all_to_all x1, starting transfers between devices, body(): lax.all_to_all(slab, 'blk', split_axis=0, concat_axis=0, tiled=True)  3.36 us
    pallas_call x1, Pallas kernels, body(): call(functools.partial(start_kernel, planes), [(blocks, HEAD, LANES), air...  2.27 us
    ppermute x1, starting transfers between devices, body(): high = lax.ppermute(down, 'face', [(to, source) for source, to in after_me])  2.25 us
    ppermute x1, starting transfers between devices, body(): lax.ppermute(to_before, 'blk', [(to, source) for source, to in onward])  2.24 us
    pallas_call x1, Pallas kernels, body(): call(functools.partial(rim_kernel, starts), [ocean.shape, area.shape, (RO...  1.9 us
    ppermute x1, starting transfers between devices, body(): low = lax.ppermute(up, 'face', after_me)  1.63 us
  transfers between devices with their start and end apart: 6, of which 3 were waited for; matrix products, arithmetic and copies ran while one was open for 0% of the time, Pallas kernels for 24%

profile of v11, /device:TPU:0, one launch (start us, length us, event | category | flops | bytes accessed | tf_op | source)
XLA Modules:
  0.0 32.3 jit_solution(592128344247630877)
XLA Ops:
  0.6 0.0 copy-start
  0.6 2.3 %start_kernel.1 = (f32[8,8,128]{2,1,0:T(8,128)}, f32[768,128]{1,0:T(8,128)S(1)}, f32[24,128]{1,0:T(8,128)S(1)}, f32[24,128]{1,0:T(8,128)S(1)}, s32[8,128]{1,0:T(...) custom-call(s32[8,128]{1,0:T(8,128)} %bitcast.26, f32[8,128]{1,0:T(8,128)} %bitcast.27, ...), custom_call_target="tpu_custom_call" | custom-call | tf_op jit(solution)/shard_map/start_kernel/pallas_call | solution.py:1076
  2.9 0.0 copy-start.3
  2.9 0.0 copy-start.4
  2.9 5.3 %all-to-all-start = ((f32[8,8,128]{2,1,0:T(8,128)}), f32[8,8,128]{2,1,0:T(8,128)S(1)}, u32[]{:S(2)}, u32[]{:S(2)}) async-start(f32[8,8,128]{2,1,0:T(8,128)} %get-tuple-element.30), calls=%async_computation | async-start | bytes 65536 | tf_op jit(solution)/shard_map/all_to_all | solution.py:1096
  8.3 0.0 copy-start.5
  8.3 0.0 copy-done
  8.3 0.0 copy-start.2
  8.3 0.2 send_kernel.1
  8.5 0.0 copy-start.1
  8.5 0.5 %collective-permute-start = (f32[56,128]{1,0:T(8,128)S(1)}, f32[56,128]{1,0:T(8,128)S(1)}, u32[]{:S(2)}, u32[]{:S(2)}) collective-permute-start(f32[56,128]{1,0:T(8,128)S(1)} %get-tuple-element.34), channel_id=1, source_target_pairs={{0,1},{1,2},{2,3},{3,4},{4,5},{5,6},{6,7},{7,0},{8,9},{9,10},{10,1... | collective-permute-start | bytes 86024 | tf_op jit(solution)/shard_map/ppermute | solution.py:1119
  9.0 2.2 %collective-permute-start.1 = (f32[56,128]{1,0:T(8,128)S(1)}, f32[56,128]{1,0:T(8,128)S(1)}, u32[]{:S(2)}, u32[]{:S(2)}) collective-permute-start(f32[56,128]{1,0:T(8,128)S(1)} %get-tuple-element.35.after_ref), channel_id=1, source_target_pairs={{1,0},{2,1},{3,2},{4,3},{5,4},{6,5},{7,6},{0,7},{9,8},{10,9},{11,1... | collective-permute-start | bytes 86024 | tf_op jit(solution)/shard_map/ppermute | solution.py:1120
  11.3 0.0 copy-done.3
  11.3 0.0 copy-done.4
  11.3 0.0 copy-done.5
  11.3 0.0 copy-start.6
  11.3 0.0 copy-start.7
  11.3 1.1 %ocean_kernel.3.ocean_ref.refs_0_ = f32[32,512]{1,0:T(8,128)S(1)} custom-call(f32[32,2048]{1,0:T(8,128)S(1)} %bitcast.12, f32[6,2048]{1,0:T(8,128)S(1)} %copy-done.3, s32[6,2048]{1,0:T(8,128)S(1)} %copy-done.4, f32[16,128]{1,0:T(8,128)S(1)} %bitcast.21, f32[56,128]{1,0:T(8,128)S(1)} %get-tuple-element.35.after_ref), custom_call_target="tpu_custom_call" | custom-call | bytes 3145728 | tf_op jit(solution)/shard_map/ocean_kernel/pallas_call | solution.py:1103
  12.4 0.7 %all-to-all-done.recv_ref = f32[8,8,128]{2,1,0:T(8,128)S(1)} async-done(((f32[8,8,128]{2,1,0:T(8,128)}), f32[8,8,128]{2,1,0:T(8,128)S(1)}, u32[]{:S(2)}, u32[]{:S(2)}) %all-to-all-start) | async-done | bytes 32800 | tf_op jit(solution)/shard_map/all_to_all | solution.py:1096
  13.1 0.0 collective-permute-done.before_ref
  13.1 0.0 collective-permute-done.1.after_ref
  13.1 0.0 copy-done.2
  13.1 0.0 copy-done.1
  13.1 0.0 copy-done.6
  13.1 0.0 copy-done.7
  13.1 0.5 %panel_kernel.1 = (f32[768,128]{1,0:T(8,128)S(1)}, f32[144,128]{1,0:T(8,128)S(1)}, f32[144,128]{1,0:T(8,128)S(1)}, f32[192,128]{1,0:T(8,128)S(1)}) custom-call(f32[768,128]{1,0:T(8,128)S(1)} %get-tuple-element.29.moved_ref, f32[8,8,128]{2,1,0:T(8,128)S(1)} %all-to-all-done.recv_ref, f32[56,128]{1,0:T(8,128)S(1)} %collective-permute-done.before_ref, ...), custom_call_target="tpu_custom_call" | custom-call | tf_op jit(solution)/shard_map/panel_kernel/pallas_call | solution.py:1123
  13.6 1.6 %collective-permute-start.2 = (f32[144,128]{1,0:T(8,128)S(1)}, f32[144,128]{1,0:T(8,128)S(1)}, u32[]{:S(2)}, u32[]{:S(2)}) collective-permute-start(f32[144,128]{1,0:T(8,128)S(1)} %get-tuple-element.41), channel_id=1, source_target_pairs={{0,8},{8,16},{16,24},{24,0},{1,9},{9,17},{17,25},{25,1},{2,10},{10... | collective-permute-start | bytes 221192 | tf_op jit(solution)/shard_map/ppermute | solution.py:1140
  15.3 2.2 %collective-permute-start.3 = (f32[144,128]{1,0:T(8,128)S(1)}, f32[144,128]{1,0:T(8,128)S(1)}, u32[]{:S(2)}, u32[]{:S(2)}) collective-permute-start(f32[144,128]{1,0:T(8,128)S(1)} %get-tuple-element.42), channel_id=1, source_target_pairs={{8,0},{16,8},{24,16},{0,24},{9,1},{17,9},{25,17},{1,25},{10,2},{18... | collective-permute-start | bytes 221192 | tf_op jit(solution)/shard_map/ppermute | solution.py:1141
  17.5 2.1 %ocean_kernel.4.ocean_ref.refs_1_ = f32[32,1024]{1,0:T(8,128)S(1)} custom-call(f32[32,2048]{1,0:T(8,128)S(1)} %bitcast.13, f32[6,2048]{1,0:T(8,128)S(1)} %copy-done.3, s32[6,2048]{1,0:T(8,128)S(1)} %copy-done.4, f32[16,128]{1,0:T(8,128)S(1)} %bitcast.22, f32[192,128]{1,0:T(8,128)S(1)} %get-tuple-element.38.surf_ref.after_ref), custom_call_target="tpu_custom_call" | custom-call | bytes 6291456 | tf_op jit(solution)/shard_map/ocean_kernel/pallas_call | solution.py:1103
  19.6 1.1 %inner_kernel.1 = (f32[384,128]{1,0:T(8,128)S(1)}, f32[16,128]{1,0:T(8,128)S(1)}) custom-call(f32[768,128]{1,0:T(8,128)S(1)} %get-tuple-element.37.avg_ref, f32[768,128]{1,0:T(8,128)S(1)} %get-tuple-element.29.moved_ref, f32[56,128]{1,0:T(8,128)S(1)} %collective-permute-done.before_ref, f32[56,128]{1,0:T(8,128)S(1)} %collective-permute-done.1.after_ref, ...), custom_call_target="tpu_custom_call" | custom-call | bytes 786432 | tf_op jit(solution)/shard_map/inner_kernel/pallas_call | solution.py:1142
  20.8 0.0 collective-permute-done.2.low_ref
  20.8 0.8 %collective-permute-done.3.high_ref = f32[144,128]{1,0:T(8,128)S(1)} collective-permute-done((f32[144,128]{1,0:T(8,128)S(1)}, f32[144,128]{1,0:T(8,128)S(1)}, u32[]{:S(2)}, u32[]{:S(2)}) %collective-permute-start.3) | collective-permute-done | bytes 73760 | tf_op jit(solution)/shard_map/ppermute | solution.py:1141
  21.6 1.4 %second_kernel.1 = (f32[8,16,128]{2,1,0:T(8,128)}, f32[480,128]{1,0:T(8,128)S(1)}, f32[16,128]{1,0:T(8,128)S(1)}, f32[16,128]{1,0:T(8,128)S(1)}) custom-call(f32[768,128]{1,0:T(8,128)S(1)} %get-tuple-element.37.avg_ref, f32[384,128]{1,0:T(8,128)S(1)} %get-tuple-element.39.inner_ref, f32[16,128]{1,0:T(8,128)S(1)} %get-tuple-element.40.packs_ref, ...), custom_call_target="tpu_custom_call" | custom-call | tf_op jit(solution)/shard_map/second_kernel/pallas_call | solution.py:1150
  23.0 3.4 %all-to-all-start.1 = ((f32[8,16,128]{2,1,0:T(8,128)}), f32[8,16,128]{2,1,0:T(8,128)S(1)}, u32[]{:S(2)}, u32[]{:S(2)}) async-start(f32[8,16,128]{2,1,0:T(8,128)} %get-tuple-element.47), calls=%async_computation.1 | async-start | bytes 131072 | tf_op jit(solution)/shard_map/all_to_all | solution.py:1166
  26.4 1.1 %ocean_kernel.5.refs_2_ = f32[32,512]{1,0:T(8,128)S(1)} custom-call(f32[32,2048]{1,0:T(8,128)S(1)} %bitcast.14, f32[6,2048]{1,0:T(8,128)S(1)} %copy-done.3, s32[6,2048]{1,0:T(8,128)S(1)} %copy-done.4, f32[16,128]{1,0:T(8,128)S(1)} %bitcast.23, f32[16,128]{1,0:T(8,128)S(1)} %get-tuple-element.48.after_ref.rows_ref.final_ref), custom_call_target="tpu_custom_call" | custom-call | bytes 3145728 | tf_op jit(solution)/shard_map/ocean_kernel/pallas_call | solution.py:1103
  27.4 0.0 copy-start.8
  27.5 0.2 last_kernel.1
  27.7 0.5 %copy-done.8 = f32[2048]{0:T(1024)S(1)} copy-done((f32[2048]{0:T(1024)S(1)}, f32[2048]{0:T(1024)}, u32[]{:S(2)}) %copy-start.8) | copy-done | bytes 8216
  28.2 1.9 %rim_kernel.1 = (f32[32,2048]{1,0:T(8,128)}, f32[16,128]{1,0:T(8,128)S(1)}, f32[8,2048]{1,0:T(8,128)S(1)}) custom-call(f32[56,128]{1,0:T(8,128)S(1)} %collective-permute-done.before_ref, f32[56,128]{1,0:T(8,128)S(1)} %collective-permute-done.1.after_ref, f32[6,2048]{1,0:T(8,128)S(1)} %copy-done.3, s32[6,2048]{1,0:T(8,128)S(1)} %copy-done.4, ...), custom_call_target="tpu_custom_call" | custom-call | bytes 3145728 | tf_op jit(solution)/shard_map/rim_kernel/pallas_call | solution.py:1174
  30.1 1.3 %all-to-all-done.1.recv_ref = f32[8,16,128]{2,1,0:T(8,128)S(1)} async-done(((f32[8,16,128]{2,1,0:T(8,128)}), f32[8,16,128]{2,1,0:T(8,128)S(1)}, u32[]{:S(2)}, u32[]{:S(2)}) %all-to-all-start.1) | async-done | bytes 65568 | tf_op jit(solution)/shard_map/all_to_all | solution.py:1166
  31.3 1.0 %end_kernel.1 = (f32[32,2048]{1,0:T(8,128)}, f32[768,128]{1,0:T(8,128)}) custom-call(f32[768,128]{1,0:T(8,128)S(1)} %get-tuple-element.46.last_ref, f32[8,16,128]{2,1,0:T(8,128)S(1)} %all-to-all-done.1.recv_ref, f32[16,128]{1,0:T(8,128)S(1)} %get-tuple-element.48.after_ref.rows_ref.final_ref, ...), custom_call_target="tpu_custom_call", output_to_operand_aliasing={{0}: (9, {})} | custom-call | tf_op jit(solution)/shard_map/end_kernel/pallas_call | solution.py:1190
Async XLA Ops:
  0.6 7.6 %copy-start = (f32[2,16,2048]{2,1,0:T(8,128)S(1)}, f32[2,16,2048]{2,1,0:T(8,128)}, u32[]{:S(2)}) copy-start(f32[2,16,2048]{2,1,0:T(8,128)} %param.18) | copy-start | bytes 786436
  2.9 8.4 %copy-start.3 = (f32[6,2048]{1,0:T(8,128)S(1)}, f32[6,2048]{1,0:T(8,128)}, u32[]{:S(2)}) copy-start(f32[6,2048]{1,0:T(8,128)} %coef_ref.7) | copy-start | bytes 147460
  2.9 8.4 %copy-start.4 = (s32[6,2048]{1,0:T(8,128)S(1)}, s32[6,2048]{1,0:T(8,128)}, u32[]{:S(2)}) copy-start(s32[6,2048]{1,0:T(8,128)} %near_ref.7) | copy-start | bytes 147460
  2.9 10.2 %all-to-all-start = ((f32[8,8,128]{2,1,0:T(8,128)}), f32[8,8,128]{2,1,0:T(8,128)S(1)}, u32[]{:S(2)}, u32[]{:S(2)}) async-start(f32[8,8,128]{2,1,0:T(8,128)} %get-tuple-element.30), calls=%async_computation | async-start | bytes 65536 | tf_op jit(solution)/shard_map/all_to_all | solution.py:1096
  8.3 3.0 %copy-start.5 = (f32[2048]{0:T(1024)S(1)}, f32[2048]{0:T(1024)}, u32[]{:S(2)}) copy-start(f32[2048]{0:T(1024)} %param.21) | copy-start | bytes 24580
  8.3 4.8 %copy-start.2 = (f32[3,16,16,128]{3,2,1,0:T(8,128)S(1)}, f32[3,16,16,128]{3,2,1,0:T(8,128)}, u32[]{:S(2)}) copy-start(f32[3,16,16,128]{3,2,1,0:T(8,128)} %param.13) | copy-start | bytes 1179652
  8.5 4.6 %copy-start.1 = (f32[2,16,16,128]{3,2,1,0:T(8,128)S(1)}, f32[2,16,16,128]{3,2,1,0:T(8,128)}, u32[]{:S(2)}) copy-start(f32[2,16,16,128]{3,2,1,0:T(8,128)} %param.14) | copy-start | bytes 786436
  8.5 4.6 %collective-permute-start = (f32[56,128]{1,0:T(8,128)S(1)}, f32[56,128]{1,0:T(8,128)S(1)}, u32[]{:S(2)}, u32[]{:S(2)}) collective-permute-start(f32[56,128]{1,0:T(8,128)S(1)} %get-tuple-element.34), channel_id=1, source_target_pairs={{0,1},{1,2},{2,3},{3,4},{4,5},{5,6},{6,7},{7,0},{8,9},{9,10},{10,1... | collective-permute-start | bytes 86024 | tf_op jit(solution)/shard_map/ppermute | solution.py:1119
  9.0 4.1 %collective-permute-start.1 = (f32[56,128]{1,0:T(8,128)S(1)}, f32[56,128]{1,0:T(8,128)S(1)}, u32[]{:S(2)}, u32[]{:S(2)}) collective-permute-start(f32[56,128]{1,0:T(8,128)S(1)} %get-tuple-element.35.after_ref), channel_id=1, source_target_pairs={{1,0},{2,1},{3,2},{4,3},{5,4},{6,5},{7,6},{0,7},{9,8},{10,9},{11,1... | collective-permute-start | bytes 86024 | tf_op jit(solution)/shard_map/ppermute | solution.py:1120
  11.3 1.8 %copy-start.6 = (f32[16,128]{1,0:T(8,128)S(1)}, f32[16,128]{1,0:T(8,128)}, u32[]{:S(2)}) copy-start(f32[16,128]{1,0:T(8,128)} %jac_ref.1) | copy-start | bytes 24580
  11.3 1.8 %copy-start.7 = (f32[16,128]{1,0:T(8,128)S(1)}, f32[16,128]{1,0:T(8,128)}, u32[]{:S(2)}) copy-start(f32[16,128]{1,0:T(8,128)} %land_ref.1) | copy-start | bytes 24580
  13.6 7.1 %collective-permute-start.2 = (f32[144,128]{1,0:T(8,128)S(1)}, f32[144,128]{1,0:T(8,128)S(1)}, u32[]{:S(2)}, u32[]{:S(2)}) collective-permute-start(f32[144,128]{1,0:T(8,128)S(1)} %get-tuple-element.41), channel_id=1, source_target_pairs={{0,8},{8,16},{16,24},{24,0},{1,9},{9,17},{17,25},{25,1},{2,10},{10... | collective-permute-start | bytes 221192 | tf_op jit(solution)/shard_map/ppermute | solution.py:1140
  15.3 6.3 %collective-permute-start.3 = (f32[144,128]{1,0:T(8,128)S(1)}, f32[144,128]{1,0:T(8,128)S(1)}, u32[]{:S(2)}, u32[]{:S(2)}) collective-permute-start(f32[144,128]{1,0:T(8,128)S(1)} %get-tuple-element.42), channel_id=1, source_target_pairs={{8,0},{16,8},{24,16},{0,24},{9,1},{17,9},{25,17},{1,25},{10,2},{18... | collective-permute-start | bytes 221192 | tf_op jit(solution)/shard_map/ppermute | solution.py:1141
  23.0 8.3 %all-to-all-start.1 = ((f32[8,16,128]{2,1,0:T(8,128)}), f32[8,16,128]{2,1,0:T(8,128)S(1)}, u32[]{:S(2)}, u32[]{:S(2)}) async-start(f32[8,16,128]{2,1,0:T(8,128)} %get-tuple-element.47), calls=%async_computation.1 | async-start | bytes 131072 | tf_op jit(solution)/shard_map/all_to_all | solution.py:1166
  27.4 0.7 %copy-start.8 = (f32[2048]{0:T(1024)S(1)}, f32[2048]{0:T(1024)}, u32[]{:S(2)}) copy-start(f32[2048]{0:T(1024)} %param.22) | copy-start | bytes 24580

commit v12 on v11

--- a/solution.py
+++ b/solution.py
@@ -375,7 +375,6 @@
     jac_ref,
     land_ref,
     rows_ref,
-    ocean_ref,
     avg_ref,
     down_ref,
     up_ref,
@@ -507,15 +506,17 @@
         slope = sum(coef * value for coef, value in zip(coefs, lines))
         surf_slope = sum(coef * value for coef, value in zip(coefs, surf_lines))
         mass = surf_ref[4 * ROWS * MASS + r : 4 * ROWS * MASS + r + 1, :]
-        wind = time_step * mass * wind_ref[pl.ds(r, 2 * levels, stride=x_points), :]
-        out_ref[0:planes, :] = line(r)
-        for first in range(0, planes, levels):
-            out_ref[planes + first : planes + first + levels, :] = (
-                wind[:levels] * slope[first : first + levels]
-            )
-        base = 2 * planes
-        out_ref[base : base + 2 * levels, :] = wind
-        base += 2 * levels
+        wind = time_step * mass * wind_ref[pl.ds(r, levels, stride=x_points), :]
+        edge = line(r)
+        columns = [edge[plane : plane + ROWS] for plane in range(0, planes, ROWS)] + [
+            wind[plane % levels : plane % levels + ROWS] * slope[plane : plane + ROWS]
+            for plane in range(0, planes, ROWS)
+        ]
+        pack = jnp.zeros((ROWS, LANES), jnp.float32)
+        for i, tile in enumerate(columns):
+            pack = jnp.where((geo.lane >> 1) == i, pltpu.roll(tile, 2 * i + 1, 1), pack)
+        out_ref[:ROWS, :] = pack
+        base = ROWS
         for number in range(SURF_ARRAYS):
             out_ref[base + 2 * number : base + 2 * number + 2, :] = surf_line(number, r)
         base += 2 * SURF_ARRAYS
@@ -535,8 +536,52 @@
     return moved, slopes
 
 
+def rows_kernel(planes, moved_ref, wind_ref, jac_ref, before_ref, down_ref, up_ref):
+    geo = Geometry()
+    x_points = jac_ref.shape[0]
+    levels = wind_ref.shape[0] // (2 * x_points)
+    y_weight = jnp.where(geo.y_edge, 1.0 / 6.0, 5.0 / 6.0)
+
+    def mass_of(x):
+        x_weight = 1.0 / 6.0 if x % GLL in (0, GLL - 1) else 5.0 / 6.0
+        return x_weight * y_weight * spread(jac_ref[x : x + 1, :])
+
+    for out_ref, r, inward, coefs in (
+        (down_ref, 0, 1, deriv_table[0][1:]),
+        (up_ref, x_points - 1, -1, deriv_table[3][2::-1]),
+    ):
+        lines = [r + inward * step for step in range(1, GLL + 1)]
+        totals = [geo.sum_y(mass_of(x), 0.0) for x in lines]
+        totals = totals[:-2] + [totals[-2] + totals[-1]]
+        factors = [coef / total for coef, total in zip(coefs, totals)]
+        mass = mass_of(r)
+        for level in range(0, levels, ROWS):
+            wind = [tiles[0] * mass for tiles in wind_tiles(wind_ref, x_points, level, [r])]
+            for part, tile in enumerate(wind):
+                at = 2 * planes + levels * part + level
+                out_ref[at : at + ROWS, :] = tile
+            for plane in range(level, planes, levels):
+                sums = [
+                    geo.sum_y(moved_ref[planes * x + plane : planes * x + plane + ROWS, :], 0.0)
+                    for x in [r] + lines
+                ]
+                edge, inner = sums[0], sums[1:-2] + [sums[-2] + sums[-1]]
+                slope = sum(factor * total for factor, total in zip(factors, inner))
+                out_ref[plane : plane + ROWS, :] = edge
+                out_ref[planes + plane : planes + plane + ROWS, :] = wind[0] * slope
+
+
 def inner_kernel(
-    planes, avg_ref, moved_ref, before_ref, after_ref, surf_ref, wind_ref, out_ref, packs_ref
+    planes,
+    avg_ref,
+    moved_ref,
+    before_ref,
+    after_ref,
+    surf_ref,
+    wind_ref,
+    ocean_ref,
+    out_ref,
+    packs_ref,
 ):
     geo = Geometry()
     x_points = avg_ref.shape[0] // planes
@@ -608,11 +653,12 @@
     inner_ref,
     packs_ref,
     surf_ref,
+    early_low_ref,
+    early_high_ref,
     low_ref,
     high_ref,
     wind_ref,
     rows_ref,
-    ocean_ref,
     slab_out,
     sums_ref,
     final_ref,
@@ -626,7 +672,7 @@
     left, right = neighbours_of(blocks)
     x_points = final_ref.shape[0]
     levels = wind_ref.shape[0] // (2 * x_points)
-    base = low_ref.shape[0] - 2 * SURF_ARRAYS - 4
+    base = ROWS
 
     def surf_tile(number, tile, h):
         at = 4 * ROWS * number + 2 * ROWS * tile + ROWS * h
@@ -698,13 +744,18 @@
         at = planes * kept.index(x) + plane
         sums_ref[at : at + ROWS, :] = value
 
-    def beyond(ref, plane, field, slope, own_coef):
+    def fixed(early_ref, ref, number):
+        late = pltpu.roll(ref[:ROWS, :], (-(2 * number + 1)) % LANES, 1)
+        early = early_ref[ROWS * number : ROWS * (number + 1), :]
+        return jnp.where(geo.outer_lane, late, early)
+
+    def beyond(early_ref, ref, plane, field, slope, own_coef):
         wind_at = 2 * planes + plane % levels
         return (
             beside(ref, MASS, 0) * field
-            - ref[planes + plane : planes + plane + ROWS, :]
-            - ref[wind_at : wind_at + ROWS, :] * (own_coef * field)
-            - ref[wind_at + levels : wind_at + levels + ROWS, :] * slope
+            - fixed(early_ref, ref, (planes + plane) // ROWS)
+            - early_ref[wind_at : wind_at + ROWS, :] * (own_coef * field)
+            - early_ref[wind_at + levels : wind_at + levels + ROWS, :] * slope
         )
 
     def row_of(tiles, x):
@@ -725,16 +776,18 @@
                     total = avg_ref[planes * x + plane : planes * x + plane + ROWS, :]
                     other = x - 1 if i == 0 else x + 1
                     if other < 0:
-                        total = total + low_ref[here, :]
+                        total = total + fixed(early_low_ref, low_ref, plane // ROWS)
                     elif other == x_points:
-                        total = total + high_ref[here, :]
+                        total = total + fixed(early_high_ref, high_ref, plane // ROWS)
                     elif i in (0, GLL - 1):
                         at = planes * other + plane
                         total = total + avg_ref[at : at + ROWS, :]
                     fields.append(total * scale[i])
                 moved, slopes = advance(geo, fields, wind, mass)
                 if element == 0:
-                    before = beyond(low_ref, plane, fields[0], slopes[0], deriv_table[3][3])
+                    before = beyond(
+                        early_low_ref, low_ref, plane, fields[0], slopes[0], deriv_table[3][3]
+                    )
                     put(lines[0], plane, before + moved[0])
                     shared = moved[-1] + inner_ref[here, :]
                     put(lines[-1], plane, shared)
@@ -745,7 +798,7 @@
                     put(lines[0] - 1, plane, shared)
                     put(lines[0], plane, shared)
                     after = beyond(
-                        high_ref, plane, fields[-1], slopes[-1], deriv_table[0][0]
+                        early_high_ref, high_ref, plane, fields[-1], slopes[-1], deriv_table[0][0]
                     )
                     put(lines[-1], plane, moved[-1] + after)
                 for i in range(1, GLL - 1):
@@ -796,10 +849,9 @@
     hot_ref,
     weights_ref,
     gain_ref,
-    first_ref,
-    ocean_in,
+    ocean_ref,
+    air_out,
     ocean_out,
-    air_out,
     air_ref,
     row_ref,
     semaphores,
@@ -817,6 +869,7 @@
         )
         copies[-1].start()
 
+    send(ocean_ref.at[ROWS:], ocean_out.at[ROWS:])
     joined = join_edges(
         geo,
         recv_ref[left, EDGE_AT : EDGE_AT + ROWS, :],
@@ -846,10 +899,10 @@
         [weights_ref[...] * arrived], cols_ref[...], chunks, hot_ref[...]
     )
     gain = inflow * gain_ref[...]
-    row_ref[...] = first_ref[...]
+    row_ref[...] = ocean_ref[:ROWS, :]
     for k in range(chunks):
         at = slice(LANES * k, LANES * (k + 1))
-        row_ref[0:1, at] = first_ref[0:1, at] + gain[k : k + 1]
+        row_ref[0:1, at] = ocean_ref[0:1, at] + gain[k : k + 1]
     send(row_ref, ocean_out.at[:ROWS])
     for copy in copies:
         copy.wait()
@@ -985,7 +1038,7 @@
     rows_ref,
     *refs,
 ):
-    partial_refs, (out_ref, gain_ref, first_ref) = refs[: len(starts)], refs[len(starts) :]
+    partial_refs, (out_ref, gain_ref) = refs[: len(starts)], refs[len(starts) :]
     chunks = coef_ref.shape[1] // LANES
     groups = out_ref.shape[0] // ROWS
     rim_at = before_ref.shape[0] - out_ref.shape[0]
@@ -1004,7 +1057,6 @@
         for g in range(groups):
             half = slice(ROWS * g, ROWS * (g + 1))
             out_ref[half, at] = partial_refs[part][half, place] + totals[g]
-    first_ref[...] = out_ref[:ROWS, :]
 
 
 VMEM_SPEC = pl.BlockSpec(memory_space=pltpu.VMEM)
@@ -1012,10 +1064,10 @@
 HBM_SPEC = pl.BlockSpec(memory_space=pltpu.HBM)
 
 
-def call(kernel, outs, specs, scratch=(), cost=0, hbm_outs=0, aliases=None):
+def call(kernel, outs, specs, scratch=(), cost=0, hbm_outs=0):
     estimate = None
     if cost:
-        estimate = pl.CostEstimate(flops=0, bytes_accessed=cost, transcendentals=0)
+        estimate = pl.CostEstimate(flops=cost * 1000, bytes_accessed=cost, transcendentals=0)
     outs = [
         out if isinstance(out, jax.ShapeDtypeStruct) else jax.ShapeDtypeStruct(out, jnp.float32)
         for out in outs
@@ -1028,7 +1080,6 @@
         in_specs=specs,
         out_specs=out_specs,
         scratch_shapes=list(scratch),
-        input_output_aliases=aliases or {},
         cost_estimate=estimate,
         compiler_params=pltpu.CompilerParams(vmem_limit_bytes=32 * 2**20),
         name=getattr(kernel, "func", kernel).__name__,
@@ -1097,7 +1148,7 @@
 
     chunks = cells // LANES
     reads_per_chunk = edge_coef.shape[0] * chunks * (ocean_planes // ROWS)
-    starts = (0, chunks // 4, chunks * 3 // 4)
+    starts = (0, chunks * 6 // 16)
 
     def ocean_part(start, end, after):
         (result,) = call(
@@ -1118,12 +1169,22 @@
     onward = [(i, (i + 1) % blocks) for i in range(blocks)]
     before = lax.ppermute(to_after, "blk", onward)
     after = lax.ppermute(to_before, "blk", [(to, source) for source, to in onward])
-    first_part = ocean_part(starts[0], starts[1], to_before)
-    side_rows = 2 * planes + 2 * levels + 2 * SURF_ARRAYS + 4
+    down, up = call(
+        functools.partial(rows_kernel, planes),
+        [(2 * planes + 2 * levels, LANES)] * 2,
+        [VMEM_SPEC] * 3 + [ANY_SPEC],
+    )(moved, wind, jacobian, to_before)
+    after_me = [(i, (i + 1) % faces) for i in range(faces)]
+    before_me = [(to, source) for source, to in after_me]
+    early_low = lax.ppermute(up, "face", after_me)
+    early_high = lax.ppermute(down, "face", before_me)
+
+    side_rows = ROWS + 2 * SURF_ARRAYS + 4
     avg, down, up, surf = call(
         functools.partial(panel_kernel, planes),
         [air.shape, (side_rows, LANES), (side_rows, LANES), (4 * ROWS * SURF_ARRAYS, LANES)],
-        [VMEM_SPEC] * 9 + [ANY_SPEC],
+        [VMEM_SPEC] * 9,
+        cost=60 * air.size * 4,
     )(
         moved,
         recv,
@@ -1134,18 +1195,16 @@
         jacobian,
         land_area,
         point_ids,
-        first_part,
-    )
-    after_me = [(i, (i + 1) % faces) for i in range(faces)]
+    )
     low = lax.ppermute(up, "face", after_me)
-    high = lax.ppermute(down, "face", [(to, source) for source, to in after_me])
+    high = lax.ppermute(down, "face", before_me)
+    first_part = ocean_part(starts[0], starts[1], surf)
     inner, packs = call(
         functools.partial(inner_kernel, planes),
         [((x_points - 2 * GLL) * planes, LANES), (2 * ROWS, LANES)],
-        [VMEM_SPEC] * 6,
-        cost=2 * air.size * 4,
-    )(avg, moved, before, after, surf, wind)
-    second_part = ocean_part(starts[1], starts[2], surf)
+        [VMEM_SPEC] * 6 + [ANY_SPEC],
+        cost=40 * air.size * 4,
+    )(avg, moved, before, after, surf, wind, first_part)
 
     slab, outer, final, inverse = call(
         functools.partial(second_kernel, planes),
@@ -1155,14 +1214,14 @@
             (x_points, y_points),
             (x_points, y_points),
         ],
-        [VMEM_SPEC] * 8 + [ANY_SPEC],
+        [VMEM_SPEC] * 10,
         [
             pltpu.VMEM((blocks, HEAD, LANES), jnp.float32),
             pltpu.VMEM((2, ROWS, LANES), jnp.float32),
             pltpu.SemaphoreType.DMA((3,)),
         ],
         hbm_outs=1,
-    )(avg, inner, packs, surf, low, high, wind, point_ids, second_part)
+    )(avg, inner, packs, surf, early_low, early_high, low, high, wind, point_ids)
     arrived = lax.all_to_all(slab, "blk", split_axis=0, concat_axis=0, tiled=True)
     last, hot = call(
         functools.partial(last_kernel, planes),
@@ -1170,10 +1229,10 @@
         [VMEM_SPEC] * 4,
         cost=2 * air.size * 4,
     )(inner, outer, inverse, cell_ids)
-    third_part = ocean_part(starts[2], chunks, final)
-    partial, gain, first_rows = call(
+    second_part = ocean_part(starts[1], chunks, final)
+    partial, gain = call(
         functools.partial(rim_kernel, starts),
-        [ocean.shape, area.shape, (ROWS, cells)],
+        [ocean.shape, area.shape],
         [VMEM_SPEC] * 5 + [ANY_SPEC] + [VMEM_SPEC] * len(starts),
         cost=chunks * reads_per_chunk // 8 * ROWS * LANES * 4,
     )(
@@ -1185,31 +1244,18 @@
         final,
         first_part,
         second_part,
-        third_part,
-    )
-    ocean_final, air_final = call(
+    )
+    air_final, ocean_final = call(
         functools.partial(end_kernel, planes),
-        [ocean.shape, air.shape],
-        [VMEM_SPEC] * 9 + [HBM_SPEC],
+        [air.shape, ocean.shape],
+        [VMEM_SPEC] * 9,
         [
             pltpu.VMEM(air.shape, jnp.float32),
             pltpu.VMEM((ROWS, cells), jnp.float32),
-            pltpu.SemaphoreType.DMA((1 + planes // ROWS,)),
+            pltpu.SemaphoreType.DMA((2 + planes // ROWS,)),
         ],
         hbm_outs=2,
-        aliases={9: 0},
-    )(
-        last,
-        arrived,
-        final,
-        inverse,
-        cell_ids,
-        hot,
-        weights,
-        gain,
-        first_rows,
-        pltpu.with_memory_space_constraint(partial, pltpu.HBM),
-    )
+    )(last, arrived, final, inverse, cell_ids, hot, weights, gain, partial)
     return air_final.reshape(air_state.shape), ocean_final.reshape(tracers.shape)
 
 

time: 32.7 us -> 33.5 us (1.024)
  starting transfers between devices: 15.3 us -> 19.1 us
  waiting for transfers between devices: 2.77 us -> 0.89 us
  Pallas kernels: 12.9 us -> 12.4 us
  local copies, waits for them, and re-layouts: 0.53 us -> 0.05 us
    ppermute x1 -> x3, starting transfers between devices: 2.25 us -> 7.69 us  [the longest x1 3.81 us: body(): high = lax.ppermute(down, 'face', before_me)]
    ppermute x1, starting transfers between devices: 1.63 us -> 0.06 us  [body(): low = lax.ppermute(up, 'face', after_me)]
    ppermute x1 -> x3, waiting for transfers between devices: 0.81 us -> 0.01 us  [the longest x1 0.01 us: body(): high = lax.ppermute(down, 'face', before_me)]
    all_to_all x1, waiting for transfers between devices: 0.69 us -> 0.01 us  [body(): recv = lax.all_to_all(slab, 'blk', split_axis=0, concat_axis=0, tiled=True)]
    pallas_call x2 -> x3, Pallas kernels: 2.93 us -> 2.38 us  [the longest x1 1.19 us: body(): call(functools.partial(rim_kernel, starts), [ocean.shape, area.shape], [V...]
    unnamed x18, local copies, waits for them, and re-layouts: 0.53 us -> 0.05 us
    all_to_all x1, waiting for transfers between devices: 1.26 us -> 0.87 us  [body(): lax.all_to_all(slab, 'blk', split_axis=0, concat_axis=0, tiled=True)]
    pallas_call x3 -> x2, Pallas kernels: 4.29 us -> 4.25 us  [ocean_part(): call(functools.partial(ocean_kernel, ocean_levels, start), [(ocean_planes...]
  transfers between devices with their start and end apart: 6 -> 8, of which waited for: 3 -> 1; matrix products, arithmetic and copies ran while one was open for 0% -> 0% of each run, Pallas kernels for 24% -> 23%
where the time goes in v12:
time: 33.5 us; the launch traced here: 33.2 us
  starting transfers between devices  19.1 us (57%)
  Pallas kernels  12.4 us (37%)
  waiting for transfers between devices  0.89 us (3%)
  between operations  0.84 us (3%)
    all_to_all x1, starting transfers between devices, body(): recv = lax.all_to_all(slab, 'blk', split_axis=0, concat_axis=0, tiled=True)  5.18 us
    pallas_call x2, Pallas kernels, ocean_part(): call(functools.partial(ocean_kernel, ocean_levels, start), [(ocean_planes...  4.25 us
    ppermute x1, starting transfers between devices, body(): high = lax.ppermute(down, 'face', before_me)  3.81 us
    all_to_all x1, starting transfers between devices, body(): lax.all_to_all(slab, 'blk', split_axis=0, concat_axis=0, tiled=True)  3.36 us
    pallas_call x1, Pallas kernels, body(): call(functools.partial(start_kernel, planes), [(blocks, HEAD, LANES), air...  2.27 us
    ppermute x1, starting transfers between devices, body(): early_high = lax.ppermute(down, 'face', before_me)  2.25 us
    ppermute x1, starting transfers between devices, body(): lax.ppermute(to_before, 'blk', [(to, source) for source, to in onward])  2.24 us
    ppermute x1, starting transfers between devices, body(): early_low = lax.ppermute(up, 'face', after_me)  1.63 us
  transfers between devices with their start and end apart: 8, of which 1 were waited for; matrix products, arithmetic and copies ran while one was open for 0% of the time, Pallas kernels for 23%

profile of v12, /device:TPU:0, one launch (start us, length us, event | category | flops | bytes accessed | tf_op | source)
XLA Modules:
  0.0 33.2 jit_solution(4378305293111974943)
XLA Ops:
  0.6 0.0 copy-start.2
  0.6 2.3 %start_kernel.1 = (f32[8,8,128]{2,1,0:T(8,128)}, f32[768,128]{1,0:T(8,128)S(1)}, f32[24,128]{1,0:T(8,128)S(1)}, f32[24,128]{1,0:T(8,128)S(1)}, s32[8,128]{1,0:T(...) custom-call(s32[8,128]{1,0:T(8,128)} %bitcast.24, f32[8,128]{1,0:T(8,128)} %bitcast.25, ...), custom_call_target="tpu_custom_call" | custom-call | tf_op jit(solution)/shard_map/start_kernel/pallas_call | solution.py:1127
  2.9 5.2 %all-to-all-start = ((f32[8,8,128]{2,1,0:T(8,128)}), f32[8,8,128]{2,1,0:T(8,128)S(1)}, u32[]{:S(2)}, u32[]{:S(2)}) async-start(f32[8,8,128]{2,1,0:T(8,128)} %get-tuple-element.31), calls=%async_computation | async-start | bytes 65536 | tf_op jit(solution)/shard_map/all_to_all | solution.py:1147
  8.1 0.0 copy-done.2
  8.1 0.0 copy-start
  8.1 0.0 copy-start.3
  8.1 0.2 send_kernel.1
  8.3 0.0 copy-start.1
  8.4 0.5 %collective-permute-start = (f32[56,128]{1,0:T(8,128)S(1)}, f32[56,128]{1,0:T(8,128)S(1)}, u32[]{:S(2)}, u32[]{:S(2)}) collective-permute-start(f32[56,128]{1,0:T(8,128)S(1)} %get-tuple-element.35), channel_id=1, source_target_pairs={{0,1},{1,2},{2,3},{3,4},{4,5},{5,6},{6,7},{7,0},{8,9},{9,10},{10,1... | collective-permute-start | bytes 86024 | tf_op jit(solution)/shard_map/ppermute | solution.py:1170
  8.9 2.2 %collective-permute-start.1 = (f32[56,128]{1,0:T(8,128)S(1)}, f32[56,128]{1,0:T(8,128)S(1)}, u32[]{:S(2)}, u32[]{:S(2)}) collective-permute-start(f32[56,128]{1,0:T(8,128)S(1)} %get-tuple-element.36.before_ref), channel_id=1, source_target_pairs={{1,0},{2,1},{3,2},{4,3},{5,4},{6,5},{7,6},{0,7},{9,8},{10,9},{11,1... | collective-permute-start | bytes 86024 | tf_op jit(solution)/shard_map/ppermute | solution.py:1171
  11.1 0.0 copy-done
  11.1 0.0 copy-done.3
  11.1 0.0 copy-start.4
  11.1 0.1 rows_kernel.1
  11.3 1.6 %collective-permute-start.2 = (f32[128,128]{1,0:T(8,128)S(1)}, f32[128,128]{1,0:T(8,128)S(1)}, u32[]{:S(2)}, u32[]{:S(2)}) collective-permute-start(f32[128,128]{1,0:T(8,128)S(1)} %get-tuple-element.42), channel_id=1, source_target_pairs={{0,8},{8,16},{16,24},{24,0},{1,9},{9,17},{17,25},{25,1},{2,10},{10... | collective-permute-start | bytes 196616 | tf_op jit(solution)/shard_map/ppermute | solution.py:1179
  12.9 2.2 %collective-permute-start.3 = (f32[128,128]{1,0:T(8,128)S(1)}, f32[128,128]{1,0:T(8,128)S(1)}, u32[]{:S(2)}, u32[]{:S(2)}) collective-permute-start(f32[128,128]{1,0:T(8,128)S(1)} %get-tuple-element.43), channel_id=1, source_target_pairs={{8,0},{16,8},{24,16},{0,24},{9,1},{17,9},{25,17},{1,25},{10,2},{18... | collective-permute-start | bytes 196616 | tf_op jit(solution)/shard_map/ppermute | solution.py:1180
  15.2 0.0 all-to-all-done.recv_ref
  15.2 0.0 collective-permute-done.before_ref
  15.2 0.0 collective-permute-done.1.after_ref
  15.2 0.0 copy-done.1
  15.2 0.0 copy-done.4
  15.2 0.0 copy-start.5
  15.2 0.0 copy-start.6
  15.2 0.0 copy-start.7
  15.2 0.5 %panel_kernel.1 = (f32[768,128]{1,0:T(8,128)S(1)}, f32[24,128]{1,0:T(8,128)S(1)}, f32[24,128]{1,0:T(8,128)S(1)}, f32[192,128]{1,0:T(8,128)S(1)}) custom-call(f32[768,128]{1,0:T(8,128)S(1)} %get-tuple-element.30.moved_ref, f32[8,8,128]{2,1,0:T(8,128)S(1)} %all-to-all-done.recv_ref, f32[56,128]{1,0:T(8,128)S(1)} %collective-permute-done.before_ref, ...), custom_call_target="tpu_custom_call" | custom-call | flops 23592960000 | bytes 23592960 | tf_op jit(solution)/shard_map/panel_kernel/pallas_call | solution.py:1183
  15.7 0.1 collective-permute-start.4
  15.8 3.8 %collective-permute-start.5 = (f32[24,128]{1,0:T(8,128)S(1)}, f32[24,128]{1,0:T(8,128)S(1)}, u32[]{:S(2)}, u32[]{:S(2)}) collective-permute-start(f32[24,128]{1,0:T(8,128)S(1)} %get-tuple-element.45), channel_id=1, source_target_pairs={{8,0},{16,8},{24,16},{0,24},{9,1},{17,9},{25,17},{1,25},{10,2},{18... | collective-permute-start | bytes 36872 | tf_op jit(solution)/shard_map/ppermute | solution.py:1200
  19.6 0.0 copy-done.5
  19.6 0.0 copy-done.6
  19.6 0.0 copy-done.7
  19.6 1.6 %ocean_kernel.2.ocean_ref.refs_0_ = f32[32,768]{1,0:T(8,128)S(1)} custom-call(f32[32,2048]{1,0:T(8,128)S(1)} %bitcast.19, f32[6,2048]{1,0:T(8,128)S(1)} %copy-done.5, s32[6,2048]{1,0:T(8,128)S(1)} %copy-done.6, f32[16,128]{1,0:T(8,128)S(1)} %bitcast.21, f32[192,128]{1,0:T(8,128)S(1)} %get-tuple-element.39.after_ref.surf_ref), custom_call_target="tpu_custom_call" | custom-call | flops 4718592000 | bytes 4718592 | tf_op jit(solution)/shard_map/ocean_kernel/pallas_call | solution.py:1154
  21.2 1.1 %inner_kernel.1 = (f32[384,128]{1,0:T(8,128)S(1)}, f32[16,128]{1,0:T(8,128)S(1)}) custom-call(f32[768,128]{1,0:T(8,128)S(1)} %get-tuple-element.38.avg_ref, f32[768,128]{1,0:T(8,128)S(1)} %get-tuple-element.30.moved_ref, f32[56,128]{1,0:T(8,128)S(1)} %collective-permute-done.before_ref, f32[56,128]{1,0:T(8,128)S(1)} %collective-permute-done.1.after_ref, ...), custom_call_target="tpu_custom_call" | custom-call | flops 15728640000 | bytes 15728640 | tf_op jit(solution)/shard_map/inner_kernel/pallas_call | solution.py:1202
  22.4 0.0 collective-permute-done.4.low_ref
  22.4 0.0 collective-permute-done.5.high_ref
  22.4 0.0 collective-permute-done.2.early_low_ref
  22.4 0.0 collective-permute-done.3.early_high_ref
  22.4 1.4 %second_kernel.1 = (f32[8,16,128]{2,1,0:T(8,128)}, f32[480,128]{1,0:T(8,128)S(1)}, f32[16,128]{1,0:T(8,128)S(1)}, f32[16,128]{1,0:T(8,128)S(1)}) custom-call(f32[768,128]{1,0:T(8,128)S(1)} %get-tuple-element.38.avg_ref, f32[384,128]{1,0:T(8,128)S(1)} %get-tuple-element.40.inner_ref, f32[16,128]{1,0:T(8,128)S(1)} %get-tuple-element.41.packs_ref, ...), custom_call_target="tpu_custom_call" | custom-call | tf_op jit(solution)/shard_map/second_kernel/pallas_call | solution.py:1209
  23.9 3.4 %all-to-all-start.1 = ((f32[8,16,128]{2,1,0:T(8,128)}), f32[8,16,128]{2,1,0:T(8,128)S(1)}, u32[]{:S(2)}, u32[]{:S(2)}) async-start(f32[8,16,128]{2,1,0:T(8,128)} %get-tuple-element.50), calls=%async_computation.1 | async-start | bytes 131072 | tf_op jit(solution)/shard_map/all_to_all | solution.py:1225
  27.2 0.0 copy-start.8
  27.2 2.6 %ocean_kernel.3.refs_1_ = f32[32,1280]{1,0:T(8,128)S(1)} custom-call(f32[32,2048]{1,0:T(8,128)S(1)} %bitcast.20, f32[6,2048]{1,0:T(8,128)S(1)} %copy-done.5, s32[6,2048]{1,0:T(8,128)S(1)} %copy-done.6, f32[16,128]{1,0:T(8,128)S(1)} %bitcast.22, f32[16,128]{1,0:T(8,128)S(1)} %get-tuple-element.51.after_ref.rows_ref.final_ref), custom_call_target="tpu_custom_call" | custom-call | flops 7864320000 | bytes 7864320 | tf_op jit(solution)/shard_map/ocean_kernel/pallas_call | solution.py:1154
  29.9 0.0 copy-done.8
  29.9 1.2 %rim_kernel.1 = (f32[32,2048]{1,0:T(8,128)S(1)}, f32[16,128]{1,0:T(8,128)S(1)}) custom-call(f32[56,128]{1,0:T(8,128)S(1)} %collective-permute-done.before_ref, f32[56,128]{1,0:T(8,128)S(1)} %collective-permute-done.1.after_ref, f32[6,2048]{1,0:T(8,128)S(1)} %copy-done.5, s32[6,2048]{1,0:T(8,128)S(1)} %copy-done.6, f32[16,128]{1,0:T(8,128)S(1)} %bitcast.23, ...), custom_call_target="tpu_custom_call" | custom-call | flops 3145728000 | bytes 3145728 | tf_op jit(solution)/shard_map/rim_kernel/pallas_call | solution.py:1233
  31.1 0.2 last_kernel.1
  31.3 0.9 %all-to-all-done.1.recv_ref = f32[8,16,128]{2,1,0:T(8,128)S(1)} async-done(((f32[8,16,128]{2,1,0:T(8,128)}), f32[8,16,128]{2,1,0:T(8,128)S(1)}, u32[]{:S(2)}, u32[]{:S(2)}) %all-to-all-start.1) | async-done | bytes 65568 | tf_op jit(solution)/shard_map/all_to_all | solution.py:1225
  32.2 1.0 %end_kernel.1 = (f32[768,128]{1,0:T(8,128)}, f32[32,2048]{1,0:T(8,128)}) custom-call(f32[768,128]{1,0:T(8,128)S(1)} %get-tuple-element.49.last_ref, f32[8,16,128]{2,1,0:T(8,128)S(1)} %all-to-all-done.1.recv_ref, f32[16,128]{1,0:T(8,128)S(1)} %get-tuple-element.51.after_ref.rows_ref.final_ref, f32[16,128]{1,0:T(8,128)S(1)} %get-tuple-element.47.inverse_ref, ...), custom_call_target="tpu_custom_call" | custom-call | tf_op jit(solution)/shard_map/end_kernel/pallas_call | solution.py:1248
Async XLA Ops:
  0.6 7.5 %copy-start.2 = (f32[2,16,2048]{2,1,0:T(8,128)S(1)}, f32[2,16,2048]{2,1,0:T(8,128)}, u32[]{:S(2)}) copy-start(f32[2,16,2048]{2,1,0:T(8,128)} %param.18) | copy-start | bytes 786436
  2.9 12.3 %all-to-all-start = ((f32[8,8,128]{2,1,0:T(8,128)}), f32[8,8,128]{2,1,0:T(8,128)S(1)}, u32[]{:S(2)}, u32[]{:S(2)}) async-start(f32[8,8,128]{2,1,0:T(8,128)} %get-tuple-element.31), calls=%async_computation | async-start | bytes 65536 | tf_op jit(solution)/shard_map/all_to_all | solution.py:1147
  8.1 3.0 %copy-start = (f32[2,16,16,128]{3,2,1,0:T(8,128)S(1)}, f32[2,16,16,128]{3,2,1,0:T(8,128)}, u32[]{:S(2)}) copy-start(f32[2,16,16,128]{3,2,1,0:T(8,128)} %param.14) | copy-start | bytes 786436
  8.1 3.0 %copy-start.3 = (f32[16,128]{1,0:T(8,128)S(1)}, f32[16,128]{1,0:T(8,128)}, u32[]{:S(2)}) copy-start(f32[16,128]{1,0:T(8,128)} %jac_ref.3) | copy-start | bytes 24580
  8.3 6.8 %copy-start.1 = (f32[3,16,16,128]{3,2,1,0:T(8,128)S(1)}, f32[3,16,16,128]{3,2,1,0:T(8,128)}, u32[]{:S(2)}) copy-start(f32[3,16,16,128]{3,2,1,0:T(8,128)} %param.13) | copy-start | bytes 1179652
  8.4 6.8 %collective-permute-start = (f32[56,128]{1,0:T(8,128)S(1)}, f32[56,128]{1,0:T(8,128)S(1)}, u32[]{:S(2)}, u32[]{:S(2)}) collective-permute-start(f32[56,128]{1,0:T(8,128)S(1)} %get-tuple-element.35), channel_id=1, source_target_pairs={{0,1},{1,2},{2,3},{3,4},{4,5},{5,6},{6,7},{7,0},{8,9},{9,10},{10,1... | collective-permute-start | bytes 86024 | tf_op jit(solution)/shard_map/ppermute | solution.py:1170
  8.9 6.3 %collective-permute-start.1 = (f32[56,128]{1,0:T(8,128)S(1)}, f32[56,128]{1,0:T(8,128)S(1)}, u32[]{:S(2)}, u32[]{:S(2)}) collective-permute-start(f32[56,128]{1,0:T(8,128)S(1)} %get-tuple-element.36.before_ref), channel_id=1, source_target_pairs={{1,0},{2,1},{3,2},{4,3},{5,4},{6,5},{7,6},{0,7},{9,8},{10,9},{11,1... | collective-permute-start | bytes 86024 | tf_op jit(solution)/shard_map/ppermute | solution.py:1171
  11.1 4.1 %copy-start.4 = (f32[16,128]{1,0:T(8,128)S(1)}, f32[16,128]{1,0:T(8,128)}, u32[]{:S(2)}) copy-start(f32[16,128]{1,0:T(8,128)} %land_ref.1) | copy-start | bytes 24580
  11.3 11.1 %collective-permute-start.2 = (f32[128,128]{1,0:T(8,128)S(1)}, f32[128,128]{1,0:T(8,128)S(1)}, u32[]{:S(2)}, u32[]{:S(2)}) collective-permute-start(f32[128,128]{1,0:T(8,128)S(1)} %get-tuple-element.42), channel_id=1, source_target_pairs={{0,8},{8,16},{16,24},{24,0},{1,9},{9,17},{17,25},{25,1},{2,10},{10... | collective-permute-start | bytes 196616 | tf_op jit(solution)/shard_map/ppermute | solution.py:1179
  12.9 9.5 %collective-permute-start.3 = (f32[128,128]{1,0:T(8,128)S(1)}, f32[128,128]{1,0:T(8,128)S(1)}, u32[]{:S(2)}, u32[]{:S(2)}) collective-permute-start(f32[128,128]{1,0:T(8,128)S(1)} %get-tuple-element.43), channel_id=1, source_target_pairs={{8,0},{16,8},{24,16},{0,24},{9,1},{17,9},{25,17},{1,25},{10,2},{18... | collective-permute-start | bytes 196616 | tf_op jit(solution)/shard_map/ppermute | solution.py:1180
  15.2 4.4 %copy-start.5 = (f32[6,2048]{1,0:T(8,128)S(1)}, f32[6,2048]{1,0:T(8,128)}, u32[]{:S(2)}) copy-start(f32[6,2048]{1,0:T(8,128)} %coef_ref.5) | copy-start | bytes 147460
  15.2 4.4 %copy-start.6 = (s32[6,2048]{1,0:T(8,128)S(1)}, s32[6,2048]{1,0:T(8,128)}, u32[]{:S(2)}) copy-start(s32[6,2048]{1,0:T(8,128)} %near_ref.5) | copy-start | bytes 147460
  15.2 4.4 %copy-start.7 = (f32[2048]{0:T(1024)S(1)}, f32[2048]{0:T(1024)}, u32[]{:S(2)}) copy-start(f32[2048]{0:T(1024)} %param.21) | copy-start | bytes 24580
  15.7 6.6 %collective-permute-start.4 = (f32[24,128]{1,0:T(8,128)S(1)}, f32[24,128]{1,0:T(8,128)S(1)}, u32[]{:S(2)}, u32[]{:S(2)}) collective-permute-start(f32[24,128]{1,0:T(8,128)S(1)} %get-tuple-element.44), channel_id=1, source_target_pairs={{0,8},{8,16},{16,24},{24,0},{1,9},{9,17},{17,25},{25,1},{2,10},{10... | collective-permute-start | bytes 36872 | tf_op jit(solution)/shard_map/ppermute | solution.py:1199
  15.8 6.6 %collective-permute-start.5 = (f32[24,128]{1,0:T(8,128)S(1)}, f32[24,128]{1,0:T(8,128)S(1)}, u32[]{:S(2)}, u32[]{:S(2)}) collective-permute-start(f32[24,128]{1,0:T(8,128)S(1)} %get-tuple-element.45), channel_id=1, source_target_pairs={{8,0},{16,8},{24,16},{0,24},{9,1},{17,9},{25,17},{1,25},{10,2},{18... | collective-permute-start | bytes 36872 | tf_op jit(solution)/shard_map/ppermute | solution.py:1200
  23.9 8.3 %all-to-all-start.1 = ((f32[8,16,128]{2,1,0:T(8,128)}), f32[8,16,128]{2,1,0:T(8,128)S(1)}, u32[]{:S(2)}, u32[]{:S(2)}) async-start(f32[8,16,128]{2,1,0:T(8,128)} %get-tuple-element.50), calls=%async_computation.1 | async-start | bytes 131072 | tf_op jit(solution)/shard_map/all_to_all | solution.py:1225
  27.2 2.7 %copy-start.8 = (f32[2048]{0:T(1024)S(1)}, f32[2048]{0:T(1024)}, u32[]{:S(2)}) copy-start(f32[2048]{0:T(1024)} %param.22) | copy-start | bytes 24580

commit v13 on v11

--- a/solution.py
+++ b/solution.py
@@ -173,6 +173,15 @@
 def neighbours_of(blocks):
     here = lax.axis_index("blk")
     return lax.rem(here + blocks - 1, blocks), lax.rem(here + 1, blocks)
+
+
+def is_odd(axis):
+    return lax.rem(lax.axis_index(axis), 2)
+
+
+def sort_sides(axis, first, second):
+    odd = is_odd(axis) == 1
+    return jnp.where(odd, second, first), jnp.where(odd, first, second)
 
 
 def one_hot(index, allowed=None):
@@ -368,8 +377,8 @@
     planes,
     moved_ref,
     recv_ref,
-    before_ref,
-    after_ref,
+    first_ref,
+    second_ref,
     air_ref,
     wind_ref,
     jac_ref,
@@ -377,11 +386,20 @@
     rows_ref,
     ocean_ref,
     avg_ref,
-    down_ref,
-    up_ref,
+    face_first_ref,
+    face_second_ref,
     surf_ref,
+    before_ref,
+    after_ref,
+    held_ref,
 ):
     geo = Geometry()
+    side = slice(0, before_ref.shape[0])
+    before_ref[...], after_ref[...] = sort_sides(
+        "blk", first_ref[side, :], second_ref[side, :]
+    )
+    odd_face = is_odd("face")
+    down_ref, up_ref = held_ref.at[odd_face], held_ref.at[1 - odd_face]
     blocks = rows_ref.shape[0]
     x_points = jac_ref.shape[0]
     levels = wind_ref.shape[0] // (2 * x_points)
@@ -520,6 +538,8 @@
             out_ref[base + 2 * number : base + 2 * number + 2, :] = surf_line(number, r)
         base += 2 * SURF_ARRAYS
         out_ref[base : base + 2, :] = surf_line(COEF_X, r) * surf_slope
+    face_first_ref[...] = held_ref[0]
+    face_second_ref[...] = held_ref[1]
 
 
 def outer_rows(x_points):
@@ -536,15 +556,18 @@
 
 
 def inner_kernel(
-    planes, avg_ref, moved_ref, before_ref, after_ref, surf_ref, wind_ref, out_ref, packs_ref
+    planes, avg_ref, moved_ref, first_ref, second_ref, surf_ref, wind_ref, out_ref, packs_ref
 ):
     geo = Geometry()
     x_points = avg_ref.shape[0] // planes
     levels = wind_ref.shape[0] // (2 * x_points)
     joined = join_edges(
         geo,
-        before_ref[SIDE_EDGE : SIDE_EDGE + ROWS, :],
-        after_ref[SIDE_EDGE : SIDE_EDGE + ROWS, :],
+        *sort_sides(
+            "blk",
+            first_ref[SIDE_EDGE : SIDE_EDGE + ROWS, :],
+            second_ref[SIDE_EDGE : SIDE_EDGE + ROWS, :],
+        ),
     )
     outer = outer_rows(x_points)
 
@@ -608,8 +631,8 @@
     inner_ref,
     packs_ref,
     surf_ref,
-    low_ref,
-    high_ref,
+    first_ref,
+    second_ref,
     wind_ref,
     rows_ref,
     ocean_ref,
@@ -619,9 +642,12 @@
     inverse_ref,
     flux_ref,
     edges_ref,
+    low_ref,
+    high_ref,
     semaphores,
 ):
     geo = Geometry()
+    low_ref[...], high_ref[...] = sort_sides("face", first_ref[...], second_ref[...])
     blocks = rows_ref.shape[0]
     left, right = neighbours_of(blocks)
     x_points = final_ref.shape[0]
@@ -959,9 +985,13 @@
     lax.fori_loop(0, count // step, some_chunks, 0)
 
 
-def send_kernel(tracers_ref, send_ref, before_ref, after_ref, *out_refs):
+def send_kernel(
+    tracers_ref, send_ref, before_ref, after_ref, first_ref, second_ref, held_ref
+):
     chunks = tracers_ref.shape[1] // LANES
-    for part, (side_ref, out_ref) in enumerate(zip((before_ref, after_ref), out_refs)):
+    odd = is_odd("blk")
+    for part, side_ref in enumerate((before_ref, after_ref)):
+        out_ref = held_ref.at[1 - odd if part else odd]
         base = side_ref.shape[0]
         out_ref[:base, :] = side_ref[...]
         cells = spread(send_ref[0:1, LANES * part : LANES * (part + 1)])
@@ -973,28 +1003,34 @@
                 tile = tracers_ref[half, LANES * k : LANES * (k + 1)]
                 rim = jnp.where(high == k, take(tile, low, 1), rim)
             out_ref[base + ROWS * group : base + ROWS * (group + 1), :] = rim
+    first_ref[...] = held_ref[0]
+    second_ref[...] = held_ref[1]
 
 
 def rim_kernel(
     starts,
-    before_ref,
-    after_ref,
+    first_ref,
+    second_ref,
     coef_ref,
     near_ref,
     area_ref,
     rows_ref,
     *refs,
 ):
-    partial_refs, (out_ref, gain_ref, first_ref) = refs[: len(starts)], refs[len(starts) :]
+    partial_refs, (out_ref, gain_ref, top_ref, sides_ref) = (
+        refs[: len(starts)],
+        refs[len(starts) :],
+    )
     chunks = coef_ref.shape[1] // LANES
     groups = out_ref.shape[0] // ROWS
-    rim_at = before_ref.shape[0] - out_ref.shape[0]
-    sides = before_ref, after_ref
+    rim_at = first_ref.shape[0] - out_ref.shape[0]
+    sides_ref[0], sides_ref[1] = sort_sides(
+        "blk", first_ref[rim_at:, :], second_ref[rim_at:, :]
+    )
     gain_ref[...] = flux_gain / area_ref[...]
 
     def source(group, s):
-        at = rim_at + ROWS * group
-        return sides[s][at : at + ROWS, :]
+        return sides_ref[s, ROWS * group : ROWS * (group + 1), :]
 
     for k in range(chunks):
         at = slice(LANES * k, LANES * (k + 1))
@@ -1004,7 +1040,7 @@
         for g in range(groups):
             half = slice(ROWS * g, ROWS * (g + 1))
             out_ref[half, at] = partial_refs[part][half, place] + totals[g]
-    first_ref[...] = out_ref[:ROWS, :]
+    top_ref[...] = out_ref[:ROWS, :]
 
 
 VMEM_SPEC = pl.BlockSpec(memory_space=pltpu.VMEM)
@@ -1033,6 +1069,18 @@
         compiler_params=pltpu.CompilerParams(vmem_limit_bytes=32 * 2**20),
         name=getattr(kernel, "func", kernel).__name__,
     )
+
+
+def swap_sides(first, second, axis):
+    count = lax.axis_size(axis)
+
+    def pairs(start):
+        swaps = []
+        for i in range(start, count, 2):
+            swaps += [(i, (i + 1) % count), ((i + 1) % count, i)]
+        return swaps
+
+    return lax.ppermute(first, axis, pairs(1)), lax.ppermute(second, axis, pairs(0))
 
 
 def body(
@@ -1109,26 +1157,27 @@
         )(ocean, edge_coef, neighbours, rate, after)
         return result
 
-    to_before, to_after = call(
+    first, second = call(
         send_kernel,
         [(SIDE_IDS + blocks + ocean_planes, LANES)] * 2,
         [VMEM_SPEC] * 4,
+        [pltpu.VMEM((2, SIDE_IDS + blocks + ocean_planes, LANES), jnp.float32)],
         cost=reads_per_chunk * ROWS * LANES,
     )(ocean, send_list, to_before, to_after)
-    onward = [(i, (i + 1) % blocks) for i in range(blocks)]
-    before = lax.ppermute(to_after, "blk", onward)
-    after = lax.ppermute(to_before, "blk", [(to, source) for source, to in onward])
-    first_part = ocean_part(starts[0], starts[1], to_before)
+    side_first, side_second = swap_sides(first, second, "blk")
+    first_part = ocean_part(starts[0], starts[1], first)
     side_rows = 2 * planes + 2 * levels + 2 * SURF_ARRAYS + 4
-    avg, down, up, surf = call(
+    avg, first, second, surf = call(
         functools.partial(panel_kernel, planes),
         [air.shape, (side_rows, LANES), (side_rows, LANES), (4 * ROWS * SURF_ARRAYS, LANES)],
         [VMEM_SPEC] * 9 + [ANY_SPEC],
+        [pltpu.VMEM((SIDE_IDS + blocks, LANES), jnp.float32) for _ in range(2)]
+        + [pltpu.VMEM((2, side_rows, LANES), jnp.float32)],
     )(
         moved,
         recv,
-        before,
-        after,
+        side_first,
+        side_second,
         air,
         wind,
         jacobian,
@@ -1136,15 +1185,13 @@
         point_ids,
         first_part,
     )
-    after_me = [(i, (i + 1) % faces) for i in range(faces)]
-    low = lax.ppermute(up, "face", after_me)
-    high = lax.ppermute(down, "face", [(to, source) for source, to in after_me])
+    face_first, face_second = swap_sides(first, second, "face")
     inner, packs = call(
         functools.partial(inner_kernel, planes),
         [((x_points - 2 * GLL) * planes, LANES), (2 * ROWS, LANES)],
         [VMEM_SPEC] * 6,
         cost=2 * air.size * 4,
-    )(avg, moved, before, after, surf, wind)
+    )(avg, moved, side_first, side_second, surf, wind)
     second_part = ocean_part(starts[1], starts[2], surf)
 
     slab, outer, final, inverse = call(
@@ -1159,10 +1206,12 @@
         [
             pltpu.VMEM((blocks, HEAD, LANES), jnp.float32),
             pltpu.VMEM((2, ROWS, LANES), jnp.float32),
+            pltpu.VMEM((side_rows, LANES), jnp.float32),
+            pltpu.VMEM((side_rows, LANES), jnp.float32),
             pltpu.SemaphoreType.DMA((3,)),
         ],
         hbm_outs=1,
-    )(avg, inner, packs, surf, low, high, wind, point_ids, second_part)
+    )(avg, inner, packs, surf, face_first, face_second, wind, point_ids, second_part)
     arrived = lax.all_to_all(slab, "blk", split_axis=0, concat_axis=0, tiled=True)
     last, hot = call(
         functools.partial(last_kernel, planes),
@@ -1175,10 +1224,11 @@
         functools.partial(rim_kernel, starts),
         [ocean.shape, area.shape, (ROWS, cells)],
         [VMEM_SPEC] * 5 + [ANY_SPEC] + [VMEM_SPEC] * len(starts),
+        [pltpu.VMEM((2, ocean_planes, LANES), jnp.float32)],
         cost=chunks * reads_per_chunk // 8 * ROWS * LANES * 4,
     )(
-        before,
-        after,
+        side_first,
+        side_second,
         edge_coef,
         neighbours,
         area,

time: 32.7 us -> 33.4 us (1.021)
  starting transfers between devices: 15.3 us -> 15.7 us
    ppermute x4, waiting for transfers between devices: 0.82 us -> 1.25 us  [the longest x2 1.08 us: swap_sides(): lax.ppermute(second, axis, pairs(0))]
  transfers between devices with their start and end apart: 6 -> 6, of which waited for: 3 -> 4; matrix products, arithmetic and copies ran while one was open for 0% -> 0% of each run, Pallas kernels for 24% -> 23%
where the time goes in v13:
time: 33.4 us; the launch traced here: 33.1 us
  starting transfers between devices  15.7 us (47%)
  Pallas kernels  12.9 us (39%)
  waiting for transfers between devices  3.09 us (9%)
  between operations  0.78 us (2%)
  local copies, waits for them, and re-layouts  0.53 us (2%)
    ppermute x2, starting transfers between devices, swap_sides(): lax.ppermute(first, axis, pairs(1))  6.2 us
    all_to_all x1, starting transfers between devices, body(): recv = lax.all_to_all(slab, 'blk', split_axis=0, concat_axis=0, tiled=True)  5.31 us
    pallas_call x3, Pallas kernels, ocean_part(): call(functools.partial(ocean_kernel, ocean_levels, start), [(ocean_planes...  4.29 us
    all_to_all x1, starting transfers between devices, body(): lax.all_to_all(slab, 'blk', split_axis=0, concat_axis=0, tiled=True)  3.64 us
    pallas_call x1, Pallas kernels, body(): call(functools.partial(start_kernel, planes), [(blocks, HEAD, LANES), air...  2.27 us
    pallas_call x1, Pallas kernels, body(): call(functools.partial(rim_kernel, starts), [ocean.shape, area.shape, (RO...  1.9 us
    pallas_call x1, Pallas kernels, body(): call(functools.partial(second_kernel, planes), [(blocks, EDGE_AT + ROWS,...  1.39 us
    all_to_all x1, waiting for transfers between devices, body(): lax.all_to_all(slab, 'blk', split_axis=0, concat_axis=0, tiled=True)  1.33 us
  transfers between devices with their start and end apart: 6, of which 4 were waited for; matrix products, arithmetic and copies ran while one was open for 0% of the time, Pallas kernels for 23%

profile of v13, /device:TPU:0, one launch (start us, length us, event | category | flops | bytes accessed | tf_op | source)
XLA Modules:
  0.0 33.1 jit_solution(9613569591869205369)
XLA Ops:
  0.6 0.0 copy-start
  0.6 2.3 %start_kernel.1 = (f32[8,8,128]{2,1,0:T(8,128)}, f32[768,128]{1,0:T(8,128)S(1)}, f32[24,128]{1,0:T(8,128)S(1)}, f32[24,128]{1,0:T(8,128)S(1)}, s32[8,128]{1,0:T(...) custom-call(s32[8,128]{1,0:T(8,128)} %bitcast.26, f32[8,128]{1,0:T(8,128)} %bitcast.27, ...), custom_call_target="tpu_custom_call" | custom-call | tf_op jit(solution)/shard_map/start_kernel/pallas_call | solution.py:1124
  2.9 0.0 copy-start.3
  2.9 0.0 copy-start.4
  2.9 5.3 %all-to-all-start = ((f32[8,8,128]{2,1,0:T(8,128)}), f32[8,8,128]{2,1,0:T(8,128)S(1)}, u32[]{:S(2)}, u32[]{:S(2)}) async-start(f32[8,8,128]{2,1,0:T(8,128)} %get-tuple-element.30), calls=%async_computation | async-start | bytes 65536 | tf_op jit(solution)/shard_map/all_to_all | solution.py:1144
  8.3 0.0 copy-start.5
  8.3 0.0 copy-done
  8.3 0.0 copy-start.2
  8.3 0.2 send_kernel.1
  8.5 0.0 copy-start.1
  8.5 0.6 %collective-permute-start.1 = (f32[56,128]{1,0:T(8,128)S(1)}, f32[56,128]{1,0:T(8,128)S(1)}, u32[]{:S(2)}, u32[]{:S(2)}) collective-permute-start(f32[56,128]{1,0:T(8,128)S(1)} %get-tuple-element.35), channel_id=1, source_target_pairs={{0,1},{1,0},{2,3},{3,2},{4,5},{5,4},{6,7},{7,6},{8,9},{9,8},{10,11... | collective-permute-start | bytes 86024 | tf_op jit(solution)/shard_map/ppermute | solution.py:1083
  9.1 2.5 %collective-permute-start = (f32[56,128]{1,0:T(8,128)S(1)}, f32[56,128]{1,0:T(8,128)S(1)}, u32[]{:S(2)}, u32[]{:S(2)}) collective-permute-start(f32[56,128]{1,0:T(8,128)S(1)} %get-tuple-element.34.after_ref), channel_id=1, source_target_pairs={{1,2},{2,1},{3,4},{4,3},{5,6},{6,5},{7,0},{0,7},{9,10},{10,9},{11,... | collective-permute-start | bytes 86024 | tf_op jit(solution)/shard_map/ppermute | solution.py:1083
  11.6 0.0 copy-done.3
  11.6 0.0 copy-done.4
  11.6 0.0 copy-done.5
  11.6 0.0 copy-start.6
  11.6 0.0 copy-start.7
  11.6 1.1 %ocean_kernel.3.ocean_ref.refs_0_ = f32[32,512]{1,0:T(8,128)S(1)} custom-call(f32[32,2048]{1,0:T(8,128)S(1)} %bitcast.12, f32[6,2048]{1,0:T(8,128)S(1)} %copy-done.3, s32[6,2048]{1,0:T(8,128)S(1)} %copy-done.4, f32[16,128]{1,0:T(8,128)S(1)} %bitcast.21, f32[56,128]{1,0:T(8,128)S(1)} %get-tuple-element.34.after_ref), custom_call_target="tpu_custom_call" | custom-call | bytes 3145728 | tf_op jit(solution)/shard_map/ocean_kernel/pallas_call | solution.py:1151
  12.7 0.5 %all-to-all-done.recv_ref = f32[8,8,128]{2,1,0:T(8,128)S(1)} async-done(((f32[8,8,128]{2,1,0:T(8,128)}), f32[8,8,128]{2,1,0:T(8,128)S(1)}, u32[]{:S(2)}, u32[]{:S(2)}) %all-to-all-start) | async-done | bytes 32800 | tf_op jit(solution)/shard_map/all_to_all | solution.py:1144
  13.2 0.0 collective-permute-done.1.second_ref
  13.2 0.2 collective-permute-done.first_ref
  13.4 0.0 copy-done.2
  13.4 0.0 copy-done.1
  13.4 0.0 copy-done.6
  13.4 0.0 copy-done.7
  13.4 0.5 %panel_kernel.1 = (f32[768,128]{1,0:T(8,128)S(1)}, f32[144,128]{1,0:T(8,128)S(1)}, f32[144,128]{1,0:T(8,128)S(1)}, f32[192,128]{1,0:T(8,128)S(1)}) custom-call(f32[768,128]{1,0:T(8,128)S(1)} %get-tuple-element.29.moved_ref, f32[8,8,128]{2,1,0:T(8,128)S(1)} %all-to-all-done.recv_ref, f32[56,128]{1,0:T(8,128)S(1)} %collective-permute-done.first_ref, ...), custom_call_target="tpu_custom_call" | custom-call | tf_op jit(solution)/shard_map/panel_kernel/pallas_call | solution.py:1170
  14.0 3.7 %collective-permute-start.2 = (f32[144,128]{1,0:T(8,128)S(1)}, f32[144,128]{1,0:T(8,128)S(1)}, u32[]{:S(2)}, u32[]{:S(2)}) collective-permute-start(f32[144,128]{1,0:T(8,128)S(1)} %get-tuple-element.41), channel_id=1, source_target_pairs={{8,16},{16,8},{24,0},{0,24},{9,17},{17,9},{25,1},{1,25},{10,18},{1... | collective-permute-start | bytes 221192 | tf_op jit(solution)/shard_map/ppermute | solution.py:1083
  17.6 0.0 collective-permute-start.3
  17.6 2.1 %ocean_kernel.4.ocean_ref.refs_1_ = f32[32,1024]{1,0:T(8,128)S(1)} custom-call(f32[32,2048]{1,0:T(8,128)S(1)} %bitcast.13, f32[6,2048]{1,0:T(8,128)S(1)} %copy-done.3, s32[6,2048]{1,0:T(8,128)S(1)} %copy-done.4, f32[16,128]{1,0:T(8,128)S(1)} %bitcast.22, f32[192,128]{1,0:T(8,128)S(1)} %get-tuple-element.38.surf_ref.after_ref), custom_call_target="tpu_custom_call" | custom-call | bytes 6291456 | tf_op jit(solution)/shard_map/ocean_kernel/pallas_call | solution.py:1151
  19.8 1.1 %inner_kernel.1 = (f32[384,128]{1,0:T(8,128)S(1)}, f32[16,128]{1,0:T(8,128)S(1)}) custom-call(f32[768,128]{1,0:T(8,128)S(1)} %get-tuple-element.37.avg_ref, f32[768,128]{1,0:T(8,128)S(1)} %get-tuple-element.29.moved_ref, f32[56,128]{1,0:T(8,128)S(1)} %collective-permute-done.first_ref, f32[56,128]{1,0:T(8,128)S(1)} %collective-permute-done.1.second_ref, ...), custom_call_target="tpu_custom_call" | custom-call | bytes 786432 | tf_op jit(solution)/shard_map/inner_kernel/pallas_call | solution.py:1189
  20.9 0.0 collective-permute-done.2.first_ref
  20.9 1.1 %collective-permute-done.3.second_ref = f32[144,128]{1,0:T(8,128)S(1)} collective-permute-done((f32[144,128]{1,0:T(8,128)S(1)}, f32[144,128]{1,0:T(8,128)S(1)}, u32[]{:S(2)}, u32[]{:S(2)}) %collective-permute-start.3) | collective-permute-done | bytes 73760 | tf_op jit(solution)/shard_map/ppermute | solution.py:1083
  22.0 1.4 %second_kernel.1 = (f32[8,16,128]{2,1,0:T(8,128)}, f32[480,128]{1,0:T(8,128)S(1)}, f32[16,128]{1,0:T(8,128)S(1)}, f32[16,128]{1,0:T(8,128)S(1)}) custom-call(f32[768,128]{1,0:T(8,128)S(1)} %get-tuple-element.37.avg_ref, f32[384,128]{1,0:T(8,128)S(1)} %get-tuple-element.39.inner_ref, f32[16,128]{1,0:T(8,128)S(1)} %get-tuple-element.40.packs_ref, ...), custom_call_target="tpu_custom_call" | custom-call | tf_op jit(solution)/shard_map/second_kernel/pallas_call | solution.py:1197
  23.4 3.6 %all-to-all-start.1 = ((f32[8,16,128]{2,1,0:T(8,128)}), f32[8,16,128]{2,1,0:T(8,128)S(1)}, u32[]{:S(2)}, u32[]{:S(2)}) async-start(f32[8,16,128]{2,1,0:T(8,128)} %get-tuple-element.47), calls=%async_computation.1 | async-start | bytes 131072 | tf_op jit(solution)/shard_map/all_to_all | solution.py:1215
  27.0 1.1 %ocean_kernel.5.refs_2_ = f32[32,512]{1,0:T(8,128)S(1)} custom-call(f32[32,2048]{1,0:T(8,128)S(1)} %bitcast.14, f32[6,2048]{1,0:T(8,128)S(1)} %copy-done.3, s32[6,2048]{1,0:T(8,128)S(1)} %copy-done.4, f32[16,128]{1,0:T(8,128)S(1)} %bitcast.23, f32[16,128]{1,0:T(8,128)S(1)} %get-tuple-element.48.after_ref.rows_ref.final_ref), custom_call_target="tpu_custom_call" | custom-call | bytes 3145728 | tf_op jit(solution)/shard_map/ocean_kernel/pallas_call | solution.py:1151
  28.1 0.0 copy-start.8
  28.1 0.2 last_kernel.1
  28.3 0.5 %copy-done.8 = f32[2048]{0:T(1024)S(1)} copy-done((f32[2048]{0:T(1024)S(1)}, f32[2048]{0:T(1024)}, u32[]{:S(2)}) %copy-start.8) | copy-done | bytes 8216
  28.8 1.9 %rim_kernel.1 = (f32[32,2048]{1,0:T(8,128)}, f32[16,128]{1,0:T(8,128)S(1)}, f32[8,2048]{1,0:T(8,128)S(1)}) custom-call(f32[56,128]{1,0:T(8,128)S(1)} %collective-permute-done.first_ref, f32[56,128]{1,0:T(8,128)S(1)} %collective-permute-done.1.second_ref, f32[6,2048]{1,0:T(8,128)S(1)} %copy-done.3, s32[6,2048]{1,0:T(8,128)S(1)} %copy-done.4, ...), custom_call_target="tpu_custom_call" | custom-call | bytes 3145728 | tf_op jit(solution)/shard_map/rim_kernel/pallas_call | solution.py:1223
  30.7 1.3 %all-to-all-done.1.recv_ref = f32[8,16,128]{2,1,0:T(8,128)S(1)} async-done(((f32[8,16,128]{2,1,0:T(8,128)}), f32[8,16,128]{2,1,0:T(8,128)S(1)}, u32[]{:S(2)}, u32[]{:S(2)}) %all-to-all-start.1) | async-done | bytes 65568 | tf_op jit(solution)/shard_map/all_to_all | solution.py:1215
  32.0 1.0 %end_kernel.1 = (f32[32,2048]{1,0:T(8,128)}, f32[768,128]{1,0:T(8,128)}) custom-call(f32[768,128]{1,0:T(8,128)S(1)} %get-tuple-element.46.last_ref, f32[8,16,128]{2,1,0:T(8,128)S(1)} %all-to-all-done.1.recv_ref, f32[16,128]{1,0:T(8,128)S(1)} %get-tuple-element.48.after_ref.rows_ref.final_ref, ...), custom_call_target="tpu_custom_call", output_to_operand_aliasing={{0}: (9, {})} | custom-call | tf_op jit(solution)/shard_map/end_kernel/pallas_call | solution.py:1240
Async XLA Ops:
  0.6 7.6 %copy-start = (f32[2,16,2048]{2,1,0:T(8,128)S(1)}, f32[2,16,2048]{2,1,0:T(8,128)}, u32[]{:S(2)}) copy-start(f32[2,16,2048]{2,1,0:T(8,128)} %param.18) | copy-start | bytes 786436
  2.9 8.7 %copy-start.3 = (f32[6,2048]{1,0:T(8,128)S(1)}, f32[6,2048]{1,0:T(8,128)}, u32[]{:S(2)}) copy-start(f32[6,2048]{1,0:T(8,128)} %coef_ref.7) | copy-start | bytes 147460
  2.9 8.7 %copy-start.4 = (s32[6,2048]{1,0:T(8,128)S(1)}, s32[6,2048]{1,0:T(8,128)}, u32[]{:S(2)}) copy-start(s32[6,2048]{1,0:T(8,128)} %near_ref.7) | copy-start | bytes 147460
  2.9 10.3 %all-to-all-start = ((f32[8,8,128]{2,1,0:T(8,128)}), f32[8,8,128]{2,1,0:T(8,128)S(1)}, u32[]{:S(2)}, u32[]{:S(2)}) async-start(f32[8,8,128]{2,1,0:T(8,128)} %get-tuple-element.30), calls=%async_computation | async-start | bytes 65536 | tf_op jit(solution)/shard_map/all_to_all | solution.py:1144
  8.3 3.4 %copy-start.5 = (f32[2048]{0:T(1024)S(1)}, f32[2048]{0:T(1024)}, u32[]{:S(2)}) copy-start(f32[2048]{0:T(1024)} %param.21) | copy-start | bytes 24580
  8.3 5.1 %copy-start.2 = (f32[3,16,16,128]{3,2,1,0:T(8,128)S(1)}, f32[3,16,16,128]{3,2,1,0:T(8,128)}, u32[]{:S(2)}) copy-start(f32[3,16,16,128]{3,2,1,0:T(8,128)} %param.13) | copy-start | bytes 1179652
  8.5 4.9 %copy-start.1 = (f32[2,16,16,128]{3,2,1,0:T(8,128)S(1)}, f32[2,16,16,128]{3,2,1,0:T(8,128)}, u32[]{:S(2)}) copy-start(f32[2,16,16,128]{3,2,1,0:T(8,128)} %param.14) | copy-start | bytes 786436
  8.5 4.7 %collective-permute-start.1 = (f32[56,128]{1,0:T(8,128)S(1)}, f32[56,128]{1,0:T(8,128)S(1)}, u32[]{:S(2)}, u32[]{:S(2)}) collective-permute-start(f32[56,128]{1,0:T(8,128)S(1)} %get-tuple-element.35), channel_id=1, source_target_pairs={{0,1},{1,0},{2,3},{3,2},{4,5},{5,4},{6,7},{7,6},{8,9},{9,8},{10,11... | collective-permute-start | bytes 86024 | tf_op jit(solution)/shard_map/ppermute | solution.py:1083
  9.1 4.3 %collective-permute-start = (f32[56,128]{1,0:T(8,128)S(1)}, f32[56,128]{1,0:T(8,128)S(1)}, u32[]{:S(2)}, u32[]{:S(2)}) collective-permute-start(f32[56,128]{1,0:T(8,128)S(1)} %get-tuple-element.34.after_ref), channel_id=1, source_target_pairs={{1,2},{2,1},{3,4},{4,3},{5,6},{6,5},{7,0},{0,7},{9,10},{10,9},{11,... | collective-permute-start | bytes 86024 | tf_op jit(solution)/shard_map/ppermute | solution.py:1083
  11.6 1.8 %copy-start.6 = (f32[16,128]{1,0:T(8,128)S(1)}, f32[16,128]{1,0:T(8,128)}, u32[]{:S(2)}) copy-start(f32[16,128]{1,0:T(8,128)} %jac_ref.1) | copy-start | bytes 24580
  11.6 1.8 %copy-start.7 = (f32[16,128]{1,0:T(8,128)S(1)}, f32[16,128]{1,0:T(8,128)}, u32[]{:S(2)}) copy-start(f32[16,128]{1,0:T(8,128)} %land_ref.1) | copy-start | bytes 24580
  14.0 6.9 %collective-permute-start.2 = (f32[144,128]{1,0:T(8,128)S(1)}, f32[144,128]{1,0:T(8,128)S(1)}, u32[]{:S(2)}, u32[]{:S(2)}) collective-permute-start(f32[144,128]{1,0:T(8,128)S(1)} %get-tuple-element.41), channel_id=1, source_target_pairs={{8,16},{16,8},{24,0},{0,24},{9,17},{17,9},{25,1},{1,25},{10,18},{1... | collective-permute-start | bytes 221192 | tf_op jit(solution)/shard_map/ppermute | solution.py:1083
  17.6 4.4 %collective-permute-start.3 = (f32[144,128]{1,0:T(8,128)S(1)}, f32[144,128]{1,0:T(8,128)S(1)}, u32[]{:S(2)}, u32[]{:S(2)}) collective-permute-start(f32[144,128]{1,0:T(8,128)S(1)} %get-tuple-element.42), channel_id=1, source_target_pairs={{0,8},{8,0},{16,24},{24,16},{1,9},{9,1},{17,25},{25,17},{2,10},{10... | collective-permute-start | bytes 221192 | tf_op jit(solution)/shard_map/ppermute | solution.py:1083
  23.4 8.7 %all-to-all-start.1 = ((f32[8,16,128]{2,1,0:T(8,128)}), f32[8,16,128]{2,1,0:T(8,128)S(1)}, u32[]{:S(2)}, u32[]{:S(2)}) async-start(f32[8,16,128]{2,1,0:T(8,128)} %get-tuple-element.47), calls=%async_computation.1 | async-start | bytes 131072 | tf_op jit(solution)/shard_map/all_to_all | solution.py:1215
  28.1 0.7 %copy-start.8 = (f32[2048]{0:T(1024)S(1)}, f32[2048]{0:T(1024)}, u32[]{:S(2)}) copy-start(f32[2048]{0:T(1024)} %param.22) | copy-start | bytes 24580

commit v14 on v11

--- a/solution.py
+++ b/solution.py
@@ -379,6 +379,8 @@
     avg_ref,
     down_ref,
     up_ref,
+    down_again_ref,
+    up_again_ref,
     surf_ref,
 ):
     geo = Geometry()
@@ -520,6 +522,8 @@
             out_ref[base + 2 * number : base + 2 * number + 2, :] = surf_line(number, r)
         base += 2 * SURF_ARRAYS
         out_ref[base : base + 2, :] = surf_line(COEF_X, r) * surf_slope
+    down_again_ref[...] = down_ref[...]
+    up_again_ref[...] = up_ref[...]
 
 
 def outer_rows(x_points):
@@ -608,20 +612,26 @@
     inner_ref,
     packs_ref,
     surf_ref,
-    low_ref,
-    high_ref,
+    high_odd_ref,
+    low_odd_ref,
+    low_even_ref,
+    high_even_ref,
     wind_ref,
     rows_ref,
-    ocean_ref,
     slab_out,
     sums_ref,
     final_ref,
     inverse_ref,
     flux_ref,
     edges_ref,
+    low_ref,
+    high_ref,
     semaphores,
 ):
     geo = Geometry()
+    odd = lax.rem(lax.axis_index("face"), 2) == 1
+    low_ref[...] = jnp.where(odd, low_even_ref[...], low_odd_ref[...])
+    high_ref[...] = jnp.where(odd, high_even_ref[...], high_odd_ref[...])
     blocks = rows_ref.shape[0]
     left, right = neighbours_of(blocks)
     x_points = final_ref.shape[0]
@@ -1097,7 +1107,7 @@
 
     chunks = cells // LANES
     reads_per_chunk = edge_coef.shape[0] * chunks * (ocean_planes // ROWS)
-    starts = (0, chunks // 4, chunks * 3 // 4)
+    starts = (0, chunks * 6 // 16)
 
     def ocean_part(start, end, after):
         (result,) = call(
@@ -1120,9 +1130,9 @@
     after = lax.ppermute(to_before, "blk", [(to, source) for source, to in onward])
     first_part = ocean_part(starts[0], starts[1], to_before)
     side_rows = 2 * planes + 2 * levels + 2 * SURF_ARRAYS + 4
-    avg, down, up, surf = call(
+    avg, down, up, down_again, up_again, surf = call(
         functools.partial(panel_kernel, planes),
-        [air.shape, (side_rows, LANES), (side_rows, LANES), (4 * ROWS * SURF_ARRAYS, LANES)],
+        [air.shape] + [(side_rows, LANES)] * 4 + [(4 * ROWS * SURF_ARRAYS, LANES)],
         [VMEM_SPEC] * 9 + [ANY_SPEC],
     )(
         moved,
@@ -1136,17 +1146,17 @@
         point_ids,
         first_part,
     )
-    after_me = [(i, (i + 1) % faces) for i in range(faces)]
-    low = lax.ppermute(up, "face", after_me)
-    high = lax.ppermute(down, "face", [(to, source) for source, to in after_me])
+    odd_faces, even_faces = range(1, faces, 2), range(0, faces, 2)
+    high_odd = lax.ppermute(down, "face", [(i, (i - 1) % faces) for i in odd_faces])
+    low_odd = lax.ppermute(up, "face", [(i, (i + 1) % faces) for i in odd_faces])
+    low_even = lax.ppermute(up_again, "face", [(i, (i + 1) % faces) for i in even_faces])
+    high_even = lax.ppermute(down_again, "face", [(i, (i - 1) % faces) for i in even_faces])
     inner, packs = call(
         functools.partial(inner_kernel, planes),
         [((x_points - 2 * GLL) * planes, LANES), (2 * ROWS, LANES)],
         [VMEM_SPEC] * 6,
         cost=2 * air.size * 4,
     )(avg, moved, before, after, surf, wind)
-    second_part = ocean_part(starts[1], starts[2], surf)
-
     slab, outer, final, inverse = call(
         functools.partial(second_kernel, planes),
         [
@@ -1155,14 +1165,27 @@
             (x_points, y_points),
             (x_points, y_points),
         ],
-        [VMEM_SPEC] * 8 + [ANY_SPEC],
+        [VMEM_SPEC] * 10,
         [
             pltpu.VMEM((blocks, HEAD, LANES), jnp.float32),
             pltpu.VMEM((2, ROWS, LANES), jnp.float32),
+            pltpu.VMEM((side_rows, LANES), jnp.float32),
+            pltpu.VMEM((side_rows, LANES), jnp.float32),
             pltpu.SemaphoreType.DMA((3,)),
         ],
         hbm_outs=1,
-    )(avg, inner, packs, surf, low, high, wind, point_ids, second_part)
+    )(
+        avg,
+        inner,
+        packs,
+        surf,
+        high_odd,
+        low_odd,
+        low_even,
+        high_even,
+        wind,
+        point_ids,
+    )
     arrived = lax.all_to_all(slab, "blk", split_axis=0, concat_axis=0, tiled=True)
     last, hot = call(
         functools.partial(last_kernel, planes),
@@ -1170,7 +1193,7 @@
         [VMEM_SPEC] * 4,
         cost=2 * air.size * 4,
     )(inner, outer, inverse, cell_ids)
-    third_part = ocean_part(starts[2], chunks, final)
+    second_part = ocean_part(starts[1], chunks, final)
     partial, gain, first_rows = call(
         functools.partial(rim_kernel, starts),
         [ocean.shape, area.shape, (ROWS, cells)],
@@ -1185,7 +1208,6 @@
         final,
         first_part,
         second_part,
-        third_part,
     )
     ocean_final, air_final = call(
         functools.partial(end_kernel, planes),

time: 32.7 us -> 37.9 us (1.16)
  starting transfers between devices: 15.3 us -> 21.9 us
  waiting for transfers between devices: 2.77 us -> 1.26 us
    ppermute x2 -> x4, starting transfers between devices: 3.88 us -> 10.5 us  [the longest x1 5.68 us: body(): lax.ppermute(up_again, 'face', [(i, (i + 1) % faces) for i in even_faces])]
    all_to_all x1, waiting for transfers between devices: 1.26 us -> 0.01 us  [body(): lax.all_to_all(slab, 'blk', split_axis=0, concat_axis=0, tiled=True)]
    all_to_all x1, waiting for transfers between devices: 0.69 us -> 0.17 us  [body(): recv = lax.all_to_all(slab, 'blk', split_axis=0, concat_axis=0, tiled=True)]
    ppermute x2 -> x4, waiting for transfers between devices: 0.82 us -> 1.08 us  [the longest x1 1.08 us: body(): lax.ppermute(down_again, 'face', [(i, (i - 1) % faces) for i in even_faces])]
    pallas_call x3 -> x2, Pallas kernels: 4.29 us -> 4.25 us  [ocean_part(): call(functools.partial(ocean_kernel, ocean_levels, start), [(ocean_planes...]
  transfers between devices with their start and end apart: 6 -> 8, of which waited for: 3 -> 2; matrix products, arithmetic and copies ran while one was open for 0% -> 0% of each run, Pallas kernels for 24% -> 21%
where the time goes in v14:
time: 37.9 us; the launch traced here: 37.4 us
  starting transfers between devices  21.9 us (58%)
  Pallas kernels  12.9 us (34%)
  waiting for transfers between devices  1.26 us (3%)
  between operations  0.85 us (2%)
  local copies, waits for them, and re-layouts  0.53 us (1%)
    ppermute x1, starting transfers between devices, body(): lax.ppermute(up_again, 'face', [(i, (i + 1) % faces) for i in even_faces])  5.68 us
    all_to_all x1, starting transfers between devices, body(): recv = lax.all_to_all(slab, 'blk', split_axis=0, concat_axis=0, tiled=True)  5.31 us
    pallas_call x2, Pallas kernels, ocean_part(): call(functools.partial(ocean_kernel, ocean_levels, start), [(ocean_planes...  4.25 us
    all_to_all x1, starting transfers between devices, body(): lax.all_to_all(slab, 'blk', split_axis=0, concat_axis=0, tiled=True)  3.36 us
    pallas_call x1, Pallas kernels, body(): call(functools.partial(start_kernel, planes), [(blocks, HEAD, LANES), air...  2.27 us
    ppermute x1, starting transfers between devices, body(): lax.ppermute(to_before, 'blk', [(to, source) for source, to in onward])  2.24 us
    ppermute x1, starting transfers between devices, body(): lax.ppermute(down_again, 'face', [(i, (i - 1) % faces) for i in even_faces])  2.19 us
    pallas_call x1, Pallas kernels, body(): call(functools.partial(rim_kernel, starts), [ocean.shape, area.shape, (RO...  1.9 us
  transfers between devices with their start and end apart: 8, of which 2 were waited for; matrix products, arithmetic and copies ran while one was open for 0% of the time, Pallas kernels for 21%

profile of v14, /device:TPU:0, one launch (start us, length us, event | category | flops | bytes accessed | tf_op | source)
XLA Modules:
  0.0 37.4 jit_solution(3985677788594441114)
XLA Ops:
  0.6 0.0 copy-start.1
  0.6 2.3 %start_kernel.1 = (f32[8,8,128]{2,1,0:T(8,128)}, f32[768,128]{1,0:T(8,128)S(1)}, f32[24,128]{1,0:T(8,128)S(1)}, f32[24,128]{1,0:T(8,128)S(1)}, s32[8,128]{1,0:T(...) custom-call(s32[8,128]{1,0:T(8,128)} %bitcast.24, f32[8,128]{1,0:T(8,128)} %bitcast.25, ...), custom_call_target="tpu_custom_call" | custom-call | tf_op jit(solution)/shard_map/start_kernel/pallas_call | solution.py:1086
  2.9 0.0 copy-start.3
  2.9 0.0 copy-start.4
  2.9 5.3 %all-to-all-start = ((f32[8,8,128]{2,1,0:T(8,128)}), f32[8,8,128]{2,1,0:T(8,128)S(1)}, u32[]{:S(2)}, u32[]{:S(2)}) async-start(f32[8,8,128]{2,1,0:T(8,128)} %get-tuple-element.32), calls=%async_computation | async-start | bytes 65536 | tf_op jit(solution)/shard_map/all_to_all | solution.py:1106
  8.3 0.0 copy-start.7
  8.3 0.0 copy-done.1
  8.3 0.0 copy-start.2
  8.3 0.2 send_kernel.1
  8.5 0.5 %collective-permute-start = (f32[56,128]{1,0:T(8,128)S(1)}, f32[56,128]{1,0:T(8,128)S(1)}, u32[]{:S(2)}, u32[]{:S(2)}) collective-permute-start(f32[56,128]{1,0:T(8,128)S(1)} %get-tuple-element.36), channel_id=1, source_target_pairs={{0,1},{1,2},{2,3},{3,4},{4,5},{5,6},{6,7},{7,0},{8,9},{9,10},{10,1... | collective-permute-start | bytes 86024 | tf_op jit(solution)/shard_map/ppermute | solution.py:1129
  9.0 2.2 %collective-permute-start.1 = (f32[56,128]{1,0:T(8,128)S(1)}, f32[56,128]{1,0:T(8,128)S(1)}, u32[]{:S(2)}, u32[]{:S(2)}) collective-permute-start(f32[56,128]{1,0:T(8,128)S(1)} %get-tuple-element.37.after_ref), channel_id=1, source_target_pairs={{1,0},{2,1},{3,2},{4,3},{5,4},{6,5},{7,6},{0,7},{9,8},{10,9},{11,1... | collective-permute-start | bytes 86024 | tf_op jit(solution)/shard_map/ppermute | solution.py:1130
  11.3 0.0 copy-done.3
  11.3 0.0 copy-done.4
  11.3 0.0 copy-done.7
  11.3 0.0 copy-start
  11.3 0.0 copy-start.5
  11.3 0.0 copy-start.6
  11.3 1.6 %ocean_kernel.2.ocean_ref.refs_0_ = f32[32,768]{1,0:T(8,128)S(1)} custom-call(f32[32,2048]{1,0:T(8,128)S(1)} %bitcast.16, f32[6,2048]{1,0:T(8,128)S(1)} %copy-done.3, s32[6,2048]{1,0:T(8,128)S(1)} %copy-done.4, f32[16,128]{1,0:T(8,128)S(1)} %bitcast.20, f32[56,128]{1,0:T(8,128)S(1)} %get-tuple-element.37.after_ref), custom_call_target="tpu_custom_call" | custom-call | bytes 4718592 | tf_op jit(solution)/shard_map/ocean_kernel/pallas_call | solution.py:1113
  12.9 0.2 all-to-all-done.recv_ref
  13.1 0.0 collective-permute-done.before_ref
  13.1 0.0 collective-permute-done.1.after_ref
  13.1 0.0 copy-done.2
  13.1 0.0 copy-done
  13.1 0.0 copy-done.5
  13.1 0.0 copy-done.6
  13.1 0.5 %panel_kernel.1 = (f32[768,128]{1,0:T(8,128)S(1)}, f32[144,128]{1,0:T(8,128)S(1)}, f32[144,128]{1,0:T(8,128)S(1)}, f32[144,128]{1,0:T(8,128)S(1)}, f32[144,128]{1,0:T(8,128)S(1)}, /*index=5*/f32[192,128]{1,0:T(8,128)S(1)}) custom-call(f32[768,128]{1,0:T(8,128)S(1)} %get-tuple-element.31.moved_ref, f32[8,8,128]{2,1,0:T(8,128)S(1)} %all-to-all-done.recv_ref, ...), custom_call_target="tpu_custom_call" | custom-call | tf_op jit(solution)/shard_map/panel_kernel/pallas_call | solution.py:1133
  13.6 1.3 %collective-permute-start.2 = (f32[144,128]{1,0:T(8,128)S(1)}, f32[144,128]{1,0:T(8,128)S(1)}, u32[]{:S(2)}, u32[]{:S(2)}) collective-permute-start(f32[144,128]{1,0:T(8,128)S(1)} %get-tuple-element.43), channel_id=1, source_target_pairs={{8,0},{24,16},{9,1},{25,17},{10,2},{26,18},{11,3},{27,19},{12,4},{... | collective-permute-start | bytes 221192 | tf_op jit(solution)/shard_map/ppermute | solution.py:1150
  14.9 1.3 %collective-permute-start.3 = (f32[144,128]{1,0:T(8,128)S(1)}, f32[144,128]{1,0:T(8,128)S(1)}, u32[]{:S(2)}, u32[]{:S(2)}) collective-permute-start(f32[144,128]{1,0:T(8,128)S(1)} %get-tuple-element.44), channel_id=1, source_target_pairs={{8,16},{24,0},{9,17},{25,1},{10,18},{26,2},{11,19},{27,3},{12,20},... | collective-permute-start | bytes 221192 | tf_op jit(solution)/shard_map/ppermute | solution.py:1151
  16.2 5.7 %collective-permute-start.4 = (f32[144,128]{1,0:T(8,128)S(1)}, f32[144,128]{1,0:T(8,128)S(1)}, u32[]{:S(2)}, u32[]{:S(2)}) collective-permute-start(f32[144,128]{1,0:T(8,128)S(1)} %get-tuple-element.45), channel_id=1, source_target_pairs={{0,8},{16,24},{1,9},{17,25},{2,10},{18,26},{3,11},{19,27},{4,12},{... | collective-permute-start | bytes 221192 | tf_op jit(solution)/shard_map/ppermute | solution.py:1152
  21.9 2.2 %collective-permute-start.5 = (f32[144,128]{1,0:T(8,128)S(1)}, f32[144,128]{1,0:T(8,128)S(1)}, u32[]{:S(2)}, u32[]{:S(2)}) collective-permute-start(f32[144,128]{1,0:T(8,128)S(1)} %get-tuple-element.46), channel_id=1, source_target_pairs={{0,24},{16,8},{1,25},{17,9},{2,26},{18,10},{3,27},{19,11},{4,28},{... | collective-permute-start | bytes 221192 | tf_op jit(solution)/shard_map/ppermute | solution.py:1153
  24.1 1.1 %inner_kernel.1 = (f32[384,128]{1,0:T(8,128)S(1)}, f32[16,128]{1,0:T(8,128)S(1)}) custom-call(f32[768,128]{1,0:T(8,128)S(1)} %get-tuple-element.39.avg_ref, f32[768,128]{1,0:T(8,128)S(1)} %get-tuple-element.31.moved_ref, f32[56,128]{1,0:T(8,128)S(1)} %collective-permute-done.before_ref, f32[56,128]{1,0:T(8,128)S(1)} %collective-permute-done.1.after_ref, ...), custom_call_target="tpu_custom_call" | custom-call | bytes 786432 | tf_op jit(solution)/shard_map/inner_kernel/pallas_call | solution.py:1154
  25.3 0.0 collective-permute-done.2.high_odd_ref
  25.3 0.0 collective-permute-done.3.low_odd_ref
  25.3 0.0 collective-permute-done.4.low_even_ref
  25.3 1.1 %collective-permute-done.5.high_even_ref = f32[144,128]{1,0:T(8,128)S(1)} collective-permute-done((f32[144,128]{1,0:T(8,128)S(1)}, f32[144,128]{1,0:T(8,128)S(1)}, u32[]{:S(2)}, u32[]{:S(2)}) %collective-permute-start.5) | collective-permute-done | bytes 73760 | tf_op jit(solution)/shard_map/ppermute | solution.py:1153
  26.4 1.4 %second_kernel.1 = (f32[8,16,128]{2,1,0:T(8,128)}, f32[480,128]{1,0:T(8,128)S(1)}, f32[16,128]{1,0:T(8,128)S(1)}, f32[16,128]{1,0:T(8,128)S(1)}) custom-call(f32[768,128]{1,0:T(8,128)S(1)} %get-tuple-element.39.avg_ref, f32[384,128]{1,0:T(8,128)S(1)} %get-tuple-element.41.inner_ref, f32[16,128]{1,0:T(8,128)S(1)} %get-tuple-element.42.packs_ref, ...), custom_call_target="tpu_custom_call" | custom-call | tf_op jit(solution)/shard_map/second_kernel/pallas_call | solution.py:1160
  27.8 3.4 %all-to-all-start.1 = ((f32[8,16,128]{2,1,0:T(8,128)}), f32[8,16,128]{2,1,0:T(8,128)S(1)}, u32[]{:S(2)}, u32[]{:S(2)}) async-start(f32[8,16,128]{2,1,0:T(8,128)} %get-tuple-element.51), calls=%async_computation.1 | async-start | bytes 131072 | tf_op jit(solution)/shard_map/all_to_all | solution.py:1189
  31.1 2.6 %ocean_kernel.3.refs_1_ = f32[32,1280]{1,0:T(8,128)S(1)} custom-call(f32[32,2048]{1,0:T(8,128)S(1)} %bitcast.17, f32[6,2048]{1,0:T(8,128)S(1)} %copy-done.3, s32[6,2048]{1,0:T(8,128)S(1)} %copy-done.4, f32[16,128]{1,0:T(8,128)S(1)} %bitcast.21, f32[16,128]{1,0:T(8,128)S(1)} %get-tuple-element.52.after_ref.rows_ref.final_ref), custom_call_target="tpu_custom_call" | custom-call | bytes 7864320 | tf_op jit(solution)/shard_map/ocean_kernel/pallas_call | solution.py:1113
  33.8 0.0 copy-start.8
  33.8 0.2 last_kernel.1
  34.0 0.5 %copy-done.8 = f32[2048]{0:T(1024)S(1)} copy-done((f32[2048]{0:T(1024)S(1)}, f32[2048]{0:T(1024)}, u32[]{:S(2)}) %copy-start.8) | copy-done | bytes 8216
  34.5 1.9 %rim_kernel.1 = (f32[32,2048]{1,0:T(8,128)}, f32[16,128]{1,0:T(8,128)S(1)}, f32[8,2048]{1,0:T(8,128)S(1)}) custom-call(f32[56,128]{1,0:T(8,128)S(1)} %collective-permute-done.before_ref, f32[56,128]{1,0:T(8,128)S(1)} %collective-permute-done.1.after_ref, f32[6,2048]{1,0:T(8,128)S(1)} %copy-done.3, s32[6,2048]{1,0:T(8,128)S(1)} %copy-done.4, ...), custom_call_target="tpu_custom_call" | custom-call | bytes 3145728 | tf_op jit(solution)/shard_map/rim_kernel/pallas_call | solution.py:1197
  36.4 0.0 all-to-all-done.1.recv_ref
  36.4 1.0 %end_kernel.1 = (f32[32,2048]{1,0:T(8,128)}, f32[768,128]{1,0:T(8,128)}) custom-call(f32[768,128]{1,0:T(8,128)S(1)} %get-tuple-element.50.last_ref, f32[8,16,128]{2,1,0:T(8,128)S(1)} %all-to-all-done.1.recv_ref, f32[16,128]{1,0:T(8,128)S(1)} %get-tuple-element.52.after_ref.rows_ref.final_ref, ...), custom_call_target="tpu_custom_call", output_to_operand_aliasing={{0}: (9, {})} | custom-call | tf_op jit(solution)/shard_map/end_kernel/pallas_call | solution.py:1212
Async XLA Ops:
  0.6 7.6 %copy-start.1 = (f32[2,16,2048]{2,1,0:T(8,128)S(1)}, f32[2,16,2048]{2,1,0:T(8,128)}, u32[]{:S(2)}) copy-start(f32[2,16,2048]{2,1,0:T(8,128)} %param.18) | copy-start | bytes 786436
  2.9 8.4 %copy-start.3 = (f32[6,2048]{1,0:T(8,128)S(1)}, f32[6,2048]{1,0:T(8,128)}, u32[]{:S(2)}) copy-start(f32[6,2048]{1,0:T(8,128)} %coef_ref.5) | copy-start | bytes 147460
  2.9 8.3 %copy-start.4 = (s32[6,2048]{1,0:T(8,128)S(1)}, s32[6,2048]{1,0:T(8,128)}, u32[]{:S(2)}) copy-start(s32[6,2048]{1,0:T(8,128)} %near_ref.5) | copy-start | bytes 147460
  2.9 10.2 %all-to-all-start = ((f32[8,8,128]{2,1,0:T(8,128)}), f32[8,8,128]{2,1,0:T(8,128)S(1)}, u32[]{:S(2)}, u32[]{:S(2)}) async-start(f32[8,8,128]{2,1,0:T(8,128)} %get-tuple-element.32), calls=%async_computation | async-start | bytes 65536 | tf_op jit(solution)/shard_map/all_to_all | solution.py:1106
  8.3 3.0 %copy-start.7 = (f32[2048]{0:T(1024)S(1)}, f32[2048]{0:T(1024)}, u32[]{:S(2)}) copy-start(f32[2048]{0:T(1024)} %param.21) | copy-start | bytes 24580
  8.3 4.8 %copy-start.2 = (f32[3,16,16,128]{3,2,1,0:T(8,128)S(1)}, f32[3,16,16,128]{3,2,1,0:T(8,128)}, u32[]{:S(2)}) copy-start(f32[3,16,16,128]{3,2,1,0:T(8,128)} %param.13) | copy-start | bytes 1179652
  8.5 4.6 %collective-permute-start = (f32[56,128]{1,0:T(8,128)S(1)}, f32[56,128]{1,0:T(8,128)S(1)}, u32[]{:S(2)}, u32[]{:S(2)}) collective-permute-start(f32[56,128]{1,0:T(8,128)S(1)} %get-tuple-element.36), channel_id=1, source_target_pairs={{0,1},{1,2},{2,3},{3,4},{4,5},{5,6},{6,7},{7,0},{8,9},{9,10},{10,1... | collective-permute-start | bytes 86024 | tf_op jit(solution)/shard_map/ppermute | solution.py:1129
  9.0 4.1 %collective-permute-start.1 = (f32[56,128]{1,0:T(8,128)S(1)}, f32[56,128]{1,0:T(8,128)S(1)}, u32[]{:S(2)}, u32[]{:S(2)}) collective-permute-start(f32[56,128]{1,0:T(8,128)S(1)} %get-tuple-element.37.after_ref), channel_id=1, source_target_pairs={{1,0},{2,1},{3,2},{4,3},{5,4},{6,5},{7,6},{0,7},{9,8},{10,9},{11,1... | collective-permute-start | bytes 86024 | tf_op jit(solution)/shard_map/ppermute | solution.py:1130
  11.3 1.8 %copy-start = (f32[2,16,16,128]{3,2,1,0:T(8,128)S(1)}, f32[2,16,16,128]{3,2,1,0:T(8,128)}, u32[]{:S(2)}) copy-start(f32[2,16,16,128]{3,2,1,0:T(8,128)} %param.14) | copy-start | bytes 786436
  11.3 1.8 %copy-start.5 = (f32[16,128]{1,0:T(8,128)S(1)}, f32[16,128]{1,0:T(8,128)}, u32[]{:S(2)}) copy-start(f32[16,128]{1,0:T(8,128)} %jac_ref.1) | copy-start | bytes 24580
  11.3 1.8 %copy-start.6 = (f32[16,128]{1,0:T(8,128)S(1)}, f32[16,128]{1,0:T(8,128)}, u32[]{:S(2)}) copy-start(f32[16,128]{1,0:T(8,128)} %land_ref.1) | copy-start | bytes 24580
  13.6 11.6 %collective-permute-start.2 = (f32[144,128]{1,0:T(8,128)S(1)}, f32[144,128]{1,0:T(8,128)S(1)}, u32[]{:S(2)}, u32[]{:S(2)}) collective-permute-start(f32[144,128]{1,0:T(8,128)S(1)} %get-tuple-element.43), channel_id=1, source_target_pairs={{8,0},{24,16},{9,1},{25,17},{10,2},{26,18},{11,3},{27,19},{12,4},{... | collective-permute-start | bytes 221192 | tf_op jit(solution)/shard_map/ppermute | solution.py:1150
  14.9 10.3 %collective-permute-start.3 = (f32[144,128]{1,0:T(8,128)S(1)}, f32[144,128]{1,0:T(8,128)S(1)}, u32[]{:S(2)}, u32[]{:S(2)}) collective-permute-start(f32[144,128]{1,0:T(8,128)S(1)} %get-tuple-element.44), channel_id=1, source_target_pairs={{8,16},{24,0},{9,17},{25,1},{10,18},{26,2},{11,19},{27,3},{12,20},... | collective-permute-start | bytes 221192 | tf_op jit(solution)/shard_map/ppermute | solution.py:1151
  16.2 9.0 %collective-permute-start.4 = (f32[144,128]{1,0:T(8,128)S(1)}, f32[144,128]{1,0:T(8,128)S(1)}, u32[]{:S(2)}, u32[]{:S(2)}) collective-permute-start(f32[144,128]{1,0:T(8,128)S(1)} %get-tuple-element.45), channel_id=1, source_target_pairs={{0,8},{16,24},{1,9},{17,25},{2,10},{18,26},{3,11},{19,27},{4,12},{... | collective-permute-start | bytes 221192 | tf_op jit(solution)/shard_map/ppermute | solution.py:1152
  21.9 4.4 %collective-permute-start.5 = (f32[144,128]{1,0:T(8,128)S(1)}, f32[144,128]{1,0:T(8,128)S(1)}, u32[]{:S(2)}, u32[]{:S(2)}) collective-permute-start(f32[144,128]{1,0:T(8,128)S(1)} %get-tuple-element.46), channel_id=1, source_target_pairs={{0,24},{16,8},{1,25},{17,9},{2,26},{18,10},{3,27},{19,11},{4,28},{... | collective-permute-start | bytes 221192 | tf_op jit(solution)/shard_map/ppermute | solution.py:1153
  27.8 8.6 %all-to-all-start.1 = ((f32[8,16,128]{2,1,0:T(8,128)}), f32[8,16,128]{2,1,0:T(8,128)S(1)}, u32[]{:S(2)}, u32[]{:S(2)}) async-start(f32[8,16,128]{2,1,0:T(8,128)} %get-tuple-element.51), calls=%async_computation.1 | async-start | bytes 131072 | tf_op jit(solution)/shard_map/all_to_all | solution.py:1189
  33.8 0.7 %copy-start.8 = (f32[2048]{0:T(1024)S(1)}, f32[2048]{0:T(1024)}, u32[]{:S(2)}) copy-start(f32[2048]{0:T(1024)} %param.22) | copy-start | bytes 24580

commit v15 on v11

--- a/solution.py
+++ b/solution.py
@@ -21,7 +21,7 @@
 relax_rate = 0.3
 flux_gain = 0.2
 
-HEAD, EDGE_AT = 8, 8
+HEAD = 8
 SIDE_EDGE, SIDE_STRIP, SIDE_IDS = 0, 8, 16
 AVG, MASS_SUM, MASS, COEF_X, COEF_Y, SURF = range(6)
 SURF_ARRAYS = 6
@@ -617,13 +617,12 @@
     sums_ref,
     final_ref,
     inverse_ref,
+    edges_ref,
     flux_ref,
-    edges_ref,
-    semaphores,
+    semaphore,
 ):
     geo = Geometry()
     blocks = rows_ref.shape[0]
-    left, right = neighbours_of(blocks)
     x_points = final_ref.shape[0]
     levels = wind_ref.shape[0] // (2 * x_points)
     base = low_ref.shape[0] - 2 * SURF_ARRAYS - 4
@@ -691,6 +690,9 @@
             picked = jnp.where(high == x, take(line, low, 1), picked)
         for c in range(ROWS):
             flux_ref[ROWS * group + c, 0:1, :] = picked[c : c + 1]
+
+    out = pltpu.make_async_copy(flux_ref, slab_out, semaphore)
+    out.start()
 
     kept = outer_rows(x_points)
 
@@ -752,29 +754,30 @@
                     put(lines[i], plane, moved[i])
     packs = [packs_ref[:ROWS, :], packs_ref[ROWS:, :]]
     packs = edges_of(geo, packs, sums_ref, planes, kept)
-    to_right, to_left = split_sides(geo, packs[0], packs[1], 1)
-    edges_ref[0] = to_right
-    edges_ref[1] = to_left
-    copies = [
-        pltpu.make_async_copy(
-            edges_ref.at[i], slab_out.at[to, EDGE_AT : EDGE_AT + ROWS], semaphores.at[i]
-        )
-        for i, to in enumerate((right, left))
-    ]
-    copies.append(
-        pltpu.make_async_copy(flux_ref, slab_out.at[:, :HEAD], semaphores.at[2])
-    )
-    for copy in copies:
-        copy.start()
-    for copy in copies:
-        copy.wait()
-
-
-def last_kernel(planes, inner_ref, outer_ref, inverse_ref, cols_ref, out_ref, hot_ref):
+    for q, pack in enumerate(packs):
+        edges_ref[ROWS * q : ROWS * (q + 1), :] = pack
+    out.wait()
+
+
+def last_kernel(
+    planes,
+    inner_ref,
+    outer_ref,
+    inverse_ref,
+    edges_ref,
+    cols_ref,
+    out_ref,
+    hot_ref,
+    before_ref,
+    after_ref,
+):
     geo = Geometry()
     x_points = inverse_ref.shape[0]
     kept = outer_rows(x_points)
     hot_ref[...] = one_hot(cols_ref[...])
+    after_ref[...], before_ref[...] = split_sides(
+        geo, edges_ref[:ROWS, :], edges_ref[ROWS:, :], 1
+    )
     for x in range(x_points):
         inverse = spread(inverse_ref[x : x + 1, :])
         ref, first = inner_ref, planes * (x - GLL)
@@ -789,6 +792,8 @@
 def end_kernel(
     planes,
     last_ref,
+    before_ref,
+    after_ref,
     recv_ref,
     final_ref,
     inverse_ref,
@@ -796,17 +801,15 @@
     hot_ref,
     weights_ref,
     gain_ref,
-    first_ref,
-    ocean_in,
+    ocean_ref,
+    air_out,
     ocean_out,
-    air_out,
     air_ref,
     row_ref,
     semaphores,
 ):
     geo = Geometry()
     blocks = cols_ref.shape[0]
-    left, right = neighbours_of(blocks)
     chunks = gain_ref.shape[0]
     x_points = inverse_ref.shape[0]
     copies = []
@@ -817,11 +820,8 @@
         )
         copies[-1].start()
 
-    joined = join_edges(
-        geo,
-        recv_ref[left, EDGE_AT : EDGE_AT + ROWS, :],
-        recv_ref[right, EDGE_AT : EDGE_AT + ROWS, :],
-    )
+    send(ocean_ref.at[ROWS:], ocean_out.at[ROWS:])
+    joined = join_edges(geo, before_ref[...], after_ref[...])
     groups = planes // ROWS
     for group in range(groups):
         for x in range(x_points):
@@ -846,10 +846,10 @@
         [weights_ref[...] * arrived], cols_ref[...], chunks, hot_ref[...]
     )
     gain = inflow * gain_ref[...]
-    row_ref[...] = first_ref[...]
+    row_ref[...] = ocean_ref[:ROWS, :]
     for k in range(chunks):
         at = slice(LANES * k, LANES * (k + 1))
-        row_ref[0:1, at] = first_ref[0:1, at] + gain[k : k + 1]
+        row_ref[0:1, at] = ocean_ref[0:1, at] + gain[k : k + 1]
     send(row_ref, ocean_out.at[:ROWS])
     for copy in copies:
         copy.wait()
@@ -985,7 +985,7 @@
     rows_ref,
     *refs,
 ):
-    partial_refs, (out_ref, gain_ref, first_ref) = refs[: len(starts)], refs[len(starts) :]
+    partial_refs, (out_ref, gain_ref) = refs[: len(starts)], refs[len(starts) :]
     chunks = coef_ref.shape[1] // LANES
     groups = out_ref.shape[0] // ROWS
     rim_at = before_ref.shape[0] - out_ref.shape[0]
@@ -1004,7 +1004,6 @@
         for g in range(groups):
             half = slice(ROWS * g, ROWS * (g + 1))
             out_ref[half, at] = partial_refs[part][half, place] + totals[g]
-    first_ref[...] = out_ref[:ROWS, :]
 
 
 VMEM_SPEC = pl.BlockSpec(memory_space=pltpu.VMEM)
@@ -1012,7 +1011,7 @@
 HBM_SPEC = pl.BlockSpec(memory_space=pltpu.HBM)
 
 
-def call(kernel, outs, specs, scratch=(), cost=0, hbm_outs=0, aliases=None):
+def call(kernel, outs, specs, scratch=(), cost=0, hbm_outs=0):
     estimate = None
     if cost:
         estimate = pl.CostEstimate(flops=0, bytes_accessed=cost, transcendentals=0)
@@ -1028,7 +1027,6 @@
         in_specs=specs,
         out_specs=out_specs,
         scratch_shapes=list(scratch),
-        input_output_aliases=aliases or {},
         cost_estimate=estimate,
         compiler_params=pltpu.CompilerParams(vmem_limit_bytes=32 * 2**20),
         name=getattr(kernel, "func", kernel).__name__,
@@ -1097,7 +1095,7 @@
 
     chunks = cells // LANES
     reads_per_chunk = edge_coef.shape[0] * chunks * (ocean_planes // ROWS)
-    starts = (0, chunks // 4, chunks * 3 // 4)
+    starts = (0, chunks * 6 // 16)
 
     def ocean_part(start, end, after):
         (result,) = call(
@@ -1145,35 +1143,34 @@
         [VMEM_SPEC] * 6,
         cost=2 * air.size * 4,
     )(avg, moved, before, after, surf, wind)
-    second_part = ocean_part(starts[1], starts[2], surf)
-
-    slab, outer, final, inverse = call(
+    second_part = ocean_part(starts[1], chunks, surf)
+
+    slab, outer, final, inverse, edges = call(
         functools.partial(second_kernel, planes),
         [
-            (blocks, EDGE_AT + ROWS, LANES),
+            (blocks, HEAD, LANES),
             (len(outer_rows(x_points)) * planes, LANES),
             (x_points, y_points),
             (x_points, y_points),
+            (2 * ROWS, LANES),
         ],
         [VMEM_SPEC] * 8 + [ANY_SPEC],
-        [
-            pltpu.VMEM((blocks, HEAD, LANES), jnp.float32),
-            pltpu.VMEM((2, ROWS, LANES), jnp.float32),
-            pltpu.SemaphoreType.DMA((3,)),
-        ],
+        [pltpu.VMEM((blocks, HEAD, LANES), jnp.float32), pltpu.SemaphoreType.DMA(())],
         hbm_outs=1,
     )(avg, inner, packs, surf, low, high, wind, point_ids, second_part)
     arrived = lax.all_to_all(slab, "blk", split_axis=0, concat_axis=0, tiled=True)
-    last, hot = call(
+    last, hot, to_before, to_after = call(
         functools.partial(last_kernel, planes),
-        [air.shape, jax.ShapeDtypeStruct((LANES, blocks * LANES), jnp.bfloat16)],
-        [VMEM_SPEC] * 4,
+        [air.shape, jax.ShapeDtypeStruct((LANES, blocks * LANES), jnp.bfloat16)]
+        + [(ROWS, LANES)] * 2,
+        [VMEM_SPEC] * 5,
         cost=2 * air.size * 4,
-    )(inner, outer, inverse, cell_ids)
-    third_part = ocean_part(starts[2], chunks, final)
-    partial, gain, first_rows = call(
+    )(inner, outer, inverse, edges, cell_ids)
+    edge_before = lax.ppermute(to_after, "blk", onward)
+    edge_after = lax.ppermute(to_before, "blk", [(to, source) for source, to in onward])
+    partial, gain = call(
         functools.partial(rim_kernel, starts),
-        [ocean.shape, area.shape, (ROWS, cells)],
+        [ocean.shape, area.shape],
         [VMEM_SPEC] * 5 + [ANY_SPEC] + [VMEM_SPEC] * len(starts),
         cost=chunks * reads_per_chunk // 8 * ROWS * LANES * 4,
     )(
@@ -1182,24 +1179,24 @@
         edge_coef,
         neighbours,
         area,
-        final,
+        to_before,
         first_part,
         second_part,
-        third_part,
-    )
-    ocean_final, air_final = call(
+    )
+    air_final, ocean_final = call(
         functools.partial(end_kernel, planes),
-        [ocean.shape, air.shape],
-        [VMEM_SPEC] * 9 + [HBM_SPEC],
+        [air.shape, ocean.shape],
+        [VMEM_SPEC] * 11,
         [
             pltpu.VMEM(air.shape, jnp.float32),
             pltpu.VMEM((ROWS, cells), jnp.float32),
-            pltpu.SemaphoreType.DMA((1 + planes // ROWS,)),
+            pltpu.SemaphoreType.DMA((2 + planes // ROWS,)),
         ],
         hbm_outs=2,
-        aliases={9: 0},
     )(
         last,
+        edge_before,
+        edge_after,
         arrived,
         final,
         inverse,
@@ -1207,8 +1204,7 @@
         hot,
         weights,
         gain,
-        first_rows,
-        pltpu.with_memory_space_constraint(partial, pltpu.HBM),
+        partial,
     )
     return air_final.reshape(air_state.shape), ocean_final.reshape(tracers.shape)
 

time: 32.7 us -> 32.6 us (level)
  starting transfers between devices: 15.3 us -> 18.2 us
  waiting for transfers between devices: 2.77 us -> 1.11 us
  Pallas kernels: 12.9 us -> 12 us
  local copies, waits for them, and re-layouts: 0.53 us -> 0.05 us
    ppermute x1 -> x2, starting transfers between devices: 2.24 us -> 4.47 us  [body(): lax.ppermute(to_before, 'blk', [(to, source) for source, to in onward])]
    pallas_call x3, Pallas kernels: 4.31 us -> 3.41 us  [the longest x1 1.21 us: body(): call(functools.partial(second_kernel, planes), [(blocks, HEAD, LANES), (l...]
    all_to_all x1, waiting for transfers between devices: 1.26 us -> 0.49 us  [body(): lax.all_to_all(slab, 'blk', split_axis=0, concat_axis=0, tiled=True)]
    ppermute x0 -> x1, starting transfers between devices: none -> 0.55 us  [body(): edge_before = lax.ppermute(to_after, 'blk', onward)]
    ppermute x1, waiting for transfers between devices: 0.81 us -> 0.28 us  [body(): high = lax.ppermute(down, 'face', [(to, source) for source, to in after_me])]
    all_to_all x1, waiting for transfers between devices: 0.69 us -> 0.17 us  [body(): recv = lax.all_to_all(slab, 'blk', split_axis=0, concat_axis=0, tiled=True)]
    unnamed x18, local copies, waits for them, and re-layouts: 0.53 us -> 0.05 us
    pallas_call x3 -> x2, Pallas kernels: 4.29 us -> 4.25 us  [ocean_part(): call(functools.partial(ocean_kernel, ocean_levels, start), [(ocean_planes...]
  transfers between devices with their start and end apart: 6 -> 8, of which waited for: 3 -> 4; matrix products, arithmetic and copies ran while one was open for 0% -> 0% of each run, Pallas kernels for 24% -> 22%
where the time goes in v15:
time: 32.6 us; the launch traced here: 32.1 us
  starting transfers between devices  18.2 us (56%)
  Pallas kernels  12 us (37%)
  waiting for transfers between devices  1.11 us (3%)
  between operations  0.8 us (2%)
    all_to_all x1, starting transfers between devices, body(): recv = lax.all_to_all(slab, 'blk', split_axis=0, concat_axis=0, tiled=True)  5.31 us
    ppermute x2, starting transfers between devices, body(): lax.ppermute(to_before, 'blk', [(to, source) for source, to in onward])  4.47 us
    pallas_call x2, Pallas kernels, ocean_part(): call(functools.partial(ocean_kernel, ocean_levels, start), [(ocean_planes...  4.25 us
    all_to_all x1, starting transfers between devices, body(): lax.all_to_all(slab, 'blk', split_axis=0, concat_axis=0, tiled=True)  3.4 us
    pallas_call x1, Pallas kernels, body(): call(functools.partial(start_kernel, planes), [(blocks, HEAD, LANES), air...  2.27 us
    ppermute x1, starting transfers between devices, body(): high = lax.ppermute(down, 'face', [(to, source) for source, to in after_me])  2.25 us
    ppermute x1, starting transfers between devices, body(): low = lax.ppermute(up, 'face', after_me)  1.63 us
    pallas_call x1, Pallas kernels, body(): call(functools.partial(second_kernel, planes), [(blocks, HEAD, LANES), (l...  1.21 us
  transfers between devices with their start and end apart: 8, of which 4 were waited for; matrix products, arithmetic and copies ran while one was open for 0% of the time, Pallas kernels for 22%

profile of v15, /device:TPU:0, one launch (start us, length us, event | category | flops | bytes accessed | tf_op | source)
XLA Modules:
  0.0 32.1 jit_solution(8610686760579973449)
XLA Ops:
  0.6 0.0 copy-start.1
  0.6 2.3 %start_kernel.1 = (f32[8,8,128]{2,1,0:T(8,128)}, f32[768,128]{1,0:T(8,128)S(1)}, f32[24,128]{1,0:T(8,128)S(1)}, f32[24,128]{1,0:T(8,128)S(1)}, s32[8,128]{1,0:T(...) custom-call(s32[8,128]{1,0:T(8,128)} %bitcast.23, f32[8,128]{1,0:T(8,128)} %bitcast.24, ...), custom_call_target="tpu_custom_call" | custom-call | tf_op jit(solution)/shard_map/start_kernel/pallas_call | solution.py:1074
  2.9 0.0 copy-start.3
  2.9 0.0 copy-start.4
  2.9 5.3 %all-to-all-start = ((f32[8,8,128]{2,1,0:T(8,128)}), f32[8,8,128]{2,1,0:T(8,128)S(1)}, u32[]{:S(2)}, u32[]{:S(2)}) async-start(f32[8,8,128]{2,1,0:T(8,128)} %get-tuple-element.32), calls=%async_computation | async-start | bytes 65536 | tf_op jit(solution)/shard_map/all_to_all | solution.py:1094
  8.3 0.0 copy-start.7
  8.3 0.0 copy-done.1
  8.3 0.0 copy-start.2
  8.3 0.2 send_kernel.1
  8.5 0.5 %collective-permute-start = (f32[56,128]{1,0:T(8,128)S(1)}, f32[56,128]{1,0:T(8,128)S(1)}, u32[]{:S(2)}, u32[]{:S(2)}) collective-permute-start(f32[56,128]{1,0:T(8,128)S(1)} %get-tuple-element.36), channel_id=1, source_target_pairs={{0,1},{1,2},{2,3},{3,4},{4,5},{5,6},{6,7},{7,0},{8,9},{9,10},{10,1... | collective-permute-start | bytes 86024 | tf_op jit(solution)/shard_map/ppermute | solution.py:1117
  9.0 2.2 %collective-permute-start.1 = (f32[56,128]{1,0:T(8,128)S(1)}, f32[56,128]{1,0:T(8,128)S(1)}, u32[]{:S(2)}, u32[]{:S(2)}) collective-permute-start(f32[56,128]{1,0:T(8,128)S(1)} %get-tuple-element.37.after_ref), channel_id=1, source_target_pairs={{1,0},{2,1},{3,2},{4,3},{5,4},{6,5},{7,6},{0,7},{9,8},{10,9},{11,1... | collective-permute-start | bytes 86024 | tf_op jit(solution)/shard_map/ppermute | solution.py:1118
  11.3 0.0 copy-done.3
  11.3 0.0 copy-done.4
  11.3 0.0 copy-done.7
  11.3 0.0 copy-start
  11.3 0.0 copy-start.5
  11.3 0.0 copy-start.6
  11.3 1.6 %ocean_kernel.2.ocean_ref.refs_0_ = f32[32,768]{1,0:T(8,128)S(1)} custom-call(f32[32,2048]{1,0:T(8,128)S(1)} %bitcast.16, f32[6,2048]{1,0:T(8,128)S(1)} %copy-done.3, s32[6,2048]{1,0:T(8,128)S(1)} %copy-done.4, f32[16,128]{1,0:T(8,128)S(1)} %bitcast.20, f32[56,128]{1,0:T(8,128)S(1)} %get-tuple-element.37.after_ref), custom_call_target="tpu_custom_call" | custom-call | bytes 4718592 | tf_op jit(solution)/shard_map/ocean_kernel/pallas_call | solution.py:1101
  12.9 0.2 all-to-all-done.recv_ref
  13.1 0.0 collective-permute-done.before_ref
  13.1 0.0 collective-permute-done.1.after_ref
  13.1 0.0 copy-done.2
  13.1 0.0 copy-done
  13.1 0.0 copy-done.5
  13.1 0.0 copy-done.6
  13.1 0.5 %panel_kernel.1 = (f32[768,128]{1,0:T(8,128)S(1)}, f32[144,128]{1,0:T(8,128)S(1)}, f32[144,128]{1,0:T(8,128)S(1)}, f32[192,128]{1,0:T(8,128)S(1)}) custom-call(f32[768,128]{1,0:T(8,128)S(1)} %get-tuple-element.31.moved_ref, f32[8,8,128]{2,1,0:T(8,128)S(1)} %all-to-all-done.recv_ref, f32[56,128]{1,0:T(8,128)S(1)} %collective-permute-done.before_ref, ...), custom_call_target="tpu_custom_call" | custom-call | tf_op jit(solution)/shard_map/panel_kernel/pallas_call | solution.py:1121
  13.6 1.6 %collective-permute-start.2 = (f32[144,128]{1,0:T(8,128)S(1)}, f32[144,128]{1,0:T(8,128)S(1)}, u32[]{:S(2)}, u32[]{:S(2)}) collective-permute-start(f32[144,128]{1,0:T(8,128)S(1)} %get-tuple-element.43), channel_id=1, source_target_pairs={{0,8},{8,16},{16,24},{24,0},{1,9},{9,17},{17,25},{25,1},{2,10},{10... | collective-permute-start | bytes 221192 | tf_op jit(solution)/shard_map/ppermute | solution.py:1138
  15.3 2.2 %collective-permute-start.3 = (f32[144,128]{1,0:T(8,128)S(1)}, f32[144,128]{1,0:T(8,128)S(1)}, u32[]{:S(2)}, u32[]{:S(2)}) collective-permute-start(f32[144,128]{1,0:T(8,128)S(1)} %get-tuple-element.44), channel_id=1, source_target_pairs={{8,0},{16,8},{24,16},{0,24},{9,1},{17,9},{25,17},{1,25},{10,2},{18... | collective-permute-start | bytes 221192 | tf_op jit(solution)/shard_map/ppermute | solution.py:1139
  17.5 2.6 %ocean_kernel.3.ocean_ref.refs_1_ = f32[32,1280]{1,0:T(8,128)S(1)} custom-call(f32[32,2048]{1,0:T(8,128)S(1)} %bitcast.17, f32[6,2048]{1,0:T(8,128)S(1)} %copy-done.3, s32[6,2048]{1,0:T(8,128)S(1)} %copy-done.4, f32[16,128]{1,0:T(8,128)S(1)} %bitcast.21, f32[192,128]{1,0:T(8,128)S(1)} %get-tuple-element.40.surf_ref.after_ref), custom_call_target="tpu_custom_call" | custom-call | bytes 7864320 | tf_op jit(solution)/shard_map/ocean_kernel/pallas_call | solution.py:1101
  20.2 1.1 %inner_kernel.1 = (f32[384,128]{1,0:T(8,128)S(1)}, f32[16,128]{1,0:T(8,128)S(1)}) custom-call(f32[768,128]{1,0:T(8,128)S(1)} %get-tuple-element.39.avg_ref, f32[768,128]{1,0:T(8,128)S(1)} %get-tuple-element.31.moved_ref, f32[56,128]{1,0:T(8,128)S(1)} %collective-permute-done.before_ref, f32[56,128]{1,0:T(8,128)S(1)} %collective-permute-done.1.after_ref, ...), custom_call_target="tpu_custom_call" | custom-call | bytes 786432 | tf_op jit(solution)/shard_map/inner_kernel/pallas_call | solution.py:1140
  21.3 0.0 collective-permute-done.2.low_ref
  21.3 0.3 collective-permute-done.3.high_ref
  21.6 1.2 %second_kernel.1 = (f32[8,8,128]{2,1,0:T(8,128)}, f32[480,128]{1,0:T(8,128)S(1)}, f32[16,128]{1,0:T(8,128)S(1)}, f32[16,128]{1,0:T(8,128)S(1)}, f32[16,128]{1,0:T(8,128)S(1)}) custom-call(f32[768,128]{1,0:T(8,128)S(1)} %get-tuple-element.39.avg_ref, f32[384,128]{1,0:T(8,128)S(1)} %get-tuple-element.41.inner_ref, f32[16,128]{1,0:T(8,128)S(1)} %get-tuple-element.42.packs_ref, ...), custom_call_target="tpu_custom_call" | custom-call | tf_op jit(solution)/shard_map/second_kernel/pallas_call | solution.py:1148
  22.8 3.4 %all-to-all-start.1 = ((f32[8,8,128]{2,1,0:T(8,128)}), f32[8,8,128]{2,1,0:T(8,128)S(1)}, u32[]{:S(2)}, u32[]{:S(2)}) async-start(f32[8,8,128]{2,1,0:T(8,128)} %get-tuple-element.52), calls=%async_computation.1 | async-start | bytes 65536 | tf_op jit(solution)/shard_map/all_to_all | solution.py:1161
  26.2 0.0 copy-start.8
  26.2 0.2 last_kernel.1
  26.4 0.6 %collective-permute-start.4 = (f32[8,128]{1,0:T(8,128)S(1)}, f32[8,128]{1,0:T(8,128)S(1)}, u32[]{:S(2)}, u32[]{:S(2)}) collective-permute-start(f32[8,128]{1,0:T(8,128)S(1)} %get-tuple-element.50), channel_id=1, source_target_pairs={{0,1},{1,2},{2,3},{3,4},{4,5},{5,6},{6,7},{7,0},{8,9},{9,10},{10,1... | collective-permute-start | bytes 12296 | tf_op jit(solution)/shard_map/ppermute | solution.py:1169
  27.0 2.2 %collective-permute-start.5 = (f32[8,128]{1,0:T(8,128)S(1)}, f32[8,128]{1,0:T(8,128)S(1)}, u32[]{:S(2)}, u32[]{:S(2)}) collective-permute-start(f32[8,128]{1,0:T(8,128)S(1)} %get-tuple-element.51.rows_ref), channel_id=1, source_target_pairs={{1,0},{2,1},{3,2},{4,3},{5,4},{6,5},{7,6},{0,7},{9,8},{10,9},{11,1... | collective-permute-start | bytes 12296 | tf_op jit(solution)/shard_map/ppermute | solution.py:1170
  29.2 0.0 copy-done.8
  29.2 1.2 %rim_kernel.1 = (f32[32,2048]{1,0:T(8,128)S(1)}, f32[16,128]{1,0:T(8,128)S(1)}) custom-call(f32[56,128]{1,0:T(8,128)S(1)} %collective-permute-done.before_ref, f32[56,128]{1,0:T(8,128)S(1)} %collective-permute-done.1.after_ref, f32[6,2048]{1,0:T(8,128)S(1)} %copy-done.3, s32[6,2048]{1,0:T(8,128)S(1)} %copy-done.4, f32[16,128]{1,0:T(8,128)S(1)} %bitcast.22, ...), custom_call_target="tpu_custom_call" | custom-call | bytes 3145728 | tf_op jit(solution)/shard_map/rim_kernel/pallas_call | solution.py:1171
  30.4 0.2 collective-permute-done.4.before_ref
  30.5 0.0 collective-permute-done.5.after_ref
  30.5 0.5 %all-to-all-done.1.recv_ref = f32[8,8,128]{2,1,0:T(8,128)S(1)} async-done(((f32[8,8,128]{2,1,0:T(8,128)}), f32[8,8,128]{2,1,0:T(8,128)S(1)}, u32[]{:S(2)}, u32[]{:S(2)}) %all-to-all-start.1) | async-done | bytes 32800 | tf_op jit(solution)/shard_map/all_to_all | solution.py:1161
  31.0 1.0 %end_kernel.1 = (f32[768,128]{1,0:T(8,128)}, f32[32,2048]{1,0:T(8,128)}) custom-call(f32[768,128]{1,0:T(8,128)S(1)} %get-tuple-element.49.last_ref, f32[8,128]{1,0:T(8,128)S(1)} %collective-permute-done.4.before_ref, f32[8,128]{1,0:T(8,128)S(1)} %collective-permute-done.5.after_ref, f32[8,8,128]{2,1,0:T(8,128)S(1)} %all-to-all-done.1.recv_ref, ...), custom_call_target="tpu_custom_call" | custom-call | tf_op jit(solution)/shard_map/end_kernel/pallas_call | solution.py:1186
Async XLA Ops:
  0.6 7.6 %copy-start.1 = (f32[2,16,2048]{2,1,0:T(8,128)S(1)}, f32[2,16,2048]{2,1,0:T(8,128)}, u32[]{:S(2)}) copy-start(f32[2,16,2048]{2,1,0:T(8,128)} %param.18) | copy-start | bytes 786436
  2.9 8.4 %copy-start.3 = (f32[6,2048]{1,0:T(8,128)S(1)}, f32[6,2048]{1,0:T(8,128)}, u32[]{:S(2)}) copy-start(f32[6,2048]{1,0:T(8,128)} %coef_ref.5) | copy-start | bytes 147460
  2.9 8.3 %copy-start.4 = (s32[6,2048]{1,0:T(8,128)S(1)}, s32[6,2048]{1,0:T(8,128)}, u32[]{:S(2)}) copy-start(s32[6,2048]{1,0:T(8,128)} %near_ref.5) | copy-start | bytes 147460
  2.9 10.2 %all-to-all-start = ((f32[8,8,128]{2,1,0:T(8,128)}), f32[8,8,128]{2,1,0:T(8,128)S(1)}, u32[]{:S(2)}, u32[]{:S(2)}) async-start(f32[8,8,128]{2,1,0:T(8,128)} %get-tuple-element.32), calls=%async_computation | async-start | bytes 65536 | tf_op jit(solution)/shard_map/all_to_all | solution.py:1094
  8.3 3.0 %copy-start.7 = (f32[2048]{0:T(1024)S(1)}, f32[2048]{0:T(1024)}, u32[]{:S(2)}) copy-start(f32[2048]{0:T(1024)} %param.21) | copy-start | bytes 24580
  8.3 4.8 %copy-start.2 = (f32[3,16,16,128]{3,2,1,0:T(8,128)S(1)}, f32[3,16,16,128]{3,2,1,0:T(8,128)}, u32[]{:S(2)}) copy-start(f32[3,16,16,128]{3,2,1,0:T(8,128)} %param.13) | copy-start | bytes 1179652
  8.5 4.6 %collective-permute-start = (f32[56,128]{1,0:T(8,128)S(1)}, f32[56,128]{1,0:T(8,128)S(1)}, u32[]{:S(2)}, u32[]{:S(2)}) collective-permute-start(f32[56,128]{1,0:T(8,128)S(1)} %get-tuple-element.36), channel_id=1, source_target_pairs={{0,1},{1,2},{2,3},{3,4},{4,5},{5,6},{6,7},{7,0},{8,9},{9,10},{10,1... | collective-permute-start | bytes 86024 | tf_op jit(solution)/shard_map/ppermute | solution.py:1117
  9.0 4.1 %collective-permute-start.1 = (f32[56,128]{1,0:T(8,128)S(1)}, f32[56,128]{1,0:T(8,128)S(1)}, u32[]{:S(2)}, u32[]{:S(2)}) collective-permute-start(f32[56,128]{1,0:T(8,128)S(1)} %get-tuple-element.37.after_ref), channel_id=1, source_target_pairs={{1,0},{2,1},{3,2},{4,3},{5,4},{6,5},{7,6},{0,7},{9,8},{10,9},{11,1... | collective-permute-start | bytes 86024 | tf_op jit(solution)/shard_map/ppermute | solution.py:1118
  11.3 1.8 %copy-start = (f32[2,16,16,128]{3,2,1,0:T(8,128)S(1)}, f32[2,16,16,128]{3,2,1,0:T(8,128)}, u32[]{:S(2)}) copy-start(f32[2,16,16,128]{3,2,1,0:T(8,128)} %param.14) | copy-start | bytes 786436
  11.3 1.8 %copy-start.5 = (f32[16,128]{1,0:T(8,128)S(1)}, f32[16,128]{1,0:T(8,128)}, u32[]{:S(2)}) copy-start(f32[16,128]{1,0:T(8,128)} %jac_ref.1) | copy-start | bytes 24580
  11.3 1.8 %copy-start.6 = (f32[16,128]{1,0:T(8,128)S(1)}, f32[16,128]{1,0:T(8,128)}, u32[]{:S(2)}) copy-start(f32[16,128]{1,0:T(8,128)} %land_ref.1) | copy-start | bytes 24580
  13.6 7.7 %collective-permute-start.2 = (f32[144,128]{1,0:T(8,128)S(1)}, f32[144,128]{1,0:T(8,128)S(1)}, u32[]{:S(2)}, u32[]{:S(2)}) collective-permute-start(f32[144,128]{1,0:T(8,128)S(1)} %get-tuple-element.43), channel_id=1, source_target_pairs={{0,8},{8,16},{16,24},{24,0},{1,9},{9,17},{17,25},{25,1},{2,10},{10... | collective-permute-start | bytes 221192 | tf_op jit(solution)/shard_map/ppermute | solution.py:1138
  15.3 6.3 %collective-permute-start.3 = (f32[144,128]{1,0:T(8,128)S(1)}, f32[144,128]{1,0:T(8,128)S(1)}, u32[]{:S(2)}, u32[]{:S(2)}) collective-permute-start(f32[144,128]{1,0:T(8,128)S(1)} %get-tuple-element.44), channel_id=1, source_target_pairs={{8,0},{16,8},{24,16},{0,24},{9,1},{17,9},{25,17},{1,25},{10,2},{18... | collective-permute-start | bytes 221192 | tf_op jit(solution)/shard_map/ppermute | solution.py:1139
  22.8 8.2 %all-to-all-start.1 = ((f32[8,8,128]{2,1,0:T(8,128)}), f32[8,8,128]{2,1,0:T(8,128)S(1)}, u32[]{:S(2)}, u32[]{:S(2)}) async-start(f32[8,8,128]{2,1,0:T(8,128)} %get-tuple-element.52), calls=%async_computation.1 | async-start | bytes 65536 | tf_op jit(solution)/shard_map/all_to_all | solution.py:1161
  26.2 3.0 %copy-start.8 = (f32[2048]{0:T(1024)S(1)}, f32[2048]{0:T(1024)}, u32[]{:S(2)}) copy-start(f32[2048]{0:T(1024)} %param.22) | copy-start | bytes 24580
  26.4 4.1 %collective-permute-start.4 = (f32[8,128]{1,0:T(8,128)S(1)}, f32[8,128]{1,0:T(8,128)S(1)}, u32[]{:S(2)}, u32[]{:S(2)}) collective-permute-start(f32[8,128]{1,0:T(8,128)S(1)} %get-tuple-element.50), channel_id=1, source_target_pairs={{0,1},{1,2},{2,3},{3,4},{4,5},{5,6},{6,7},{7,0},{8,9},{9,10},{10,1... | collective-permute-start | bytes 12296 | tf_op jit(solution)/shard_map/ppermute | solution.py:1169
  27.0 3.6 %collective-permute-start.5 = (f32[8,128]{1,0:T(8,128)S(1)}, f32[8,128]{1,0:T(8,128)S(1)}, u32[]{:S(2)}, u32[]{:S(2)}) collective-permute-start(f32[8,128]{1,0:T(8,128)S(1)} %get-tuple-element.51.rows_ref), channel_id=1, source_target_pairs={{1,0},{2,1},{3,2},{4,3},{5,4},{6,5},{7,6},{0,7},{9,8},{10,9},{11,1... | collective-permute-start | bytes 12296 | tf_op jit(solution)/shard_map/ppermute | solution.py:1170

commit v16 on v15

--- a/solution.py
+++ b/solution.py
@@ -516,10 +516,16 @@
         base = 2 * planes
         out_ref[base : base + 2 * levels, :] = wind
         base += 2 * levels
-        for number in range(SURF_ARRAYS):
-            out_ref[base + 2 * number : base + 2 * number + 2, :] = surf_line(number, r)
-        base += 2 * SURF_ARRAYS
-        out_ref[base : base + 2, :] = surf_line(COEF_X, r) * surf_slope
+        pairs = [surf_line(number, r) for number in range(SURF_ARRAYS)]
+        pairs.append(surf_line(COEF_X, r) * surf_slope)
+        pack = jnp.zeros((ROWS, LANES), jnp.float32)
+        for i, pair in enumerate(pairs):
+            out_ref[base + i : base + i + 1, :] = pair[:1]
+            pack = jnp.where(
+                (geo.lane >> 4) == i, pltpu.roll(spread(pair[1:]), 16 * i + 8, 1), pack
+            )
+        base += len(pairs)
+        out_ref[base : base + 1, :] = pack[:1]
 
 
 def outer_rows(x_points):
@@ -625,15 +631,22 @@
     blocks = rows_ref.shape[0]
     x_points = final_ref.shape[0]
     levels = wind_ref.shape[0] // (2 * x_points)
-    base = low_ref.shape[0] - 2 * SURF_ARRAYS - 4
+    base = low_ref.shape[0] - SURF_ARRAYS - 2
 
     def surf_tile(number, tile, h):
         at = 4 * ROWS * number + 2 * ROWS * tile + ROWS * h
         return surf_ref[at : at + ROWS, :]
 
+    in_strip = (geo.lane < ROWS) | (geo.lane >= LANES - ROWS)
+
     def beside(ref, number, tile):
-        at = base + 2 * number + tile
-        return spread(ref[at : at + 1, :])
+        if tile == 0:
+            return spread(ref[base + number : base + number + 1, :])
+        at = base + SURF_ARRAYS + 1
+        strips = spread(ref[at : at + 1, :])
+        return jnp.where(
+            in_strip, pltpu.roll(strips, (-(16 * number + 8)) % LANES, 1), 1.0
+        )
 
     ends = []
     inverse = []
@@ -1095,7 +1108,7 @@
 
     chunks = cells // LANES
     reads_per_chunk = edge_coef.shape[0] * chunks * (ocean_planes // ROWS)
-    starts = (0, chunks * 6 // 16)
+    starts = (0, chunks * 6 // 16, chunks * 14 // 16)
 
     def ocean_part(start, end, after):
         (result,) = call(
@@ -1117,7 +1130,7 @@
     before = lax.ppermute(to_after, "blk", onward)
     after = lax.ppermute(to_before, "blk", [(to, source) for source, to in onward])
     first_part = ocean_part(starts[0], starts[1], to_before)
-    side_rows = 2 * planes + 2 * levels + 2 * SURF_ARRAYS + 4
+    side_rows = 2 * planes + 2 * levels + SURF_ARRAYS + 2
     avg, down, up, surf = call(
         functools.partial(panel_kernel, planes),
         [air.shape, (side_rows, LANES), (side_rows, LANES), (4 * ROWS * SURF_ARRAYS, LANES)],
@@ -1143,7 +1156,7 @@
         [VMEM_SPEC] * 6,
         cost=2 * air.size * 4,
     )(avg, moved, before, after, surf, wind)
-    second_part = ocean_part(starts[1], chunks, surf)
+    second_part = ocean_part(starts[1], starts[2], surf)
 
     slab, outer, final, inverse, edges = call(
         functools.partial(second_kernel, planes),
@@ -1168,6 +1181,7 @@
     )(inner, outer, inverse, edges, cell_ids)
     edge_before = lax.ppermute(to_after, "blk", onward)
     edge_after = lax.ppermute(to_before, "blk", [(to, source) for source, to in onward])
+    third_part = ocean_part(starts[2], chunks, to_before)
     partial, gain = call(
         functools.partial(rim_kernel, starts),
         [ocean.shape, area.shape],
@@ -1182,6 +1196,7 @@
         to_before,
         first_part,
         second_part,
+        third_part,
     )
     air_final, ocean_final = call(
         functools.partial(end_kernel, planes),

time: 32.6 us -> 32.4 us (level)
    all_to_all x1, waiting for transfers between devices: 0.49 us -> 0.07 us  [body(): lax.all_to_all(slab, 'blk', split_axis=0, concat_axis=0, tiled=True)]
    ppermute x1, waiting for transfers between devices: 0.28 us -> 0.63 us  [body(): high = lax.ppermute(down, 'face', [(to, source) for source, to in after_me])]
    pallas_call x2 -> x3, Pallas kernels: 4.25 us -> 4.26 us  [ocean_part(): call(functools.partial(ocean_kernel, ocean_levels, start), [(ocean_planes...]
  transfers between devices with their start and end apart: 8 -> 8, of which waited for: 4 -> 3; matrix products, arithmetic and copies ran while one was open for 0% -> 0% of each run, Pallas kernels for 22% -> 22%
where the time goes in v16:
time: 32.4 us; the launch traced here: 31.9 us
  starting transfers between devices  18 us (56%)
  Pallas kernels  12.1 us (37%)
  waiting for transfers between devices  0.88 us (3%)
  between operations  0.83 us (3%)
    all_to_all x1, starting transfers between devices, body(): recv = lax.all_to_all(slab, 'blk', split_axis=0, concat_axis=0, tiled=True)  5.31 us
    ppermute x2, starting transfers between devices, body(): lax.ppermute(to_before, 'blk', [(to, source) for source, to in onward])  4.51 us
    pallas_call x3, Pallas kernels, ocean_part(): call(functools.partial(ocean_kernel, ocean_levels, start), [(ocean_planes...  4.26 us
    all_to_all x1, starting transfers between devices, body(): lax.all_to_all(slab, 'blk', split_axis=0, concat_axis=0, tiled=True)  3.35 us
    pallas_call x1, Pallas kernels, body(): call(functools.partial(start_kernel, planes), [(blocks, HEAD, LANES), air...  2.27 us
    ppermute x1, starting transfers between devices, body(): high = lax.ppermute(down, 'face', [(to, source) for source, to in after_me])  2.25 us
    ppermute x1, starting transfers between devices, body(): low = lax.ppermute(up, 'face', after_me)  1.62 us
    pallas_call x1, Pallas kernels, body(): call(functools.partial(second_kernel, planes), [(blocks, HEAD, LANES), (l...  1.24 us
  transfers between devices with their start and end apart: 8, of which 3 were waited for; matrix products, arithmetic and copies ran while one was open for 0% of the time, Pallas kernels for 22%

profile of v16, /device:TPU:0, one launch (start us, length us, event | category | flops | bytes accessed | tf_op | source)
XLA Modules:
  0.0 31.9 jit_solution(10929463893770546510)
XLA Ops:
  0.6 0.0 copy-start
  0.6 2.3 %start_kernel.1 = (f32[8,8,128]{2,1,0:T(8,128)}, f32[768,128]{1,0:T(8,128)S(1)}, f32[24,128]{1,0:T(8,128)S(1)}, f32[24,128]{1,0:T(8,128)S(1)}, s32[8,128]{1,0:T(...) custom-call(s32[8,128]{1,0:T(8,128)} %bitcast.25, f32[8,128]{1,0:T(8,128)} %bitcast.26, ...), custom_call_target="tpu_custom_call" | custom-call | tf_op jit(solution)/shard_map/start_kernel/pallas_call | solution.py:1087
  2.9 0.0 copy-start.3
  2.9 0.0 copy-start.4
  2.9 5.3 %all-to-all-start = ((f32[8,8,128]{2,1,0:T(8,128)}), f32[8,8,128]{2,1,0:T(8,128)S(1)}, u32[]{:S(2)}, u32[]{:S(2)}) async-start(f32[8,8,128]{2,1,0:T(8,128)} %get-tuple-element.32), calls=%async_computation | async-start | bytes 65536 | tf_op jit(solution)/shard_map/all_to_all | solution.py:1107
  8.3 0.0 copy-start.5
  8.3 0.0 copy-done
  8.3 0.0 copy-start.2
  8.3 0.2 send_kernel.1
  8.5 0.5 %collective-permute-start = (f32[56,128]{1,0:T(8,128)S(1)}, f32[56,128]{1,0:T(8,128)S(1)}, u32[]{:S(2)}, u32[]{:S(2)}) collective-permute-start(f32[56,128]{1,0:T(8,128)S(1)} %get-tuple-element.36), channel_id=1, source_target_pairs={{0,1},{1,2},{2,3},{3,4},{4,5},{5,6},{6,7},{7,0},{8,9},{9,10},{10,1... | collective-permute-start | bytes 86024 | tf_op jit(solution)/shard_map/ppermute | solution.py:1130
  9.0 2.2 %collective-permute-start.1 = (f32[56,128]{1,0:T(8,128)S(1)}, f32[56,128]{1,0:T(8,128)S(1)}, u32[]{:S(2)}, u32[]{:S(2)}) collective-permute-start(f32[56,128]{1,0:T(8,128)S(1)} %get-tuple-element.37.after_ref), channel_id=1, source_target_pairs={{1,0},{2,1},{3,2},{4,3},{5,4},{6,5},{7,6},{0,7},{9,8},{10,9},{11,1... | collective-permute-start | bytes 86024 | tf_op jit(solution)/shard_map/ppermute | solution.py:1131
  11.3 0.0 copy-done.3
  11.3 0.0 copy-done.4
  11.3 0.0 copy-done.5
  11.3 0.0 copy-start.1
  11.3 0.0 copy-start.6
  11.3 0.0 copy-start.7
  11.3 1.6 %ocean_kernel.3.ocean_ref.refs_0_ = f32[32,768]{1,0:T(8,128)S(1)} custom-call(f32[32,2048]{1,0:T(8,128)S(1)} %bitcast.12, f32[6,2048]{1,0:T(8,128)S(1)} %copy-done.3, s32[6,2048]{1,0:T(8,128)S(1)} %copy-done.4, f32[16,128]{1,0:T(8,128)S(1)} %bitcast.21, f32[56,128]{1,0:T(8,128)S(1)} %get-tuple-element.37.after_ref), custom_call_target="tpu_custom_call" | custom-call | bytes 4718592 | tf_op jit(solution)/shard_map/ocean_kernel/pallas_call | solution.py:1114
  12.9 0.2 all-to-all-done.recv_ref
  13.1 0.0 collective-permute-done.before_ref
  13.1 0.0 collective-permute-done.1.after_ref
  13.1 0.0 copy-done.2
  13.1 0.0 copy-done.1
  13.1 0.0 copy-done.6
  13.1 0.0 copy-done.7
  13.1 0.6 %panel_kernel.1 = (f32[768,128]{1,0:T(8,128)S(1)}, f32[136,128]{1,0:T(8,128)S(1)}, f32[136,128]{1,0:T(8,128)S(1)}, f32[192,128]{1,0:T(8,128)S(1)}) custom-call(f32[768,128]{1,0:T(8,128)S(1)} %get-tuple-element.31.moved_ref, f32[8,8,128]{2,1,0:T(8,128)S(1)} %all-to-all-done.recv_ref, f32[56,128]{1,0:T(8,128)S(1)} %collective-permute-done.before_ref, ...), custom_call_target="tpu_custom_call" | custom-call | tf_op jit(solution)/shard_map/panel_kernel/pallas_call | solution.py:1134
  13.7 1.6 %collective-permute-start.2 = (f32[136,128]{1,0:T(8,128)S(1)}, f32[136,128]{1,0:T(8,128)S(1)}, u32[]{:S(2)}, u32[]{:S(2)}) collective-permute-start(f32[136,128]{1,0:T(8,128)S(1)} %get-tuple-element.43), channel_id=1, source_target_pairs={{0,8},{8,16},{16,24},{24,0},{1,9},{9,17},{17,25},{25,1},{2,10},{10... | collective-permute-start | bytes 208904 | tf_op jit(solution)/shard_map/ppermute | solution.py:1151
  15.3 2.2 %collective-permute-start.3 = (f32[136,128]{1,0:T(8,128)S(1)}, f32[136,128]{1,0:T(8,128)S(1)}, u32[]{:S(2)}, u32[]{:S(2)}) collective-permute-start(f32[136,128]{1,0:T(8,128)S(1)} %get-tuple-element.44), channel_id=1, source_target_pairs={{8,0},{16,8},{24,16},{0,24},{9,1},{17,9},{25,17},{1,25},{10,2},{18... | collective-permute-start | bytes 208904 | tf_op jit(solution)/shard_map/ppermute | solution.py:1152
  17.6 2.1 %ocean_kernel.4.ocean_ref.refs_1_ = f32[32,1024]{1,0:T(8,128)S(1)} custom-call(f32[32,2048]{1,0:T(8,128)S(1)} %bitcast.13, f32[6,2048]{1,0:T(8,128)S(1)} %copy-done.3, s32[6,2048]{1,0:T(8,128)S(1)} %copy-done.4, f32[16,128]{1,0:T(8,128)S(1)} %bitcast.22, f32[192,128]{1,0:T(8,128)S(1)} %get-tuple-element.40.surf_ref.after_ref), custom_call_target="tpu_custom_call" | custom-call | bytes 6291456 | tf_op jit(solution)/shard_map/ocean_kernel/pallas_call | solution.py:1114
  19.7 1.1 %inner_kernel.1 = (f32[384,128]{1,0:T(8,128)S(1)}, f32[16,128]{1,0:T(8,128)S(1)}) custom-call(f32[768,128]{1,0:T(8,128)S(1)} %get-tuple-element.39.avg_ref, f32[768,128]{1,0:T(8,128)S(1)} %get-tuple-element.31.moved_ref, f32[56,128]{1,0:T(8,128)S(1)} %collective-permute-done.before_ref, f32[56,128]{1,0:T(8,128)S(1)} %collective-permute-done.1.after_ref, ...), custom_call_target="tpu_custom_call" | custom-call | bytes 786432 | tf_op jit(solution)/shard_map/inner_kernel/pallas_call | solution.py:1153
  20.8 0.0 collective-permute-done.2.low_ref
  20.8 0.6 %collective-permute-done.3.high_ref = f32[136,128]{1,0:T(8,128)S(1)} collective-permute-done((f32[136,128]{1,0:T(8,128)S(1)}, f32[136,128]{1,0:T(8,128)S(1)}, u32[]{:S(2)}, u32[]{:S(2)}) %collective-permute-start.3) | collective-permute-done | bytes 69664 | tf_op jit(solution)/shard_map/ppermute | solution.py:1152
  21.5 1.2 %second_kernel.1 = (f32[8,8,128]{2,1,0:T(8,128)}, f32[480,128]{1,0:T(8,128)S(1)}, f32[16,128]{1,0:T(8,128)S(1)}, f32[16,128]{1,0:T(8,128)S(1)}, f32[16,128]{1,0:T(8,128)S(1)}) custom-call(f32[768,128]{1,0:T(8,128)S(1)} %get-tuple-element.39.avg_ref, f32[384,128]{1,0:T(8,128)S(1)} %get-tuple-element.41.inner_ref, f32[16,128]{1,0:T(8,128)S(1)} %get-tuple-element.42.packs_ref, ...), custom_call_target="tpu_custom_call" | custom-call | tf_op jit(solution)/shard_map/second_kernel/pallas_call | solution.py:1161
  22.7 3.4 %all-to-all-start.1 = ((f32[8,8,128]{2,1,0:T(8,128)}), f32[8,8,128]{2,1,0:T(8,128)S(1)}, u32[]{:S(2)}, u32[]{:S(2)}) async-start(f32[8,8,128]{2,1,0:T(8,128)} %get-tuple-element.52), calls=%async_computation.1 | async-start | bytes 65536 | tf_op jit(solution)/shard_map/all_to_all | solution.py:1174
  26.1 0.2 last_kernel.1
  26.3 0.5 %collective-permute-start.4 = (f32[8,128]{1,0:T(8,128)S(1)}, f32[8,128]{1,0:T(8,128)S(1)}, u32[]{:S(2)}, u32[]{:S(2)}) collective-permute-start(f32[8,128]{1,0:T(8,128)S(1)} %get-tuple-element.50), channel_id=1, source_target_pairs={{0,1},{1,2},{2,3},{3,4},{4,5},{5,6},{6,7},{7,0},{8,9},{9,10},{10,1... | collective-permute-start | bytes 12296 | tf_op jit(solution)/shard_map/ppermute | solution.py:1182
  26.7 0.0 copy-start.8
  26.7 2.3 %collective-permute-start.5 = (f32[8,128]{1,0:T(8,128)S(1)}, f32[8,128]{1,0:T(8,128)S(1)}, u32[]{:S(2)}, u32[]{:S(2)}) collective-permute-start(f32[8,128]{1,0:T(8,128)S(1)} %get-tuple-element.51.after_ref.rows_ref), channel_id=1, source_target_pairs={{1,0},{2,1},{3,2},{4,3},{5,4},{6,5},{7,6},{0,7},{9,8},{10,9},{11,1... | collective-permute-start | bytes 12296 | tf_op jit(solution)/shard_map/ppermute | solution.py:1183
  29.0 0.5 %ocean_kernel.5.refs_2_ = f32[32,256]{1,0:T(8,128)S(1)} custom-call(f32[32,2048]{1,0:T(8,128)S(1)} %bitcast.14, f32[6,2048]{1,0:T(8,128)S(1)} %copy-done.3, s32[6,2048]{1,0:T(8,128)S(1)} %copy-done.4, f32[16,128]{1,0:T(8,128)S(1)} %bitcast.23, f32[8,128]{1,0:T(8,128)S(1)} %get-tuple-element.51.after_ref.rows_ref), custom_call_target="tpu_custom_call" | custom-call | bytes 1572864 | tf_op jit(solution)/shard_map/ocean_kernel/pallas_call | solution.py:1114
  29.6 0.0 copy-done.8
  29.6 1.2 %rim_kernel.1 = (f32[32,2048]{1,0:T(8,128)S(1)}, f32[16,128]{1,0:T(8,128)S(1)}) custom-call(f32[56,128]{1,0:T(8,128)S(1)} %collective-permute-done.before_ref, f32[56,128]{1,0:T(8,128)S(1)} %collective-permute-done.1.after_ref, f32[6,2048]{1,0:T(8,128)S(1)} %copy-done.3, s32[6,2048]{1,0:T(8,128)S(1)} %copy-done.4, f32[16,128]{1,0:T(8,128)S(1)} %bitcast.24, ...), custom_call_target="tpu_custom_call" | custom-call | bytes 3145728 | tf_op jit(solution)/shard_map/rim_kernel/pallas_call | solution.py:1185
  30.8 0.0 collective-permute-done.4.before_ref
  30.8 0.0 collective-permute-done.5.after_ref
  30.8 0.1 all-to-all-done.1.recv_ref
  30.8 1.0 %end_kernel.1 = (f32[768,128]{1,0:T(8,128)}, f32[32,2048]{1,0:T(8,128)}) custom-call(f32[768,128]{1,0:T(8,128)S(1)} %get-tuple-element.49.last_ref, f32[8,128]{1,0:T(8,128)S(1)} %collective-permute-done.4.before_ref, f32[8,128]{1,0:T(8,128)S(1)} %collective-permute-done.5.after_ref, f32[8,8,128]{2,1,0:T(8,128)S(1)} %all-to-all-done.1.recv_ref, ...), custom_call_target="tpu_custom_call" | custom-call | tf_op jit(solution)/shard_map/end_kernel/pallas_call | solution.py:1201
Async XLA Ops:
  0.6 7.6 %copy-start = (f32[2,16,2048]{2,1,0:T(8,128)S(1)}, f32[2,16,2048]{2,1,0:T(8,128)}, u32[]{:S(2)}) copy-start(f32[2,16,2048]{2,1,0:T(8,128)} %param.18) | copy-start | bytes 786436
  2.9 8.4 %copy-start.3 = (f32[6,2048]{1,0:T(8,128)S(1)}, f32[6,2048]{1,0:T(8,128)}, u32[]{:S(2)}) copy-start(f32[6,2048]{1,0:T(8,128)} %coef_ref.7) | copy-start | bytes 147460
  2.9 8.3 %copy-start.4 = (s32[6,2048]{1,0:T(8,128)S(1)}, s32[6,2048]{1,0:T(8,128)}, u32[]{:S(2)}) copy-start(s32[6,2048]{1,0:T(8,128)} %near_ref.7) | copy-start | bytes 147460
  2.9 10.2 %all-to-all-start = ((f32[8,8,128]{2,1,0:T(8,128)}), f32[8,8,128]{2,1,0:T(8,128)S(1)}, u32[]{:S(2)}, u32[]{:S(2)}) async-start(f32[8,8,128]{2,1,0:T(8,128)} %get-tuple-element.32), calls=%async_computation | async-start | bytes 65536 | tf_op jit(solution)/shard_map/all_to_all | solution.py:1107
  8.3 3.0 %copy-start.5 = (f32[2048]{0:T(1024)S(1)}, f32[2048]{0:T(1024)}, u32[]{:S(2)}) copy-start(f32[2048]{0:T(1024)} %param.21) | copy-start | bytes 24580
  8.3 4.8 %copy-start.2 = (f32[3,16,16,128]{3,2,1,0:T(8,128)S(1)}, f32[3,16,16,128]{3,2,1,0:T(8,128)}, u32[]{:S(2)}) copy-start(f32[3,16,16,128]{3,2,1,0:T(8,128)} %param.13) | copy-start | bytes 1179652
  8.5 4.6 %collective-permute-start = (f32[56,128]{1,0:T(8,128)S(1)}, f32[56,128]{1,0:T(8,128)S(1)}, u32[]{:S(2)}, u32[]{:S(2)}) collective-permute-start(f32[56,128]{1,0:T(8,128)S(1)} %get-tuple-element.36), channel_id=1, source_target_pairs={{0,1},{1,2},{2,3},{3,4},{4,5},{5,6},{6,7},{7,0},{8,9},{9,10},{10,1... | collective-permute-start | bytes 86024 | tf_op jit(solution)/shard_map/ppermute | solution.py:1130
  9.0 4.1 %collective-permute-start.1 = (f32[56,128]{1,0:T(8,128)S(1)}, f32[56,128]{1,0:T(8,128)S(1)}, u32[]{:S(2)}, u32[]{:S(2)}) collective-permute-start(f32[56,128]{1,0:T(8,128)S(1)} %get-tuple-element.37.after_ref), channel_id=1, source_target_pairs={{1,0},{2,1},{3,2},{4,3},{5,4},{6,5},{7,6},{0,7},{9,8},{10,9},{11,1... | collective-permute-start | bytes 86024 | tf_op jit(solution)/shard_map/ppermute | solution.py:1131
  11.3 1.8 %copy-start.1 = (f32[2,16,16,128]{3,2,1,0:T(8,128)S(1)}, f32[2,16,16,128]{3,2,1,0:T(8,128)}, u32[]{:S(2)}) copy-start(f32[2,16,16,128]{3,2,1,0:T(8,128)} %param.14) | copy-start | bytes 786436
  11.3 1.8 %copy-start.6 = (f32[16,128]{1,0:T(8,128)S(1)}, f32[16,128]{1,0:T(8,128)}, u32[]{:S(2)}) copy-start(f32[16,128]{1,0:T(8,128)} %jac_ref.1) | copy-start | bytes 24580
  11.3 1.8 %copy-start.7 = (f32[16,128]{1,0:T(8,128)S(1)}, f32[16,128]{1,0:T(8,128)}, u32[]{:S(2)}) copy-start(f32[16,128]{1,0:T(8,128)} %land_ref.1) | copy-start | bytes 24580
  13.7 7.1 %collective-permute-start.2 = (f32[136,128]{1,0:T(8,128)S(1)}, f32[136,128]{1,0:T(8,128)S(1)}, u32[]{:S(2)}, u32[]{:S(2)}) collective-permute-start(f32[136,128]{1,0:T(8,128)S(1)} %get-tuple-element.43), channel_id=1, source_target_pairs={{0,8},{8,16},{16,24},{24,0},{1,9},{9,17},{17,25},{25,1},{2,10},{10... | collective-permute-start | bytes 208904 | tf_op jit(solution)/shard_map/ppermute | solution.py:1151
  15.3 6.1 %collective-permute-start.3 = (f32[136,128]{1,0:T(8,128)S(1)}, f32[136,128]{1,0:T(8,128)S(1)}, u32[]{:S(2)}, u32[]{:S(2)}) collective-permute-start(f32[136,128]{1,0:T(8,128)S(1)} %get-tuple-element.44), channel_id=1, source_target_pairs={{8,0},{16,8},{24,16},{0,24},{9,1},{17,9},{25,17},{1,25},{10,2},{18... | collective-permute-start | bytes 208904 | tf_op jit(solution)/shard_map/ppermute | solution.py:1152
  22.7 8.1 %all-to-all-start.1 = ((f32[8,8,128]{2,1,0:T(8,128)}), f32[8,8,128]{2,1,0:T(8,128)S(1)}, u32[]{:S(2)}, u32[]{:S(2)}) async-start(f32[8,8,128]{2,1,0:T(8,128)} %get-tuple-element.52), calls=%async_computation.1 | async-start | bytes 65536 | tf_op jit(solution)/shard_map/all_to_all | solution.py:1174
  26.3 4.5 %collective-permute-start.4 = (f32[8,128]{1,0:T(8,128)S(1)}, f32[8,128]{1,0:T(8,128)S(1)}, u32[]{:S(2)}, u32[]{:S(2)}) collective-permute-start(f32[8,128]{1,0:T(8,128)S(1)} %get-tuple-element.50), channel_id=1, source_target_pairs={{0,1},{1,2},{2,3},{3,4},{4,5},{5,6},{6,7},{7,0},{8,9},{9,10},{10,1... | collective-permute-start | bytes 12296 | tf_op jit(solution)/shard_map/ppermute | solution.py:1182
  26.7 2.8 %copy-start.8 = (f32[2048]{0:T(1024)S(1)}, f32[2048]{0:T(1024)}, u32[]{:S(2)}) copy-start(f32[2048]{0:T(1024)} %param.22) | copy-start | bytes 24580
  26.7 4.0 %collective-permute-start.5 = (f32[8,128]{1,0:T(8,128)S(1)}, f32[8,128]{1,0:T(8,128)S(1)}, u32[]{:S(2)}, u32[]{:S(2)}) collective-permute-start(f32[8,128]{1,0:T(8,128)S(1)} %get-tuple-element.51.after_ref.rows_ref), channel_id=1, source_target_pairs={{1,0},{2,1},{3,2},{4,3},{5,4},{6,5},{7,6},{0,7},{9,8},{10,9},{11,1... | collective-permute-start | bytes 12296 | tf_op jit(solution)/shard_map/ppermute | solution.py:1183

commit v17 on v16

--- a/solution.py
+++ b/solution.py
@@ -393,12 +393,12 @@
         jnp.concatenate([recv_ref[c, i : i + 1, :] for c in range(blocks)], axis=0)
         for i in range(6)
     ]
-    heat, frac = scatter_sum(head[2:4], own_ids, 2 * ROWS, one_hot(own_ids))
+    heat, frac = scatter_sum(head[2:4], own_ids, x_points, one_hot(own_ids))
     from_left = scatter_sum(
-        head[0:2], left_ids, 2 * ROWS, one_hot(left_ids, lambda lane: lane >= LANES - ROWS)
+        head[0:2], left_ids, x_points, one_hot(left_ids, lambda lane: lane >= LANES - ROWS)
     )
     from_right = scatter_sum(
-        head[4:6], right_ids, 2 * ROWS, one_hot(right_ids, lambda lane: lane < ROWS)
+        head[4:6], right_ids, x_points, one_hot(right_ids, lambda lane: lane < ROWS)
     )
     strip_heat = from_left[0] + from_right[0]
     strip_frac = from_left[1] + from_right[1]
@@ -450,17 +450,17 @@
                 - coef_y * geo.d_y(field)[0]
             )
             pair.append((moved, mass))
-            at = 2 * ROWS * tile + ROWS * h
+            at = x_points * tile + ROWS * h
             for number, value in (
                 (MASS, mass),
                 (COEF_X, coef_x),
                 (COEF_Y, coef_y),
                 (SURF, surf),
             ):
-                surf_ref[4 * ROWS * number + at : 4 * ROWS * number + at + ROWS, :] = value
+                surf_ref[2 * x_points * number + at : 2 * x_points * number + at + ROWS, :] = value
         for number, i in ((AVG, 0), (MASS_SUM, 1)):
             for tile, value in enumerate(geo.sum_y_pair(pair[0][i], pair[1][i])):
-                at = 4 * ROWS * number + 2 * ROWS * tile + ROWS * h
+                at = 2 * x_points * number + x_points * tile + ROWS * h
                 surf_ref[at : at + ROWS, :] = value
 
     joined = join_edges(
@@ -477,24 +477,25 @@
         return avg_ref[planes * r : planes * (r + 1), :]
 
     def surf_line(number, r):
-        return surf_ref[pl.ds(4 * ROWS * number + r, 2, stride=x_points), :]
+        return surf_ref[pl.ds(2 * x_points * number + r, 2, stride=x_points), :]
 
     def first_step(get, mass_at):
+        top = x_points - 1
         return (
             [
                 get(1) / mass_at(1),
                 get(2) / mass_at(2),
-                (get(3) + get(4)) / (mass_at(3) + mass_at(4)),
+                (get(3) + get(GLL)) / (mass_at(3) + mass_at(GLL)),
             ],
             [
-                (get(11) + get(12)) / (mass_at(11) + mass_at(12)),
-                get(13) / mass_at(13),
-                get(14) / mass_at(14),
+                (get(top - 4) + get(top - 3)) / (mass_at(top - 4) + mass_at(top - 3)),
+                get(top - 2) / mass_at(top - 2),
+                get(top - 1) / mass_at(top - 1),
             ],
         )
 
     def own_mass_sum(r):
-        return surf_ref[4 * ROWS * MASS_SUM + r : 4 * ROWS * MASS_SUM + r + 1, :]
+        return surf_ref[2 * x_points * MASS_SUM + r : 2 * x_points * MASS_SUM + r + 1, :]
 
     low_lines, high_lines = first_step(line, own_mass_sum)
     surf_low, surf_high = first_step(
@@ -502,11 +503,11 @@
     )
     for out_ref, r, lines, surf_lines, coefs in (
         (down_ref, 0, low_lines, surf_low, deriv_table[0][1:]),
-        (up_ref, 15, high_lines, surf_high, deriv_table[3][:3]),
+        (up_ref, x_points - 1, high_lines, surf_high, deriv_table[3][:3]),
     ):
         slope = sum(coef * value for coef, value in zip(coefs, lines))
         surf_slope = sum(coef * value for coef, value in zip(coefs, surf_lines))
-        mass = surf_ref[4 * ROWS * MASS + r : 4 * ROWS * MASS + r + 1, :]
+        mass = surf_ref[2 * x_points * MASS + r : 2 * x_points * MASS + r + 1, :]
         wind = time_step * mass * wind_ref[pl.ds(r, 2 * levels, stride=x_points), :]
         out_ref[0:planes, :] = line(r)
         for first in range(0, planes, levels):
@@ -561,7 +562,7 @@
         return geo.sum_y(moved_ref[at, :], outer_edges(joined, x, plane // ROWS))
 
     def surf_row(number, x):
-        at = 4 * ROWS * number + x
+        at = 2 * x_points * number + x
         return spread(surf_ref[at : at + 1, :])
 
     def put(x, plane, value):
@@ -634,7 +635,7 @@
     base = low_ref.shape[0] - SURF_ARRAYS - 2
 
     def surf_tile(number, tile, h):
-        at = 4 * ROWS * number + 2 * ROWS * tile + ROWS * h
+        at = 2 * x_points * number + x_points * tile + ROWS * h
         return surf_ref[at : at + ROWS, :]
 
     in_strip = (geo.lane < ROWS) | (geo.lane >= LANES - ROWS)
@@ -698,7 +699,7 @@
         ids = rows_ref[ROWS * group : ROWS * (group + 1), :]
         high, low = ids >> 7, ids & (LANES - 1)
         picked = jnp.zeros((ROWS, LANES), jnp.float32)
-        for x in range(2 * ROWS):
+        for x in range(x_points):
             line = spread(flux[x // ROWS][x % ROWS : x % ROWS + 1])
             picked = jnp.where(high == x, take(line, low, 1), picked)
         for c in range(ROWS):
@@ -1062,6 +1063,8 @@
     xgrid_weights,
 ):
     field_count, levels, x_points, y_points = air_state.shape
+    assert (x_points, y_points) == (2 * ROWS, LANES), air_state.shape
+    assert xgrid_rows.shape[2] == send_list.shape[1] // 2 == LANES, xgrid_rows.shape
     planes = field_count * levels
     ocean_levels, cells = tracers.shape[1:]
     ocean_planes = tracers.shape[0] * ocean_levels
@@ -1133,7 +1136,7 @@
     side_rows = 2 * planes + 2 * levels + SURF_ARRAYS + 2
     avg, down, up, surf = call(
         functools.partial(panel_kernel, planes),
-        [air.shape, (side_rows, LANES), (side_rows, LANES), (4 * ROWS * SURF_ARRAYS, LANES)],
+        [air.shape, (side_rows, LANES), (side_rows, LANES), (2 * x_points * SURF_ARRAYS, LANES)],
         [VMEM_SPEC] * 9 + [ANY_SPEC],
     )(
         moved,

time: 32.4 us -> 32.4 us (level)
  no operation moved by 1% of the time
where the time goes in v17:
time: 32.4 us; the launch traced here: 31.9 us
  starting transfers between devices  18 us (56%)
  Pallas kernels  12.1 us (37%)
  waiting for transfers between devices  0.88 us (3%)
  between operations  0.83 us (3%)
    all_to_all x1, starting transfers between devices, body(): recv = lax.all_to_all(slab, 'blk', split_axis=0, concat_axis=0, tiled=True)  5.31 us
    ppermute x2, starting transfers between devices, body(): lax.ppermute(to_before, 'blk', [(to, source) for source, to in onward])  4.51 us
    pallas_call x3, Pallas kernels, ocean_part(): call(functools.partial(ocean_kernel, ocean_levels, start), [(ocean_planes...  4.26 us
    all_to_all x1, starting transfers between devices, body(): lax.all_to_all(slab, 'blk', split_axis=0, concat_axis=0, tiled=True)  3.35 us
    pallas_call x1, Pallas kernels, body(): call(functools.partial(start_kernel, planes), [(blocks, HEAD, LANES), air...  2.27 us
    ppermute x1, starting transfers between devices, body(): high = lax.ppermute(down, 'face', [(to, source) for source, to in after_me])  2.25 us
    ppermute x1, starting transfers between devices, body(): low = lax.ppermute(up, 'face', after_me)  1.62 us
    pallas_call x1, Pallas kernels, body(): call(functools.partial(second_kernel, planes), [(blocks, HEAD, LANES), (l...  1.24 us
  transfers between devices with their start and end apart: 8, of which 3 were waited for; matrix products, arithmetic and copies ran while one was open for 0% of the time, Pallas kernels for 22%

profile of v17, /device:TPU:0, one launch (start us, length us, event | category | flops | bytes accessed | tf_op | source)
XLA Modules:
  0.0 31.9 jit_solution(10929463893770546510)
XLA Ops:
  0.6 0.0 copy-start
  0.6 2.3 %start_kernel.1 = (f32[8,8,128]{2,1,0:T(8,128)}, f32[768,128]{1,0:T(8,128)S(1)}, f32[24,128]{1,0:T(8,128)S(1)}, f32[24,128]{1,0:T(8,128)S(1)}, s32[8,128]{1,0:T(...) custom-call(s32[8,128]{1,0:T(8,128)} %bitcast.25, f32[8,128]{1,0:T(8,128)} %bitcast.26, ...), custom_call_target="tpu_custom_call" | custom-call | tf_op jit(solution)/shard_map/start_kernel/pallas_call | solution.py:1090
  2.9 0.0 copy-start.3
  2.9 0.0 copy-start.4
  2.9 5.3 %all-to-all-start = ((f32[8,8,128]{2,1,0:T(8,128)}), f32[8,8,128]{2,1,0:T(8,128)S(1)}, u32[]{:S(2)}, u32[]{:S(2)}) async-start(f32[8,8,128]{2,1,0:T(8,128)} %get-tuple-element.32), calls=%async_computation | async-start | bytes 65536 | tf_op jit(solution)/shard_map/all_to_all | solution.py:1110
  8.3 0.0 copy-start.5
  8.3 0.0 copy-done
  8.3 0.0 copy-start.2
  8.3 0.2 send_kernel.1
  8.5 0.5 %collective-permute-start = (f32[56,128]{1,0:T(8,128)S(1)}, f32[56,128]{1,0:T(8,128)S(1)}, u32[]{:S(2)}, u32[]{:S(2)}) collective-permute-start(f32[56,128]{1,0:T(8,128)S(1)} %get-tuple-element.36), channel_id=1, source_target_pairs={{0,1},{1,2},{2,3},{3,4},{4,5},{5,6},{6,7},{7,0},{8,9},{9,10},{10,1... | collective-permute-start | bytes 86024 | tf_op jit(solution)/shard_map/ppermute | solution.py:1133
  9.0 2.2 %collective-permute-start.1 = (f32[56,128]{1,0:T(8,128)S(1)}, f32[56,128]{1,0:T(8,128)S(1)}, u32[]{:S(2)}, u32[]{:S(2)}) collective-permute-start(f32[56,128]{1,0:T(8,128)S(1)} %get-tuple-element.37.after_ref), channel_id=1, source_target_pairs={{1,0},{2,1},{3,2},{4,3},{5,4},{6,5},{7,6},{0,7},{9,8},{10,9},{11,1... | collective-permute-start | bytes 86024 | tf_op jit(solution)/shard_map/ppermute | solution.py:1134
  11.3 0.0 copy-done.3
  11.3 0.0 copy-done.4
  11.3 0.0 copy-done.5
  11.3 0.0 copy-start.1
  11.3 0.0 copy-start.6
  11.3 0.0 copy-start.7
  11.3 1.6 %ocean_kernel.3.ocean_ref.refs_0_ = f32[32,768]{1,0:T(8,128)S(1)} custom-call(f32[32,2048]{1,0:T(8,128)S(1)} %bitcast.12, f32[6,2048]{1,0:T(8,128)S(1)} %copy-done.3, s32[6,2048]{1,0:T(8,128)S(1)} %copy-done.4, f32[16,128]{1,0:T(8,128)S(1)} %bitcast.21, f32[56,128]{1,0:T(8,128)S(1)} %get-tuple-element.37.after_ref), custom_call_target="tpu_custom_call" | custom-call | bytes 4718592 | tf_op jit(solution)/shard_map/ocean_kernel/pallas_call | solution.py:1117
  12.9 0.2 all-to-all-done.recv_ref
  13.1 0.0 collective-permute-done.before_ref
  13.1 0.0 collective-permute-done.1.after_ref
  13.1 0.0 copy-done.2
  13.1 0.0 copy-done.1
  13.1 0.0 copy-done.6
  13.1 0.0 copy-done.7
  13.1 0.6 %panel_kernel.1 = (f32[768,128]{1,0:T(8,128)S(1)}, f32[136,128]{1,0:T(8,128)S(1)}, f32[136,128]{1,0:T(8,128)S(1)}, f32[192,128]{1,0:T(8,128)S(1)}) custom-call(f32[768,128]{1,0:T(8,128)S(1)} %get-tuple-element.31.moved_ref, f32[8,8,128]{2,1,0:T(8,128)S(1)} %all-to-all-done.recv_ref, f32[56,128]{1,0:T(8,128)S(1)} %collective-permute-done.before_ref, ...), custom_call_target="tpu_custom_call" | custom-call | tf_op jit(solution)/shard_map/panel_kernel/pallas_call | solution.py:1137
  13.7 1.6 %collective-permute-start.2 = (f32[136,128]{1,0:T(8,128)S(1)}, f32[136,128]{1,0:T(8,128)S(1)}, u32[]{:S(2)}, u32[]{:S(2)}) collective-permute-start(f32[136,128]{1,0:T(8,128)S(1)} %get-tuple-element.43), channel_id=1, source_target_pairs={{0,8},{8,16},{16,24},{24,0},{1,9},{9,17},{17,25},{25,1},{2,10},{10... | collective-permute-start | bytes 208904 | tf_op jit(solution)/shard_map/ppermute | solution.py:1154
  15.3 2.2 %collective-permute-start.3 = (f32[136,128]{1,0:T(8,128)S(1)}, f32[136,128]{1,0:T(8,128)S(1)}, u32[]{:S(2)}, u32[]{:S(2)}) collective-permute-start(f32[136,128]{1,0:T(8,128)S(1)} %get-tuple-element.44), channel_id=1, source_target_pairs={{8,0},{16,8},{24,16},{0,24},{9,1},{17,9},{25,17},{1,25},{10,2},{18... | collective-permute-start | bytes 208904 | tf_op jit(solution)/shard_map/ppermute | solution.py:1155
  17.6 2.1 %ocean_kernel.4.ocean_ref.refs_1_ = f32[32,1024]{1,0:T(8,128)S(1)} custom-call(f32[32,2048]{1,0:T(8,128)S(1)} %bitcast.13, f32[6,2048]{1,0:T(8,128)S(1)} %copy-done.3, s32[6,2048]{1,0:T(8,128)S(1)} %copy-done.4, f32[16,128]{1,0:T(8,128)S(1)} %bitcast.22, f32[192,128]{1,0:T(8,128)S(1)} %get-tuple-element.40.surf_ref.after_ref), custom_call_target="tpu_custom_call" | custom-call | bytes 6291456 | tf_op jit(solution)/shard_map/ocean_kernel/pallas_call | solution.py:1117
  19.7 1.1 %inner_kernel.1 = (f32[384,128]{1,0:T(8,128)S(1)}, f32[16,128]{1,0:T(8,128)S(1)}) custom-call(f32[768,128]{1,0:T(8,128)S(1)} %get-tuple-element.39.avg_ref, f32[768,128]{1,0:T(8,128)S(1)} %get-tuple-element.31.moved_ref, f32[56,128]{1,0:T(8,128)S(1)} %collective-permute-done.before_ref, f32[56,128]{1,0:T(8,128)S(1)} %collective-permute-done.1.after_ref, ...), custom_call_target="tpu_custom_call" | custom-call | bytes 786432 | tf_op jit(solution)/shard_map/inner_kernel/pallas_call | solution.py:1156
  20.8 0.0 collective-permute-done.2.low_ref
  20.8 0.6 %collective-permute-done.3.high_ref = f32[136,128]{1,0:T(8,128)S(1)} collective-permute-done((f32[136,128]{1,0:T(8,128)S(1)}, f32[136,128]{1,0:T(8,128)S(1)}, u32[]{:S(2)}, u32[]{:S(2)}) %collective-permute-start.3) | collective-permute-done | bytes 69664 | tf_op jit(solution)/shard_map/ppermute | solution.py:1155
  21.5 1.2 %second_kernel.1 = (f32[8,8,128]{2,1,0:T(8,128)}, f32[480,128]{1,0:T(8,128)S(1)}, f32[16,128]{1,0:T(8,128)S(1)}, f32[16,128]{1,0:T(8,128)S(1)}, f32[16,128]{1,0:T(8,128)S(1)}) custom-call(f32[768,128]{1,0:T(8,128)S(1)} %get-tuple-element.39.avg_ref, f32[384,128]{1,0:T(8,128)S(1)} %get-tuple-element.41.inner_ref, f32[16,128]{1,0:T(8,128)S(1)} %get-tuple-element.42.packs_ref, ...), custom_call_target="tpu_custom_call" | custom-call | tf_op jit(solution)/shard_map/second_kernel/pallas_call | solution.py:1164
  22.7 3.4 %all-to-all-start.1 = ((f32[8,8,128]{2,1,0:T(8,128)}), f32[8,8,128]{2,1,0:T(8,128)S(1)}, u32[]{:S(2)}, u32[]{:S(2)}) async-start(f32[8,8,128]{2,1,0:T(8,128)} %get-tuple-element.52), calls=%async_computation.1 | async-start | bytes 65536 | tf_op jit(solution)/shard_map/all_to_all | solution.py:1177
  26.1 0.2 last_kernel.1
  26.3 0.5 %collective-permute-start.4 = (f32[8,128]{1,0:T(8,128)S(1)}, f32[8,128]{1,0:T(8,128)S(1)}, u32[]{:S(2)}, u32[]{:S(2)}) collective-permute-start(f32[8,128]{1,0:T(8,128)S(1)} %get-tuple-element.50), channel_id=1, source_target_pairs={{0,1},{1,2},{2,3},{3,4},{4,5},{5,6},{6,7},{7,0},{8,9},{9,10},{10,1... | collective-permute-start | bytes 12296 | tf_op jit(solution)/shard_map/ppermute | solution.py:1185
  26.7 0.0 copy-start.8
  26.7 2.3 %collective-permute-start.5 = (f32[8,128]{1,0:T(8,128)S(1)}, f32[8,128]{1,0:T(8,128)S(1)}, u32[]{:S(2)}, u32[]{:S(2)}) collective-permute-start(f32[8,128]{1,0:T(8,128)S(1)} %get-tuple-element.51.after_ref.rows_ref), channel_id=1, source_target_pairs={{1,0},{2,1},{3,2},{4,3},{5,4},{6,5},{7,6},{0,7},{9,8},{10,9},{11,1... | collective-permute-start | bytes 12296 | tf_op jit(solution)/shard_map/ppermute | solution.py:1186
  29.0 0.5 %ocean_kernel.5.refs_2_ = f32[32,256]{1,0:T(8,128)S(1)} custom-call(f32[32,2048]{1,0:T(8,128)S(1)} %bitcast.14, f32[6,2048]{1,0:T(8,128)S(1)} %copy-done.3, s32[6,2048]{1,0:T(8,128)S(1)} %copy-done.4, f32[16,128]{1,0:T(8,128)S(1)} %bitcast.23, f32[8,128]{1,0:T(8,128)S(1)} %get-tuple-element.51.after_ref.rows_ref), custom_call_target="tpu_custom_call" | custom-call | bytes 1572864 | tf_op jit(solution)/shard_map/ocean_kernel/pallas_call | solution.py:1117
  29.6 0.0 copy-done.8
  29.6 1.2 %rim_kernel.1 = (f32[32,2048]{1,0:T(8,128)S(1)}, f32[16,128]{1,0:T(8,128)S(1)}) custom-call(f32[56,128]{1,0:T(8,128)S(1)} %collective-permute-done.before_ref, f32[56,128]{1,0:T(8,128)S(1)} %collective-permute-done.1.after_ref, f32[6,2048]{1,0:T(8,128)S(1)} %copy-done.3, s32[6,2048]{1,0:T(8,128)S(1)} %copy-done.4, f32[16,128]{1,0:T(8,128)S(1)} %bitcast.24, ...), custom_call_target="tpu_custom_call" | custom-call | bytes 3145728 | tf_op jit(solution)/shard_map/rim_kernel/pallas_call | solution.py:1188
  30.8 0.0 collective-permute-done.4.before_ref
  30.8 0.0 collective-permute-done.5.after_ref
  30.8 0.1 all-to-all-done.1.recv_ref
  30.8 1.0 %end_kernel.1 = (f32[768,128]{1,0:T(8,128)}, f32[32,2048]{1,0:T(8,128)}) custom-call(f32[768,128]{1,0:T(8,128)S(1)} %get-tuple-element.49.last_ref, f32[8,128]{1,0:T(8,128)S(1)} %collective-permute-done.4.before_ref, f32[8,128]{1,0:T(8,128)S(1)} %collective-permute-done.5.after_ref, f32[8,8,128]{2,1,0:T(8,128)S(1)} %all-to-all-done.1.recv_ref, ...), custom_call_target="tpu_custom_call" | custom-call | tf_op jit(solution)/shard_map/end_kernel/pallas_call | solution.py:1204
Async XLA Ops:
  0.6 7.6 %copy-start = (f32[2,16,2048]{2,1,0:T(8,128)S(1)}, f32[2,16,2048]{2,1,0:T(8,128)}, u32[]{:S(2)}) copy-start(f32[2,16,2048]{2,1,0:T(8,128)} %param.18) | copy-start | bytes 786436
  2.9 8.4 %copy-start.3 = (f32[6,2048]{1,0:T(8,128)S(1)}, f32[6,2048]{1,0:T(8,128)}, u32[]{:S(2)}) copy-start(f32[6,2048]{1,0:T(8,128)} %coef_ref.7) | copy-start | bytes 147460
  2.9 8.3 %copy-start.4 = (s32[6,2048]{1,0:T(8,128)S(1)}, s32[6,2048]{1,0:T(8,128)}, u32[]{:S(2)}) copy-start(s32[6,2048]{1,0:T(8,128)} %near_ref.7) | copy-start | bytes 147460
  2.9 10.2 %all-to-all-start = ((f32[8,8,128]{2,1,0:T(8,128)}), f32[8,8,128]{2,1,0:T(8,128)S(1)}, u32[]{:S(2)}, u32[]{:S(2)}) async-start(f32[8,8,128]{2,1,0:T(8,128)} %get-tuple-element.32), calls=%async_computation | async-start | bytes 65536 | tf_op jit(solution)/shard_map/all_to_all | solution.py:1110
  8.3 3.0 %copy-start.5 = (f32[2048]{0:T(1024)S(1)}, f32[2048]{0:T(1024)}, u32[]{:S(2)}) copy-start(f32[2048]{0:T(1024)} %param.21) | copy-start | bytes 24580
  8.3 4.8 %copy-start.2 = (f32[3,16,16,128]{3,2,1,0:T(8,128)S(1)}, f32[3,16,16,128]{3,2,1,0:T(8,128)}, u32[]{:S(2)}) copy-start(f32[3,16,16,128]{3,2,1,0:T(8,128)} %param.13) | copy-start | bytes 1179652
  8.5 4.6 %collective-permute-start = (f32[56,128]{1,0:T(8,128)S(1)}, f32[56,128]{1,0:T(8,128)S(1)}, u32[]{:S(2)}, u32[]{:S(2)}) collective-permute-start(f32[56,128]{1,0:T(8,128)S(1)} %get-tuple-element.36), channel_id=1, source_target_pairs={{0,1},{1,2},{2,3},{3,4},{4,5},{5,6},{6,7},{7,0},{8,9},{9,10},{10,1... | collective-permute-start | bytes 86024 | tf_op jit(solution)/shard_map/ppermute | solution.py:1133
  9.0 4.1 %collective-permute-start.1 = (f32[56,128]{1,0:T(8,128)S(1)}, f32[56,128]{1,0:T(8,128)S(1)}, u32[]{:S(2)}, u32[]{:S(2)}) collective-permute-start(f32[56,128]{1,0:T(8,128)S(1)} %get-tuple-element.37.after_ref), channel_id=1, source_target_pairs={{1,0},{2,1},{3,2},{4,3},{5,4},{6,5},{7,6},{0,7},{9,8},{10,9},{11,1... | collective-permute-start | bytes 86024 | tf_op jit(solution)/shard_map/ppermute | solution.py:1134
  11.3 1.8 %copy-start.1 = (f32[2,16,16,128]{3,2,1,0:T(8,128)S(1)}, f32[2,16,16,128]{3,2,1,0:T(8,128)}, u32[]{:S(2)}) copy-start(f32[2,16,16,128]{3,2,1,0:T(8,128)} %param.14) | copy-start | bytes 786436
  11.3 1.8 %copy-start.6 = (f32[16,128]{1,0:T(8,128)S(1)}, f32[16,128]{1,0:T(8,128)}, u32[]{:S(2)}) copy-start(f32[16,128]{1,0:T(8,128)} %jac_ref.1) | copy-start | bytes 24580
  11.3 1.8 %copy-start.7 = (f32[16,128]{1,0:T(8,128)S(1)}, f32[16,128]{1,0:T(8,128)}, u32[]{:S(2)}) copy-start(f32[16,128]{1,0:T(8,128)} %land_ref.1) | copy-start | bytes 24580
  13.7 7.1 %collective-permute-start.2 = (f32[136,128]{1,0:T(8,128)S(1)}, f32[136,128]{1,0:T(8,128)S(1)}, u32[]{:S(2)}, u32[]{:S(2)}) collective-permute-start(f32[136,128]{1,0:T(8,128)S(1)} %get-tuple-element.43), channel_id=1, source_target_pairs={{0,8},{8,16},{16,24},{24,0},{1,9},{9,17},{17,25},{25,1},{2,10},{10... | collective-permute-start | bytes 208904 | tf_op jit(solution)/shard_map/ppermute | solution.py:1154
  15.3 6.1 %collective-permute-start.3 = (f32[136,128]{1,0:T(8,128)S(1)}, f32[136,128]{1,0:T(8,128)S(1)}, u32[]{:S(2)}, u32[]{:S(2)}) collective-permute-start(f32[136,128]{1,0:T(8,128)S(1)} %get-tuple-element.44), channel_id=1, source_target_pairs={{8,0},{16,8},{24,16},{0,24},{9,1},{17,9},{25,17},{1,25},{10,2},{18... | collective-permute-start | bytes 208904 | tf_op jit(solution)/shard_map/ppermute | solution.py:1155
  22.7 8.1 %all-to-all-start.1 = ((f32[8,8,128]{2,1,0:T(8,128)}), f32[8,8,128]{2,1,0:T(8,128)S(1)}, u32[]{:S(2)}, u32[]{:S(2)}) async-start(f32[8,8,128]{2,1,0:T(8,128)} %get-tuple-element.52), calls=%async_computation.1 | async-start | bytes 65536 | tf_op jit(solution)/shard_map/all_to_all | solution.py:1177
  26.3 4.5 %collective-permute-start.4 = (f32[8,128]{1,0:T(8,128)S(1)}, f32[8,128]{1,0:T(8,128)S(1)}, u32[]{:S(2)}, u32[]{:S(2)}) collective-permute-start(f32[8,128]{1,0:T(8,128)S(1)} %get-tuple-element.50), channel_id=1, source_target_pairs={{0,1},{1,2},{2,3},{3,4},{4,5},{5,6},{6,7},{7,0},{8,9},{9,10},{10,1... | collective-permute-start | bytes 12296 | tf_op jit(solution)/shard_map/ppermute | solution.py:1185
  26.7 2.8 %copy-start.8 = (f32[2048]{0:T(1024)S(1)}, f32[2048]{0:T(1024)}, u32[]{:S(2)}) copy-start(f32[2048]{0:T(1024)} %param.22) | copy-start | bytes 24580
  26.7 4.0 %collective-permute-start.5 = (f32[8,128]{1,0:T(8,128)S(1)}, f32[8,128]{1,0:T(8,128)S(1)}, u32[]{:S(2)}, u32[]{:S(2)}) collective-permute-start(f32[8,128]{1,0:T(8,128)S(1)} %get-tuple-element.51.after_ref.rows_ref), channel_id=1, source_target_pairs={{1,0},{2,1},{3,2},{4,3},{5,4},{6,5},{7,6},{0,7},{9,8},{10,9},{11,1... | collective-permute-start | bytes 12296 | tf_op jit(solution)/shard_map/ppermute | solution.py:1186

commit v18 on v17

--- a/solution.py
+++ b/solution.py
@@ -260,21 +260,24 @@
     air_ref,
     semaphores,
 ):
+    pairs = []
+    for source, target in ((wind_in, wind_ref), (air_in, air_ref)):
+        middle = target.shape[0] // 2
+        for part in (slice(0, middle), slice(middle, target.shape[0])):
+            pairs.append((source.at[part], target.at[part]))
+    large = len(pairs)
+    pairs += [
+        (cols_in, cols_ref),
+        (tracers_in.at[:ROWS], tracers_ref),
+        (weights_in, weights_ref),
+        (rows_in, rows_ref),
+        (jac_in, jac_ref),
+        (land_in, land_ref),
+        (send_in, send_ref),
+    ]
     copies = [
         pltpu.make_async_copy(source, target, semaphores.at[i])
-        for i, (source, target) in enumerate(
-            (
-                (cols_in, cols_ref),
-                (tracers_in.at[:ROWS], tracers_ref),
-                (weights_in, weights_ref),
-                (rows_in, rows_ref),
-                (air_in, air_ref),
-                (wind_in, wind_ref),
-                (jac_in, jac_ref),
-                (land_in, land_ref),
-                (send_in, send_ref),
-            )
-        )
+        for i, (source, target) in enumerate(pairs)
     ]
     for copy in copies:
         copy.start()
@@ -283,7 +286,7 @@
     x_points = jac_ref.shape[0]
     levels = wind_ref.shape[0] // (2 * x_points)
     chunks = tracers_ref.shape[1] // LANES
-    for copy in copies[:4]:
+    for copy in copies[large : large + 4]:
         copy.wait()
 
     for group in range(blocks // ROWS):
@@ -309,7 +312,7 @@
     for side_ref in (before_ref, after_ref):
         side_ref[SIDE_IDS : SIDE_IDS + blocks, :] = ids
 
-    for copy in copies[4:]:
+    for copy in copies[:large] + copies[large + 4 :]:
         copy.wait()
     strips = []
     for h in range(2):
@@ -1104,7 +1107,7 @@
                 air.shape,
             )
         ]
-        + [pltpu.SemaphoreType.DMA((len(first_inputs) + 1,))],
+        + [pltpu.SemaphoreType.DMA((len(first_inputs) + 3,))],
         hbm_outs=1,
     )(*(pltpu.with_memory_space_constraint(array, pltpu.HBM) for array in first_inputs))
     recv = lax.all_to_all(slab, "blk", split_axis=0, concat_axis=0, tiled=True)

time: 32.4 us -> 32.5 us (level)
  no operation moved by 1% of the time
where the time goes in v18:
time: 32.5 us; the launch traced here: 32 us
  starting transfers between devices  18 us (55%)
  Pallas kernels  12.2 us (38%)
  waiting for transfers between devices  0.88 us (3%)
  between operations  0.83 us (3%)
    all_to_all x1, starting transfers between devices, body(): recv = lax.all_to_all(slab, 'blk', split_axis=0, concat_axis=0, tiled=True)  5.31 us
    ppermute x2, starting transfers between devices, body(): lax.ppermute(to_before, 'blk', [(to, source) for source, to in onward])  4.51 us
    pallas_call x3, Pallas kernels, ocean_part(): call(functools.partial(ocean_kernel, ocean_levels, start), [(ocean_planes...  4.26 us
    all_to_all x1, starting transfers between devices, body(): lax.all_to_all(slab, 'blk', split_axis=0, concat_axis=0, tiled=True)  3.35 us
    pallas_call x1, Pallas kernels, body(): call(functools.partial(start_kernel, planes), [(blocks, HEAD, LANES), air...  2.41 us
    ppermute x1, starting transfers between devices, body(): high = lax.ppermute(down, 'face', [(to, source) for source, to in after_me])  2.25 us
    ppermute x1, starting transfers between devices, body(): low = lax.ppermute(up, 'face', after_me)  1.62 us
    pallas_call x1, Pallas kernels, body(): call(functools.partial(second_kernel, planes), [(blocks, HEAD, LANES), (l...  1.24 us
  transfers between devices with their start and end apart: 8, of which 3 were waited for; matrix products, arithmetic and copies ran while one was open for 0% of the time, Pallas kernels for 22%

profile of v18, /device:TPU:0, one launch (start us, length us, event | category | flops | bytes accessed | tf_op | source)
XLA Modules:
  0.0 32.0 jit_solution(3256855039313899122)
XLA Ops:
  0.6 0.0 copy-start
  0.6 2.4 %start_kernel.1 = (f32[8,8,128]{2,1,0:T(8,128)}, f32[768,128]{1,0:T(8,128)S(1)}, f32[24,128]{1,0:T(8,128)S(1)}, f32[24,128]{1,0:T(8,128)S(1)}, s32[8,128]{1,0:T(...) custom-call(s32[8,128]{1,0:T(8,128)} %bitcast.25, f32[8,128]{1,0:T(8,128)} %bitcast.26, ...), custom_call_target="tpu_custom_call" | custom-call | tf_op jit(solution)/shard_map/start_kernel/pallas_call | solution.py:1093
  3.1 0.0 copy-start.3
  3.1 0.0 copy-start.4
  3.1 5.3 %all-to-all-start = ((f32[8,8,128]{2,1,0:T(8,128)}), f32[8,8,128]{2,1,0:T(8,128)S(1)}, u32[]{:S(2)}, u32[]{:S(2)}) async-start(f32[8,8,128]{2,1,0:T(8,128)} %get-tuple-element.32), calls=%async_computation | async-start | bytes 65536 | tf_op jit(solution)/shard_map/all_to_all | solution.py:1113
  8.4 0.0 copy-start.5
  8.4 0.0 copy-done
  8.4 0.0 copy-start.2
  8.4 0.2 send_kernel.1
  8.6 0.5 %collective-permute-start = (f32[56,128]{1,0:T(8,128)S(1)}, f32[56,128]{1,0:T(8,128)S(1)}, u32[]{:S(2)}, u32[]{:S(2)}) collective-permute-start(f32[56,128]{1,0:T(8,128)S(1)} %get-tuple-element.36), channel_id=1, source_target_pairs={{0,1},{1,2},{2,3},{3,4},{4,5},{5,6},{6,7},{7,0},{8,9},{9,10},{10,1... | collective-permute-start | bytes 86024 | tf_op jit(solution)/shard_map/ppermute | solution.py:1136
  9.2 2.2 %collective-permute-start.1 = (f32[56,128]{1,0:T(8,128)S(1)}, f32[56,128]{1,0:T(8,128)S(1)}, u32[]{:S(2)}, u32[]{:S(2)}) collective-permute-start(f32[56,128]{1,0:T(8,128)S(1)} %get-tuple-element.37.after_ref), channel_id=1, source_target_pairs={{1,0},{2,1},{3,2},{4,3},{5,4},{6,5},{7,6},{0,7},{9,8},{10,9},{11,1... | collective-permute-start | bytes 86024 | tf_op jit(solution)/shard_map/ppermute | solution.py:1137
  11.4 0.0 copy-done.3
  11.4 0.0 copy-done.4
  11.4 0.0 copy-done.5
  11.4 0.0 copy-start.1
  11.4 0.0 copy-start.6
  11.4 0.0 copy-start.7
  11.5 1.6 %ocean_kernel.3.ocean_ref.refs_0_ = f32[32,768]{1,0:T(8,128)S(1)} custom-call(f32[32,2048]{1,0:T(8,128)S(1)} %bitcast.12, f32[6,2048]{1,0:T(8,128)S(1)} %copy-done.3, s32[6,2048]{1,0:T(8,128)S(1)} %copy-done.4, f32[16,128]{1,0:T(8,128)S(1)} %bitcast.21, f32[56,128]{1,0:T(8,128)S(1)} %get-tuple-element.37.after_ref), custom_call_target="tpu_custom_call" | custom-call | bytes 4718592 | tf_op jit(solution)/shard_map/ocean_kernel/pallas_call | solution.py:1120
  13.1 0.2 all-to-all-done.recv_ref
  13.2 0.0 collective-permute-done.before_ref
  13.2 0.0 collective-permute-done.1.after_ref
  13.2 0.0 copy-done.2
  13.3 0.0 copy-done.1
  13.3 0.0 copy-done.6
  13.3 0.0 copy-done.7
  13.3 0.6 %panel_kernel.1 = (f32[768,128]{1,0:T(8,128)S(1)}, f32[136,128]{1,0:T(8,128)S(1)}, f32[136,128]{1,0:T(8,128)S(1)}, f32[192,128]{1,0:T(8,128)S(1)}) custom-call(f32[768,128]{1,0:T(8,128)S(1)} %get-tuple-element.31.moved_ref, f32[8,8,128]{2,1,0:T(8,128)S(1)} %all-to-all-done.recv_ref, f32[56,128]{1,0:T(8,128)S(1)} %collective-permute-done.before_ref, ...), custom_call_target="tpu_custom_call" | custom-call | tf_op jit(solution)/shard_map/panel_kernel/pallas_call | solution.py:1140
  13.8 1.6 %collective-permute-start.2 = (f32[136,128]{1,0:T(8,128)S(1)}, f32[136,128]{1,0:T(8,128)S(1)}, u32[]{:S(2)}, u32[]{:S(2)}) collective-permute-start(f32[136,128]{1,0:T(8,128)S(1)} %get-tuple-element.43), channel_id=1, source_target_pairs={{0,8},{8,16},{16,24},{24,0},{1,9},{9,17},{17,25},{25,1},{2,10},{10... | collective-permute-start | bytes 208904 | tf_op jit(solution)/shard_map/ppermute | solution.py:1157
  15.5 2.2 %collective-permute-start.3 = (f32[136,128]{1,0:T(8,128)S(1)}, f32[136,128]{1,0:T(8,128)S(1)}, u32[]{:S(2)}, u32[]{:S(2)}) collective-permute-start(f32[136,128]{1,0:T(8,128)S(1)} %get-tuple-element.44), channel_id=1, source_target_pairs={{8,0},{16,8},{24,16},{0,24},{9,1},{17,9},{25,17},{1,25},{10,2},{18... | collective-permute-start | bytes 208904 | tf_op jit(solution)/shard_map/ppermute | solution.py:1158
  17.7 2.1 %ocean_kernel.4.ocean_ref.refs_1_ = f32[32,1024]{1,0:T(8,128)S(1)} custom-call(f32[32,2048]{1,0:T(8,128)S(1)} %bitcast.13, f32[6,2048]{1,0:T(8,128)S(1)} %copy-done.3, s32[6,2048]{1,0:T(8,128)S(1)} %copy-done.4, f32[16,128]{1,0:T(8,128)S(1)} %bitcast.22, f32[192,128]{1,0:T(8,128)S(1)} %get-tuple-element.40.surf_ref.after_ref), custom_call_target="tpu_custom_call" | custom-call | bytes 6291456 | tf_op jit(solution)/shard_map/ocean_kernel/pallas_call | solution.py:1120
  19.8 1.1 %inner_kernel.1 = (f32[384,128]{1,0:T(8,128)S(1)}, f32[16,128]{1,0:T(8,128)S(1)}) custom-call(f32[768,128]{1,0:T(8,128)S(1)} %get-tuple-element.39.avg_ref, f32[768,128]{1,0:T(8,128)S(1)} %get-tuple-element.31.moved_ref, f32[56,128]{1,0:T(8,128)S(1)} %collective-permute-done.before_ref, f32[56,128]{1,0:T(8,128)S(1)} %collective-permute-done.1.after_ref, ...), custom_call_target="tpu_custom_call" | custom-call | bytes 786432 | tf_op jit(solution)/shard_map/inner_kernel/pallas_call | solution.py:1159
  21.0 0.0 collective-permute-done.2.low_ref
  21.0 0.6 %collective-permute-done.3.high_ref = f32[136,128]{1,0:T(8,128)S(1)} collective-permute-done((f32[136,128]{1,0:T(8,128)S(1)}, f32[136,128]{1,0:T(8,128)S(1)}, u32[]{:S(2)}, u32[]{:S(2)}) %collective-permute-start.3) | collective-permute-done | bytes 69664 | tf_op jit(solution)/shard_map/ppermute | solution.py:1158
  21.6 1.2 %second_kernel.1 = (f32[8,8,128]{2,1,0:T(8,128)}, f32[480,128]{1,0:T(8,128)S(1)}, f32[16,128]{1,0:T(8,128)S(1)}, f32[16,128]{1,0:T(8,128)S(1)}, f32[16,128]{1,0:T(8,128)S(1)}) custom-call(f32[768,128]{1,0:T(8,128)S(1)} %get-tuple-element.39.avg_ref, f32[384,128]{1,0:T(8,128)S(1)} %get-tuple-element.41.inner_ref, f32[16,128]{1,0:T(8,128)S(1)} %get-tuple-element.42.packs_ref, ...), custom_call_target="tpu_custom_call" | custom-call | tf_op jit(solution)/shard_map/second_kernel/pallas_call | solution.py:1167
  22.9 3.4 %all-to-all-start.1 = ((f32[8,8,128]{2,1,0:T(8,128)}), f32[8,8,128]{2,1,0:T(8,128)S(1)}, u32[]{:S(2)}, u32[]{:S(2)}) async-start(f32[8,8,128]{2,1,0:T(8,128)} %get-tuple-element.52), calls=%async_computation.1 | async-start | bytes 65536 | tf_op jit(solution)/shard_map/all_to_all | solution.py:1180
  26.2 0.2 last_kernel.1
  26.4 0.5 %collective-permute-start.4 = (f32[8,128]{1,0:T(8,128)S(1)}, f32[8,128]{1,0:T(8,128)S(1)}, u32[]{:S(2)}, u32[]{:S(2)}) collective-permute-start(f32[8,128]{1,0:T(8,128)S(1)} %get-tuple-element.50), channel_id=1, source_target_pairs={{0,1},{1,2},{2,3},{3,4},{4,5},{5,6},{6,7},{7,0},{8,9},{9,10},{10,1... | collective-permute-start | bytes 12296 | tf_op jit(solution)/shard_map/ppermute | solution.py:1188
  26.9 0.0 copy-start.8
  26.9 2.3 %collective-permute-start.5 = (f32[8,128]{1,0:T(8,128)S(1)}, f32[8,128]{1,0:T(8,128)S(1)}, u32[]{:S(2)}, u32[]{:S(2)}) collective-permute-start(f32[8,128]{1,0:T(8,128)S(1)} %get-tuple-element.51.after_ref.rows_ref), channel_id=1, source_target_pairs={{1,0},{2,1},{3,2},{4,3},{5,4},{6,5},{7,6},{0,7},{9,8},{10,9},{11,1... | collective-permute-start | bytes 12296 | tf_op jit(solution)/shard_map/ppermute | solution.py:1189
  29.2 0.5 %ocean_kernel.5.refs_2_ = f32[32,256]{1,0:T(8,128)S(1)} custom-call(f32[32,2048]{1,0:T(8,128)S(1)} %bitcast.14, f32[6,2048]{1,0:T(8,128)S(1)} %copy-done.3, s32[6,2048]{1,0:T(8,128)S(1)} %copy-done.4, f32[16,128]{1,0:T(8,128)S(1)} %bitcast.23, f32[8,128]{1,0:T(8,128)S(1)} %get-tuple-element.51.after_ref.rows_ref), custom_call_target="tpu_custom_call" | custom-call | bytes 1572864 | tf_op jit(solution)/shard_map/ocean_kernel/pallas_call | solution.py:1120
  29.7 0.0 copy-done.8
  29.7 1.2 %rim_kernel.1 = (f32[32,2048]{1,0:T(8,128)S(1)}, f32[16,128]{1,0:T(8,128)S(1)}) custom-call(f32[56,128]{1,0:T(8,128)S(1)} %collective-permute-done.before_ref, f32[56,128]{1,0:T(8,128)S(1)} %collective-permute-done.1.after_ref, f32[6,2048]{1,0:T(8,128)S(1)} %copy-done.3, s32[6,2048]{1,0:T(8,128)S(1)} %copy-done.4, f32[16,128]{1,0:T(8,128)S(1)} %bitcast.24, ...), custom_call_target="tpu_custom_call" | custom-call | bytes 3145728 | tf_op jit(solution)/shard_map/rim_kernel/pallas_call | solution.py:1191
  30.9 0.0 collective-permute-done.4.before_ref
  30.9 0.0 collective-permute-done.5.after_ref
  30.9 0.1 all-to-all-done.1.recv_ref
  31.0 1.0 %end_kernel.1 = (f32[768,128]{1,0:T(8,128)}, f32[32,2048]{1,0:T(8,128)}) custom-call(f32[768,128]{1,0:T(8,128)S(1)} %get-tuple-element.49.last_ref, f32[8,128]{1,0:T(8,128)S(1)} %collective-permute-done.4.before_ref, f32[8,128]{1,0:T(8,128)S(1)} %collective-permute-done.5.after_ref, f32[8,8,128]{2,1,0:T(8,128)S(1)} %all-to-all-done.1.recv_ref, ...), custom_call_target="tpu_custom_call" | custom-call | tf_op jit(solution)/shard_map/end_kernel/pallas_call | solution.py:1207
Async XLA Ops:
  0.6 7.8 %copy-start = (f32[2,16,2048]{2,1,0:T(8,128)S(1)}, f32[2,16,2048]{2,1,0:T(8,128)}, u32[]{:S(2)}) copy-start(f32[2,16,2048]{2,1,0:T(8,128)} %param.18) | copy-start | bytes 786436
  3.1 8.4 %copy-start.3 = (f32[6,2048]{1,0:T(8,128)S(1)}, f32[6,2048]{1,0:T(8,128)}, u32[]{:S(2)}) copy-start(f32[6,2048]{1,0:T(8,128)} %coef_ref.7) | copy-start | bytes 147460
  3.1 8.3 %copy-start.4 = (s32[6,2048]{1,0:T(8,128)S(1)}, s32[6,2048]{1,0:T(8,128)}, u32[]{:S(2)}) copy-start(s32[6,2048]{1,0:T(8,128)} %near_ref.7) | copy-start | bytes 147460
  3.1 10.2 %all-to-all-start = ((f32[8,8,128]{2,1,0:T(8,128)}), f32[8,8,128]{2,1,0:T(8,128)S(1)}, u32[]{:S(2)}, u32[]{:S(2)}) async-start(f32[8,8,128]{2,1,0:T(8,128)} %get-tuple-element.32), calls=%async_computation | async-start | bytes 65536 | tf_op jit(solution)/shard_map/all_to_all | solution.py:1113
  8.4 3.0 %copy-start.5 = (f32[2048]{0:T(1024)S(1)}, f32[2048]{0:T(1024)}, u32[]{:S(2)}) copy-start(f32[2048]{0:T(1024)} %param.21) | copy-start | bytes 24580
  8.4 4.8 %copy-start.2 = (f32[3,16,16,128]{3,2,1,0:T(8,128)S(1)}, f32[3,16,16,128]{3,2,1,0:T(8,128)}, u32[]{:S(2)}) copy-start(f32[3,16,16,128]{3,2,1,0:T(8,128)} %param.13) | copy-start | bytes 1179652
  8.6 4.6 %collective-permute-start = (f32[56,128]{1,0:T(8,128)S(1)}, f32[56,128]{1,0:T(8,128)S(1)}, u32[]{:S(2)}, u32[]{:S(2)}) collective-permute-start(f32[56,128]{1,0:T(8,128)S(1)} %get-tuple-element.36), channel_id=1, source_target_pairs={{0,1},{1,2},{2,3},{3,4},{4,5},{5,6},{6,7},{7,0},{8,9},{9,10},{10,1... | collective-permute-start | bytes 86024 | tf_op jit(solution)/shard_map/ppermute | solution.py:1136
  9.2 4.1 %collective-permute-start.1 = (f32[56,128]{1,0:T(8,128)S(1)}, f32[56,128]{1,0:T(8,128)S(1)}, u32[]{:S(2)}, u32[]{:S(2)}) collective-permute-start(f32[56,128]{1,0:T(8,128)S(1)} %get-tuple-element.37.after_ref), channel_id=1, source_target_pairs={{1,0},{2,1},{3,2},{4,3},{5,4},{6,5},{7,6},{0,7},{9,8},{10,9},{11,1... | collective-permute-start | bytes 86024 | tf_op jit(solution)/shard_map/ppermute | solution.py:1137
  11.4 1.8 %copy-start.1 = (f32[2,16,16,128]{3,2,1,0:T(8,128)S(1)}, f32[2,16,16,128]{3,2,1,0:T(8,128)}, u32[]{:S(2)}) copy-start(f32[2,16,16,128]{3,2,1,0:T(8,128)} %param.14) | copy-start | bytes 786436
  11.4 1.8 %copy-start.6 = (f32[16,128]{1,0:T(8,128)S(1)}, f32[16,128]{1,0:T(8,128)}, u32[]{:S(2)}) copy-start(f32[16,128]{1,0:T(8,128)} %jac_ref.1) | copy-start | bytes 24580
  11.4 1.8 %copy-start.7 = (f32[16,128]{1,0:T(8,128)S(1)}, f32[16,128]{1,0:T(8,128)}, u32[]{:S(2)}) copy-start(f32[16,128]{1,0:T(8,128)} %land_ref.1) | copy-start | bytes 24580
  13.8 7.1 %collective-permute-start.2 = (f32[136,128]{1,0:T(8,128)S(1)}, f32[136,128]{1,0:T(8,128)S(1)}, u32[]{:S(2)}, u32[]{:S(2)}) collective-permute-start(f32[136,128]{1,0:T(8,128)S(1)} %get-tuple-element.43), channel_id=1, source_target_pairs={{0,8},{8,16},{16,24},{24,0},{1,9},{9,17},{17,25},{25,1},{2,10},{10... | collective-permute-start | bytes 208904 | tf_op jit(solution)/shard_map/ppermute | solution.py:1157
  15.5 6.1 %collective-permute-start.3 = (f32[136,128]{1,0:T(8,128)S(1)}, f32[136,128]{1,0:T(8,128)S(1)}, u32[]{:S(2)}, u32[]{:S(2)}) collective-permute-start(f32[136,128]{1,0:T(8,128)S(1)} %get-tuple-element.44), channel_id=1, source_target_pairs={{8,0},{16,8},{24,16},{0,24},{9,1},{17,9},{25,17},{1,25},{10,2},{18... | collective-permute-start | bytes 208904 | tf_op jit(solution)/shard_map/ppermute | solution.py:1158
  22.9 8.1 %all-to-all-start.1 = ((f32[8,8,128]{2,1,0:T(8,128)}), f32[8,8,128]{2,1,0:T(8,128)S(1)}, u32[]{:S(2)}, u32[]{:S(2)}) async-start(f32[8,8,128]{2,1,0:T(8,128)} %get-tuple-element.52), calls=%async_computation.1 | async-start | bytes 65536 | tf_op jit(solution)/shard_map/all_to_all | solution.py:1180
  26.4 4.5 %collective-permute-start.4 = (f32[8,128]{1,0:T(8,128)S(1)}, f32[8,128]{1,0:T(8,128)S(1)}, u32[]{:S(2)}, u32[]{:S(2)}) collective-permute-start(f32[8,128]{1,0:T(8,128)S(1)} %get-tuple-element.50), channel_id=1, source_target_pairs={{0,1},{1,2},{2,3},{3,4},{4,5},{5,6},{6,7},{7,0},{8,9},{9,10},{10,1... | collective-permute-start | bytes 12296 | tf_op jit(solution)/shard_map/ppermute | solution.py:1188
  26.9 2.8 %copy-start.8 = (f32[2048]{0:T(1024)S(1)}, f32[2048]{0:T(1024)}, u32[]{:S(2)}) copy-start(f32[2048]{0:T(1024)} %param.22) | copy-start | bytes 24580
  26.9 4.0 %collective-permute-start.5 = (f32[8,128]{1,0:T(8,128)S(1)}, f32[8,128]{1,0:T(8,128)S(1)}, u32[]{:S(2)}, u32[]{:S(2)}) collective-permute-start(f32[8,128]{1,0:T(8,128)S(1)} %get-tuple-element.51.after_ref.rows_ref), channel_id=1, source_target_pairs={{1,0},{2,1},{3,2},{4,3},{5,4},{6,5},{7,6},{0,7},{9,8},{10,9},{11,1... | collective-permute-start | bytes 12296 | tf_op jit(solution)/shard_map/ppermute | solution.py:1189
